TPU v7x, 32 devices: a whole 2x2x4 slice. The times are simulated.
32 devices in a mesh: grp: 4 (over y, x), seq: 8 (over z, core).
Axes of the slice: x: 2, y: 2, z: 4, core: 2. Of those that a mesh axis runs over, the one named last changes fastest.
Arguments:
- tokens: bfloat16 [8, 4096, 1536], P('grp', 'seq'), may hold values from -6 to 6
- seg_ids: int32 [8, 4096], P('grp', 'seq'), may hold values from 0 to 7, never falling along the last dimension, each value on 1 to 2048 neighbouring positions
- cotangent: bfloat16 [8, 4096, 1536], P('grp', 'seq'), may hold values from -6 to 6
- first_gain: bfloat16 [1536], P('seq'), may hold values from 0.099609375 to 1.8984375
- in_proj: bfloat16 [1536, 4096], P('seq'), may hold values from -0.15625 to 0.15625
- conv_taps: bfloat16 [4, 2048], P(None, 'seq'), may hold values from -3 to 3
- decay_param: bfloat16 [2048], P('seq'), may hold values from 4 to 10
- gate_heads: bfloat16 [16, 128, 256], P('seq'), may hold values from -0.5 to 0.5
- out_proj: bfloat16 [2048, 1536], P('seq'), may hold values from -0.5 to 0.5
- second_gain: bfloat16 [1536], P('seq'), may hold values from 0.099609375 to 1.8984375
- up_proj: bfloat16 [1536, 9216], P('seq'), may hold values from -0.15625 to 0.15625
- down_proj: bfloat16 [4608, 1536], P('seq'), may hold values from -0.1875 to 0.1875
Outputs:
- block_out: bfloat16 [8, 4096, 1536], P('grp', 'seq')
- grad_tokens: bfloat16 [8, 4096, 1536], P('grp', 'seq')
- grad_first_gain: float32 [1536], P('seq')
- grad_in_proj: float32 [1536, 4096], P('seq')
- grad_conv_taps: float32 [4, 2048], P(None, 'seq')
- grad_decay_param: float32 [2048], P('seq')
- grad_gate_heads: float32 [16, 128, 256], P('seq')
- grad_out_proj: float32 [2048, 1536], P('seq')
- grad_second_gain: float32 [1536], P('seq')
- grad_up_proj: float32 [1536, 9216], P('seq')
- grad_down_proj: float32 [4608, 1536], P('seq')
Inputs may be any that keep to these rules, and one draw needn't show every extreme that they name: `seg_ids`: along each sequence the ids never fall and each id covers one run of consecutive tokens; a run is 1 to 2048 tokens long, and one run in each sequence has exactly that length.
All inputs are finite; a program needn't handle non-finite values.
Results may differ from a plain program's by a relative error of at most 0.012.
Values may be sent and summed in bfloat16 or wider, within the bound.
No kernel may reach another device: no remote copies, remote signals or barrier semaphores. Data moves between devices by JAX's collectives and lax.ppermute only.
A program may use at most 448 MiB of HBM per device.

v0:
```python
import jax
import jax.numpy as jnp
from jax import lax
from jax.sharding import PartitionSpec as P

D = 1536
HEADS = 16
HS = 128
LRU = 2048
FF = 4608
CONV = 4


def from_behind(value, axis, steps):
    count = lax.axis_size(axis)
    first, last = (max(0, -steps), min(count, count - steps))
    return lax.ppermute(value, axis, [(source, source + steps) for source in range(first, last)])


def prefix(part, axis, combine, identity, reverse):
    count = lax.axis_size(axis)
    place = lax.axis_index(axis)
    ahead = count - 1 - place if reverse else place
    gathered = jax.tree.map(lambda a: lax.all_gather(a, axis), part)
    state = jax.tree.map(lambda a, e: jnp.zeros_like(a) + jnp.asarray(e, a.dtype), part, identity)

    def one(step, state):
        source = count - 1 - step if reverse else step
        return combine(
            state, jax.tree.map(lambda a: lax.dynamic_index_in_dim(a, source, 0, False), gathered)
        )

    return lax.fori_loop(0, ahead, one, state)


def as_sent(shard):

    def short(part):
        return part.astype(jnp.bfloat16) if part.dtype == jnp.float32 else part

    return jax.tree.map(short, shard)


def gelu_tanh(values):
    return jax.nn.gelu(values, approximate=True)


def combine_pairs(earlier, later_pair):
    return (earlier[0] * later_pair[0], later_pair[0] * earlier[1] + later_pair[1])


def norm_back(values, scale, gain, grad_normed):
    weighted = grad_normed * gain
    grad_gain = jnp.sum(grad_normed * values * scale, axis=0)
    cubed = scale * scale * scale
    grad_values = scale * weighted - values * cubed * jnp.mean(
        weighted * values, axis=-1, keepdims=True
    )
    return (grad_gain, grad_values)


def body(
    tokens,
    seg_ids,
    cotangent,
    first_gain,
    in_proj,
    conv_taps,
    decay_param,
    gate_heads,
    out_proj,
    second_gain,
    up_proj,
    down_proj,
):
    seq_count = tokens.shape[0]
    shard_len = tokens.shape[1]
    row_count = seq_count * shard_len
    edge_len = CONV - 1
    gathered = (
        lax.all_gather(first_gain, "seq", axis=0, tiled=True),
        lax.all_gather(in_proj, "seq", axis=0, tiled=True),
        lax.all_gather(conv_taps, "seq", axis=1, tiled=True),
        lax.all_gather(decay_param, "seq", axis=0, tiled=True),
        lax.all_gather(gate_heads, "seq", axis=0, tiled=True),
        lax.all_gather(out_proj, "seq", axis=0, tiled=True),
        lax.all_gather(second_gain, "seq", axis=0, tiled=True),
        lax.all_gather(up_proj, "seq", axis=0, tiled=True),
        lax.all_gather(down_proj, "seq", axis=0, tiled=True),
    )
    gain_one, proj_in, taps_all, decay_all, gates_all, proj_out, gain_two, proj_up, proj_down = (
        gathered
    )
    inputs = tokens.reshape(row_count, D).astype(jnp.float32)
    first_scale = lax.rsqrt(jnp.mean(inputs * inputs, axis=-1, keepdims=True) + 1e-06)
    first_normed = (inputs * first_scale * gain_one.astype(jnp.float32)).astype(jnp.bfloat16)
    projected = jnp.dot(first_normed, proj_in, preferred_element_type=jnp.float32)
    inner_low = projected[:, :LRU].astype(jnp.bfloat16).reshape(seq_count, shard_len, LRU)
    gate_pre = projected[:, LRU:]
    seg_low = seg_ids.astype(jnp.float32).astype(jnp.bfloat16)
    prev_inner, prev_ids = from_behind(
        (inner_low[:, shard_len - edge_len :], seg_low[:, shard_len - edge_len :]), "seq", 1
    )
    extended = jnp.concatenate([prev_inner, inner_low], axis=1)
    own_ids = seg_low.astype(jnp.float32)
    ext_ids = jnp.concatenate([prev_ids.astype(jnp.float32), own_ids], axis=1)
    taps_float = taps_all.astype(jnp.float32)
    same_docs = []
    windows = []
    conv_sum = jnp.zeros((seq_count, shard_len, LRU), jnp.float32)
    for tap_index in range(CONV):
        offset = CONV - 1 - tap_index
        same_doc = (ext_ids[:, offset : offset + shard_len] == own_ids).astype(jnp.float32)[
            :, :, None
        ]
        window = extended[:, offset : offset + shard_len].astype(jnp.float32)
        same_docs.append(same_doc)
        windows.append(window)
        conv_sum = conv_sum + taps_float[tap_index] * window * same_doc
    conv_low = conv_sum.reshape(row_count, LRU).astype(jnp.bfloat16)
    conv_heads = conv_low.reshape(row_count, HEADS, HS)
    gate_raw = jnp.einsum("rhi,hij->rhj", conv_heads, gates_all, preferred_element_type=jnp.float32)
    rate_gate = jax.nn.sigmoid(gate_raw[:, :, :HS]).reshape(seq_count, shard_len, LRU)
    input_gate = jax.nn.sigmoid(gate_raw[:, :, HS:]).reshape(seq_count, shard_len, LRU)
    decay_float = decay_all.astype(jnp.float32)
    softened = jax.nn.softplus(-decay_float)
    decay_step = jnp.exp(-8.0 * rate_gate * softened)
    root_term = jnp.sqrt(1.0 - decay_step * decay_step + 0.001)
    conv_value = conv_low.astype(jnp.float32).reshape(seq_count, shard_len, LRU)
    drive_term = root_term * input_gate * conv_value
    before_ids = jnp.concatenate([ext_ids[:, edge_len - 1 : edge_len], own_ids[:, :-1]], axis=1)
    open_mask = (before_ids == own_ids).astype(jnp.float32)[:, :, None]
    keep_rate = decay_step * open_mask
    local_prod, local_state = lax.associative_scan(combine_pairs, (keep_rate, drive_term), axis=1)
    identity = (jnp.ones((seq_count, LRU), jnp.float32), jnp.zeros((seq_count, LRU), jnp.float32))
    carry_pair = prefix(
        (local_prod[:, -1], local_state[:, -1]), "seq", combine_pairs, identity, False
    )
    carry_in = carry_pair[1]
    lru_state = local_state + local_prod * carry_in[:, None]
    state_flat = lru_state.reshape(row_count, LRU)
    gate_act, gate_pull = jax.vjp(gelu_tanh, gate_pre)
    branch = (state_flat * gate_act).astype(jnp.bfloat16)
    mixer_out = jnp.dot(branch, proj_out, preferred_element_type=jnp.float32)
    resid = inputs + mixer_out
    second_scale = lax.rsqrt(jnp.mean(resid * resid, axis=-1, keepdims=True) + 1e-06)
    second_normed = (resid * second_scale * gain_two.astype(jnp.float32)).astype(jnp.bfloat16)
    expanded = jnp.dot(second_normed, proj_up, preferred_element_type=jnp.float32)
    up_part = expanded[:, FF:]
    ffn_gate, ffn_pull = jax.vjp(gelu_tanh, expanded[:, :FF])
    hidden = (ffn_gate * up_part).astype(jnp.bfloat16)
    ffn_out = jnp.dot(hidden, proj_down, preferred_element_type=jnp.float32)
    block_out = (resid + ffn_out).astype(jnp.bfloat16).reshape(seq_count, shard_len, D)
    again = (
        lax.all_gather(first_gain, "seq", axis=0, tiled=True),
        lax.all_gather(in_proj, "seq", axis=0, tiled=True),
        lax.all_gather(conv_taps, "seq", axis=1, tiled=True),
        lax.all_gather(decay_param, "seq", axis=0, tiled=True),
        lax.all_gather(gate_heads, "seq", axis=0, tiled=True),
        lax.all_gather(out_proj, "seq", axis=0, tiled=True),
        lax.all_gather(second_gain, "seq", axis=0, tiled=True),
        lax.all_gather(up_proj, "seq", axis=0, tiled=True),
        lax.all_gather(down_proj, "seq", axis=0, tiled=True),
    )
    (
        back_gain_one,
        back_in,
        back_taps,
        back_decay,
        back_gates,
        back_out,
        back_gain_two,
        back_up,
        back_down,
    ) = again
    grad_out = cotangent.reshape(row_count, D)
    grad_down = jnp.einsum("rf,rd->fd", hidden, grad_out, preferred_element_type=jnp.float32)
    grad_hidden = jnp.einsum("rd,fd->rf", grad_out, back_down, preferred_element_type=jnp.float32)
    grad_gate_part = ffn_pull(grad_hidden * up_part)[0]
    grad_up_part = grad_hidden * ffn_gate
    grad_expanded = jnp.concatenate([grad_gate_part, grad_up_part], axis=1).astype(jnp.bfloat16)
    grad_up = jnp.einsum(
        "rd,rf->df", second_normed, grad_expanded, preferred_element_type=jnp.float32
    )
    grad_second_normed = jnp.einsum(
        "rf,df->rd", grad_expanded, back_up, preferred_element_type=jnp.float32
    )
    grad_gain_two, grad_from_second = norm_back(
        resid, second_scale, back_gain_two.astype(jnp.float32), grad_second_normed
    )
    grad_resid = grad_out.astype(jnp.float32) + grad_from_second
    grad_mixer = grad_resid.astype(jnp.bfloat16)
    grad_out_proj = jnp.einsum("rl,rd->ld", branch, grad_mixer, preferred_element_type=jnp.float32)
    grad_branch = jnp.einsum("rd,ld->rl", grad_mixer, back_out, preferred_element_type=jnp.float32)
    grad_state = (grad_branch * gate_act).reshape(seq_count, shard_len, LRU)
    grad_gate_pre = gate_pull(grad_branch * state_flat)[0]
    keep_next = jnp.concatenate(
        [keep_rate[:, 1:], jnp.ones((seq_count, 1, LRU), jnp.float32)], axis=1
    )
    rev_prod, rev_local = lax.associative_scan(
        combine_pairs, (keep_next, grad_state), reverse=True, axis=1
    )
    back_pair = prefix(
        (local_prod[:, -1], keep_rate[:, 0] * rev_local[:, 0]), "seq", combine_pairs, identity, True
    )
    adjoint = rev_local + rev_prod * back_pair[1][:, None]
    state_prev = jnp.concatenate([carry_in[:, None], lru_state[:, :-1]], axis=1)
    grad_root = adjoint * input_gate * conv_value
    grad_decay = adjoint * state_prev * open_mask - grad_root * decay_step / root_term
    grad_log = grad_decay * decay_step
    grad_decay_param = jnp.sum(8.0 * grad_log * rate_gate, axis=(0, 1)) * jax.nn.sigmoid(
        -decay_float
    )
    grad_rate = -8.0 * grad_log * softened
    grad_input = adjoint * root_term * conv_value
    rate_part = (grad_rate * rate_gate * (1.0 - rate_gate)).reshape(row_count, HEADS, HS)
    input_part = (grad_input * input_gate * (1.0 - input_gate)).reshape(row_count, HEADS, HS)
    grad_gates = jnp.concatenate([rate_part, input_part], axis=2).astype(jnp.bfloat16)
    grad_gate_heads = jnp.einsum(
        "rhi,rhj->hij", conv_heads, grad_gates, preferred_element_type=jnp.float32
    )
    grad_conv = adjoint * root_term * input_gate + jnp.einsum(
        "rhj,hij->rhi", grad_gates, back_gates, preferred_element_type=jnp.float32
    ).reshape(seq_count, shard_len, LRU)
    back_taps_float = back_taps.astype(jnp.float32)
    tap_grads = []
    grad_ext = jnp.zeros((seq_count, shard_len + edge_len, LRU), jnp.float32)
    for tap_index in range(CONV):
        offset = CONV - 1 - tap_index
        masked = grad_conv * same_docs[tap_index]
        tap_grads.append(jnp.sum(masked * windows[tap_index], axis=(0, 1)))
        grad_ext = grad_ext + jnp.pad(
            back_taps_float[tap_index] * masked, ((0, 0), (offset, edge_len - offset), (0, 0))
        )
    grad_taps = jnp.stack(tap_grads, axis=0)
    returned = from_behind(as_sent(grad_ext[:, :edge_len]), "seq", -1)
    grad_inner = grad_ext[:, edge_len:] + jnp.pad(
        returned, ((0, 0), (shard_len - edge_len, 0), (0, 0))
    )
    grad_projected = jnp.concatenate(
        [grad_inner.reshape(row_count, LRU), grad_gate_pre], axis=1
    ).astype(jnp.bfloat16)
    grad_in = jnp.einsum(
        "rd,rp->dp", first_normed, grad_projected, preferred_element_type=jnp.float32
    )
    grad_first_normed = jnp.einsum(
        "rp,dp->rd", grad_projected, back_in, preferred_element_type=jnp.float32
    )
    grad_gain_one, grad_from_first = norm_back(
        inputs, first_scale, back_gain_one.astype(jnp.float32), grad_first_normed
    )
    grad_tokens = (
        (grad_resid + grad_from_first).astype(jnp.bfloat16).reshape(seq_count, shard_len, D)
    )
    group_sums = (
        lax.psum_scatter(grad_gain_one, "seq", scatter_dimension=0, tiled=True),
        lax.psum_scatter(grad_in, "seq", scatter_dimension=0, tiled=True),
        lax.psum_scatter(grad_taps, "seq", scatter_dimension=1, tiled=True),
        lax.psum_scatter(grad_decay_param, "seq", scatter_dimension=0, tiled=True),
        lax.psum_scatter(grad_gate_heads, "seq", scatter_dimension=0, tiled=True),
        lax.psum_scatter(grad_out_proj, "seq", scatter_dimension=0, tiled=True),
        lax.psum_scatter(grad_gain_two, "seq", scatter_dimension=0, tiled=True),
        lax.psum_scatter(grad_up, "seq", scatter_dimension=0, tiled=True),
        lax.psum_scatter(grad_down, "seq", scatter_dimension=0, tiled=True),
    )
    totals = lax.psum(
        (
            group_sums[0],
            group_sums[1],
            group_sums[2],
            group_sums[3],
            group_sums[4],
            group_sums[5],
            group_sums[6],
            group_sums[7],
            group_sums[8],
        ),
        "grp",
    )
    return (
        block_out,
        grad_tokens,
        totals[0],
        totals[1],
        totals[2],
        totals[3],
        totals[4],
        totals[5],
        totals[6],
        totals[7],
        totals[8],
    )


def solution(mesh):
    in_specs = (
        P("grp", "seq", None),
        P("grp", "seq"),
        P("grp", "seq", None),
        P("seq"),
        P("seq", None),
        P(None, "seq"),
        P("seq"),
        P("seq", None, None),
        P("seq", None),
        P("seq"),
        P("seq", None),
        P("seq", None),
    )
    out_specs = (
        P("grp", "seq", None),
        P("grp", "seq", None),
        P("seq"),
        P("seq", None),
        P(None, "seq"),
        P("seq"),
        P("seq", None, None),
        P("seq", None),
        P("seq"),
        P("seq", None),
        P("seq", None),
    )
    return jax.shard_map(body, mesh=mesh, in_specs=in_specs, out_specs=out_specs, check_vma=False)
```

profile of v0, /device:TPU:18, one launch (start us, length us, event | category | flops | bytes accessed | tf_op | source)
XLA Modules:
  0.0 3397.4 jit_solution(8177084994726809553)
XLA Ops:
  16.6 18.5 all-reduce.87
  65.6 60.7 %all-gather.10.cloned.1.call-done = bf16[1536,4096]{1,0:T(8,128)(2,1)} async-done(((bf16[192,4096]{1,0:T(8,128)(2,1)}), bf16[1536,4096]{1,0:T(8,128)(2,1)}) %all-gather.10.cloned.1.call-update) | async-done | bytes 12582928 | tf_op jit(solution)/shard_map/all_gather | solution.py:82
  126.3 17.0 fusion.109
  225.1 19.2 convert_multiply_fusion.2
  244.3 19.1 slice.711
  263.4 18.6 slice.649
  281.9 19.1 slice.646
  301.0 18.5 slice.647
  319.5 18.5 slice.648
  338.1 18.5 slice.651
  534.1 18.6 slice.736
  552.7 18.6 slice.745
  571.4 18.7 slice.738
  697.3 19.5 pad.276
  716.8 19.4 pad.277
  754.8 19.2 pad.258
  774.0 19.2 pad.259
  808.5 33.5 slice.737
  842.0 32.6 slice.746
  874.7 32.6 slice.739
  943.5 37.6 %fusion.94 = f32[1024,9216]{1,0:T(8,128)} fusion(bf16[1536,9216]{1,0:T(8,128)(2,1)} %all-gather.16.cloned.1.call-done, f32[1024,1536]{1,0:T(8,128)} %get-tuple-element.296, f32[1536]{0:T(1024)S(1)} %copy-done.89, f32[1024]{0:T(1024)S(1)} %get-tuple-element.291), kind=kOutput, calls=%fused_computation.275 | convolution fusion | flops 28995747840 | bytes 72361984 | tf_op jit(solution)/shard_map/dot_general | solution.py:148
  981.1 38.3 %fusion.6 = (bf16[1024,4608]{1,0:T(8,128)(2,1)}, bf16[1024,4608]{1,0:T(8,128)(2,1)}, bf16[1024,4608]{1,0:T(8,128)(2,1)}) fusion(f32[1024,9216]{1,0:T(8,128)} %fusion.94, bf16[1024,1536]{1,0:T(8,128)(2,1)S(1)} %bitcast.141, bf16[4608,1536]{1,0:T(8,128)(2,1)} %all-gather.18.cloned.1.call-done), kind=kOutput, calls=%fused_computation.12 | convolution fusion | flops 14618198016 | bytes 83361792 | tf_op jit(solution)/shard_map/rd,fd->rf/dot_general | solution.py:178
  1019.4 40.6 %multiply_reduce_fusion.1 = (f32[1536]{0:T(1024)}, f32[1024]{0:T(1024)S(1)}, f32[1024,1536]{1,0:T(8,128)}) fusion(f32[1024,1536]{1,0:T(8,128)} %get-tuple-element.296, f32[1024]{0:T(1024)S(1)} %get-tuple-element.291, f32[1536]{0:T(1024)S(1)} %copy-done.89, bf16[1536,9216]{1,0:T(8,128)(2,1)} %all-gather.16.cloned.1.call-done, ...), kind=kOutput, calls=%fused_computation.106 | convolution fusion | flops 29038211072 | bytes 59789312 | tf_op jit(solution)/shard_map/rf,df->rd/dot_general | solution.py:185
  1066.4 22.3 fusion.62
  1088.7 18.5 slice.742
  1107.2 18.5 slice.740
  1125.8 32.8 slice.743
  1158.6 32.6 slice.741
  1361.0 18.6 slice.806
  1381.4 33.4 slice.807
  1521.4 19.9 pad.294
  1541.3 19.4 pad.295
  1573.6 64.2 %rev.8 = f32[2,512,2048]{2,1,0:T(8,128)} reverse(f32[2,512,2048]{2,1,0:T(8,128)} %add.618), dimensions={1} | reverse | bytes 16777216 | tf_op jit(solution)/shard_map/rev | solution.py:200
  1642.7 19.2 pad.312
  1661.9 19.1 pad.313
  1692.8 64.4 %rev.9 = f32[2,512,2048]{2,1,0:T(8,128)} reverse(f32[2,512,2048]{2,1,0:T(8,128)} %add.627), dimensions={1} | reverse | bytes 16777216 | tf_op jit(solution)/shard_map/rev | solution.py:200
  1773.7 21.0 fusion.34
  1849.0 19.6 fusion.16
  1903.8 19.6 fusion.56
  1925.3 21.0 fusion.111
  1947.0 41.6 %fusion.7 = f32[1536,9216]{1,0:T(8,128)} fusion(bf16[1024,4608]{1,0:T(8,128)(2,1)} %get-tuple-element.191, bf16[1024,4608]{1,0:T(8,128)(2,1)} %get-tuple-element.190, f32[1024,1536]{1,0:T(8,128)} %get-tuple-element.296, f32[1536]{0:T(1024)S(1)} %copy-done.90, f32[1024]{0:T(1024)S(1)} %copy-done.93), kind=kOutput, calls=%fused_computation.20 | convolution fusion | flops 29033496576 | bytes 81799168 | tf_op jit(solution)/shard_map/rd,rf->df/dot_general | solution.py:182
  1990.2 235.1 %reduce-scatter.9.cloned.1.call-done = f32[192,4096]{1,0:T(8,128)} async-done(((f32[1536,4096]{1,0:T(8,128)}), f32[192,4096]{1,0:T(8,128)}) %reduce-scatter.9.cloned.1.call-update) | async-done | bytes 3145744 | tf_op jit(solution)/shard_map/reduce_scatter | solution.py:257
  2225.3 277.5 %reduce-scatter.17.cloned.1.call-done = f32[576,1536]{1,0:T(8,128)} async-done(((f32[4608,1536]{1,0:T(8,128)}), f32[576,1536]{1,0:T(8,128)}) %reduce-scatter.17.cloned.1.call-update) | async-done | bytes 3538960 | tf_op jit(solution)/shard_map/reduce_scatter | solution.py:264
  2502.9 542.8 %reduce-scatter.15.cloned.1.call-done = f32[192,9216]{1,0:T(8,128)} async-done(((f32[1536,9216]{1,0:T(8,128)}), f32[192,9216]{1,0:T(8,128)}) %reduce-scatter.15.cloned.1.call-update) | async-done | bytes 7077904 | tf_op jit(solution)/shard_map/reduce_scatter | solution.py:263
  3047.1 22.2 add_convert_fusion
  3069.3 21.5 fusion.54
  3090.7 21.6 all-reduce.84
  3130.6 246.4 %all-reduce.90.cloned.1.call-done = (f32[192,4096]{1,0:T(8,128)}, f32[2,128,256]{2,1,0:T(8,128)}, f32[256,1536]{1,0:T(8,128)}, f32[192,9216]{1,0:T(8,128)}, f32[576,1536]{1,0:T(8,128)}) async-done(((f32[192,4096]{1,0:T(8,128)}, f32[2,128,256]{2,1,0:T(8,128)}, f32[256,1536]{1,0:T(8,128)}, f32[192,9216]{1,0:T(8,128)}, f32[576,1536]{1,0:T(8,128)}), (f32[192,4096]{1,0:T(8,128)}, f32[2,128,256]{2,1,0:T(8,128)}, ...) | async-done | bytes 15597584 | tf_op jit(solution)/shard_map/psum | solution.py:266
  (591 shorter events, 932.2 us)
Async XLA Ops:
  7.2 42.7 %copy-start.97 = (bf16[256]{0:T(256)(128)(2,1)S(1)}, bf16[256]{0:T(256)(128)(2,1)}, u32[]{:S(2)}) copy-start(bf16[256]{0:T(256)(128)(2,1)} %param.22) | copy-start | bytes 1540
  7.2 119.1 %all-gather.10.cloned.1.call-start = ((), (), s32[]{:S(2)}) async-start(), calls=%async_computation.6 | async-start | bytes 14155776 | tf_op jit(solution)/shard_map/all_gather | solution.py:82
  7.9 161.7 %all-gather.12.cloned.1.call-start = ((), (), s32[]{:S(2)}) async-start(), calls=%async_computation.7 | async-start | bytes 1179648 | tf_op jit(solution)/shard_map/all_gather | solution.py:85
  8.7 922.2 %all-gather.14.cloned.1.call-start = ((), (), s32[]{:S(2)}) async-start(), calls=%async_computation.8 | async-start | bytes 7077888 | tf_op jit(solution)/shard_map/all_gather | solution.py:86
  9.4 934.1 %all-gather.16.cloned.1.call-start = ((), (), s32[]{:S(2)}) async-start(), calls=%async_computation.9 | async-start | bytes 31850496 | tf_op jit(solution)/shard_map/all_gather | solution.py:88
  10.0 971.1 %all-gather.18.cloned.1.call-start = ((), (), s32[]{:S(2)}) async-start(), calls=%async_computation.10 | async-start | bytes 15925248 | tf_op jit(solution)/shard_map/all_gather | solution.py:89
  10.7 138.6 %copy-start.71 = (f32[2,512]{1,0:T(2,128)}, f32[2,512]{1,0:T(2,128)S(1)}, u32[]{:S(2)}) copy-start(f32[2,512]{1,0:T(2,128)S(1)} %get-tuple-element.188) | copy-start | bytes 12292
  10.8 54.7 %collective-permute-start.1 = (bf16[2,3]{1,0:T(2,128)(2,1)S(1)}, bf16[2,3]{1,0:T(2,128)(2,1)S(1)}, u32[]{:S(2)}, u32[]{:S(2)}) collective-permute-start(bf16[2,3]{1,0:T(2,128)(2,1)S(1)} %slice.834), channel_id=1, source_target_pairs={{0,1},{1,2},{2,3},{3,4},{4,5},{5,6},{6,7},{8,9},{9,10},{10,11},{11... | collective-permute-start | bytes 44 | tf_op jit(solution)/shard_map/ppermute | solution.py:17
  12.8 1977.4 %reduce-scatter.11.cloned.1.call-start = ((), (), s32[]{:S(2)}) async-start(), calls=%async_computation.12 | async-start | bytes 2359296 | tf_op jit(solution)/shard_map/reduce_scatter | solution.py:260
  35.0 108.4 %copy-start.55 = (f32[1536]{0:T(1024)}, f32[1536]{0:T(1024)S(1)}, u32[]{:S(2)}) copy-start(f32[1536]{0:T(1024)S(1)} %convert_element_type.121) | copy-start | bytes 18436
  35.8 107.6 %copy-start.84 = (f32[1,4,2,128]{3,1,2,0:T(4,128)}, f32[1,4,2,128]{3,1,2,0:T(4,128)S(1)}, u32[]{:S(2)}) copy-start(f32[1,4,2,128]{3,1,2,0:T(4,128)S(1)} %copy.45) | copy-start | bytes 12292
  49.9 99.5 %copy-start.57 = (f32[1,2048]{1,0:T(1,128)}, f32[1,2048]{1,0:T(1,128)S(1)}, u32[]{:S(2)}) copy-start(f32[1,2048]{1,0:T(1,128)S(1)} %get-tuple-element.281) | copy-start | bytes 24580
  49.9 99.5 %copy-start.59 = (f32[1,2048]{1,0:T(1,128)}, f32[1,2048]{1,0:T(1,128)S(1)}, u32[]{:S(2)}) copy-start(f32[1,2048]{1,0:T(1,128)S(1)} %get-tuple-element.282) | copy-start | bytes 24580
  49.9 99.5 %copy-start.61 = (f32[1,2048]{1,0:T(1,128)}, f32[1,2048]{1,0:T(1,128)S(1)}, u32[]{:S(2)}) copy-start(f32[1,2048]{1,0:T(1,128)S(1)} %get-tuple-element.283) | copy-start | bytes 24580
  49.9 99.5 %copy-start.63 = (f32[1,2048]{1,0:T(1,128)}, f32[1,2048]{1,0:T(1,128)S(1)}, u32[]{:S(2)}) copy-start(f32[1,2048]{1,0:T(1,128)S(1)} %get-tuple-element.284) | copy-start | bytes 24580
  62.5 162.6 %copy-start.53 = (f32[2048]{0:T(1024)}, f32[2048]{0:T(1024)S(1)}, u32[]{:S(2)}) copy-start(f32[2048]{0:T(1024)S(1)} %fusion.87) | copy-start | bytes 24580
  144.1 5.2 collective-permute-start
  146.6 78.4 %copy-start.86 = (f32[2,512]{1,0:T(2,128)}, f32[2,512]{1,0:T(2,128)S(1)}, u32[]{:S(2)}) copy-start(f32[2,512]{1,0:T(2,128)S(1)} %get-tuple-element.292) | copy-start | bytes 12292
  552.7 38.1 %copy-start.76 = (f32[2,1,2048]{2,1,0:T(1,128)S(1)}, f32[2,1,2048]{2,1,0:T(1,128)}, u32[]{:S(2)}) copy-start(f32[2,1,2048]{2,1,0:T(1,128)} %slice.852) | copy-start | bytes 49156
  552.7 38.4 %copy-start.75 = (f32[2,1,2048]{2,1,0:T(1,128)S(1)}, f32[2,1,2048]{2,1,0:T(1,128)}, u32[]{:S(2)}) copy-start(f32[2,1,2048]{2,1,0:T(1,128)} %slice.881) | copy-start | bytes 49156
  943.5 116.6 %copy-start.92 = (f32[1024]{0:T(1024)}, f32[1024]{0:T(1024)S(1)}, u32[]{:S(2)}) copy-start(f32[1024]{0:T(1024)S(1)} %get-tuple-element.291) | copy-start | bytes 12292
  1019.4 40.7 %copy-start.22 = (f32[1024,1536]{1,0:T(8,128)S(1)}, f32[1024,1536]{1,0:T(8,128)}, u32[]{:S(2)}) copy-start(f32[1024,1536]{1,0:T(8,128)} %get-tuple-element.296) | copy-start | bytes 18874372
  1019.4 40.7 %copy-start.94 = (f32[1024]{0:T(1024)S(1)}, f32[1024]{0:T(1024)}, u32[]{:S(2)}) copy-start(f32[1024]{0:T(1024)} %get-tuple-element.290) | copy-start | bytes 12292
  1360.8 54.0 %copy-start.47 = (f32[2,2,2048]{2,1,0:T(2,128)S(1)}, f32[2,2,2048]{2,1,0:T(2,128)}, u32[]{:S(2)}) copy-start(f32[2,2,2048]{2,1,0:T(2,128)} %pad_add_fusion.1) | copy-start | bytes 98308
  1360.8 54.1 %copy-start.82 = (f32[2,1,2048]{2,1,0:T(1,128)S(1)}, f32[2,1,2048]{2,1,0:T(1,128)}, u32[]{:S(2)}) copy-start(f32[2,1,2048]{2,1,0:T(1,128)} %get-tuple-element.255) | copy-start | bytes 49156
  1360.9 54.1 %copy-start.83 = (f32[2,1,2048]{2,1,0:T(1,128)S(1)}, f32[2,1,2048]{2,1,0:T(1,128)}, u32[]{:S(2)}) copy-start(f32[2,1,2048]{2,1,0:T(1,128)} %get-tuple-element.256) | copy-start | bytes 49156
  1360.9 54.2 %copy-start.48 = (f32[2,2,2048]{2,1,0:T(2,128)S(1)}, f32[2,2,2048]{2,1,0:T(2,128)}, u32[]{:S(2)}) copy-start(f32[2,2,2048]{2,1,0:T(2,128)} %pad_add_fusion.2) | copy-start | bytes 98308
  1360.9 54.2 %copy-start.80 = (f32[2,1,2048]{2,1,0:T(1,128)S(1)}, f32[2,1,2048]{2,1,0:T(1,128)}, u32[]{:S(2)}) copy-start(f32[2,1,2048]{2,1,0:T(1,128)} %get-tuple-element.257) | copy-start | bytes 49156
  1360.9 54.2 %copy-start.81 = (f32[2,1,2048]{2,1,0:T(1,128)S(1)}, f32[2,1,2048]{2,1,0:T(1,128)}, u32[]{:S(2)}) copy-start(f32[2,1,2048]{2,1,0:T(1,128)} %get-tuple-element.258) | copy-start | bytes 49156
  1360.9 54.4 %copy-start.43 = (f32[2,3,2048]{2,1,0:T(4,128)S(1)}, f32[2,3,2048]{2,1,0:T(4,128)}, u32[]{:S(2)}) copy-start(f32[2,3,2048]{2,1,0:T(4,128)} %slice.777) | copy-start | bytes 147460
  1360.9 54.4 %copy-start.44 = (f32[2,3,2048]{2,1,0:T(4,128)S(1)}, f32[2,3,2048]{2,1,0:T(4,128)}, u32[]{:S(2)}) copy-start(f32[2,3,2048]{2,1,0:T(4,128)} %slice.794) | copy-start | bytes 147460
  1360.9 54.5 %copy-start.79 = (f32[2,1,2048]{2,1,0:T(1,128)S(1)}, f32[2,1,2048]{2,1,0:T(1,128)}, u32[]{:S(2)}) copy-start(f32[2,1,2048]{2,1,0:T(1,128)} %slice.942) | copy-start | bytes 49156
  1360.9 55.0 %copy-start.78 = (f32[2,1,2048]{2,1,0:T(1,128)S(1)}, f32[2,1,2048]{2,1,0:T(1,128)}, u32[]{:S(2)}) copy-start(f32[2,1,2048]{2,1,0:T(1,128)} %slice.914) | copy-start | bytes 49156
  1360.9 55.1 %copy-start.37 = (f32[2,7,2048]{2,1,0:T(8,128)S(1)}, f32[2,7,2048]{2,1,0:T(8,128)}, u32[]{:S(2)}) copy-start(f32[2,7,2048]{2,1,0:T(8,128)} %slice.771) | copy-start | bytes 344068
  1360.9 55.1 %copy-start.38 = (f32[2,7,2048]{2,1,0:T(8,128)S(1)}, f32[2,7,2048]{2,1,0:T(8,128)}, u32[]{:S(2)}) copy-start(f32[2,7,2048]{2,1,0:T(8,128)} %slice.796) | copy-start | bytes 344068
  1692.8 80.9 %copy-start.54 = (f32[2048]{0:T(1024)S(1)}, f32[2048]{0:T(1024)}, u32[]{:S(2)}) copy-start(f32[2048]{0:T(1024)} %copy-done.53) | copy-start | bytes 24580
  1692.8 80.9 %copy-start.73 = (f32[2,1,2048]{2,1,0:T(1,128)S(1)}, f32[2,1,2048]{2,1,0:T(1,128)}, u32[]{:S(2)}) copy-start(f32[2,1,2048]{2,1,0:T(1,128)} %broadcast_in_dim.5) | copy-start | bytes 49156
  1692.8 80.9 %copy-start.87 = (f32[2,512]{1,0:T(2,128)S(1)}, f32[2,512]{1,0:T(2,128)}, u32[]{:S(2)}) copy-start(f32[2,512]{1,0:T(2,128)} %copy-done.86) | copy-start | bytes 12292
  1810.8 179.4 %reduce-scatter.13.cloned.1.call-start = ((), (), s32[]{:S(2)}) async-start(), calls=%async_computation.13 | async-start | bytes 14155776 | tf_op jit(solution)/shard_map/reduce_scatter | solution.py:261
  1824.1 401.3 %reduce-scatter.9.cloned.1.call-start = ((), (), s32[]{:S(2)}) async-start(), calls=%async_computation.11 | async-start | bytes 28311552 | tf_op jit(solution)/shard_map/reduce_scatter | solution.py:257
  1894.2 6.3 collective-permute-start.2
  1923.4 579.4 %reduce-scatter.17.cloned.1.call-start = ((), (), s32[]{:S(2)}) async-start(), calls=%async_computation.15 | async-start | bytes 31850496 | tf_op jit(solution)/shard_map/reduce_scatter | solution.py:264
  1946.3 1099.3 %reduce-scatter.15.cloned.1.call-start = ((), (), s32[]{:S(2)}) async-start(), calls=%async_computation.14 | async-start | bytes 63700992 | tf_op jit(solution)/shard_map/reduce_scatter | solution.py:263
  1988.6 1131.6 %reduce-scatter.19.cloned.1.call-start = ((), (), s32[]{:S(2)}) async-start(), calls=%async_computation.16 | async-start | bytes 1179648
  1990.1 1056.9 %copy-start.85 = (f32[1,4,2,128]{3,1,2,0:T(4,128)S(1)}, f32[1,4,2,128]{3,1,2,0:T(4,128)}, u32[]{:S(2)}) copy-start(f32[1,4,2,128]{3,1,2,0:T(4,128)} %copy-done.84) | copy-start | bytes 12292
  1990.1 1057.0 %copy-start.88 = (f32[2048]{0:T(1024)S(1)}, f32[2048]{0:T(1024)}, u32[]{:S(2)}) copy-start(f32[2048]{0:T(1024)} %get-tuple-element.192) | copy-start | bytes 24580
  1990.1 1057.0 %copy-start.91 = (f32[8,1,256]{2,1,0:T(1,128)S(1)}, f32[8,1,256]{2,1,0:T(1,128)}, u32[]{:S(2)}) copy-start(f32[8,1,256]{2,1,0:T(1,128)} %get-tuple-element.285) | copy-start | bytes 24580
  1990.1 1386.9 %all-reduce.90.cloned.1.call-start = ((), (), s32[]{:S(2)}) async-start(), calls=%async_computation.17 | async-start | bytes 31195136 | tf_op jit(solution)/shard_map/psum | solution.py:266
  (65 other events, 1071.3 us)
Sparse Core Ops, SparseCore 0:
  9.7 116.6 all-gather.9
  127.9 21.7 all-gather.11
  151.3 63.3 all-gather.13
  216.3 243.8 all-gather.15
  461.6 127.8 all-gather.17
  1810.9 32.1 reduce-scatter.10
  1845.4 131.8 reduce-scatter.12
  1979.6 245.6 reduce-scatter.8
  2227.7 275.1 reduce-scatter.16
  2505.1 540.5 reduce-scatter.14
  3048.6 27.1 reduce-scatter.18
  3080.8 296.2 all-reduce.89
where the time goes:
time: 3440 us; the launch traced here: 3400 us
  waiting for transfers between devices  1370 us (40%)
  local copies, waits for them, and re-layouts  1220 us (35%)
  other arithmetic  348 us (10%)
  matrix products  320 us (9%)
  blocking collectives  115 us (3%)
    reduce_scatter x1, waiting for transfers between devices, body(): lax.psum_scatter(grad_up, 'seq', scatter_dimension=0, tiled=True)  543 us
    slice x65, local copies, waits for them, and re-layouts, body(): lax.associative_scan(combine_pairs, (keep_next, grad_state), reverse=True...  448 us
    reduce_scatter x1, waiting for transfers between devices, body(): lax.psum_scatter(grad_down, 'seq', scatter_dimension=0, tiled=True)  278 us
    slice x60, local copies, waits for them, and re-layouts, body(): lax.associative_scan(combine_pairs, (keep_rate, drive_term), axis=1)  252 us
    psum x1, waiting for transfers between devices, body(): lax.psum((group_sums[0], group_sums[1], group_sums[2], group_sums[3], gro...  246 us
    reduce_scatter x1, waiting for transfers between devices, body(): lax.psum_scatter(grad_in, 'seq', scatter_dimension=0, tiled=True)  235 us
    pad x32, local copies, waits for them, and re-layouts, body(): lax.associative_scan(combine_pairs, (keep_next, grad_state), reverse=True...  129 us
    pad x32, local copies, waits for them, and re-layouts, body(): lax.associative_scan(combine_pairs, (keep_rate, drive_term), axis=1)  129 us
  transfers between devices with their start and end apart: 15, of which 7 were waited for; matrix products, arithmetic and copies ran while one was open for 31% of the time, Pallas kernels for 0%

commit v1 on v0

v1 whole, which is shorter than its diff:
```python
import functools

import jax
import jax.numpy as jnp
from jax import lax
from jax.experimental import pallas as pl
from jax.experimental.pallas import tpu as pltpu
from jax.sharding import PartitionSpec as P

D = 1536
HEADS = 16
HS = 128
LRU = 2048
FF = 4608
CONV = 4
CHUNKS = 8
HALO = 8
F32 = jnp.float32
BF16 = jnp.bfloat16


def from_behind(value, axis, steps):
    count = lax.axis_size(axis)
    first, last = (max(0, -steps), min(count, count - steps))
    return lax.ppermute(value, axis, [(source, source + steps) for source in range(first, last)])


def gelu_parts(v):
    k = 0.7978845608028654
    square = v * v
    t = jnp.tanh(k * v * (1.0 + 0.044715 * square))
    half = 0.5 * (1.0 + t)
    slope = half + 0.5 * v * (1.0 - t * t) * (k * (1.0 + 3.0 * 0.044715 * square))
    return v * half, slope


def gelu_tanh(v):
    k = 0.7978845608028654
    return 0.5 * v * (1.0 + jnp.tanh(k * v * (1.0 + 0.044715 * v * v)))


def sigmoid(v):
    return 0.5 * jnp.tanh(0.5 * v) + 0.5


def drive_values(q_rate, q_input, soft):
    rate = sigmoid(q_rate)
    inp = sigmoid(q_input)
    decay = jnp.exp(-8.0 * rate * soft)
    root = jnp.sqrt(1.0 - decay * decay + 0.001)
    return rate, inp, decay, root


def mixer_forward_kernel(
    u_ref, halo_ref, dist_ref, gates_ref, taps_ref, soft_ref,
    c_ref, keep_ref, state_ref, prod_ref, chunk_ref,
    ext_s, c_s, rate_s, inp_s,
):
    seqs, rows, _ = u_ref.shape
    step = rows // CHUNKS
    soft = soft_ref[...]
    for b in range(seqs):
        ext_s[b, pl.ds(0, HALO), :] = halo_ref[b].astype(F32)
        ext_s[b, pl.ds(HALO, rows), :] = u_ref[b].astype(F32)

        def conv_chunk(n, _):
            at = pl.multiple_of(n * 64, 64)
            total = taps_ref[0:1, :] * ext_s[b, pl.ds(at + HALO, 64), :]
            for k in range(1, CONV):
                same = (dist_ref[b, pl.ds(at, 64), :] >= float(k)).astype(F32)
                total = total + taps_ref[k : k + 1, :] * ext_s[b, pl.ds(at + HALO - k, 64), :] * same
            low = total.astype(BF16)
            c_ref[b, pl.ds(at, 64), :] = low
            c_s[b, pl.ds(at, 64), :] = low.astype(F32)
            return 0

        lax.fori_loop(0, rows // 64, conv_chunk, 0)
        both = jnp.dot(c_ref[b], gates_ref[0], preferred_element_type=F32)
        rate_s[b] = both[:, :HS]
        inp_s[b] = both[:, HS:]

    def scan_step(j, carry):
        new = []
        for b in range(seqs):
            at = pl.ds(j, CHUNKS, stride=step)
            state, prod = carry[b]
            _, inp, decay, root = drive_values(rate_s[b, at, :], inp_s[b, at, :], soft)
            keep = decay * (dist_ref[b, at, :] >= 1.0).astype(F32)
            state = keep * state + root * inp * c_s[b, at, :]
            prod = keep * prod
            keep_ref[b, at, :] = keep
            state_ref[b, at, :] = state
            prod_ref[b, at, :] = prod
            new.append((state, prod))
        return tuple(new)

    zero, one = jnp.zeros((CHUNKS, HS), F32), jnp.ones((CHUNKS, HS), F32)
    ends = lax.fori_loop(0, step, scan_step, ((zero, one),) * seqs, unroll=4)
    for b in range(seqs):
        chunk_ref[b, 0] = ends[b][0]
        chunk_ref[b, 1] = ends[b][1]


def reverse_kernel(
    grad_ref, gate_ref, keep_ref, state_ref,
    dg_ref, local_ref, prod_ref, chunk_ref,
    dh_s,
):
    seqs, rows, _ = grad_ref.shape
    step = rows // CHUNKS
    for b in range(seqs):

        def point(n, _):
            at = pl.ds(pl.multiple_of(n * 64, 64), 64)
            act, slope = gelu_parts(gate_ref[b, at, :])
            grad = grad_ref[b, at, :]
            dh_s[b, at, :] = grad * act
            dg_ref[b, at, :] = (grad * state_ref[b, at, :] * slope).astype(BF16)
            return 0

        lax.fori_loop(0, rows // 64, point, 0)

    def scan_step(n, carry):
        j = step - 1 - n
        new = []
        for b in range(seqs):
            at = pl.ds(j, CHUNKS, stride=step)
            pull, prod = carry[b]
            keep = keep_ref[b, at, :]
            local = dh_s[b, at, :] + pull
            local_ref[b, at, :] = local
            prod_ref[b, at, :] = prod
            new.append((keep * local, keep * prod))
        return tuple(new)

    zero, one = jnp.zeros((CHUNKS, HS), F32), jnp.ones((CHUNKS, HS), F32)
    ends = lax.fori_loop(0, step, scan_step, ((zero, one),) * seqs, unroll=4)
    for b in range(seqs):
        chunk_ref[b, 0] = ends[b][0]
        chunk_ref[b, 1] = ends[b][1]


def mixer_backward_kernel(
    local_ref, prod_ref, carry_ref, state_ref, before_ref, c_ref, u_ref, halo_ref, dist_ref,
    gates_ref, taps_ref, soft_ref,
    du_ref, tail_ref, edge_ref, ggate_ref, gtaps_ref, gdecay_ref,
    q_s, dq_s, dc_s, h_s, ext_s, dist_s,
):
    seqs, rows, _ = local_ref.shape
    step = rows // CHUNKS
    soft = soft_ref[...]
    ggate = jnp.zeros((HS, 2 * HS), F32)
    decay_sum = jnp.zeros((8, HS), F32)
    taps_sum = [jnp.zeros((8, HS), F32) for _ in range(CONV)]

    def fold(value):
        return jnp.sum(value.reshape(value.shape[0] // 8, 8, HS), axis=0)

    for b in range(seqs):
        q_s[...] = jnp.dot(c_ref[b], gates_ref[0], preferred_element_type=F32)
        h_s[pl.ds(0, HALO), :] = before_ref[b]
        h_s[pl.ds(HALO, rows), :] = state_ref[b]

        def point(n, total):
            at = pl.ds(pl.multiple_of(n * step, step), step)
            lam = local_ref[b, at, :] + prod_ref[b, at, :] * carry_ref[b, pl.ds(n, 1), :]
            rate, inp, decay, root = drive_values(q_s[at, :HS], q_s[at, HS:], soft)
            conv = c_ref[b, at, :].astype(F32)
            is_open = (dist_ref[b, at, :] >= 1.0).astype(F32)
            prev = h_s[pl.ds(pl.multiple_of(n * step, step) + HALO - 1, step), :]
            lam_root = lam * root
            lam_inp = lam * inp
            grad_decay = lam * prev * is_open - lam_inp * conv * decay / root
            grad_log = grad_decay * decay
            rated = grad_log * rate
            dq_s[at, :HS] = (-8.0 * soft * rated * (1.0 - rate)).astype(BF16)
            dq_s[at, HS:] = (lam_root * conv * inp * (1.0 - inp)).astype(BF16)
            dc_s[at, :] = lam_root * inp
            return total + fold(rated)

        decay_sum = lax.fori_loop(0, CHUNKS, point, decay_sum)
        dc_s[pl.ds(0, rows), :] += lax.dot_general(
            dq_s[...], gates_ref[0], (((1,), (1,)), ((), ())), preferred_element_type=F32
        )
        dc_s[pl.ds(rows, HALO), :] = jnp.zeros((HALO, HS), F32)
        ggate = ggate + lax.dot_general(
            c_ref[b], dq_s[...], (((0,), (0,)), ((), ())), preferred_element_type=F32
        )
        ext_s[pl.ds(0, HALO), :] = halo_ref[b].astype(F32)
        ext_s[pl.ds(HALO, rows), :] = u_ref[b].astype(F32)
        dist_s[pl.ds(0, rows), :] = dist_ref[b]
        dist_s[pl.ds(rows, HALO), :] = jnp.zeros((HALO, HS), F32)

        def conv_chunk(n, totals):
            at = pl.multiple_of(n * 64, 64)
            grad = dc_s[pl.ds(at, 64), :]
            far = dist_s[pl.ds(at, 64), :]
            out = taps_ref[0:1, :] * grad
            totals = list(totals)
            totals[0] = totals[0] + fold(grad * ext_s[pl.ds(at + HALO, 64), :])
            for k in range(1, CONV):
                masked = jnp.where(far >= float(k), grad, 0.0)
                totals[k] = totals[k] + fold(masked * ext_s[pl.ds(at + HALO - k, 64), :])
                ahead = jnp.where(
                    dist_s[pl.ds(at + k, 64), :] >= float(k), dc_s[pl.ds(at + k, 64), :], 0.0
                )
                out = out + taps_ref[k : k + 1, :] * ahead
            du_ref[b, pl.ds(at, 64), :] = out.astype(BF16)

            @pl.when(n == rows // 64 - 1)
            def _():
                tail_ref[b] = out[64 - HALO :, :]

            return tuple(totals)

        taps_sum = list(lax.fori_loop(0, rows // 64, conv_chunk, tuple(taps_sum)))
        head = dc_s[pl.ds(0, HALO), :]
        far = dist_s[pl.ds(0, HALO), :]
        zeros = jnp.zeros((HALO, HS), F32)
        edge = zeros
        for k in range(1, CONV):
            masked = jnp.where(far >= float(k), head, 0.0)
            both = jnp.concatenate([zeros, masked], axis=0)
            edge = edge + taps_ref[k : k + 1, :] * both[k : k + HALO, :]
        edge_ref[b] = edge
    ggate_ref[0] = ggate
    gdecay_ref[...] = jnp.broadcast_to(
        8.0 * jnp.sum(decay_sum, axis=0, keepdims=True), (8, HS)
    )
    gtaps_ref[...] = jnp.concatenate(
        [jnp.sum(t, axis=0, keepdims=True) for t in taps_sum] + [jnp.zeros((8 - CONV, HS), F32)],
        axis=0,
    )


def head_block(lead, rows):
    return pl.BlockSpec((lead, rows, HS), lambda h: (0, 0, h))


def shared_block(shape):
    return pl.BlockSpec(shape, lambda h: (0,) * len(shape))


def pair_block(seqs):
    return pl.BlockSpec((seqs, 2, CHUNKS, HS), lambda h: (0, 0, 0, h))


PARAMS = pltpu.CompilerParams(vmem_limit_bytes=40 * 1024 * 1024)


def mixer_forward(u, halo, dist, gates, taps, soft):
    seqs, rows, _ = u.shape
    full = head_block(seqs, rows)
    wide = jax.ShapeDtypeStruct((seqs, rows, LRU), F32)
    return pl.pallas_call(
        mixer_forward_kernel,
        grid=(HEADS,),
        in_specs=[
            full,
            head_block(seqs, HALO),
            shared_block((seqs, rows, HS)),
            pl.BlockSpec((1, HS, 2 * HS), lambda h: (h, 0, 0)),
            pl.BlockSpec((CONV, HS), lambda h: (0, h)),
            pl.BlockSpec((1, HS), lambda h: (0, h)),
        ],
        out_specs=[full, full, full, full, pair_block(seqs)],
        out_shape=[
            jax.ShapeDtypeStruct((seqs, rows, LRU), BF16),
            wide,
            wide,
            wide,
            jax.ShapeDtypeStruct((seqs, 2, CHUNKS, LRU), F32),
        ],
        scratch_shapes=[
            pltpu.VMEM((seqs, rows + HALO, HS), F32),
            pltpu.VMEM((seqs, rows, HS), F32),
            pltpu.VMEM((seqs, rows, HS), F32),
            pltpu.VMEM((seqs, rows, HS), F32),
        ],
        compiler_params=PARAMS,
        name="mixer_forward",
    )(u, halo, dist, gates, taps, soft)


def mixer_reverse(grad, gate, keep, state):
    seqs, rows, _ = grad.shape
    full = head_block(seqs, rows)
    wide = jax.ShapeDtypeStruct((seqs, rows, LRU), F32)
    return pl.pallas_call(
        reverse_kernel,
        grid=(HEADS,),
        in_specs=[full, full, full, full],
        out_specs=[full, full, full, pair_block(seqs)],
        out_shape=[
            jax.ShapeDtypeStruct((seqs, rows, LRU), BF16),
            wide,
            wide,
            jax.ShapeDtypeStruct((seqs, 2, CHUNKS, LRU), F32),
        ],
        scratch_shapes=[pltpu.VMEM((seqs, rows, HS), F32)],
        compiler_params=PARAMS,
        name="mixer_reverse",
    )(grad, gate, keep, state)


def mixer_backward(local, prod, carry, state, before, c, u, halo, dist, gates, taps, soft):
    seqs, rows, _ = local.shape
    full = head_block(seqs, rows)
    small = head_block(seqs, HALO)
    gate_block = pl.BlockSpec((1, HS, 2 * HS), lambda h: (h, 0, 0))
    row_block = pl.BlockSpec((8, HS), lambda h: (0, h))
    return pl.pallas_call(
        mixer_backward_kernel,
        grid=(HEADS,),
        in_specs=[
            full,
            full,
            head_block(seqs, CHUNKS),
            full,
            small,
            full,
            full,
            small,
            shared_block((seqs, rows, HS)),
            gate_block,
            pl.BlockSpec((CONV, HS), lambda h: (0, h)),
            pl.BlockSpec((1, HS), lambda h: (0, h)),
        ],
        out_specs=[full, small, small, gate_block, row_block, row_block],
        out_shape=[
            jax.ShapeDtypeStruct((seqs, rows, LRU), BF16),
            jax.ShapeDtypeStruct((seqs, HALO, LRU), F32),
            jax.ShapeDtypeStruct((seqs, HALO, LRU), F32),
            jax.ShapeDtypeStruct((HEADS, HS, 2 * HS), F32),
            jax.ShapeDtypeStruct((8, LRU), F32),
            jax.ShapeDtypeStruct((8, LRU), F32),
        ],
        scratch_shapes=[
            pltpu.VMEM((rows, 2 * HS), F32),
            pltpu.VMEM((rows, 2 * HS), BF16),
            pltpu.VMEM((rows + HALO, HS), F32),
            pltpu.VMEM((rows + HALO, HS), F32),
            pltpu.VMEM((rows + HALO, HS), F32),
            pltpu.VMEM((rows + HALO, HS), F32),
        ],
        compiler_params=PARAMS,
        name="mixer_backward",
    )(local, prod, carry, state, before, c, u, halo, dist, gates, taps, soft)


def gather_rows(shard):
    parts = lax.axis_size("grp")
    rows = shard.shape[0] // parts
    own = lax.dynamic_slice_in_dim(shard, lax.axis_index("grp") * rows, rows, 0)
    return lax.all_gather(own, ("seq", "grp"), axis=0, tiled=True)


def reduce_rows(partial):
    part = lax.psum_scatter(partial, ("seq", "grp"), scatter_dimension=0, tiled=True)
    return lax.all_gather(part, "grp", axis=0, tiled=True).astype(F32)


def shard_carry(ends, prods, reverse):
    count = lax.axis_size("seq")
    place = lax.axis_index("seq")
    both = lax.all_gather(jnp.stack([ends, prods]), "seq")
    carry = jnp.zeros_like(ends)
    for step in range(count - 1):
        source = count - 1 - step if reverse else step
        ahead = source > place if reverse else source < place
        carry = jnp.where(ahead, both[source, 0] + both[source, 1] * carry, carry)
    return carry


def chunk_ends(chunks, reverse):
    state = jnp.zeros_like(chunks[:, 0, 0])
    prod = jnp.ones_like(state)
    order = range(CHUNKS - 1, -1, -1) if reverse else range(CHUNKS)
    for n in order:
        state = chunks[:, 0, n] + chunks[:, 1, n] * state
        prod = chunks[:, 1, n] * prod
    return state, prod


def chunk_carries(chunks, carry, reverse):
    order = range(CHUNKS - 1, -1, -1) if reverse else range(CHUNKS)
    found = [None] * CHUNKS
    for n in order:
        found[n] = carry
        carry = chunks[:, 0, n] + chunks[:, 1, n] * carry
    return jnp.stack(found, axis=1)


def norm_back(values, scale, gain, grad_normed):
    weighted = grad_normed * gain
    grad_gain = jnp.sum(grad_normed * values * scale, axis=0)
    cubed = scale * scale * scale
    grad_values = scale * weighted - values * cubed * jnp.mean(
        weighted * values, axis=-1, keepdims=True
    )
    return (grad_gain, grad_values)


def body(
    tokens, seg_ids, cotangent, first_gain, in_proj, conv_taps, decay_param, gate_heads,
    out_proj, second_gain, up_proj, down_proj,
):
    seq_count, shard_len, _ = tokens.shape
    row_count = seq_count * shard_len
    edge_len = CONV - 1
    place = lax.axis_index("seq")
    last = lax.axis_size("seq") - 1

    small = jnp.concatenate(
        [first_gain, second_gain, decay_param, conv_taps.reshape(-1)]
    )
    small_all = lax.all_gather(small, "seq")
    n_gain, n_lru = first_gain.shape[0], decay_param.shape[0]
    gain_one = small_all[:, :n_gain].reshape(D).astype(F32)
    gain_two = small_all[:, n_gain : 2 * n_gain].reshape(D).astype(F32)
    decay_float = small_all[:, 2 * n_gain : 2 * n_gain + n_lru].reshape(LRU).astype(F32)
    taps_all = (
        small_all[:, 2 * n_gain + n_lru :].reshape(-1, CONV, n_lru).transpose(1, 0, 2)
    ).reshape(CONV, LRU).astype(F32)
    proj_in = gather_rows(in_proj)
    gates_all = lax.all_gather(gate_heads, "seq", axis=0, tiled=True)
    proj_out = gather_rows(out_proj)
    proj_up = gather_rows(up_proj)
    proj_down = gather_rows(down_proj)

    inputs = tokens.reshape(row_count, D).astype(F32)
    first_scale = lax.rsqrt(jnp.mean(inputs * inputs, axis=-1, keepdims=True) + 1e-06)
    first_normed = (inputs * first_scale * gain_one).astype(BF16)
    inner_low = jnp.dot(first_normed, proj_in[:, :LRU], preferred_element_type=F32).astype(BF16)
    inner_low = inner_low.reshape(seq_count, shard_len, LRU)
    gate_pre = jnp.dot(first_normed, proj_in[:, LRU:], preferred_element_type=F32)

    prev_inner = from_behind(inner_low[:, shard_len - HALO :], "seq", 1)
    prev_ids = from_behind(seg_ids[:, shard_len - edge_len :], "seq", 1)
    prev_ids = jnp.where(place == 0, -1, prev_ids)
    ext_ids = jnp.concatenate([prev_ids, seg_ids], axis=1)
    dist = jnp.zeros((seq_count, shard_len), F32)
    for k in range(1, CONV):
        dist = dist + (ext_ids[:, edge_len - k : edge_len - k + shard_len] == seg_ids).astype(F32)
    dist = jnp.broadcast_to(dist[:, :, None], (seq_count, shard_len, HS))
    soft = jax.nn.softplus(-decay_float).reshape(1, LRU)

    conv_low, keep, state_part, prod_part, chunks = mixer_forward(
        inner_low, prev_inner, dist, gates_all, taps_all, soft
    )
    end_state, end_prod = chunk_ends(chunks, False)
    carry_in = shard_carry(end_state, end_prod, False)
    carries = chunk_carries(chunks, carry_in, False)
    chunked = (seq_count, CHUNKS, shard_len // CHUNKS, LRU)
    state = (
        state_part.reshape(chunked) + prod_part.reshape(chunked) * carries[:, :, None, :]
    ).reshape(row_count, LRU)
    branch = (state * gelu_tanh(gate_pre)).astype(BF16)
    resid = inputs + jnp.dot(branch, proj_out, preferred_element_type=F32)
    second_scale = lax.rsqrt(jnp.mean(resid * resid, axis=-1, keepdims=True) + 1e-06)
    second_normed = (resid * second_scale * gain_two).astype(BF16)
    expanded_gate = jnp.dot(second_normed, proj_up[:, :FF], preferred_element_type=F32)
    expanded_up = jnp.dot(second_normed, proj_up[:, FF:], preferred_element_type=F32)
    hidden = (gelu_tanh(expanded_gate) * expanded_up).astype(BF16)
    ffn_out = jnp.dot(hidden, proj_down, preferred_element_type=F32)
    block_out = (resid + ffn_out).astype(BF16).reshape(seq_count, shard_len, D)

    grad_out = cotangent.reshape(row_count, D)
    grad_down = jnp.einsum("rf,rd->fd", hidden, grad_out, preferred_element_type=F32).astype(BF16)
    down_total = reduce_rows(grad_down)
    grad_hidden = jnp.einsum("rd,fd->rf", grad_out, proj_down, preferred_element_type=F32)
    act, slope = gelu_parts(expanded_gate)
    grad_expanded = jnp.concatenate(
        [(grad_hidden * expanded_up * slope).astype(BF16), (grad_hidden * act).astype(BF16)], axis=1
    )
    grad_up = jnp.einsum(
        "rd,rf->df", second_normed, grad_expanded, preferred_element_type=F32
    ).astype(BF16)
    up_total = reduce_rows(grad_up)
    grad_second_normed = jnp.einsum(
        "rf,df->rd", grad_expanded, proj_up, preferred_element_type=F32
    )
    grad_gain_two, grad_from_second = norm_back(resid, second_scale, gain_two, grad_second_normed)
    grad_resid = grad_out.astype(F32) + grad_from_second
    grad_mixer = grad_resid.astype(BF16)
    grad_out_proj = jnp.einsum(
        "rl,rd->ld", branch, grad_mixer, preferred_element_type=F32
    ).astype(BF16)
    out_total = reduce_rows(grad_out_proj)
    grad_branch = jnp.einsum("rd,ld->rl", grad_mixer, proj_out, preferred_element_type=F32)

    wide = (seq_count, shard_len, LRU)
    grad_gate, local, rev_prod, rev_chunks = mixer_reverse(
        grad_branch.reshape(wide), gate_pre.reshape(wide), keep, state.reshape(wide)
    )
    head_pull, head_prod = chunk_ends(rev_chunks, True)
    rev_carry = shard_carry(head_pull, head_prod, True)
    rev_carries = chunk_carries(rev_chunks, rev_carry, True)
    before = jnp.broadcast_to(carry_in[:, None], (seq_count, HALO, LRU))
    du, tail, edge, grad_gates, grad_taps, grad_decay = mixer_backward(
        local, rev_prod, rev_carries, state.reshape(wide), before, conv_low, inner_low,
        prev_inner, dist, gates_all, taps_all, soft,
    )
    gates_total = lax.psum_scatter(
        grad_gates.astype(BF16), "seq", scatter_dimension=0, tiled=True
    )
    gates_total = lax.psum(gates_total, "grp").astype(F32)
    returned = from_behind(edge[:, HALO - edge_len :].astype(BF16), "seq", -1).astype(F32)
    returned = jnp.pad(returned, ((0, 0), (HALO - edge_len, 0), (0, 0)))
    grad_inner = lax.dynamic_update_slice(
        du, (tail + returned).astype(BF16), (0, shard_len - HALO, 0)
    )
    grad_projected = jnp.concatenate(
        [grad_inner.reshape(row_count, LRU), grad_gate.reshape(row_count, LRU)], axis=1
    )
    grad_in = jnp.einsum(
        "rd,rp->dp", first_normed, grad_projected, preferred_element_type=F32
    ).astype(BF16)
    in_total = reduce_rows(grad_in)
    grad_first_normed = jnp.einsum(
        "rp,dp->rd", grad_projected, proj_in, preferred_element_type=F32
    )
    grad_gain_one, grad_from_first = norm_back(inputs, first_scale, gain_one, grad_first_normed)
    grad_tokens = (grad_resid + grad_from_first).astype(BF16).reshape(seq_count, shard_len, D)
    grad_decay_row = grad_decay[0] * jax.nn.sigmoid(-decay_float)
    flat = jnp.concatenate(
        [grad_gain_one, grad_gain_two, grad_decay_row, grad_taps[:CONV].reshape(-1)]
    )
    flat = lax.psum(flat, ("grp", "seq"))
    first_total = lax.dynamic_slice_in_dim(flat, place * n_gain, n_gain)
    second_total = lax.dynamic_slice_in_dim(flat, D + place * n_gain, n_gain)
    decay_total = lax.dynamic_slice_in_dim(flat, 2 * D + place * n_lru, n_lru)
    taps_total = lax.dynamic_slice_in_dim(
        flat[2 * D + LRU :].reshape(CONV, LRU), place * n_lru, n_lru, 1
    )
    return (
        block_out, grad_tokens, first_total, in_total, taps_total, decay_total, gates_total,
        out_total, second_total, up_total, down_total,
    )


def solution(mesh):
    in_specs = (
        P("grp", "seq", None),
        P("grp", "seq"),
        P("grp", "seq", None),
        P("seq"),
        P("seq", None),
        P(None, "seq"),
        P("seq"),
        P("seq", None, None),
        P("seq", None),
        P("seq"),
        P("seq", None),
        P("seq", None),
    )
    out_specs = (
        P("grp", "seq", None),
        P("grp", "seq", None),
        P("seq"),
        P("seq", None),
        P(None, "seq"),
        P("seq"),
        P("seq", None, None),
        P("seq", None),
        P("seq"),
        P("seq", None),
        P("seq", None),
    )
    return jax.shard_map(body, mesh=mesh, in_specs=in_specs, out_specs=out_specs, check_vma=False)
```

time: 3440 us -> 1650 us (0.48)
  local copies, waits for them, and re-layouts: 1220 us -> 36 us
  waiting for transfers between devices: 1370 us -> 977 us
  other arithmetic: 348 us -> 52.8 us
  Pallas kernels: 0 us -> 153 us
    slice x133 -> x7, local copies, waits for them, and re-layouts: 705 us -> 0.95 us  [the longest x1 0.9 us: body(): prev_ids = from_behind(seg_ids[:, shard_len - edge_len:], 'seq', 1)]
    reduce_scatter x5, waiting for transfers between devices: 1060 us -> 604 us  [the longest x4 604 us: reduce_rows(): lax.psum_scatter(partial, ('seq', 'grp'), scatter_dimension=0, tiled=True)]
    all_gather x5 -> x8, waiting for transfers between devices: 60.7 us -> 371 us  [the longest x4 268 us: gather_rows(): return lax.all_gather(own, ('seq', 'grp'), axis=0, tiled=True)]
    pad x64 -> x0, local copies, waits for them, and re-layouts: 257 us -> none  [the longest x32 129 us: body(): lax.associative_scan(combine_pairs, (keep_next, grad_state), reverse=True...]
    psum x1, waiting for transfers between devices: 246 us -> 0.01 us  [body(): gates_total = lax.psum(gates_total, 'grp').astype(F32)]
    pallas_call x0 -> x3, Pallas kernels: none -> 153 us  [the longest x1 63.4 us: mixer_forward(): pl.pallas_call(mixer_forward_kernel, grid=(HEADS,), in_specs=[full, head_...]
    add x61 -> x9, other arithmetic: 152 us -> 19.1 us  [the longest x1 12.1 us: body(): state_part.reshape(chunked)]
    rev x2 -> x0, local copies, waits for them, and re-layouts: 129 us -> none  [body(): lax.associative_scan(combine_pairs, (keep_next, grad_state), reverse=True...]
  transfers between devices with their start and end apart: 15 -> 17, of which waited for: 7 -> 12; matrix products, arithmetic and copies ran while one was open for 31% -> 15% of each run, Pallas kernels for 0% -> 4%
where the time goes in v1:
time: 1650 us; the launch traced here: 1640 us
  waiting for transfers between devices  977 us (59%)
  matrix products  303 us (18%)
  Pallas kernels  153 us (9%)
  blocking collectives  92.4 us (6%)
  other arithmetic  52.8 us (3%)
  local copies, waits for them, and re-layouts  36 us (2%)
    reduce_scatter x4, waiting for transfers between devices, reduce_rows(): lax.psum_scatter(partial, ('seq', 'grp'), scatter_dimension=0, tiled=True)  604 us
    all_gather x4, waiting for transfers between devices, gather_rows(): return lax.all_gather(own, ('seq', 'grp'), axis=0, tiled=True)  268 us
    all_gather x3, waiting for transfers between devices, reduce_rows(): return lax.all_gather(part, 'grp', axis=0, tiled=True).astype(F32)  94.2 us
    pallas_call x1, Pallas kernels, mixer_forward(): pl.pallas_call(mixer_forward_kernel, grid=(HEADS,), in_specs=[full, head_...  63.4 us
    pallas_call x1, Pallas kernels, mixer_backward(): pl.pallas_call(mixer_backward_kernel, grid=(HEADS,), in_specs=[full, full...  51.5 us
    dot_general x1, matrix products, body(): jnp.einsum('rf,df->rd', grad_expanded, proj_up, preferred_element_type=F32)  40.6 us
    psum x1, blocking collectives, body(): flat = lax.psum(flat, ('grp', 'seq'))  40.5 us
    dot_general x1, matrix products, body(): jnp.dot(second_normed, proj_up[:, FF:], preferred_element_type=F32)  38.8 us
  transfers between devices with their start and end apart: 17, of which 12 were waited for; matrix products, arithmetic and copies ran while one was open for 15% of the time, Pallas kernels for 4%

profile of v1, /device:TPU:18, one launch (start us, length us, event | category | flops | bytes accessed | tf_op | source)
XLA Modules:
  0.0 1635.9 jit_solution(6340649339146823534)
XLA Ops:
  18.2 2.1 concatenate.15
  20.3 2.7 fusion.28
  23.1 12.2 all-gather.3
  36.3 2.4 fusion.30
  38.7 69.1 %all-gather.13.cloned.1.call-done = bf16[1536,4096]{1,0:T(8,128)(2,1)} async-done(((bf16[48,4096]{1,0:T(8,128)(2,1)}), bf16[1536,4096]{1,0:T(8,128)(2,1)}) %all-gather.13.cloned.1.call-update) | async-done | bytes 12582928 | tf_op jit(solution)/shard_map/all_gather | solution.py:355
  107.8 9.7 fusion.39
  119.6 2.2 collective-permute-start
  121.9 8.7 all-gather.15.cloned.1.call-done.gates_ref
  130.8 2.2 copy-done.3
  134.2 63.4 %mixer_forward.1 = (bf16[2,512,2048]{2,1,0:T(8,128)(2,1)S(1)}, f32[2,512,2048]{2,1,0:T(8,128)}, f32[2,512,2048]{2,1,0:T(8,128)}, f32[2,512,2048]{2,1,0:T(8,128)}, f32[2,2,8,2048]{3,2,1,0:T(8,128)S(1)}) custom-call(bf16[2,512,2048]{2,1,0:T(8,128)(2,1)S(1)} %bitcast.729, bf16[2,8,2048]{2,1,0:T(8,128)(2,1)S(1)} %collective-permute-done.halo_ref, ...), custom_call_target="tpu_custom_call" | custom-call | tf_op jit(solution)/shard_map/mixer_forward/pallas_call | solution.py:255
  197.6 2.0 copy-done.9
  200.2 12.5 all-gather.1
  213.9 12.1 fusion.22.state_ref
  226.0 18.5 %fusion.21 = (bf16[1024,2048]{1,0:T(8,128)(2,1)}, f32[1024,2048]{1,0:T(8,128)}) fusion(f32[2,512,2048]{2,1,0:T(8,128)} %get-tuple-element.27, f32[2,512,2048]{2,1,0:T(8,128)} %get-tuple-element.26, f32[2,8,2048]{2,1,0:T(8,128)} %copy-done.28, bf16[1024,1536]{1,0:T(8,128)(2,1)} %fusion.30, bf16[1536,4096]{1,0:T(8,128)(2,1)} %all-gather.13.cloned.1.call-done), kind=kOutput, calls=%fused_computation.31 | convolution fusion | flops 6467616768 | bytes 38928384 | tf_op jit(solution)/shard_map/dot_general | solution.py:436
  244.5 10.5 multiply_reduce_fusion.2
  258.4 49.1 %all-gather.21.cloned.1.call-done = bf16[4608,1536]{1,0:T(8,128)(2,1)} async-done(((bf16[144,1536]{1,0:T(8,128)(2,1)}), bf16[4608,1536]{1,0:T(8,128)(2,1)}) %all-gather.21.cloned.1.call-update) | async-done | bytes 14155792 | tf_op jit(solution)/shard_map/all_gather | solution.py:355
  307.5 21.2 %fusion.163 = f32[4608,1024]{0,1:T(8,128)} fusion(bf16[4608,1536]{1,0:T(8,128)(2,1)} %all-gather.21.cloned.1.call-done, bf16[1024,1536]{1,0:T(8,128)(2,1)} %bitcast.738), kind=kOutput, calls=%fused_computation.270 | convolution fusion | flops 14495514624 | bytes 36175872 | tf_op jit(solution)/shard_map/rd,fd->rf/dot_general | solution.py:471
  328.8 150.0 %all-gather.19.cloned.1.call-done = bf16[1536,9216]{1,0:T(8,128)(2,1)} async-done(((bf16[48,9216]{1,0:T(8,128)(2,1)}), bf16[1536,9216]{1,0:T(8,128)(2,1)}) %all-gather.19.cloned.1.call-update) | async-done | bytes 28311568 | tf_op jit(solution)/shard_map/all_gather | solution.py:355
  478.8 20.1 %fusion.12 = f32[1024,4608]{1,0:T(8,128)} fusion(bf16[1024,1536]{1,0:T(8,128)(2,1)S(1)} %multiply_convert_fusion, bf16[1536,9216]{1,0:T(8,128)(2,1)} %all-gather.19.cloned.1.call-done), kind=kOutput, calls=%fused_computation.21 | convolution fusion | flops 14495514624 | bytes 36175872 | tf_op jit(solution)/shard_map/dot_general | solution.py:462
  498.9 38.8 %fusion.8 = (bf16[1024,4608]{1,0:T(8,128)(2,1)}, bf16[1024,4608]{1,0:T(8,128)(2,1)}, bf16[1024,4608]{1,0:T(8,128)(2,1)}) fusion(f32[4608,1024]{0,1:T(8,128)} %fusion.163, f32[1024,4608]{1,0:T(8,128)} %fusion.12, bf16[1024,1536]{1,0:T(8,128)(2,1)S(1)} %multiply_convert_fusion, bf16[1536,9216]{1,0:T(8,128)(2,1)} %all-gather.19.cloned.1.call-done), kind=kOutput, calls=%fused_computation.14 | convolution fusion | flops 14637072384 | bytes 83361792 | tf_op jit(solution)/shard_map/dot_general | solution.py:463
  537.7 40.6 %multiply_reduce_fusion = (f32[1536]{0:T(1024)}, f32[1024]{0:T(1024)S(1)}, f32[1024,1536]{1,0:T(8,128)}) fusion(f32[1024,1536]{1,0:T(8,128)} %copy-done.22, f32[1024]{0:T(1024)S(1)} %get-tuple-element.77, f32[1536]{0:T(1024)S(1)} %reshape.2431, bf16[1536,9216]{1,0:T(8,128)(2,1)} %all-gather.19.cloned.1.call-done, bf16[1024,4608]{1,0:T(8,128)(2,1)} %get-tuple-element.66, ...), kind=kOutput, calls=%fused_computation.58 | convolution fusion | flops 29038211072 | bytes 59789312 | tf_op jit(solution)/shard_map/rf,df->rd/dot_general | solution.py:480
  578.3 6.1 subtract_add_fusion
  584.8 9.0 fusion.43
  593.8 38.2 %mixer_reverse.1 = (bf16[2,512,2048]{2,1,0:T(8,128)(2,1)S(1)}, f32[2,512,2048]{2,1,0:T(8,128)S(1)}, f32[2,512,2048]{2,1,0:T(8,128)}, f32[2,2,8,2048]{3,2,1,0:T(8,128)S(1)}) custom-call(f32[2,512,2048]{2,1,0:T(8,128)} %bitcast.737, f32[2,512,2048]{2,1,0:T(8,128)} %bitcast.736, f32[2,512,2048]{2,1,0:T(8,128)} %get-tuple-element.29.keep_ref, ...), custom_call_target="tpu_custom_call" | custom-call | tf_op jit(solution)/shard_map/mixer_reverse/pallas_call | solution.py:289
  632.0 3.3 copy-done.4
  637.8 13.3 all-gather.2
  651.7 2.2 copy-done.10
  653.8 51.5 %mixer_backward.1 = (bf16[2,512,2048]{2,1,0:T(8,128)(2,1)S(1)}, f32[2,8,2048]{2,1,0:T(8,128)S(1)}, f32[2,8,2048]{2,1,0:T(8,128)S(1)}, f32[16,128,256]{2,1,0:T(8,...) custom-call(f32[2,512,2048]{2,1,0:T(8,128)} %copy-done.4, f32[2,512,2048]{2,1,0:T(8,128)} %get-tuple-element.31.prod_ref, ...), custom_call_target="tpu_custom_call" | custom-call | tf_op jit(solution)/shard_map/mixer_backward/pallas_call | solution.py:312
  707.4 2.3 collective-permute-start.2
  711.9 20.2 %convolution_convert_fusion.2 = bf16[1536,4096]{1,0:T(8,128)(2,1)} fusion(bf16[1024,1536]{1,0:T(8,128)(2,1)} %fusion.30, bf16[1024,2048]{1,0:T(8,128)(2,1)} %bitcast.732, bf16[1024,2048]{1,0:T(8,128)(2,1)} %bitcast.734), kind=kOutput, calls=%fused_computation.18 | convolution fusion | flops 12907970560 | bytes 24117248 | tf_op jit(solution)/shard_map/rd,rp->dp/dot_general | solution.py:516
  734.1 21.3 %convolution_convert_fusion.1 = bf16[4608,1536]{1,0:T(8,128)(2,1)} fusion(bf16[1024,4608]{1,0:T(8,128)(2,1)} %get-tuple-element.67, bf16[1024,1536]{1,0:T(8,128)(2,1)S(1)} %bitcast.739), kind=kOutput, calls=%fused_computation.2 | convolution fusion | flops 14502592512 | bytes 26738688 | tf_op jit(solution)/shard_map/rf,rd->fd/dot_general | solution.py:469
  757.5 36.9 %convolution_convert_fusion = bf16[1536,9216]{1,0:T(8,128)(2,1)} fusion(bf16[1024,1536]{1,0:T(8,128)(2,1)S(1)} %copy-done.25, bf16[1024,4608]{1,0:T(8,128)(2,1)} %get-tuple-element.66, bf16[1024,4608]{1,0:T(8,128)(2,1)} %get-tuple-element.65), kind=kOutput, calls=%fused_computation | convolution fusion | flops 29042933760 | bytes 50331648 | tf_op jit(solution)/shard_map/rd,rf->df/dot_general | solution.py:476
  795.1 11.9 convolution_convert_fusion.3
  807.1 95.0 %reduce-scatter.6.cloned.1.call-done = bf16[48,4096]{1,0:T(8,128)(2,1)} async-done(((bf16[1536,4096]{1,0:T(8,128)(2,1)}), bf16[48,4096]{1,0:T(8,128)(2,1)}) %reduce-scatter.6.cloned.1.call-update) | async-done | bytes 393232 | tf_op jit(solution)/shard_map/reduce_scatter | solution.py:359
  902.3 168.5 %reduce-scatter.14.cloned.1.call-done = bf16[144,1536]{1,0:T(8,128)(2,1)} async-done(((bf16[4608,1536]{1,0:T(8,128)(2,1)}), bf16[144,1536]{1,0:T(8,128)(2,1)}) %reduce-scatter.14.cloned.1.call-update) | async-done | bytes 442384 | tf_op jit(solution)/shard_map/reduce_scatter | solution.py:359
  1070.9 22.2 %add_convert_fusion = bf16[1024,1536]{1,0:T(8,128)(2,1)} fusion(f32[1024,1536]{1,0:T(8,128)} %copy-done.22, bf16[1024,4608]{1,0:T(8,128)(2,1)} %get-tuple-element.67, bf16[4608,1536]{1,0:T(8,128)(2,1)} %all-gather.21.cloned.1.call-done), kind=kOutput, calls=%fused_computation.61 | convolution fusion | flops 14498660352 | bytes 33030144 | tf_op jit(solution)/shard_map/dot_general | solution.py:465
  1093.2 248.9 %reduce-scatter.12.cloned.1.call-done = bf16[48,9216]{1,0:T(8,128)(2,1)} async-done(((bf16[1536,9216]{1,0:T(8,128)(2,1)}), bf16[48,9216]{1,0:T(8,128)(2,1)}) %reduce-scatter.12.cloned.1.call-update) | async-done | bytes 884752 | tf_op jit(solution)/shard_map/reduce_scatter | solution.py:359
  1342.1 21.5 %fusion.37 = (f32[1536]{0:T(1024)S(1)}, f32[1024]{0:T(1024)S(1)}, f32[1024,1536]{1,0:T(8,128)}) fusion(bf16[2,512,1536]{2,1,0:T(8,128)(2,1)S(1)} %copy-done.21, f32[1024]{0:T(1024)S(1)} %bitcast.752, f32[1536]{0:T(1024)S(1)} %copy-done.30, bf16[1536,4096]{1,0:T(8,128)(2,1)} %all-gather.13.cloned.1.call-done, bf16[1024,2048]{1,0:T(8,128)(2,1)} %bitcast.733, ...), kind=kOutput, calls=%fused_computation.57 | convolution fusion | flops 12912686080 | bytes 30429184 | tf_op jit(solution)/shard_map/rp,dp->rd/dot_general | solution.py:520
  1363.6 40.5 %psum.14 = f32[13312]{0:T(1024)S(1)} all-reduce(f32[13312]{0:T(1024)S(1)} %pad_maximum_fusion.6), channel_id=1, replica_groups=mesh['grp'=4,'seq'=8] {'grp','seq'}, use_global_device_ids=true, to_apply=%region_6.7 | all-reduce | flops 13312 | bytes 106496 | tf_op jit(solution)/shard_map/psum | solution.py:529
  1406.0 7.3 fusion.34
  1414.9 91.6 %reduce-scatter.10.cloned.1.call-done = bf16[64,1536]{1,0:T(8,128)(2,1)} async-done(((bf16[2048,1536]{1,0:T(8,128)(2,1)}), bf16[64,1536]{1,0:T(8,128)(2,1)}) %reduce-scatter.10.cloned.1.call-update) | async-done | bytes 196624 | tf_op jit(solution)/shard_map/reduce_scatter | solution.py:359
  1506.5 13.8 all_gather.57
  1521.6 17.8 %all-gather.23.cloned.1.call-done = bf16[192,4096]{1,0:T(8,128)(2,1)} async-done(((bf16[48,4096]{1,0:T(8,128)(2,1)}), bf16[192,4096]{1,0:T(8,128)(2,1)}) %all-gather.23.cloned.1.call-update) | async-done | bytes 1572880 | tf_op jit(solution)/shard_map/all_gather | solution.py:360
  1539.4 3.4 convert_element_type.157
  1542.8 31.2 %all-gather.27.cloned.1.call-done = bf16[576,1536]{1,0:T(8,128)(2,1)} async-done(((bf16[144,1536]{1,0:T(8,128)(2,1)}), bf16[576,1536]{1,0:T(8,128)(2,1)}) %all-gather.27.cloned.1.call-update) | async-done | bytes 1769488 | tf_op jit(solution)/shard_map/all_gather | solution.py:360
  1574.0 3.9 convert_element_type.165
  1577.9 45.2 %all-gather.25.cloned.1.call-done = bf16[192,9216]{1,0:T(8,128)(2,1)} async-done(((bf16[48,9216]{1,0:T(8,128)(2,1)}), bf16[192,9216]{1,0:T(8,128)(2,1)}) %all-gather.25.cloned.1.call-update) | async-done | bytes 3538960 | tf_op jit(solution)/shard_map/all_gather | solution.py:360
  1623.2 5.8 convert_element_type.163
  (172 shorter events, 37.5 us)
Async XLA Ops:
  7.2 6.4 copy-start
  7.2 100.6 %all-gather.13.cloned.1.call-start = ((), (), s32[]{:S(2)}) async-start(), calls=%async_computation.5 | async-start | bytes 12976128 | tf_op jit(solution)/shard_map/all_gather | solution.py:355
  9.2 121.3 %all-gather.15.cloned.1.call-start = ((), (), s32[]{:S(2)}) async-start(), calls=%async_computation.6 | async-start | bytes 1179648 | tf_op jit(solution)/shard_map/all_gather | solution.py:426
  9.9 234.6 %all-gather.17.cloned.1.call-start = ((), (), s32[]{:S(2)}) async-start(), calls=%async_computation.7 | async-start | bytes 6488064 | tf_op jit(solution)/shard_map/all_gather | solution.py:355
  11.6 295.9 %all-gather.21.cloned.1.call-start = ((), (), s32[]{:S(2)}) async-start(), calls=%async_computation.9 | async-start | bytes 14598144 | tf_op jit(solution)/shard_map/all_gather | solution.py:355
  13.5 465.2 %all-gather.19.cloned.1.call-start = ((), (), s32[]{:S(2)}) async-start(), calls=%async_computation.8 | async-start | bytes 29196288 | tf_op jit(solution)/shard_map/all_gather | solution.py:355
  14.6 21.7 %copy-start.19 = (bf16[2,512,1536]{2,1,0:T(8,128)(2,1)S(1)}, bf16[2,512,1536]{2,1,0:T(8,128)(2,1)}, u32[]{:S(2)}) copy-start(bf16[2,512,1536]{2,1,0:T(8,128)(2,1)} %param.12) | copy-start | bytes 9437188
  14.6 779.9 %reduce-scatter.8.cloned.1.call-start = ((), (), s32[]{:S(2)}) async-start(), calls=%async_computation.12 | async-start | bytes 1179648 | tf_op jit(solution)/shard_map/reduce_scatter | solution.py:504
  15.5 23.2 %collective-permute-start.1 = (s32[2,3]{1,0:T(2,128)S(1)}, s32[2,3]{1,0:T(2,128)S(1)}, u32[]{:S(2)}, u32[]{:S(2)}) collective-permute-start(s32[2,3]{1,0:T(2,128)S(1)} %slice.279), channel_id=1, source_target_pairs={{0,1},{1,2},{2,3},{3,4},{4,5},{5,6},{6,7},{8,9},{9,10},{10,11},{11... | collective-permute-start | bytes 80 | tf_op jit(solution)/shard_map/ppermute | solution.py:25
  23.0 94.5 %copy-start.32 = (f32[1,4,2,128]{3,1,2,0:T(4,128)}, f32[1,4,2,128]{3,1,2,0:T(4,128)S(1)}, u32[]{:S(2)}) copy-start(f32[1,4,2,128]{3,1,2,0:T(4,128)S(1)} %copy.176) | copy-start | bytes 12292
  35.3 95.4 %copy-start.11 = (f32[1,4,8,256]{3,1,2,0:T(4,128)}, f32[1,4,8,256]{3,1,2,0:T(4,128)S(1)}, u32[]{:S(2)}) copy-start(f32[1,4,8,256]{3,1,2,0:T(4,128)S(1)} %copy.178) | copy-start | bytes 98308
  35.6 82.0 %copy-start.29 = (f32[1536]{0:T(1024)}, f32[1536]{0:T(1024)S(1)}, u32[]{:S(2)}) copy-start(f32[1536]{0:T(1024)S(1)} %reshape.2429) | copy-start | bytes 18436
  36.2 94.5 %copy-start.15 = (f32[1,2048]{1,0:T(1,128)}, f32[1,2048]{1,0:T(1,128)S(1)}, u32[]{:S(2)}) copy-start(f32[1,2048]{1,0:T(1,128)S(1)} %compare_select_fusion.soft_ref) | copy-start | bytes 24580
  38.7 83.1 %copy-start.37 = (s32[2,512]{1,0:T(2,128)S(1)}, s32[2,512]{1,0:T(2,128)}, u32[]{:S(2)}) copy-start(s32[2,512]{1,0:T(2,128)} %param.13) | copy-start | bytes 12292
  119.6 10.9 collective-permute-start
  130.5 95.4 %copy-start.13 = (bf16[2,8,2048]{2,1,0:T(8,128)(2,1)}, bf16[2,8,2048]{2,1,0:T(8,128)(2,1)S(1)}, u32[]{:S(2)}) copy-start(bf16[2,8,2048]{2,1,0:T(8,128)(2,1)S(1)} %collective-permute-done.halo_ref) | copy-start | bytes 196612
  130.8 2.2 copy-start.3
  134.2 63.4 %copy-start.5 = (f32[2,512,128]{2,1,0:T(8,128)}, f32[2,512,128]{2,1,0:T(8,128)S(1)}, u32[]{:S(2)}) copy-start(f32[2,512,128]{2,1,0:T(8,128)S(1)} %broadcast_in_dim.9.dist_ref) | copy-start | bytes 1572868
  226.0 18.5 %copy-start.20 = (bf16[2,512,1536]{2,1,0:T(8,128)(2,1)S(1)}, bf16[2,512,1536]{2,1,0:T(8,128)(2,1)}, u32[]{:S(2)}) copy-start(bf16[2,512,1536]{2,1,0:T(8,128)(2,1)} %param.12) | copy-start | bytes 9437188
  255.1 2.7 copy-start.22
  258.4 240.5 %copy-start.24 = (bf16[1024,1536]{1,0:T(8,128)(2,1)}, bf16[1024,1536]{1,0:T(8,128)(2,1)S(1)}, u32[]{:S(2)}) copy-start(bf16[1024,1536]{1,0:T(8,128)(2,1)S(1)} %multiply_convert_fusion) | copy-start | bytes 9437188
  537.7 40.6 %copy-start.26 = (bf16[2,512,1536]{2,1,0:T(8,128)(2,1)S(1)}, bf16[2,512,1536]{2,1,0:T(8,128)(2,1)}, u32[]{:S(2)}) copy-start(bf16[2,512,1536]{2,1,0:T(8,128)(2,1)} %param.14) | copy-start | bytes 9437188
  537.7 40.6 %copy-start.35 = (f32[1024]{0:T(1024)S(1)}, f32[1024]{0:T(1024)}, u32[]{:S(2)}) copy-start(f32[1024]{0:T(1024)} %get-tuple-element.76) | copy-start | bytes 12292
  578.3 6.4 copy-start.38
  584.8 9.0 copy-start.23
  593.8 57.8 %copy-start.31 = (f32[2,2048]{1,0:T(2,128)S(1)}, f32[2,2048]{1,0:T(2,128)}, u32[]{:S(2)}) copy-start(f32[2,2048]{1,0:T(2,128)} %fusion.70) | copy-start | bytes 49156
  593.8 57.8 %copy-start.6 = (f32[2,512,128]{2,1,0:T(8,128)S(1)}, f32[2,512,128]{2,1,0:T(8,128)}, u32[]{:S(2)}) copy-start(f32[2,512,128]{2,1,0:T(8,128)} %copy-done.5) | copy-start | bytes 1572868
  593.8 57.8 %copy-start.8 = (bf16[16,128,256]{2,1,0:T(8,128)(2,1)S(1)}, bf16[16,128,256]{2,1,0:T(8,128)(2,1)}, u32[]{:S(2)}) copy-start(bf16[16,128,256]{2,1,0:T(8,128)(2,1)} %all-gather.15.cloned.1.call-done.gates_ref) | copy-start | bytes 3145732
  593.8 57.9 %copy-start.12 = (f32[1,4,8,256]{3,1,2,0:T(4,128)S(1)}, f32[1,4,8,256]{3,1,2,0:T(4,128)}, u32[]{:S(2)}) copy-start(f32[1,4,8,256]{3,1,2,0:T(4,128)} %copy-done.11) | copy-start | bytes 98308
  593.8 57.9 %copy-start.14 = (bf16[2,8,2048]{2,1,0:T(8,128)(2,1)S(1)}, bf16[2,8,2048]{2,1,0:T(8,128)(2,1)}, u32[]{:S(2)}) copy-start(bf16[2,8,2048]{2,1,0:T(8,128)(2,1)} %copy-done.13) | copy-start | bytes 196612
  593.8 57.9 %copy-start.16 = (f32[1,2048]{1,0:T(1,128)S(1)}, f32[1,2048]{1,0:T(1,128)}, u32[]{:S(2)}) copy-start(f32[1,2048]{1,0:T(1,128)} %copy-done.15) | copy-start | bytes 24580
  632.0 3.3 copy-start.4
  651.6 2.2 copy-start.10
  707.4 3.9 collective-permute-start.2
  710.8 191.3 %reduce-scatter.6.cloned.1.call-start = ((), (), s32[]{:S(2)}) async-start(), calls=%async_computation.10 | async-start | bytes 12976128 | tf_op jit(solution)/shard_map/reduce_scatter | solution.py:359
  732.2 338.6 %reduce-scatter.14.cloned.1.call-start = ((), (), s32[]{:S(2)}) async-start(), calls=%async_computation.17 | async-start | bytes 14598144 | tf_op jit(solution)/shard_map/reduce_scatter | solution.py:359
  755.5 586.6 %reduce-scatter.12.cloned.1.call-start = ((), (), s32[]{:S(2)}) async-start(), calls=%async_computation.15 | async-start | bytes 29196288 | tf_op jit(solution)/shard_map/reduce_scatter | solution.py:359
  794.5 618.8 %all-reduce.3.cloned.1.call-start = ((), (), s32[]{:S(2)}) async-start(), calls=%async_computation.13 | async-start | bytes 262144 | tf_op jit(solution)/shard_map/psum | solution.py:507
  795.1 711.5 %reduce-scatter.10.cloned.1.call-start = ((), (), s32[]{:S(2)}) async-start(), calls=%async_computation.14 | async-start | bytes 6488064 | tf_op jit(solution)/shard_map/reduce_scatter | solution.py:359
  807.0 95.2 %copy-start.34 = (f32[1,2,8,128]{3,2,1,0:T(8,128)S(1)}, f32[1,2,8,128]{3,2,1,0:T(8,128)}, u32[]{:S(2)}) copy-start(f32[1,2,8,128]{3,2,1,0:T(8,128)} %get-tuple-element.72) | copy-start | bytes 24580
  807.0 95.2 %copy-start.33 = (f32[1,4,2,128]{3,1,2,0:T(4,128)S(1)}, f32[1,4,2,128]{3,1,2,0:T(4,128)}, u32[]{:S(2)}) copy-start(f32[1,4,2,128]{3,1,2,0:T(4,128)} %copy-done.32) | copy-start | bytes 12292
  807.1 732.4 %all-gather.23.cloned.1.call-start = ((), (), s32[]{:S(2)}) async-start(), calls=%async_computation.11 | async-start | bytes 1966080 | tf_op jit(solution)/shard_map/all_gather | solution.py:360
  902.1 671.9 %all-gather.27.cloned.1.call-start = ((), (), s32[]{:S(2)}) async-start(), calls=%async_computation.18 | async-start | bytes 2211840 | tf_op jit(solution)/shard_map/all_gather | solution.py:360
  1070.9 271.2 %copy-start.21 = (bf16[2,512,1536]{2,1,0:T(8,128)(2,1)S(1)}, bf16[2,512,1536]{2,1,0:T(8,128)(2,1)}, u32[]{:S(2)}) copy-start(bf16[2,512,1536]{2,1,0:T(8,128)(2,1)} %param.12) | copy-start | bytes 9437188
  1070.9 271.2 %copy-start.30 = (f32[1536]{0:T(1024)S(1)}, f32[1536]{0:T(1024)}, u32[]{:S(2)}) copy-start(f32[1536]{0:T(1024)} %copy-done.29) | copy-start | bytes 18436
  1070.9 552.3 %all-gather.25.cloned.1.call-start = ((), (), s32[]{:S(2)}) async-start(), calls=%async_computation.16 | async-start | bytes 4423680 | tf_op jit(solution)/shard_map/all_gather | solution.py:360
  1342.1 21.5 %copy-start.36 = (f32[1536]{0:T(1024)S(1)}, f32[1536]{0:T(1024)}, u32[]{:S(2)}) copy-start(f32[1536]{0:T(1024)} %get-tuple-element.41) | copy-start | bytes 18436
  1574.0 54.9 %copy-start.1 = (bf16[192,9216]{1,0:T(8,128)(2,1)S(1)}, bf16[192,9216]{1,0:T(8,128)(2,1)}, u32[]{:S(2)}) copy-start(bf16[192,9216]{1,0:T(8,128)(2,1)} %param.22) | copy-start | bytes 10616836
  (8 other events, 14.0 us)
Sparse Core Ops, SparseCore 0:
  11.5 96.2 all-gather.12
  109.4 21.0 all-gather.14
  134.0 68.7 all-gather.16
  206.2 101.3 all-gather.20
  310.9 167.8 all-gather.18
  711.0 26.3 reduce-scatter.7
  743.4 158.7 reduce-scatter.5
  909.2 161.6 reduce-scatter.13
  1078.4 263.5 reduce-scatter.11
  1345.0 41.9 all-reduce.2
  1392.7 113.8 reduce-scatter.9
  1508.4 30.9 all-gather.22
  1541.4 32.5 all-gather.26
  1575.9 47.2 all-gather.24

commit v2 on v1

--- a/solution.py
+++ b/solution.py
@@ -355,9 +355,77 @@
     return lax.all_gather(own, ("seq", "grp"), axis=0, tiled=True)
 
 
+def tie(value, *after):
+    return lax.optimization_barrier((value, *after))[0]
+
+
+def xor_pairs(axis, bit):
+    return [(i, i ^ bit) for i in range(lax.axis_size(axis))]
+
+
+def ring_pairs(steps):
+    count = lax.axis_size("seq")
+    return [(i, (i + steps) % count) for i in range(count)]
+
+
+def dot_rows(a, b):
+    return lax.dot_general(a, b, (((0,), (0,)), ((), ())), preferred_element_type=F32)
+
+
 def reduce_rows(partial):
-    part = lax.psum_scatter(partial, ("seq", "grp"), scatter_dimension=0, tiled=True)
+    part = lax.psum_scatter(partial, "seq", scatter_dimension=0, tiled=True)
+    part = lax.psum_scatter(part, "grp", scatter_dimension=0, tiled=True)
     return lax.all_gather(part, "grp", axis=0, tiled=True).astype(F32)
+
+
+def reduce_product(a, b):
+    count = lax.axis_size("seq")
+    if lax.axis_size("grp") != 4:
+        product = dot_rows(a, b).astype(BF16)
+        return reduce_rows(product), (product,)
+    place = lax.axis_index("seq")
+    group = lax.axis_index("grp")
+    chips = count // 2
+    chip, core = place // 2, place % 2
+    tokens, depth = a.shape
+    rows = depth // count
+    width = b.shape[1] // 4
+    full = chips * rows
+    half = full // 2
+    split = a.reshape(tokens, chips, 2, rows)
+    a_own = lax.dynamic_index_in_dim(split, core, 2, False).reshape(tokens, full)
+    a_far = lax.dynamic_index_in_dim(split, 1 - core, 2, False).reshape(tokens, full)
+    b_part = [lax.dynamic_slice_in_dim(b, (group ^ k) * width, width, 1) for k in range(4)]
+    other = xor_pairs("seq", 1)
+    x, y = xor_pairs("grp", 1), xor_pairs("grp", 2)
+    far = {}
+    for k in (3, 1, 2, 0):
+        far[k] = lax.ppermute(dot_rows(a_far, b_part[k]).astype(BF16), "seq", other)
+
+    def own(k, first, last):
+        return dot_rows(a_own[:, first:last], b_part[k]) + far[k][first:last].astype(F32)
+
+    early = [
+        own(3, 0, half).astype(BF16),
+        own(3, half, full).astype(BF16),
+        own(1, 0, half).astype(BF16),
+        own(2, half, full).astype(BF16),
+    ]
+    diag_a = lax.ppermute(early[0], "grp", x)
+    diag_b = lax.ppermute(early[1], "grp", y)
+    x_a = lax.ppermute(early[2], "grp", x)
+    y_b = lax.ppermute(early[3], "grp", y)
+    x_b = lax.ppermute((own(1, half, full) + diag_b.astype(F32)).astype(BF16), "grp", x)
+    y_a = lax.ppermute((own(2, 0, half) + diag_a.astype(F32)).astype(BF16), "grp", y)
+    mine_a = (own(0, 0, half) + x_a.astype(F32) + y_a.astype(F32)).astype(BF16)
+    mine_b = (own(0, half, full) + x_b.astype(F32) + y_b.astype(F32)).astype(BF16)
+    mine = jnp.concatenate([mine_a, mine_b], axis=0).reshape(chips, rows, width)
+    total = lax.dynamic_index_in_dim(mine, chip, 0, False).astype(F32)
+    for j in range(1, chips):
+        sent = lax.dynamic_index_in_dim(mine, (chip + j) % chips, 0, False)
+        total = total + lax.ppermute(sent, "seq", ring_pairs(2 * j)).astype(F32)
+    parts = lax.all_gather(total.astype(BF16), "grp")
+    return parts.transpose(1, 0, 2).reshape(rows, 4 * width).astype(F32), tuple(early)
 
 
 def shard_carry(ends, prods, reverse):
@@ -393,12 +461,12 @@
 
 def norm_back(values, scale, gain, grad_normed):
     weighted = grad_normed * gain
-    grad_gain = jnp.sum(grad_normed * values * scale, axis=0)
     cubed = scale * scale * scale
-    grad_values = scale * weighted - values * cubed * jnp.mean(
-        weighted * values, axis=-1, keepdims=True
-    )
-    return (grad_gain, grad_values)
+    return scale * weighted - values * cubed * jnp.mean(weighted * values, axis=-1, keepdims=True)
+
+
+def gain_grad(weight, grad_weight, gain):
+    return jnp.sum(weight.astype(F32) * grad_weight, axis=1) / gain.astype(F32)
 
 
 def body(
@@ -466,28 +534,27 @@
     block_out = (resid + ffn_out).astype(BF16).reshape(seq_count, shard_len, D)
 
     grad_out = cotangent.reshape(row_count, D)
-    grad_down = jnp.einsum("rf,rd->fd", hidden, grad_out, preferred_element_type=F32).astype(BF16)
+    grad_down = dot_rows(hidden, grad_out).astype(BF16)
     down_total = reduce_rows(grad_down)
-    grad_hidden = jnp.einsum("rd,fd->rf", grad_out, proj_down, preferred_element_type=F32)
+    grad_hidden = jnp.einsum(
+        "rd,fd->rf", tie(grad_out, grad_down), proj_down, preferred_element_type=F32
+    )
     act, slope = gelu_parts(expanded_gate)
     grad_expanded = jnp.concatenate(
         [(grad_hidden * expanded_up * slope).astype(BF16), (grad_hidden * act).astype(BF16)], axis=1
     )
-    grad_up = jnp.einsum(
-        "rd,rf->df", second_normed, grad_expanded, preferred_element_type=F32
-    ).astype(BF16)
-    up_total = reduce_rows(grad_up)
+    up_total, sent = reduce_product(second_normed, grad_expanded)
     grad_second_normed = jnp.einsum(
-        "rf,df->rd", grad_expanded, proj_up, preferred_element_type=F32
-    )
-    grad_gain_two, grad_from_second = norm_back(resid, second_scale, gain_two, grad_second_normed)
-    grad_resid = grad_out.astype(F32) + grad_from_second
+        "rf,df->rd", tie(grad_expanded, *sent), proj_up, preferred_element_type=F32
+    )
+    grad_resid = grad_out.astype(F32) + norm_back(
+        resid, second_scale, gain_two, grad_second_normed
+    )
     grad_mixer = grad_resid.astype(BF16)
-    grad_out_proj = jnp.einsum(
-        "rl,rd->ld", branch, grad_mixer, preferred_element_type=F32
-    ).astype(BF16)
-    out_total = reduce_rows(grad_out_proj)
-    grad_branch = jnp.einsum("rd,ld->rl", grad_mixer, proj_out, preferred_element_type=F32)
+    out_total, sent = reduce_product(branch, grad_mixer)
+    grad_branch = jnp.einsum(
+        "rd,ld->rl", tie(grad_mixer, *sent), proj_out, preferred_element_type=F32
+    )
 
     wide = (seq_count, shard_len, LRU)
     grad_gate, local, rev_prod, rev_chunks = mixer_reverse(
@@ -501,10 +568,21 @@
         local, rev_prod, rev_carries, state.reshape(wide), before, conv_low, inner_low,
         prev_inner, dist, gates_all, taps_all, soft,
     )
-    gates_total = lax.psum_scatter(
-        grad_gates.astype(BF16), "seq", scatter_dimension=0, tiled=True
-    )
-    gates_total = lax.psum(gates_total, "grp").astype(F32)
+    grad_decay_row = grad_decay[0] * jax.nn.sigmoid(-decay_float)
+    flat = jnp.concatenate(
+        [
+            grad_gates.reshape(last + 1, -1),
+            grad_taps[:CONV].reshape(CONV, last + 1, n_lru).transpose(1, 0, 2).reshape(last + 1, -1),
+            grad_decay_row.reshape(last + 1, n_lru),
+        ],
+        axis=1,
+    ).astype(BF16)
+    flat = lax.psum_scatter(flat.reshape(-1, HS), "seq", scatter_dimension=0, tiled=True)
+    flat = lax.psum(flat, "grp").astype(F32).reshape(-1)
+    n_gates = flat.shape[0] - (CONV + 1) * n_lru
+    gates_total = flat[:n_gates].reshape(gate_heads.shape)
+    taps_total = flat[n_gates : n_gates + CONV * n_lru].reshape(CONV, n_lru)
+    decay_total = flat[n_gates + CONV * n_lru :]
     returned = from_behind(edge[:, HALO - edge_len :].astype(BF16), "seq", -1).astype(F32)
     returned = jnp.pad(returned, ((0, 0), (HALO - edge_len, 0), (0, 0)))
     grad_inner = lax.dynamic_update_slice(
@@ -513,26 +591,14 @@
     grad_projected = jnp.concatenate(
         [grad_inner.reshape(row_count, LRU), grad_gate.reshape(row_count, LRU)], axis=1
     )
-    grad_in = jnp.einsum(
-        "rd,rp->dp", first_normed, grad_projected, preferred_element_type=F32
-    ).astype(BF16)
-    in_total = reduce_rows(grad_in)
+    in_total, sent = reduce_product(first_normed, grad_projected)
     grad_first_normed = jnp.einsum(
-        "rp,dp->rd", grad_projected, proj_in, preferred_element_type=F32
-    )
-    grad_gain_one, grad_from_first = norm_back(inputs, first_scale, gain_one, grad_first_normed)
-    grad_tokens = (grad_resid + grad_from_first).astype(BF16).reshape(seq_count, shard_len, D)
-    grad_decay_row = grad_decay[0] * jax.nn.sigmoid(-decay_float)
-    flat = jnp.concatenate(
-        [grad_gain_one, grad_gain_two, grad_decay_row, grad_taps[:CONV].reshape(-1)]
-    )
-    flat = lax.psum(flat, ("grp", "seq"))
-    first_total = lax.dynamic_slice_in_dim(flat, place * n_gain, n_gain)
-    second_total = lax.dynamic_slice_in_dim(flat, D + place * n_gain, n_gain)
-    decay_total = lax.dynamic_slice_in_dim(flat, 2 * D + place * n_lru, n_lru)
-    taps_total = lax.dynamic_slice_in_dim(
-        flat[2 * D + LRU :].reshape(CONV, LRU), place * n_lru, n_lru, 1
-    )
+        "rp,dp->rd", tie(grad_projected, *sent), proj_in, preferred_element_type=F32
+    )
+    grad_tokens = grad_resid + norm_back(inputs, first_scale, gain_one, grad_first_normed)
+    grad_tokens = grad_tokens.astype(BF16).reshape(seq_count, shard_len, D)
+    first_total = gain_grad(in_proj, in_total, first_gain)
+    second_total = gain_grad(up_proj, up_total, second_gain)
     return (
         block_out, grad_tokens, first_total, in_total, taps_total, decay_total, gates_total,
         out_total, second_total, up_total, down_total,

time: 1650 us -> 1260 us (0.76)
  waiting for transfers between devices: 977 us -> 389 us
  local copies, waits for them, and re-layouts: 36 us -> 126 us
  other arithmetic: 52.8 us -> 113 us
  starting transfers between devices: 6.96 us -> 46.9 us
  matrix products: 303 us -> 336 us
  blocking collectives: 92.4 us -> 67.7 us
    reduce_scatter x5 -> x2, waiting for transfers between devices: 604 us -> 0.01 us  [the longest x1 0.01 us: reduce_rows(): part = lax.psum_scatter(partial, 'seq', scatter_dimension=0, tiled=True)]
    ppermute x0 -> x39, waiting for transfers between devices: none -> 237 us  [the longest x9 83 us: reduce_product(): total = total + lax.ppermute(sent, 'seq', ring_pairs(2 * j)).astype(F32)]
    all_gather x4, waiting for transfers between devices: 268 us -> 143 us  [gather_rows(): return lax.all_gather(own, ('seq', 'grp'), axis=0, tiled=True)]
    all_gather x3 -> x1, waiting for transfers between devices: 94.2 us -> 0.01 us  [reduce_rows(): return lax.all_gather(part, 'grp', axis=0, tiled=True).astype(F32)]
    dot_general x8 -> x41, matrix products: 183 us -> 223 us  [the longest x37 122 us: dot_rows(): lax.dot_general(a, b, (((0,), (0,)), ((), ())), preferred_element_type=F32)]
    psum x1 -> x0, blocking collectives: 40.5 us -> none  [body(): flat = lax.psum(flat, ('grp', 'seq'))]
    concatenate x1 -> x8, other arithmetic: 0.01 us -> 39.5 us  [the longest x2 23.8 us: body(): jnp.concatenate([(grad_hidden * expanded_up * slope).astype(BF16), (grad_...]
    ppermute x0 -> x39, starting transfers between devices: none -> 37.4 us  [the longest x9 13 us: reduce_product(): total = total + lax.ppermute(sent, 'seq', ring_pairs(2 * j)).astype(F32)]
  transfers between devices with their start and end apart: 17 -> 54, of which waited for: 12 -> 22; matrix products, arithmetic and copies ran while one was open for 15% -> 45% of each run, Pallas kernels for 4% -> 12%
where the time goes in v2:
time: 1260 us; the launch traced here: 1250 us
  waiting for transfers between devices  389 us (31%)
  matrix products  336 us (27%)
  Pallas kernels  153 us (12%)
  local copies, waits for them, and re-layouts  126 us (10%)
  other arithmetic  113 us (9%)
  blocking collectives  67.7 us (5%)
  starting transfers between devices  46.9 us (4%)
  between operations  16.4 us (1%)
    all_gather x4, waiting for transfers between devices, gather_rows(): return lax.all_gather(own, ('seq', 'grp'), axis=0, tiled=True)  143 us
    dot_general x37, matrix products, dot_rows(): lax.dot_general(a, b, (((0,), (0,)), ((), ())), preferred_element_type=F32)  122 us
    ppermute x9, waiting for transfers between devices, reduce_product(): total = total + lax.ppermute(sent, 'seq', ring_pairs(2 * j)).astype(F32)  83 us
    pallas_call x1, Pallas kernels, mixer_forward(): pl.pallas_call(mixer_forward_kernel, grid=(HEADS,), in_specs=[full, head_...  63.3 us
    ppermute x3, waiting for transfers between devices, reduce_product(): lax.ppermute((own(2, 0, half) + diag_a.astype(F32)).astype(BF16), 'grp', y)  58.1 us
    unnamed x196, local copies, waits for them, and re-layouts  55.6 us
    pallas_call x1, Pallas kernels, mixer_backward(): pl.pallas_call(mixer_backward_kernel, grid=(HEADS,), in_specs=[full, full...  51.9 us
    ppermute x3, waiting for transfers between devices, reduce_product(): diag_a = lax.ppermute(early[0], 'grp', x)  43.2 us
  transfers between devices with their start and end apart: 54, of which 22 were waited for; matrix products, arithmetic and copies ran while one was open for 45% of the time, Pallas kernels for 12%

profile of v2, /device:TPU:18, one launch (start us, length us, event | category | flops | bytes accessed | tf_op | source)
XLA Modules:
  0.0 1249.0 jit_solution(14306309535919414026)
XLA Ops:
  17.1 12.3 all-gather.6
  29.6 9.0 copy.253
  41.3 9.2 reshape.2534
  59.6 48.5 %all-gather.16.cloned.1.call-done = bf16[1536,4096]{1,0:T(8,128)(2,1)} async-done(((bf16[48,4096]{1,0:T(8,128)(2,1)}), bf16[1536,4096]{1,0:T(8,128)(2,1)}) %all-gather.16.cloned.1.call-update) | async-done | bytes 12582928 | tf_op jit(solution)/shard_map/all_gather | solution.py:355
  108.1 9.7 fusion.37
  122.1 8.7 all-gather.18.cloned.1.call-done.gates_ref
  134.5 63.3 %mixer_forward.1 = (bf16[2,512,2048]{2,1,0:T(8,128)(2,1)S(1)}, f32[2,512,2048]{2,1,0:T(8,128)}, f32[2,512,2048]{2,1,0:T(8,128)}, f32[2,512,2048]{2,1,0:T(8,128)}, f32[2,2,8,2048]{3,2,1,0:T(8,128)S(1)}) custom-call(bf16[2,512,2048]{2,1,0:T(8,128)(2,1)S(1)} %bitcast.811, bf16[2,8,2048]{2,1,0:T(8,128)(2,1)S(1)} %collective-permute-done.halo_ref, ...), custom_call_target="tpu_custom_call" | custom-call | tf_op jit(solution)/shard_map/mixer_forward/pallas_call | solution.py:255
  200.4 12.5 %all-gather.1 = f32[16,2,2048]{2,1,0:T(2,128)S(1)} all-gather(f32[2,2,2048]{2,1,0:T(2,128)S(1)} %copy.226), channel_id=3, replica_groups=mesh['grp'=4,'seq'=8] {'seq'}, dimensions={0}, use_global_device_ids=true | all-gather | bytes 294912 | tf_op jit(solution)/shard_map/all_gather | solution.py:434
  213.4 12.8 %fusion.19.state_ref = f32[2,512,2048]{2,1,0:T(8,128)} fusion(f32[2,512,2048]{2,1,0:T(8,128)} %get-tuple-element.30, f32[2,512,2048]{2,1,0:T(8,128)} %get-tuple-element.31, f32[2,8,2048]{2,1,0:T(8,128)S(1)} %stack.9), kind=kLoop, calls=%fused_computation.44 | loop fusion | flops 4194304 | bytes 25296896 | tf_op jit(solution)/shard_map/add | solution.py:524
  226.2 18.0 %fusion.18 = (bf16[1024,2048]{1,0:T(8,128)(2,1)}, f32[1024,2048]{1,0:T(8,128)}) fusion(f32[2,512,2048]{2,1,0:T(8,128)} %get-tuple-element.31, f32[2,512,2048]{2,1,0:T(8,128)} %get-tuple-element.30, f32[2,8,2048]{2,1,0:T(8,128)S(1)} %stack.9, bf16[1024,1536]{1,0:T(8,128)(2,1)S(1)} %copy-done.24, bf16[1536,4096]{1,0:T(8,128)(2,1)} %all-gather.16.cloned.1.call-done), kind=kOutput, calls=%fused_computation.42 | convolution fusion | flops 6467616768 | bytes 38928384 | tf_op jit(solution)/shard_map/dot_general | solution.py:504
  244.2 7.8 reshape.2512
  252.0 11.0 multiply_reduce_fusion.2
  272.6 11.3 constant_dynamic-slice_fusion.3
  283.9 10.8 copy.260
  294.7 10.5 copy.261
  311.7 62.7 %all-gather.22.cloned.1.call-done = bf16[1536,9216]{1,0:T(8,128)(2,1)} async-done(((bf16[48,9216]{1,0:T(8,128)(2,1)}), bf16[1536,9216]{1,0:T(8,128)(2,1)}) %all-gather.22.cloned.1.call-update) | async-done | bytes 28311568 | tf_op jit(solution)/shard_map/all_gather | solution.py:355
  374.5 22.2 %fusion.10 = f32[1024,4608]{1,0:T(8,128)} fusion(bf16[1024,1536]{1,0:T(8,128)(2,1)} %multiply_convert_fusion.3, bf16[1536,9216]{1,0:T(8,128)(2,1)} %all-gather.22.cloned.1.call-done), kind=kOutput, calls=%fused_computation.24 | convolution fusion | flops 14495514624 | bytes 36175872 | tf_op jit(solution)/shard_map/dot_general | solution.py:530
  396.7 29.6 %fusion.7 = (bf16[1024,4608]{1,0:T(8,128)(2,1)}, f32[1024,4608]{1,0:T(8,128)}) fusion(f32[1024,4608]{1,0:T(8,128)} %fusion.10, bf16[1024,1536]{1,0:T(8,128)(2,1)S(1)} %copy-done.23, bf16[1536,9216]{1,0:T(8,128)(2,1)} %all-gather.22.cloned.1.call-done), kind=kOutput, calls=%fused_computation.17 | convolution fusion | flops 14542700544 | bytes 64487424 | tf_op jit(solution)/shard_map/dot_general | solution.py:531
  426.3 20.4 %convolution_convert_fusion = bf16[4608,1536]{1,0:T(8,128)(2,1)} fusion(bf16[1024,4608]{1,0:T(8,128)(2,1)} %get-tuple-element.112, bf16[1024,1536]{1,0:T(8,128)(2,1)} %bitcast.845), kind=kOutput, calls=%fused_computation.10 | convolution fusion | flops 14502592512 | bytes 26738688 | tf_op jit(solution)/shard_map/dot_general | solution.py:372
  446.8 31.8 %all-gather.24.cloned.1.call-done = bf16[4608,1536]{1,0:T(8,128)(2,1)} async-done(((bf16[144,1536]{1,0:T(8,128)(2,1)}), bf16[4608,1536]{1,0:T(8,128)(2,1)}) %all-gather.24.cloned.1.call-update) | async-done | bytes 14155792 | tf_op jit(solution)/shard_map/all_gather | solution.py:355
  478.6 35.2 %multiply_convert_fusion.1 = (bf16[1024,4608]{1,0:T(8,128)(2,1)}, bf16[1024,4608]{1,0:T(8,128)(2,1)}) fusion(f32[1024,4608]{1,0:T(8,128)} %get-tuple-element.113, f32[1024,4608]{1,0:T(8,128)} %fusion.10, bf16[1024,1536]{1,0:T(8,128)(2,1)} %bitcast.846, bf16[4608,1536]{1,0:T(8,128)(2,1)} %all-gather.24.cloned.1.call-done), kind=kOutput, calls=%fused_computation.19 | convolution fusion | flops 14599323648 | bytes 73924608 | tf_op jit(solution)/shard_map/rd,fd->rf/dot_general | solution.py:539
  513.7 12.8 %fusion.36 = (bf16[1024,2304]{1,0:T(8,128)(2,1)S(1)}, bf16[1024,2304]{1,0:T(8,128)(2,1)}, bf16[1024,2304]{1,0:T(8,128)(2,1)S(1)}, bf16[1024,2304]{1,0:T(8,128)(2,1)S(1)}) fusion(s32[]{:T(128)S(6)} %select_n.828, bf16[1024,4608]{1,0:T(8,128)(2,1)} %get-tuple-element.71, bf16[1024,4608]{1,0:T(8,128)(2,1)} %get-tuple-element.72, s32[]{:T(128)S(6)} %select_n.780, ...), kind=kLoop, calls=%fused_computation.78 | loop fusion | flops 37748736 | bytes 37748752 | tf_op jit(solution)/shard_map/concatenate | solution.py:543
  526.5 13.0 %convolution_convert_fusion.4 = bf16[768,2304]{1,0:T(8,128)(2,1)} fusion(bf16[1024,768]{0,1:T(8,128)(2,1)} %bitcast.886, bf16[1024,2304]{1,0:T(8,128)(2,1)} %get-tuple-element.74), kind=kOutput, calls=%fused_computation.74 | convolution fusion | flops 3625648128 | bytes 9830400 | tf_op jit(solution)/shard_map/dot_general | solution.py:372
  560.4 11.0 pad_maximum_fusion
  591.2 38.3 %multiply_reduce_fusion.1 = (f32[1024]{0:T(1024)S(1)}, f32[1024,1536]{1,0:T(8,128)}) fusion(f32[1024,1536]{1,0:T(8,128)S(1)} %bitcast.827, f32[1536]{0:T(1024)S(1)} %copy-done.59, bf16[1024,9216]{1,0:T(8,128)(2,1)} %pad_maximum_fusion, bf16[1536,9216]{1,0:T(8,128)(2,1)} %all-gather.22.cloned.1.call-done), kind=kOutput, calls=%fused_computation.67 | convolution fusion | flops 28995747840 | bytes 59779072 | tf_op jit(solution)/shard_map/rf,df->rd/dot_general | solution.py:547
  629.5 6.5 fusion.263
  653.9 9.0 fusion.272
  662.9 38.2 %mixer_reverse.1 = (bf16[2,512,2048]{2,1,0:T(8,128)(2,1)S(1)}, f32[2,512,2048]{2,1,0:T(8,128)S(1)}, f32[2,512,2048]{2,1,0:T(8,128)}, f32[2,2,8,2048]{3,2,1,0:T(8,128)S(1)}) custom-call(f32[2,512,2048]{2,1,0:T(8,128)} %bitcast.834, f32[2,512,2048]{2,1,0:T(8,128)} %bitcast.822, f32[2,512,2048]{2,1,0:T(8,128)} %get-tuple-element.36.keep_ref, ...), custom_call_target="tpu_custom_call" | custom-call | tf_op jit(solution)/shard_map/mixer_reverse/pallas_call | solution.py:289
  706.9 13.7 %all-gather.2 = f32[16,2,2048]{2,1,0:T(2,128)S(1)} all-gather(f32[2,2,2048]{2,1,0:T(2,128)S(1)} %copy.250), channel_id=4, replica_groups=mesh['grp'=4,'seq'=8] {'seq'}, dimensions={0}, use_global_device_ids=true | all-gather | bytes 294912 | tf_op jit(solution)/shard_map/all_gather | solution.py:434
  723.3 51.9 %mixer_backward.1 = (bf16[2,512,2048]{2,1,0:T(8,128)(2,1)S(1)}, f32[2,8,2048]{2,1,0:T(8,128)S(1)}, f32[2,8,2048]{2,1,0:T(8,128)S(1)}, f32[16,128,256]{2,1,0:T(8,...) custom-call(f32[2,512,2048]{2,1,0:T(8,128)} %copy-done.6, f32[2,512,2048]{2,1,0:T(8,128)} %get-tuple-element.38.prod_ref, ...), custom_call_target="tpu_custom_call" | custom-call | tf_op jit(solution)/shard_map/mixer_backward/pallas_call | solution.py:312
  783.1 18.1 %fusion = bf16[528,128]{1,0:T(8,128)(2,1)S(1)} fusion(bf16[4176,128]{1,0:T(8,128)(2,1)S(1)} %convert_element_type.547), kind=kCustom, calls=%all-reduce-scatter | all-reduce-scatter fusion | flops 540673 | bytes 1204736
  803.2 6.4 fusion.114
  817.1 7.3 fusion.43
  836.2 16.2 %collective-permute-done.34 = bf16[384,2304]{1,0:T(8,128)(2,1)} collective-permute-done((bf16[384,2304]{1,0:T(8,128)(2,1)}, bf16[384,2304]{1,0:T(8,128)(2,1)}, u32[]{:S(2)}, u32[]{:S(2)}) %collective-permute-start.34) | collective-permute-done | bytes 1769504 | tf_op jit(solution)/shard_map/ppermute | solution.py:414
  863.8 12.4 collective-permute-done.14
  886.9 11.3 collective-permute-done.18
  905.2 18.1 %collective-permute-done.15 = bf16[384,1024]{1,0:T(8,128)(2,1)} collective-permute-done((bf16[384,1024]{1,0:T(8,128)(2,1)}, bf16[384,1024]{1,0:T(8,128)(2,1)}, u32[]{:S(2)}, u32[]{:S(2)}) %collective-permute-start.15) | collective-permute-done | bytes 786464 | tf_op jit(solution)/shard_map/ppermute | solution.py:419
  941.0 24.8 %collective-permute-done.38 = bf16[384,2304]{1,0:T(8,128)(2,1)S(1)} collective-permute-done((bf16[384,2304]{1,0:T(8,128)(2,1)}, bf16[384,2304]{1,0:T(8,128)(2,1)S(1)}, u32[]{:S(2)}, u32[]{:S(2)}) %collective-permute-start.38) | collective-permute-done | bytes 1769504 | tf_op jit(solution)/shard_map/ppermute | solution.py:417
  969.7 32.2 %collective-permute-done.35 = bf16[384,2304]{1,0:T(8,128)(2,1)S(1)} collective-permute-done((bf16[384,2304]{1,0:T(8,128)(2,1)S(1)}, bf16[384,2304]{1,0:T(8,128)(2,1)S(1)}, u32[]{:S(2)}, u32[]{:S(2)}) %collective-permute-start.35) | collective-permute-done | bytes 1769504 | tf_op jit(solution)/shard_map/ppermute | solution.py:419
  1017.9 54.7 %collective-permute-done.39 = bf16[192,2304]{1,0:T(8,128)(2,1)S(1)} collective-permute-done((bf16[192,2304]{1,0:T(8,128)(2,1)}, bf16[192,2304]{1,0:T(8,128)(2,1)S(1)}, u32[]{:S(2)}, u32[]{:S(2)}) %collective-permute-start.39) | collective-permute-done | bytes 884768 | tf_op jit(solution)/shard_map/ppermute | solution.py:426
  1072.6 15.9 %collective-permute-done.40 = bf16[192,2304]{1,0:T(8,128)(2,1)S(1)} collective-permute-done((bf16[192,2304]{1,0:T(8,128)(2,1)S(1)}, bf16[192,2304]{1,0:T(8,128)(2,1)S(1)}, u32[]{:S(2)}, u32[]{:S(2)}) %collective-permute-start.40) | collective-permute-done | bytes 884768 | tf_op jit(solution)/shard_map/ppermute | solution.py:426
  1091.1 22.4 %add_convert_fusion = bf16[1024,1536]{1,0:T(8,128)(2,1)} fusion(f32[1024,1536]{1,0:T(8,128)} %copy-done.21, bf16[1024,4608]{1,0:T(8,128)(2,1)} %get-tuple-element.112, bf16[4608,1536]{1,0:T(8,128)(2,1)} %all-gather.24.cloned.1.call-done), kind=kOutput, calls=%fused_computation.68 | convolution fusion | flops 14498660352 | bytes 33030144 | tf_op jit(solution)/shard_map/dot_general | solution.py:533
  1123.0 14.6 %collective-permute-done.24 = bf16[512,384]{1,0:T(8,128)(2,1)S(1)} collective-permute-done((bf16[512,384]{1,0:T(8,128)(2,1)S(1)}, bf16[512,384]{1,0:T(8,128)(2,1)S(1)}, u32[]{:S(2)}, u32[]{:S(2)}) %collective-permute-start.24) | collective-permute-done | bytes 393248 | tf_op jit(solution)/shard_map/ppermute | solution.py:414
  1141.4 8.0 pad_maximum_fusion.1
  1156.5 7.8 collective-permute-done.25
  1171.3 11.4 collective-permute-done.29
  1183.8 11.0 all-gather.4
  1196.7 19.0 %fusion.32 = (f32[1024]{0:T(1024)S(1)}, f32[1024,1536]{1,0:T(8,128)S(1)}) fusion(bf16[2,512,1536]{2,1,0:T(8,128)(2,1)} %param.12, f32[1536]{0:T(1024)S(1)} %copy-done.57, bf16[1024,4096]{1,0:T(8,128)(2,1)} %pad_maximum_fusion.1, bf16[1536,4096]{1,0:T(8,128)(2,1)} %all-gather.16.cloned.1.call-done), kind=kOutput, calls=%fused_computation.64 | convolution fusion | flops 12891192320 | bytes 30418944 | tf_op jit(solution)/shard_map/rp,dp->rd/dot_general | solution.py:595
  (430 shorter events, 269.4 us)
Async XLA Ops:
  7.2 100.8 %all-gather.16.cloned.1.call-start = ((), (), s32[]{:S(2)}) async-start(), calls=%async_computation.2 | async-start | bytes 12976128 | tf_op jit(solution)/shard_map/all_gather | solution.py:355
  9.2 121.6 %all-gather.18.cloned.1.call-start = ((), (), s32[]{:S(2)}) async-start(), calls=%async_computation.3 | async-start | bytes 1179648 | tf_op jit(solution)/shard_map/all_gather | solution.py:494
  10.0 242.0 %all-gather.20.cloned.1.call-start = ((), (), s32[]{:S(2)}) async-start(), calls=%async_computation.4 | async-start | bytes 6488064 | tf_op jit(solution)/shard_map/all_gather | solution.py:355
  11.7 362.8 %all-gather.22.cloned.1.call-start = ((), (), s32[]{:S(2)}) async-start(), calls=%async_computation.5 | async-start | bytes 29196288 | tf_op jit(solution)/shard_map/all_gather | solution.py:355
  13.9 464.7 %all-gather.24.cloned.1.call-start = ((), (), s32[]{:S(2)}) async-start(), calls=%async_computation.6 | async-start | bytes 14598144 | tf_op jit(solution)/shard_map/all_gather | solution.py:355
  14.7 872.1 %reduce-scatter.5.cloned.1.call-start = ((), (), s32[]{:S(2)}) async-start(), calls=%async_computation.8 | async-start | bytes 15925248 | tf_op jit(solution)/shard_map/reduce_scatter | solution.py:376
  14.9 44.7 %collective-permute-start.1 = (s32[2,3]{1,0:T(2,128)S(1)}, s32[2,3]{1,0:T(2,128)S(1)}, u32[]{:S(2)}, u32[]{:S(2)}) collective-permute-start(s32[2,3]{1,0:T(2,128)S(1)} %slice.399), channel_id=1, source_target_pairs={{0,1},{1,2},{2,3},{3,4},{4,5},{5,6},{6,7},{8,9},{9,10},{10,11},{11... | collective-permute-start | bytes 80 | tf_op jit(solution)/shard_map/ppermute | solution.py:25
  446.7 702.6 %all-reduce.5.cloned.1.call-start = ((), (), s32[]{:S(2)}) async-start(), calls=%async_computation.7 | async-start | bytes 270336 | tf_op jit(solution)/shard_map/psum | solution.py:581
  545.2 36.1 %collective-permute-start.4 = (bf16[768,2304]{1,0:T(8,128)(2,1)}, bf16[768,2304]{1,0:T(8,128)(2,1)}, u32[]{:S(2)}, u32[]{:S(2)}) collective-permute-start(bf16[768,2304]{1,0:T(8,128)(2,1)} %convolution_convert_fusion.2), channel_id=1, source_target_pairs={{0,1},{1,0},{2,3},{3,2},{4,5},{5,4},{6,7},{7,6},{8,9},{9,8},{10,11... | collective-permute-start | bytes 10616840 | tf_op jit(solution)/shard_map/ppermute | solution.py:403
  545.4 26.0 %collective-permute-start.2 = (bf16[768,2304]{1,0:T(8,128)(2,1)}, bf16[768,2304]{1,0:T(8,128)(2,1)}, u32[]{:S(2)}, u32[]{:S(2)}) collective-permute-start(bf16[768,2304]{1,0:T(8,128)(2,1)} %convolution_convert_fusion.4), channel_id=1, source_target_pairs={{0,1},{1,0},{2,3},{3,2},{4,5},{5,4},{6,7},{7,6},{8,9},{9,8},{10,11... | collective-permute-start | bytes 10616840 | tf_op jit(solution)/shard_map/ppermute | solution.py:403
  556.4 29.9 %collective-permute-start.3 = (bf16[768,2304]{1,0:T(8,128)(2,1)}, bf16[768,2304]{1,0:T(8,128)(2,1)}, u32[]{:S(2)}, u32[]{:S(2)}) collective-permute-start(bf16[768,2304]{1,0:T(8,128)(2,1)} %convolution_convert_fusion.3), channel_id=1, source_target_pairs={{0,1},{1,0},{2,3},{3,2},{4,5},{5,4},{6,7},{7,6},{8,9},{9,8},{10,11... | collective-permute-start | bytes 10616840 | tf_op jit(solution)/shard_map/ppermute | solution.py:403
  809.5 42.9 %collective-permute-start.34 = (bf16[384,2304]{1,0:T(8,128)(2,1)}, bf16[384,2304]{1,0:T(8,128)(2,1)}, u32[]{:S(2)}, u32[]{:S(2)}) collective-permute-start(bf16[384,2304]{1,0:T(8,128)(2,1)} %add_convert_fusion.8), channel_id=1, source_target_pairs={{0,8},{8,0},{16,24},{24,16},{1,9},{9,1},{17,25},{25,17},{2,10},{10... | collective-permute-start | bytes 5308424 | tf_op jit(solution)/shard_map/ppermute | solution.py:414
  810.5 70.7 %collective-permute-start.36 = (bf16[384,2304]{1,0:T(8,128)(2,1)}, bf16[384,2304]{1,0:T(8,128)(2,1)}, u32[]{:S(2)}, u32[]{:S(2)}) collective-permute-start(bf16[384,2304]{1,0:T(8,128)(2,1)} %add_convert_fusion.7), channel_id=1, source_target_pairs={{0,16},{8,24},{16,0},{24,8},{1,17},{9,25},{17,1},{25,9},{2,18},{10... | collective-permute-start | bytes 5308424 | tf_op jit(solution)/shard_map/ppermute | solution.py:415
  816.4 380.3 %reduce-scatter.7.cloned.1.call-start = ((), (), s32[]{:S(2)}) async-start(), calls=%async_computation.9 | async-start | bytes 2211840 | tf_op jit(solution)/shard_map/reduce_scatter | solution.py:377
  826.3 29.4 %collective-permute-start.9 = (bf16[768,1024]{1,0:T(8,128)(2,1)S(1)}, bf16[768,1024]{1,0:T(8,128)(2,1)S(1)}, u32[]{:S(2)}, u32[]{:S(2)}) collective-permute-start(bf16[768,1024]{1,0:T(8,128)(2,1)S(1)} %convolution_convert_fusion.8), channel_id=1, source_target_pairs={{0,1},{1,0},{2,3},{3,2},{4,5},{5,4},{6,7},{7,6},{8,9},{9,8},{10,11... | collective-permute-start | bytes 4718600 | tf_op jit(solution)/shard_map/ppermute | solution.py:403
  833.8 25.1 %collective-permute-start.11 = (bf16[768,1024]{1,0:T(8,128)(2,1)S(1)}, bf16[768,1024]{1,0:T(8,128)(2,1)S(1)}, u32[]{:S(2)}, u32[]{:S(2)}) collective-permute-start(bf16[768,1024]{1,0:T(8,128)(2,1)S(1)} %convolution_convert_fusion.6), channel_id=1, source_target_pairs={{0,1},{1,0},{2,3},{3,2},{4,5},{5,4},{6,7},{7,6},{8,9},{9,8},{10,11... | collective-permute-start | bytes 4718600 | tf_op jit(solution)/shard_map/ppermute | solution.py:403
  834.2 27.7 %collective-permute-start.10 = (bf16[768,1024]{1,0:T(8,128)(2,1)S(1)}, bf16[768,1024]{1,0:T(8,128)(2,1)S(1)}, u32[]{:S(2)}, u32[]{:S(2)}) collective-permute-start(bf16[768,1024]{1,0:T(8,128)(2,1)S(1)} %convolution_convert_fusion.7), channel_id=1, source_target_pairs={{0,1},{1,0},{2,3},{3,2},{4,5},{5,4},{6,7},{7,6},{8,9},{9,8},{10,11... | collective-permute-start | bytes 4718600 | tf_op jit(solution)/shard_map/ppermute | solution.py:403
  852.4 29.6 %collective-permute-start.12 = (bf16[768,1024]{1,0:T(8,128)(2,1)S(1)}, bf16[768,1024]{1,0:T(8,128)(2,1)}, u32[]{:S(2)}, u32[]{:S(2)}) collective-permute-start(bf16[768,1024]{1,0:T(8,128)(2,1)S(1)} %convolution_convert_fusion.5), channel_id=1, source_target_pairs={{0,1},{1,0},{2,3},{3,2},{4,5},{5,4},{6,7},{7,6},{8,9},{9,8},{10,11... | collective-permute-start | bytes 4718600 | tf_op jit(solution)/shard_map/ppermute | solution.py:403
  856.6 19.5 %collective-permute-start.14 = (bf16[384,1024]{1,0:T(8,128)(2,1)S(1)}, bf16[384,1024]{1,0:T(8,128)(2,1)S(1)}, u32[]{:S(2)}, u32[]{:S(2)}) collective-permute-start(bf16[384,1024]{1,0:T(8,128)(2,1)S(1)} %add_convert_fusion.16), channel_id=1, source_target_pairs={{0,8},{8,0},{16,24},{24,16},{1,9},{9,1},{17,25},{25,17},{2,10},{10... | collective-permute-start | bytes 2359304 | tf_op jit(solution)/shard_map/ppermute | solution.py:414
  859.0 19.2 %collective-permute-start.16 = (bf16[384,1024]{1,0:T(8,128)(2,1)S(1)}, bf16[384,1024]{1,0:T(8,128)(2,1)S(1)}, u32[]{:S(2)}, u32[]{:S(2)}) collective-permute-start(bf16[384,1024]{1,0:T(8,128)(2,1)S(1)} %add_convert_fusion.15), channel_id=1, source_target_pairs={{0,16},{8,24},{16,0},{24,8},{1,17},{9,25},{17,1},{25,9},{2,18},{10... | collective-permute-start | bytes 2359304 | tf_op jit(solution)/shard_map/ppermute | solution.py:415
  861.9 78.9 %collective-permute-start.32 = (bf16[768,2304]{1,0:T(8,128)(2,1)}, bf16[768,2304]{1,0:T(8,128)(2,1)}, u32[]{:S(2)}, u32[]{:S(2)}) collective-permute-start(bf16[768,2304]{1,0:T(8,128)(2,1)} %convolution_convert_fusion.1), channel_id=1, source_target_pairs={{0,1},{1,0},{2,3},{3,2},{4,5},{5,4},{6,7},{7,6},{8,9},{9,8},{10,11... | collective-permute-start | bytes 10616840 | tf_op jit(solution)/shard_map/ppermute | solution.py:403
  876.2 22.1 %collective-permute-start.18 = (bf16[384,1024]{1,0:T(8,128)(2,1)}, bf16[384,1024]{1,0:T(8,128)(2,1)}, u32[]{:S(2)}, u32[]{:S(2)}) collective-permute-start(bf16[384,1024]{1,0:T(8,128)(2,1)} %add_convert_fusion.13), channel_id=1, source_target_pairs={{0,16},{8,24},{16,0},{24,8},{1,17},{9,25},{17,1},{25,9},{2,18},{10... | collective-permute-start | bytes 2359304 | tf_op jit(solution)/shard_map/ppermute | solution.py:417
  878.2 25.1 %collective-permute-start.13 = (bf16[384,1024]{1,0:T(8,128)(2,1)}, bf16[384,1024]{1,0:T(8,128)(2,1)}, u32[]{:S(2)}, u32[]{:S(2)}) collective-permute-start(bf16[384,1024]{1,0:T(8,128)(2,1)} %add_convert_fusion.14), channel_id=1, source_target_pairs={{0,8},{8,0},{16,24},{24,16},{1,9},{9,1},{17,25},{25,17},{2,10},{10... | collective-permute-start | bytes 2359304 | tf_op jit(solution)/shard_map/ppermute | solution.py:416
  881.2 42.1 %collective-permute-start.15 = (bf16[384,1024]{1,0:T(8,128)(2,1)}, bf16[384,1024]{1,0:T(8,128)(2,1)}, u32[]{:S(2)}, u32[]{:S(2)}) collective-permute-start(bf16[384,1024]{1,0:T(8,128)(2,1)} %add_convert_fusion.12), channel_id=1, source_target_pairs={{0,16},{8,24},{16,0},{24,8},{1,17},{9,25},{17,1},{25,9},{2,18},{10... | collective-permute-start | bytes 2359304 | tf_op jit(solution)/shard_map/ppermute | solution.py:419
  882.0 46.3 %collective-permute-start.17 = (bf16[384,1024]{1,0:T(8,128)(2,1)}, bf16[384,1024]{1,0:T(8,128)(2,1)}, u32[]{:S(2)}, u32[]{:S(2)}) collective-permute-start(bf16[384,1024]{1,0:T(8,128)(2,1)} %add_convert_fusion.10), channel_id=1, source_target_pairs={{0,8},{8,0},{16,24},{24,16},{1,9},{9,1},{17,25},{25,17},{2,10},{10... | collective-permute-start | bytes 2359304 | tf_op jit(solution)/shard_map/ppermute | solution.py:418
  886.9 334.0 %all-gather.28.cloned.1.call-start = ((), (), s32[]{:S(2)}) async-start(), calls=%async_computation.11 | async-start | bytes 1966080 | tf_op jit(solution)/shard_map/all_gather | solution.py:427
  898.3 67.6 %collective-permute-start.38 = (bf16[384,2304]{1,0:T(8,128)(2,1)}, bf16[384,2304]{1,0:T(8,128)(2,1)S(1)}, u32[]{:S(2)}, u32[]{:S(2)}) collective-permute-start(bf16[384,2304]{1,0:T(8,128)(2,1)} %add_convert_fusion.5), channel_id=1, source_target_pairs={{0,16},{8,24},{16,0},{24,8},{1,17},{9,25},{17,1},{25,9},{2,18},{10... | collective-permute-start | bytes 5308424 | tf_op jit(solution)/shard_map/ppermute | solution.py:417
  903.3 64.6 %collective-permute-start.33 = (bf16[384,2304]{1,0:T(8,128)(2,1)}, bf16[384,2304]{1,0:T(8,128)(2,1)S(1)}, u32[]{:S(2)}, u32[]{:S(2)}) collective-permute-start(bf16[384,2304]{1,0:T(8,128)(2,1)} %add_convert_fusion.6), channel_id=1, source_target_pairs={{0,8},{8,0},{16,24},{24,16},{1,9},{9,1},{17,25},{25,17},{2,10},{10... | collective-permute-start | bytes 5308424 | tf_op jit(solution)/shard_map/ppermute | solution.py:416
  923.3 78.6 %collective-permute-start.35 = (bf16[384,2304]{1,0:T(8,128)(2,1)S(1)}, bf16[384,2304]{1,0:T(8,128)(2,1)S(1)}, u32[]{:S(2)}, u32[]{:S(2)}) collective-permute-start(bf16[384,2304]{1,0:T(8,128)(2,1)S(1)} %add_convert_fusion.4), channel_id=1, source_target_pairs={{0,16},{8,24},{16,0},{24,8},{1,17},{9,25},{17,1},{25,9},{2,18},{10... | collective-permute-start | bytes 5308424 | tf_op jit(solution)/shard_map/ppermute | solution.py:419
  928.3 75.8 %collective-permute-start.37 = (bf16[384,2304]{1,0:T(8,128)(2,1)}, bf16[384,2304]{1,0:T(8,128)(2,1)S(1)}, u32[]{:S(2)}, u32[]{:S(2)}) collective-permute-start(bf16[384,2304]{1,0:T(8,128)(2,1)} %add_convert_fusion.2), channel_id=1, source_target_pairs={{0,8},{8,0},{16,24},{24,16},{1,9},{9,1},{17,25},{25,17},{2,10},{10... | collective-permute-start | bytes 5308424 | tf_op jit(solution)/shard_map/ppermute | solution.py:418
  940.8 66.6 %collective-permute-start.19 = (bf16[192,1024]{1,0:T(8,128)(2,1)S(1)}, bf16[192,1024]{1,0:T(8,128)(2,1)S(1)}, u32[]{:S(2)}, u32[]{:S(2)}) collective-permute-start(bf16[192,1024]{1,0:T(8,128)(2,1)S(1)} %get-tuple-element.92), channel_id=1, source_target_pairs={{0,2},{1,3},{2,4},{3,5},{4,6},{5,7},{6,0},{7,1},{8,10},{9,11},{10,... | collective-permute-start | bytes 1179656 | tf_op jit(solution)/shard_map/ppermute | solution.py:426
  965.8 41.5 %collective-permute-start.21 = (bf16[192,1024]{1,0:T(8,128)(2,1)S(1)}, bf16[192,1024]{1,0:T(8,128)(2,1)S(1)}, u32[]{:S(2)}, u32[]{:S(2)}) collective-permute-start(bf16[192,1024]{1,0:T(8,128)(2,1)S(1)} %get-tuple-element.93), channel_id=1, source_target_pairs={{0,6},{1,7},{2,0},{3,1},{4,2},{5,3},{6,4},{7,5},{8,14},{9,15},{10,... | collective-permute-start | bytes 1179656 | tf_op jit(solution)/shard_map/ppermute | solution.py:426
  967.9 39.5 %collective-permute-start.20 = (bf16[192,1024]{1,0:T(8,128)(2,1)S(1)}, bf16[192,1024]{1,0:T(8,128)(2,1)S(1)}, u32[]{:S(2)}, u32[]{:S(2)}) collective-permute-start(bf16[192,1024]{1,0:T(8,128)(2,1)S(1)} %get-tuple-element.94), channel_id=1, source_target_pairs={{0,4},{1,5},{2,6},{3,7},{4,0},{5,1},{6,2},{7,3},{8,12},{9,13},{10,... | collective-permute-start | bytes 1179656 | tf_op jit(solution)/shard_map/ppermute | solution.py:426
  1008.5 220.5 %all-gather.30.cloned.1.call-start = ((), (), s32[]{:S(2)}) async-start(), calls=%async_computation.12 | async-start | bytes 4423680 | tf_op jit(solution)/shard_map/all_gather | solution.py:427
  1011.9 60.7 %collective-permute-start.39 = (bf16[192,2304]{1,0:T(8,128)(2,1)}, bf16[192,2304]{1,0:T(8,128)(2,1)S(1)}, u32[]{:S(2)}, u32[]{:S(2)}) collective-permute-start(bf16[192,2304]{1,0:T(8,128)(2,1)} %get-tuple-element.83), channel_id=1, source_target_pairs={{0,2},{1,3},{2,4},{3,5},{4,6},{5,7},{6,0},{7,1},{8,10},{9,11},{10,... | collective-permute-start | bytes 2654216 | tf_op jit(solution)/shard_map/ppermute | solution.py:426
  1013.4 59.2 %collective-permute-start.41 = (bf16[192,2304]{1,0:T(8,128)(2,1)}, bf16[192,2304]{1,0:T(8,128)(2,1)S(1)}, u32[]{:S(2)}, u32[]{:S(2)}) collective-permute-start(bf16[192,2304]{1,0:T(8,128)(2,1)} %get-tuple-element.84), channel_id=1, source_target_pairs={{0,6},{1,7},{2,0},{3,1},{4,2},{5,3},{6,4},{7,5},{8,14},{9,15},{10,... | collective-permute-start | bytes 2654216 | tf_op jit(solution)/shard_map/ppermute | solution.py:426
  1013.9 74.6 %collective-permute-start.40 = (bf16[192,2304]{1,0:T(8,128)(2,1)S(1)}, bf16[192,2304]{1,0:T(8,128)(2,1)S(1)}, u32[]{:S(2)}, u32[]{:S(2)}) collective-permute-start(bf16[192,2304]{1,0:T(8,128)(2,1)S(1)} %get-tuple-element.85), channel_id=1, source_target_pairs={{0,4},{1,5},{2,6},{3,7},{4,0},{5,1},{6,2},{7,3},{8,12},{9,13},{10,... | collective-permute-start | bytes 2654216 | tf_op jit(solution)/shard_map/ppermute | solution.py:426
  1091.0 147.5 %all-gather.26.cloned.1.call-start = ((), (), s32[]{:S(2)}) async-start(), calls=%async_computation.10 | async-start | bytes 2211840 | tf_op jit(solution)/shard_map/all_gather | solution.py:378
  1117.3 20.3 %collective-permute-start.24 = (bf16[512,384]{1,0:T(8,128)(2,1)S(1)}, bf16[512,384]{1,0:T(8,128)(2,1)S(1)}, u32[]{:S(2)}, u32[]{:S(2)}) collective-permute-start(bf16[512,384]{1,0:T(8,128)(2,1)S(1)} %copy-done.73), channel_id=1, source_target_pairs={{0,8},{8,0},{16,24},{24,16},{1,9},{9,1},{17,25},{25,17},{2,10},{10... | collective-permute-start | bytes 1179656 | tf_op jit(solution)/shard_map/ppermute | solution.py:414
  1119.2 20.4 %collective-permute-start.26 = (bf16[512,384]{1,0:T(8,128)(2,1)S(1)}, bf16[512,384]{1,0:T(8,128)(2,1)S(1)}, u32[]{:S(2)}, u32[]{:S(2)}) collective-permute-start(bf16[512,384]{1,0:T(8,128)(2,1)S(1)} %copy-done.72), channel_id=1, source_target_pairs={{0,16},{8,24},{16,0},{24,8},{1,17},{9,25},{17,1},{25,9},{2,18},{10... | collective-permute-start | bytes 1179656 | tf_op jit(solution)/shard_map/ppermute | solution.py:415
  1120.3 32.8 %collective-permute-start.22 = (bf16[1024,384]{1,0:T(8,128)(2,1)}, bf16[1024,384]{1,0:T(8,128)(2,1)S(1)}, u32[]{:S(2)}, u32[]{:S(2)}) collective-permute-start(bf16[1024,384]{1,0:T(8,128)(2,1)} %convolution_convert_fusion.9), channel_id=1, source_target_pairs={{0,1},{1,0},{2,3},{3,2},{4,5},{5,4},{6,7},{7,6},{8,9},{9,8},{10,11... | collective-permute-start | bytes 2359304 | tf_op jit(solution)/shard_map/ppermute | solution.py:403
  1120.4 36.0 %collective-permute-start.28 = (bf16[512,384]{1,0:T(8,128)(2,1)}, bf16[512,384]{1,0:T(8,128)(2,1)S(1)}, u32[]{:S(2)}, u32[]{:S(2)}) collective-permute-start(bf16[512,384]{1,0:T(8,128)(2,1)} %add_convert_fusion.21), channel_id=1, source_target_pairs={{0,16},{8,24},{16,0},{24,8},{1,17},{9,25},{17,1},{25,9},{2,18},{10... | collective-permute-start | bytes 1179656 | tf_op jit(solution)/shard_map/ppermute | solution.py:417
  1122.1 34.3 %collective-permute-start.23 = (bf16[512,384]{1,0:T(8,128)(2,1)}, bf16[512,384]{1,0:T(8,128)(2,1)}, u32[]{:S(2)}, u32[]{:S(2)}) collective-permute-start(bf16[512,384]{1,0:T(8,128)(2,1)} %add_convert_fusion.22), channel_id=1, source_target_pairs={{0,8},{8,0},{16,24},{24,16},{1,9},{9,1},{17,25},{25,17},{2,10},{10... | collective-permute-start | bytes 1179656 | tf_op jit(solution)/shard_map/ppermute | solution.py:416
  1138.5 25.7 %collective-permute-start.25 = (bf16[512,384]{1,0:T(8,128)(2,1)}, bf16[512,384]{1,0:T(8,128)(2,1)}, u32[]{:S(2)}, u32[]{:S(2)}) collective-permute-start(bf16[512,384]{1,0:T(8,128)(2,1)} %add_convert_fusion.20), channel_id=1, source_target_pairs={{0,16},{8,24},{16,0},{24,8},{1,17},{9,25},{17,1},{25,9},{2,18},{10... | collective-permute-start | bytes 1179656 | tf_op jit(solution)/shard_map/ppermute | solution.py:419
  1140.5 23.8 %collective-permute-start.27 = (bf16[512,384]{1,0:T(8,128)(2,1)}, bf16[512,384]{1,0:T(8,128)(2,1)}, u32[]{:S(2)}, u32[]{:S(2)}) collective-permute-start(bf16[512,384]{1,0:T(8,128)(2,1)} %add_convert_fusion.18), channel_id=1, source_target_pairs={{0,8},{8,0},{16,24},{24,16},{1,9},{9,1},{17,25},{25,17},{2,10},{10... | collective-permute-start | bytes 1179656 | tf_op jit(solution)/shard_map/ppermute | solution.py:418
  1166.3 16.3 %collective-permute-start.29 = (bf16[256,384]{1,0:T(8,128)(2,1)S(1)}, bf16[256,384]{1,0:T(8,128)(2,1)S(1)}, u32[]{:S(2)}, u32[]{:S(2)}) collective-permute-start(bf16[256,384]{1,0:T(8,128)(2,1)S(1)} %get-tuple-element.97), channel_id=1, source_target_pairs={{0,2},{1,3},{2,4},{3,5},{4,6},{5,7},{6,0},{7,1},{8,10},{9,11},{10,... | collective-permute-start | bytes 589832 | tf_op jit(solution)/shard_map/ppermute | solution.py:426
  1167.6 15.0 %collective-permute-start.31 = (bf16[256,384]{1,0:T(8,128)(2,1)S(1)}, bf16[256,384]{1,0:T(8,128)(2,1)S(1)}, u32[]{:S(2)}, u32[]{:S(2)}) collective-permute-start(bf16[256,384]{1,0:T(8,128)(2,1)S(1)} %get-tuple-element.98), channel_id=1, source_target_pairs={{0,6},{1,7},{2,0},{3,1},{4,2},{5,3},{6,4},{7,5},{8,14},{9,15},{10,... | collective-permute-start | bytes 589832 | tf_op jit(solution)/shard_map/ppermute | solution.py:426
  1168.4 15.2 %collective-permute-start.30 = (bf16[256,384]{1,0:T(8,128)(2,1)S(1)}, bf16[256,384]{1,0:T(8,128)(2,1)S(1)}, u32[]{:S(2)}, u32[]{:S(2)}) collective-permute-start(bf16[256,384]{1,0:T(8,128)(2,1)S(1)} %get-tuple-element.99), channel_id=1, source_target_pairs={{0,4},{1,5},{2,6},{3,7},{4,0},{5,1},{6,2},{7,3},{8,12},{9,13},{10,... | collective-permute-start | bytes 589832 | tf_op jit(solution)/shard_map/ppermute | solution.py:426
  (96 other events, 1668.1 us)
Sparse Core Ops, SparseCore 0:
  11.5 96.4 all-gather.15
  109.7 21.0 all-gather.17
  134.3 68.8 all-gather.19
  206.5 167.8 all-gather.21
  377.2 101.3 all-gather.23
  480.7 140.5 reduce-scatter.4
  816.5 42.5 all-reduce.4
  887.0 46.7 reduce-scatter.6
  1008.6 31.1 all-gather.27
  1091.2 65.9 all-gather.29
  1196.8 34.9 all-gather.25

commit v3 on v2

--- a/solution.py
+++ b/solution.py
@@ -231,6 +231,44 @@
         [jnp.sum(t, axis=0, keepdims=True) for t in taps_sum] + [jnp.zeros((8 - CONV, HS), F32)],
         axis=0,
     )
+
+
+def norm_kernel(shards, core_ref, x_ref, gain_ref, normed_ref, own_ref, far_ref, scale_ref):
+    x = x_ref[...].astype(F32)
+    scale = lax.rsqrt(jnp.mean(x * x, axis=-1, keepdims=True) + 1e-06)
+    low = (x * scale * gain_ref[...]).astype(BF16)
+    normed_ref[...] = low
+    scale_ref[...] = jnp.broadcast_to(scale, scale_ref.shape)
+    wide = low.astype(F32)
+    size = D // shards
+    even, odd = (
+        jnp.concatenate([wide[:, n * size : (n + 1) * size] for n in range(c, shards, 2)], axis=1)
+        for c in range(2)
+    )
+    first = core_ref[0] == 0
+    own_ref[...] = jnp.where(first, even, odd).astype(BF16)
+    far_ref[...] = jnp.where(first, odd, even).astype(BF16)
+
+
+def ffn_forward_kernel(n_ref, gate_ref, up_ref, hidden_ref, pull_ref):
+    for m in range(0, n_ref.shape[0], 256):
+        at = pl.ds(m, 256)
+        e1 = jnp.dot(n_ref[at, :], gate_ref[...], preferred_element_type=F32)
+        e2 = jnp.dot(n_ref[at, :], up_ref[...], preferred_element_type=F32)
+        act, slope = gelu_parts(e1)
+        hidden_ref[at, :] = (act * e2).astype(BF16)
+        pull_ref[0, at, :] = (slope * e2).astype(BF16)
+        pull_ref[1, at, :] = act.astype(BF16)
+
+
+def ffn_backward_kernel(grad_ref, down_ref, pull_ref, out_ref):
+    for m in range(0, grad_ref.shape[0], 256):
+        at = pl.ds(m, 256)
+        dv = lax.dot_general(
+            grad_ref[at, :], down_ref[...], (((1,), (1,)), ((), ())), preferred_element_type=F32
+        )
+        out_ref[0, at, :] = (dv * pull_ref[0, at, :].astype(F32)).astype(BF16)
+        out_ref[1, at, :] = (dv * pull_ref[1, at, :].astype(F32)).astype(BF16)
 
 
 def head_block(lead, rows):
@@ -348,6 +386,78 @@
     )(local, prod, carry, state, before, c, u, halo, dist, gates, taps, soft)
 
 
+def rms_norm(x, gain, shards, core):
+    rows = x.shape[0]
+    block = min(rows, 256)
+    return pl.pallas_call(
+        functools.partial(norm_kernel, shards),
+        grid=(rows // block,),
+        in_specs=[
+            pl.BlockSpec(memory_space=pltpu.SMEM),
+            pl.BlockSpec((block, D), lambda n: (n, 0)),
+            pl.BlockSpec((1, D), lambda n: (0, 0)),
+        ],
+        out_specs=[
+            pl.BlockSpec((block, D), lambda n: (n, 0)),
+            pl.BlockSpec((block, D // 2), lambda n: (n, 0)),
+            pl.BlockSpec((block, D // 2), lambda n: (n, 0)),
+            pl.BlockSpec((block, 128), lambda n: (n, 0)),
+        ],
+        out_shape=[
+            jax.ShapeDtypeStruct((rows, D), BF16),
+            jax.ShapeDtypeStruct((rows, D // 2), BF16),
+            jax.ShapeDtypeStruct((rows, D // 2), BF16),
+            jax.ShapeDtypeStruct((rows, 128), F32),
+        ],
+        compiler_params=PARAMS,
+        name="rms_norm",
+    )(core.reshape(1), x, gain.reshape(1, D))
+
+
+FF_TILE = 512
+
+
+def ffn_forward(normed, proj_up):
+    rows = normed.shape[0]
+    steps = FF // FF_TILE
+    return pl.pallas_call(
+        ffn_forward_kernel,
+        grid=(steps,),
+        in_specs=[
+            pl.BlockSpec((rows, D), lambda n: (0, 0)),
+            pl.BlockSpec((D, FF_TILE), lambda n: (0, n)),
+            pl.BlockSpec((D, FF_TILE), lambda n: (0, n + steps)),
+        ],
+        out_specs=[
+            pl.BlockSpec((rows, FF_TILE), lambda n: (0, n)),
+            pl.BlockSpec((2, rows, FF_TILE), lambda n: (0, 0, n)),
+        ],
+        out_shape=[
+            jax.ShapeDtypeStruct((rows, FF), BF16),
+            jax.ShapeDtypeStruct((2, rows, FF), BF16),
+        ],
+        compiler_params=PARAMS,
+        name="ffn_forward",
+    )(normed, proj_up, proj_up)
+
+
+def ffn_backward(grad, proj_down, pull):
+    rows = grad.shape[0]
+    return pl.pallas_call(
+        ffn_backward_kernel,
+        grid=(FF // FF_TILE,),
+        in_specs=[
+            pl.BlockSpec((rows, D), lambda n: (0, 0)),
+            pl.BlockSpec((FF_TILE, D), lambda n: (n, 0)),
+            pl.BlockSpec((2, rows, FF_TILE), lambda n: (0, 0, n)),
+        ],
+        out_specs=pl.BlockSpec((2, rows, FF_TILE), lambda n: (0, 0, n)),
+        out_shape=jax.ShapeDtypeStruct((2, rows, FF), BF16),
+        compiler_params=PARAMS,
+        name="ffn_backward",
+    )(grad, proj_down, pull)
+
+
 def gather_rows(shard):
     parts = lax.axis_size("grp")
     rows = shard.shape[0] // parts
@@ -378,54 +488,104 @@
     return lax.all_gather(part, "grp", axis=0, tiled=True).astype(F32)
 
 
-def reduce_product(a, b):
-    count = lax.axis_size("seq")
-    if lax.axis_size("grp") != 4:
-        product = dot_rows(a, b).astype(BF16)
-        return reduce_rows(product), (product,)
-    place = lax.axis_index("seq")
-    group = lax.axis_index("grp")
-    chips = count // 2
-    chip, core = place // 2, place % 2
+def dot_far(a, b):
+    return lax.dot_general(a, b, (((1,), (1,)), ((), ())), preferred_element_type=F32)
+
+
+def split_cores(a, shards, core):
     tokens, depth = a.shape
-    rows = depth // count
-    width = b.shape[1] // 4
-    full = chips * rows
-    half = full // 2
-    split = a.reshape(tokens, chips, 2, rows)
-    a_own = lax.dynamic_index_in_dim(split, core, 2, False).reshape(tokens, full)
-    a_far = lax.dynamic_index_in_dim(split, 1 - core, 2, False).reshape(tokens, full)
-    b_part = [lax.dynamic_slice_in_dim(b, (group ^ k) * width, width, 1) for k in range(4)]
-    other = xor_pairs("seq", 1)
-    x, y = xor_pairs("grp", 1), xor_pairs("grp", 2)
-    far = {}
-    for k in (3, 1, 2, 0):
-        far[k] = lax.ppermute(dot_rows(a_far, b_part[k]).astype(BF16), "seq", other)
-
-    def own(k, first, last):
-        return dot_rows(a_own[:, first:last], b_part[k]) + far[k][first:last].astype(F32)
-
-    early = [
-        own(3, 0, half).astype(BF16),
-        own(3, half, full).astype(BF16),
-        own(1, 0, half).astype(BF16),
-        own(2, half, full).astype(BF16),
-    ]
-    diag_a = lax.ppermute(early[0], "grp", x)
-    diag_b = lax.ppermute(early[1], "grp", y)
-    x_a = lax.ppermute(early[2], "grp", x)
-    y_b = lax.ppermute(early[3], "grp", y)
-    x_b = lax.ppermute((own(1, half, full) + diag_b.astype(F32)).astype(BF16), "grp", x)
-    y_a = lax.ppermute((own(2, 0, half) + diag_a.astype(F32)).astype(BF16), "grp", y)
-    mine_a = (own(0, 0, half) + x_a.astype(F32) + y_a.astype(F32)).astype(BF16)
-    mine_b = (own(0, half, full) + x_b.astype(F32) + y_b.astype(F32)).astype(BF16)
-    mine = jnp.concatenate([mine_a, mine_b], axis=0).reshape(chips, rows, width)
-    total = lax.dynamic_index_in_dim(mine, chip, 0, False).astype(F32)
-    for j in range(1, chips):
-        sent = lax.dynamic_index_in_dim(mine, (chip + j) % chips, 0, False)
-        total = total + lax.ppermute(sent, "seq", ring_pairs(2 * j)).astype(F32)
-    parts = lax.all_gather(total.astype(BF16), "grp")
-    return parts.transpose(1, 0, 2).reshape(rows, 4 * width).astype(F32), tuple(early)
+    split = a.reshape(tokens, shards // 2, 2, depth // shards)
+    return tuple(
+        lax.dynamic_index_in_dim(split, c, 2, False).reshape(tokens, depth // 2)
+        for c in (core, 1 - core)
+    )
+
+
+class Reduction:
+    def __init__(self, a_own, a_far, columns, width):
+        self.simple = lax.axis_size("grp") != 4
+        count = lax.axis_size("seq")
+        place = lax.axis_index("seq")
+        self.chips = count // 2
+        self.chip, core = place // 2, place % 2
+        self.width = width
+        full = a_own.shape[1]
+        self.rows = full // self.chips
+        self.half = full // 2
+        self.a_own = a_own
+        if self.simple:
+            parts = [columns(k) for k in range(4)]
+            own, far = (
+                jnp.concatenate([dot_rows(a, part) for part in parts], axis=1)
+                for a in (a_own, a_far)
+            )
+            cores = jnp.stack(
+                [jnp.where(core == c, own, far).reshape(self.chips, self.rows, -1) for c in (0, 1)],
+                axis=1,
+            )
+            self.product = cores.reshape(2 * full, 4 * width).astype(BF16)
+            self.sent = (self.product,)
+            return
+        group = lax.axis_index("grp")
+        self.x, self.y = xor_pairs("grp", 1), xor_pairs("grp", 2)
+        self.b = [columns(group ^ k) for k in range(4)]
+        self.far = [None] * 4
+        for k in (3, 1, 2, 0):
+            product = dot_rows(a_far, self.b[k]).astype(BF16)
+            self.far[k] = lax.ppermute(product, "seq", xor_pairs("seq", 1))
+        half = self.half
+        self.sent = (
+            self.own(3, 0).astype(BF16),
+            self.own(3, half).astype(BF16),
+            self.own(1, 0).astype(BF16),
+            self.own(2, half).astype(BF16),
+        )
+        self.diag_a = lax.ppermute(self.sent[0], "grp", self.x)
+        self.diag_b = lax.ppermute(self.sent[1], "grp", self.y)
+        self.x_a = lax.ppermute(self.sent[2], "grp", self.x)
+        self.y_b = lax.ppermute(self.sent[3], "grp", self.y)
+
+    def own(self, k, first):
+        last = first + self.half
+        product = dot_rows(self.a_own[:, first:last], self.b[k])
+        return product + self.far[k][first:last].astype(F32)
+
+    def second(self):
+        if self.simple:
+            return ()
+        sent = (
+            (self.own(1, self.half) + self.diag_b.astype(F32)).astype(BF16),
+            (self.own(2, 0) + self.diag_a.astype(F32)).astype(BF16),
+        )
+        self.x_b = lax.ppermute(sent[0], "grp", self.x)
+        self.y_a = lax.ppermute(sent[1], "grp", self.y)
+        return sent
+
+    def third(self):
+        if self.simple:
+            return ()
+        first = self.own(0, 0) + self.x_a.astype(F32) + self.y_a.astype(F32)
+        second = self.own(0, self.half) + self.x_b.astype(F32) + self.y_b.astype(F32)
+        mine = jnp.concatenate([first.astype(BF16), second.astype(BF16)], axis=0)
+        mine = mine.reshape(self.chips, self.rows, self.width)
+        self.kept = lax.dynamic_index_in_dim(mine, self.chip, 0, False)
+        sent = tuple(
+            lax.dynamic_index_in_dim(mine, (self.chip + j) % self.chips, 0, False)
+            for j in range(1, self.chips)
+        )
+        self.arrived = [
+            lax.ppermute(part, "seq", ring_pairs(2 * j + 2)) for j, part in enumerate(sent)
+        ]
+        return sent
+
+    def finish(self):
+        if self.simple:
+            return reduce_rows(self.product)
+        total = self.kept.astype(F32)
+        for part in self.arrived:
+            total = total + part.astype(F32)
+        parts = lax.all_gather(total.astype(BF16), "grp")
+        return parts.transpose(1, 0, 2).reshape(self.rows, 4 * self.width).astype(F32)
 
 
 def shard_carry(ends, prods, reverse):
@@ -497,8 +657,10 @@
     proj_down = gather_rows(down_proj)
 
     inputs = tokens.reshape(row_count, D).astype(F32)
-    first_scale = lax.rsqrt(jnp.mean(inputs * inputs, axis=-1, keepdims=True) + 1e-06)
-    first_normed = (inputs * first_scale * gain_one).astype(BF16)
+    first_normed, first_own, first_far, first_scale = rms_norm(
+        tokens.reshape(row_count, D), gain_one, last + 1, place % 2
+    )
+    first_scale = first_scale[:, :1]
     inner_low = jnp.dot(first_normed, proj_in[:, :LRU], preferred_element_type=F32).astype(BF16)
     inner_low = inner_low.reshape(seq_count, shard_len, LRU)
     gate_pre = jnp.dot(first_normed, proj_in[:, LRU:], preferred_element_type=F32)
@@ -525,41 +687,58 @@
     ).reshape(row_count, LRU)
     branch = (state * gelu_tanh(gate_pre)).astype(BF16)
     resid = inputs + jnp.dot(branch, proj_out, preferred_element_type=F32)
-    second_scale = lax.rsqrt(jnp.mean(resid * resid, axis=-1, keepdims=True) + 1e-06)
-    second_normed = (resid * second_scale * gain_two).astype(BF16)
-    expanded_gate = jnp.dot(second_normed, proj_up[:, :FF], preferred_element_type=F32)
-    expanded_up = jnp.dot(second_normed, proj_up[:, FF:], preferred_element_type=F32)
-    hidden = (gelu_tanh(expanded_gate) * expanded_up).astype(BF16)
+    second_normed, second_own, second_far, second_scale = rms_norm(
+        resid, gain_two, last + 1, place % 2
+    )
+    second_scale = second_scale[:, :1]
+    hidden, pull = ffn_forward(second_normed, proj_up)
     ffn_out = jnp.dot(hidden, proj_down, preferred_element_type=F32)
     block_out = (resid + ffn_out).astype(BF16).reshape(seq_count, shard_len, D)
 
     grad_out = cotangent.reshape(row_count, D)
     grad_down = dot_rows(hidden, grad_out).astype(BF16)
     down_total = reduce_rows(grad_down)
-    grad_hidden = jnp.einsum(
-        "rd,fd->rf", tie(grad_out, grad_down), proj_down, preferred_element_type=F32
-    )
-    act, slope = gelu_parts(expanded_gate)
-    grad_expanded = jnp.concatenate(
-        [(grad_hidden * expanded_up * slope).astype(BF16), (grad_hidden * act).astype(BF16)], axis=1
-    )
-    up_total, sent = reduce_product(second_normed, grad_expanded)
-    grad_second_normed = jnp.einsum(
-        "rf,df->rd", tie(grad_expanded, *sent), proj_up, preferred_element_type=F32
-    )
+    grad_expanded = ffn_backward(tie(grad_out, grad_down), proj_down, pull)
+    quarter = FF // 2
+
+    def up_columns(n):
+        part = lax.dynamic_slice(
+            grad_expanded, (n // 2, 0, (n % 2) * quarter), (1, row_count, quarter)
+        )
+        return part[0]
+
+    up_sum = Reduction(second_own, second_far, up_columns, quarter)
+    grad_expanded = tie(grad_expanded, *up_sum.sent)
+    grad_second_normed = dot_far(grad_expanded[0], proj_up[:, :FF]) + dot_far(
+        grad_expanded[1], proj_up[:, FF:]
+    )
+    sent = up_sum.second()
+    grad_second_normed = tie(grad_second_normed, *sent)
     grad_resid = grad_out.astype(F32) + norm_back(
         resid, second_scale, gain_two, grad_second_normed
     )
     grad_mixer = grad_resid.astype(BF16)
-    out_total, sent = reduce_product(branch, grad_mixer)
-    grad_branch = jnp.einsum(
-        "rd,ld->rl", tie(grad_mixer, *sent), proj_out, preferred_element_type=F32
-    )
+    out_sum = Reduction(
+        *split_cores(branch, last + 1, place % 2),
+        lambda n: lax.dynamic_slice_in_dim(grad_mixer, n * (D // 4), D // 4, 1),
+        D // 4,
+    )
+    grad_branch = dot_far(tie(grad_mixer, *out_sum.sent), proj_out)
 
     wide = (seq_count, shard_len, LRU)
     grad_gate, local, rev_prod, rev_chunks = mixer_reverse(
         grad_branch.reshape(wide), gate_pre.reshape(wide), keep, state.reshape(wide)
     )
+    grad_gate = grad_gate.reshape(row_count, LRU)
+    width = LRU // 4
+    in_gate_sum = Reduction(
+        first_own,
+        first_far,
+        lambda n: lax.dynamic_slice_in_dim(grad_gate, n * width, width, 1),
+        width,
+    )
+    sent = (*up_sum.third(), *out_sum.second(), *in_gate_sum.sent)
+    local = tie(local, *sent)
     head_pull, head_prod = chunk_ends(rev_chunks, True)
     rev_carry = shard_carry(head_pull, head_prod, True)
     rev_carries = chunk_carries(rev_chunks, rev_carry, True)
@@ -583,20 +762,32 @@
     gates_total = flat[:n_gates].reshape(gate_heads.shape)
     taps_total = flat[n_gates : n_gates + CONV * n_lru].reshape(CONV, n_lru)
     decay_total = flat[n_gates + CONV * n_lru :]
+    sent = (*in_gate_sum.second(), *out_sum.third())
+    du = tie(du, *sent)
+    up_total = up_sum.finish()
     returned = from_behind(edge[:, HALO - edge_len :].astype(BF16), "seq", -1).astype(F32)
     returned = jnp.pad(returned, ((0, 0), (HALO - edge_len, 0), (0, 0)))
     grad_inner = lax.dynamic_update_slice(
         du, (tail + returned).astype(BF16), (0, shard_len - HALO, 0)
     )
-    grad_projected = jnp.concatenate(
-        [grad_inner.reshape(row_count, LRU), grad_gate.reshape(row_count, LRU)], axis=1
-    )
-    in_total, sent = reduce_product(first_normed, grad_projected)
-    grad_first_normed = jnp.einsum(
-        "rp,dp->rd", tie(grad_projected, *sent), proj_in, preferred_element_type=F32
-    )
+    grad_inner = grad_inner.reshape(row_count, LRU)
+    in_value_sum = Reduction(
+        first_own,
+        first_far,
+        lambda n: lax.dynamic_slice_in_dim(grad_inner, n * width, width, 1),
+        width,
+    )
+    grad_inner = tie(grad_inner, *in_value_sum.sent)
+    grad_first_normed = dot_far(grad_inner, proj_in[:, :LRU]) + dot_far(
+        grad_gate, proj_in[:, LRU:]
+    )
+    sent = (*in_gate_sum.third(), *in_value_sum.second())
+    grad_first_normed = tie(grad_first_normed, *sent)
+    out_total = out_sum.finish()
     grad_tokens = grad_resid + norm_back(inputs, first_scale, gain_one, grad_first_normed)
     grad_tokens = grad_tokens.astype(BF16).reshape(seq_count, shard_len, D)
+    in_value_sum.third()
+    in_total = jnp.concatenate([in_value_sum.finish(), in_gate_sum.finish()], axis=1)
     first_total = gain_grad(in_proj, in_total, first_gain)
     second_total = gain_grad(up_proj, up_total, second_gain)
     return (

time: 1260 us -> 1330 us (1.056)
  waiting for transfers between devices: 389 us -> 488 us
  matrix products: 336 us -> 267 us
  Pallas kernels: 153 us -> 219 us
  other arithmetic: 113 us -> 73 us
  blocking collectives: 67.7 us -> 102 us
  local copies, waits for them, and re-layouts: 126 us -> 106 us
    reduce_scatter x1, waiting for transfers between devices: 0.01 us -> 110 us  [reduce_rows(): part = lax.psum_scatter(partial, 'seq', scatter_dimension=0, tiled=True)]
    ppermute x39 -> x52, waiting for transfers between devices: 237 us -> 148 us  [the longest x4 49.2 us: second(): self.y_a = lax.ppermute(sent[1], 'grp', self.y)]
    dot_general x6 -> x5, matrix products: 153 us -> 72.2 us  [dot_far(): lax.dot_general(a, b, (((1,), (1,)), ((), ())), preferred_element_type=F32)]
    pallas_call x0 -> x4, Pallas kernels: none -> 66 us  [the longest x1 37.5 us: ffn_forward(): pl.pallas_call(ffn_forward_kernel, grid=(steps,), in_specs=[pl.BlockSpec(...]
    all_gather x4, waiting for transfers between devices: 143 us -> 185 us  [gather_rows(): return lax.all_gather(own, ('seq', 'grp'), axis=0, tiled=True)]
    concatenate x7 -> x4, other arithmetic: 39.5 us -> 0.42 us  [third(): mine = jnp.concatenate([first.astype(BF16), second.astype(BF16)], axis=0)]
    all_gather x1 -> x3, blocking collectives: 11 us -> 46 us  [finish(): parts = lax.all_gather(total.astype(BF16), 'grp')]
    ppermute x3, waiting for transfers between devices: 0.03 us -> 32.6 us  [from_behind(): lax.ppermute(value, axis, [(source, source + steps) for source in range(f...]
  transfers between devices with their start and end apart: 54 -> 66, of which waited for: 22 -> 23; matrix products, arithmetic and copies ran while one was open for 45% -> 29% of each run, Pallas kernels for 12% -> 11%
where the time goes in v3:
time: 1330 us; the launch traced here: 1320 us
  waiting for transfers between devices  488 us (37%)
  matrix products  267 us (20%)
  Pallas kernels  219 us (16%)
  local copies, waits for them, and re-layouts  106 us (8%)
  blocking collectives  102 us (8%)
  other arithmetic  73 us (5%)
  starting transfers between devices  47.7 us (4%)
  between operations  17 us (1%)
    all_gather x4, waiting for transfers between devices, gather_rows(): return lax.all_gather(own, ('seq', 'grp'), axis=0, tiled=True)  185 us
    dot_general x49, matrix products, dot_rows(): lax.dot_general(a, b, (((0,), (0,)), ((), ())), preferred_element_type=F32)  135 us
    reduce_scatter x1, waiting for transfers between devices, reduce_rows(): part = lax.psum_scatter(partial, 'seq', scatter_dimension=0, tiled=True)  110 us
    dot_general x5, matrix products, dot_far(): lax.dot_general(a, b, (((1,), (1,)), ((), ())), preferred_element_type=F32)  72.2 us
    unnamed x226, local copies, waits for them, and re-layouts  64.1 us
    pallas_call x1, Pallas kernels, mixer_forward(): pl.pallas_call(mixer_forward_kernel, grid=(HEADS,), in_specs=[full, head_...  63.2 us
    pallas_call x1, Pallas kernels, mixer_backward(): pl.pallas_call(mixer_backward_kernel, grid=(HEADS,), in_specs=[full, full...  51.2 us
    ppermute x4, waiting for transfers between devices, second(): self.y_a = lax.ppermute(sent[1], 'grp', self.y)  49.2 us
  transfers between devices with their start and end apart: 66, of which 23 were waited for; matrix products, arithmetic and copies ran while one was open for 29% of the time, Pallas kernels for 11%

profile of v3, /device:TPU:18, one launch (start us, length us, event | category | flops | bytes accessed | tf_op | source)
XLA Modules:
  0.0 1319.6 jit_solution(9273219063991616203)
XLA Ops:
  17.2 12.3 all-gather.7
  38.2 69.9 %all-gather.16.cloned.1.call-done = bf16[1536,4096]{1,0:T(8,128)(2,1)} async-done(((bf16[48,4096]{1,0:T(8,128)(2,1)}), bf16[1536,4096]{1,0:T(8,128)(2,1)}) %all-gather.16.cloned.1.call-update) | async-done | bytes 12582928 | tf_op jit(solution)/shard_map/all_gather | solution.py:465
  108.0 9.7 fusion.59
  122.0 8.8 all-gather.18.cloned.1.call-done.gates_ref
  134.4 63.2 %mixer_forward.1 = (bf16[2,512,2048]{2,1,0:T(8,128)(2,1)S(1)}, f32[2,512,2048]{2,1,0:T(8,128)}, f32[2,512,2048]{2,1,0:T(8,128)}, f32[2,512,2048]{2,1,0:T(8,128)}, f32[2,2,8,2048]{3,2,1,0:T(8,128)S(1)}) custom-call(bf16[2,512,2048]{2,1,0:T(8,128)(2,1)S(1)} %bitcast.821, bf16[2,8,2048]{2,1,0:T(8,128)(2,1)S(1)} %collective-permute-done.halo_ref, ...), custom_call_target="tpu_custom_call" | custom-call | tf_op jit(solution)/shard_map/mixer_forward/pallas_call | solution.py:293
  200.2 12.5 all-gather.1
  213.2 12.7 fusion.16.state_ref
  225.9 17.7 %fusion.15 = (bf16[1024,2048]{1,0:T(8,128)(2,1)}, f32[1024,2048]{1,0:T(8,128)}) fusion(f32[2,512,2048]{2,1,0:T(8,128)} %get-tuple-element.46, f32[2,512,2048]{2,1,0:T(8,128)} %get-tuple-element.45, f32[2,8,2048]{2,1,0:T(8,128)S(1)} %stack.9, bf16[1024,1536]{1,0:T(8,128)(2,1)S(1)} %copy-done.20, bf16[1536,4096]{1,0:T(8,128)(2,1)} %all-gather.16.cloned.1.call-done), kind=kOutput, calls=%fused_computation.19 | convolution fusion | flops 6467616768 | bytes 38928384 | tf_op jit(solution)/shard_map/dot_general | solution.py:666
  243.6 7.8 reshape.2467
  251.4 11.2 constant_dynamic-slice_fusion.1
  262.6 10.6 copy.258
  273.2 10.6 copy.259
  283.8 10.5 convert_add_fusion.x_ref
  302.1 71.7 %all-gather.22.cloned.1.call-done.gate_ref.up_ref = bf16[1536,9216]{1,0:T(8,128)(2,1)} async-done(((bf16[48,9216]{1,0:T(8,128)(2,1)}), bf16[1536,9216]{1,0:T(8,128)(2,1)}) %all-gather.22.cloned.1.call-update) | async-done | bytes 28311568 | tf_op jit(solution)/shard_map/all_gather | solution.py:465
  375.6 37.5 %ffn_forward.1 = (bf16[1024,4608]{1,0:T(8,128)(2,1)S(1)}, bf16[2,1024,4608]{2,1,0:T(8,128)(2,1)}) custom-call(bf16[1024,1536]{1,0:T(8,128)(2,1)S(1)} %copy-done.18, bf16[1536,9216]{1,0:T(8,128)(2,1)} %all-gather.22.cloned.1.call-done.gate_ref.up_ref, bf16[1536,9216]{1,0:T(8,128)(2,1)} %all-gather.22.cloned.1.call-done.gate_ref.up_ref), custom_call_target="tpu_custom_call" | custom-call | tf_op jit(solution)/shard_map/ffn_forward/pallas_call | solution.py:423
  416.8 18.4 %convolution_convert_fusion = bf16[4608,1536]{1,0:T(8,128)(2,1)} fusion(bf16[1024,4608]{1,0:T(8,128)(2,1)S(1)} %get-tuple-element.49, bf16[1024,1536]{1,0:T(8,128)(2,1)S(1)} %bitcast.822), kind=kOutput, calls=%fused_computation | convolution fusion | flops 14502592512 | bytes 26738688 | tf_op jit(solution)/shard_map/dot_general | solution.py:482
  435.1 43.3 %all-gather.24.cloned.1.call-done.down_ref = bf16[4608,1536]{1,0:T(8,128)(2,1)} async-done(((bf16[144,1536]{1,0:T(8,128)(2,1)}), bf16[4608,1536]{1,0:T(8,128)(2,1)}) %all-gather.24.cloned.1.call-update) | async-done | bytes 14155792 | tf_op jit(solution)/shard_map/all_gather | solution.py:465
  480.3 24.6 %ffn_backward.1 = bf16[2,1024,4608]{2,1,0:T(8,128)(2,1)} custom-call(bf16[1024,1536]{1,0:T(8,128)(2,1)S(1)} %bitcast.823, bf16[4608,1536]{1,0:T(8,128)(2,1)} %all-gather.24.cloned.1.call-done.down_ref, bf16[2,1024,4608]{2,1,0:T(8,128)(2,1)} %get-tuple-element.52.pull_ref), custom_call_target="tpu_custom_call" | custom-call | tf_op jit(solution)/shard_map/ffn_backward/pallas_call | solution.py:446
  505.0 7.8 convolution_convert_fusion.4
  514.0 5.3 convolution_convert_fusion.2
  524.1 5.5 convolution_convert_fusion.1
  549.8 4.8 add_convert_fusion.7
  564.7 21.8 %fusion.1 = f32[1024,1536]{1,0:T(8,128)} fusion(bf16[1536,9216]{1,0:T(8,128)(2,1)} %all-gather.22.cloned.1.call-done.gate_ref.up_ref, bf16[2,1024,4608]{2,1,0:T(8,128)(2,1)} %ffn_backward.1), kind=kOutput, calls=%fused_computation.1 | convolution fusion | flops 14495514624 | bytes 29884416 | tf_op jit(solution)/shard_map/dot_general | solution.py:492
  586.5 21.0 %fusion.54 = f32[1024,1536]{1,0:T(8,128)S(1)} fusion(f32[1024,1536]{1,0:T(8,128)} %fusion.1, bf16[1536,9216]{1,0:T(8,128)(2,1)} %all-gather.22.cloned.1.call-done.gate_ref.up_ref, bf16[2,1024,4608]{2,1,0:T(8,128)(2,1)} %ffn_backward.1), kind=kOutput, calls=%fused_computation.66 | convolution fusion | flops 14497087488 | bytes 36175872 | tf_op jit(solution)/shard_map/dot_general | solution.py:492
  636.3 8.9 fusion.407
  645.2 38.2 %mixer_reverse.1 = (bf16[2,512,2048]{2,1,0:T(8,128)(2,1)S(1)}, f32[2,512,2048]{2,1,0:T(8,128)S(1)}, f32[2,512,2048]{2,1,0:T(8,128)}, f32[2,2,8,2048]{3,2,1,0:T(8,128)S(1)}) custom-call(f32[2,512,2048]{2,1,0:T(8,128)} %bitcast.845, f32[2,512,2048]{2,1,0:T(8,128)} %bitcast.839, f32[2,512,2048]{2,1,0:T(8,128)} %get-tuple-element.59.keep_ref, ...), custom_call_target="tpu_custom_call" | custom-call | tf_op jit(solution)/shard_map/mixer_reverse/pallas_call | solution.py:327
  688.7 13.6 %all-gather.2 = f32[16,2,2048]{2,1,0:T(2,128)S(1)} all-gather(f32[2,2,2048]{2,1,0:T(2,128)S(1)} %copy.248), channel_id=4, replica_groups=mesh['grp'=4,'seq'=8] {'seq'}, dimensions={0}, use_global_device_ids=true | all-gather | bytes 294912 | tf_op jit(solution)/shard_map/all_gather | solution.py:594
  703.8 9.9 collective-permute-done.15
  731.0 24.5 %collective-permute-done.14 = bf16[384,2304]{1,0:T(8,128)(2,1)} collective-permute-done((bf16[384,2304]{1,0:T(8,128)(2,1)}, bf16[384,2304]{1,0:T(8,128)(2,1)}, u32[]{:S(2)}, u32[]{:S(2)}) %collective-permute-start.14) | collective-permute-done | bytes 1769504 | tf_op jit(solution)/shard_map/ppermute | solution.py:546
  757.0 35.0 %collective-permute-done.12 = bf16[384,2304]{1,0:T(8,128)(2,1)} collective-permute-done((bf16[384,2304]{1,0:T(8,128)(2,1)S(1)}, bf16[384,2304]{1,0:T(8,128)(2,1)}, u32[]{:S(2)}, u32[]{:S(2)}) %collective-permute-start.12) | collective-permute-done | bytes 1769504 | tf_op jit(solution)/shard_map/ppermute | solution.py:561
  793.1 5.1 add_convert_fusion.2
  803.0 51.2 %mixer_backward.1 = (bf16[2,512,2048]{2,1,0:T(8,128)(2,1)}, f32[2,8,2048]{2,1,0:T(8,128)S(1)}, f32[2,8,2048]{2,1,0:T(8,128)S(1)}, f32[16,128,256]{2,1,0:T(8,128)...) custom-call(f32[2,512,2048]{2,1,0:T(8,128)} %copy-done.10, f32[2,512,2048]{2,1,0:T(8,128)} %get-tuple-element.65.prod_ref, ...), custom_call_target="tpu_custom_call" | custom-call | tf_op jit(solution)/shard_map/mixer_backward/pallas_call | solution.py:350
  860.2 17.4 %fusion = bf16[528,128]{1,0:T(8,128)(2,1)S(1)} fusion(bf16[4176,128]{1,0:T(8,128)(2,1)S(1)} %convert_element_type.685), kind=kCustom, calls=%all-reduce-scatter | all-reduce-scatter fusion | flops 540673 | bytes 1204736
  885.6 22.0 %add_convert_fusion = bf16[1024,1536]{1,0:T(8,128)(2,1)} fusion(f32[1024,1536]{1,0:T(8,128)} %copy-done.2, bf16[1024,4608]{1,0:T(8,128)(2,1)} %copy-done.30, bf16[4608,1536]{1,0:T(8,128)(2,1)} %all-gather.24.cloned.1.call-done.down_ref), kind=kOutput, calls=%fused_computation.32 | convolution fusion | flops 14498660352 | bytes 33030144 | tf_op jit(solution)/shard_map/dot_general | solution.py:695
  914.6 10.5 fusion.23
  931.2 5.6 collective-permute-done.24
  944.9 4.8 collective-permute-done.51
  950.8 17.5 %collective-permute-done.50 = bf16[256,384]{1,0:T(8,128)(2,1)S(1)} collective-permute-done((bf16[256,384]{1,0:T(8,128)(2,1)S(1)}, bf16[256,384]{1,0:T(8,128)(2,1)S(1)}, u32[]{:S(2)}, u32[]{:S(2)}) %collective-permute-start.50) | collective-permute-done | bytes 196640 | tf_op jit(solution)/shard_map/ppermute | solution.py:577
  972.0 16.2 %all-gather.5 = bf16[1024,384]{1,0:T(8,128)(2,1)S(1)} all-gather(bf16[256,384]{1,0:T(8,128)(2,1)S(1)} %fusion.173), channel_id=7, replica_groups=mesh['grp'=4,'seq'=8] {'grp'}, dimensions={0}, use_global_device_ids=true | all-gather | bytes 983040 | tf_op jit(solution)/shard_map/all_gather | solution.py:587
  1001.2 32.6 %collective-permute-done.27 = bf16[2,3,2048]{2,1,0:T(4,128)(2,1)S(1)} collective-permute-done((bf16[2,3,2048]{2,1,0:T(4,128)(2,1)S(1)}, bf16[2,3,2048]{2,1,0:T(4,128)(2,1)S(1)}, u32[]{:S(2)}, u32[]{:S(2)}) %collective-permute-start.27) | collective-permute-done | bytes 24608 | tf_op jit(solution)/shard_map/ppermute | solution.py:25
  1034.4 110.0 %reduce-scatter.5.cloned.1.call-done = bf16[576,1536]{1,0:T(8,128)(2,1)} async-done(((bf16[4608,1536]{1,0:T(8,128)(2,1)}), bf16[576,1536]{1,0:T(8,128)(2,1)}) %reduce-scatter.5.cloned.1.call-update) | async-done | bytes 1769488 | tf_op jit(solution)/shard_map/reduce_scatter | solution.py:486
  1178.7 14.5 %collective-permute-done.52 = bf16[192,2304]{1,0:T(8,128)(2,1)S(1)} collective-permute-done((bf16[192,2304]{1,0:T(8,128)(2,1)S(1)}, bf16[192,2304]{1,0:T(8,128)(2,1)S(1)}, u32[]{:S(2)}, u32[]{:S(2)}) %collective-permute-start.52) | collective-permute-done | bytes 884768 | tf_op jit(solution)/shard_map/ppermute | solution.py:577
  1201.2 18.4 %all-gather.4 = bf16[768,512]{1,0:T(8,128)(2,1)S(1)} all-gather(bf16[192,512]{1,0:T(8,128)(2,1)S(1)} %fusion.176), channel_id=6, replica_groups=mesh['grp'=4,'seq'=8] {'grp'}, dimensions={0}, use_global_device_ids=true | all-gather | bytes 983040 | tf_op jit(solution)/shard_map/all_gather | solution.py:587
  1232.5 10.1 fusion.51
  1242.6 17.6 %collective-permute-done.37 = bf16[384,512]{1,0:T(8,128)(2,1)S(1)} collective-permute-done((bf16[384,512]{1,0:T(8,128)(2,1)S(1)}, bf16[384,512]{1,0:T(8,128)(2,1)S(1)}, u32[]{:S(2)}, u32[]{:S(2)}) %collective-permute-start.37) | collective-permute-done | bytes 393248 | tf_op jit(solution)/shard_map/ppermute | solution.py:543
  1276.2 8.5 fusion.21
  1284.8 11.5 all-gather.3
  1299.2 4.7 copy.254
  (492 shorter events, 275.4 us)
Async XLA Ops:
  7.2 100.8 %all-gather.16.cloned.1.call-start = ((), (), s32[]{:S(2)}) async-start(), calls=%async_computation.2 | async-start | bytes 12976128 | tf_op jit(solution)/shard_map/all_gather | solution.py:465
  9.2 121.6 %all-gather.18.cloned.1.call-start = ((), (), s32[]{:S(2)}) async-start(), calls=%async_computation.3 | async-start | bytes 1179648 | tf_op jit(solution)/shard_map/all_gather | solution.py:654
  10.0 273.8 %all-gather.20.cloned.1.call-start = ((), (), s32[]{:S(2)}) async-start(), calls=%async_computation.4 | async-start | bytes 6488064 | tf_op jit(solution)/shard_map/all_gather | solution.py:465
  11.6 362.1 %all-gather.22.cloned.1.call-start = ((), (), s32[]{:S(2)}) async-start(), calls=%async_computation.5 | async-start | bytes 29196288 | tf_op jit(solution)/shard_map/all_gather | solution.py:465
  13.9 464.6 %all-gather.24.cloned.1.call-start = ((), (), s32[]{:S(2)}) async-start(), calls=%async_computation.6 | async-start | bytes 14598144 | tf_op jit(solution)/shard_map/all_gather | solution.py:465
  14.8 975.3 %all-reduce.5.cloned.1.call-start = ((), (), s32[]{:S(2)}) async-start(), calls=%async_computation.7 | async-start | bytes 270336 | tf_op jit(solution)/shard_map/psum | solution.py:760
  14.9 23.3 %collective-permute-start.1 = (s32[2,3]{1,0:T(2,128)S(1)}, s32[2,3]{1,0:T(2,128)S(1)}, u32[]{:S(2)}, u32[]{:S(2)}) collective-permute-start(s32[2,3]{1,0:T(2,128)S(1)} %slice.445), channel_id=1, source_target_pairs={{0,1},{1,2},{2,3},{3,4},{4,5},{5,6},{6,7},{8,9},{9,10},{10,11},{11... | collective-permute-start | bytes 80 | tf_op jit(solution)/shard_map/ppermute | solution.py:25
  512.8 32.5 %collective-permute-start.2 = (bf16[768,2304]{1,0:T(8,128)(2,1)}, bf16[768,2304]{1,0:T(8,128)(2,1)}, u32[]{:S(2)}, u32[]{:S(2)}) collective-permute-start(bf16[768,2304]{1,0:T(8,128)(2,1)} %convolution_convert_fusion.4), channel_id=1, source_target_pairs={{0,1},{1,0},{2,3},{3,2},{4,5},{5,4},{6,7},{7,6},{8,9},{9,8},{10,11... | collective-permute-start | bytes 10616840 | tf_op jit(solution)/shard_map/ppermute | solution.py:535
  519.3 36.7 %collective-permute-start.4 = (bf16[768,2304]{1,0:T(8,128)(2,1)}, bf16[768,2304]{1,0:T(8,128)(2,1)S(1)}, u32[]{:S(2)}, u32[]{:S(2)}) collective-permute-start(bf16[768,2304]{1,0:T(8,128)(2,1)} %convolution_convert_fusion.2), channel_id=1, source_target_pairs={{0,1},{1,0},{2,3},{3,2},{4,5},{5,4},{6,7},{7,6},{8,9},{9,8},{10,11... | collective-permute-start | bytes 10616840 | tf_op jit(solution)/shard_map/ppermute | solution.py:535
  523.8 35.8 %collective-permute-start.3 = (bf16[768,2304]{1,0:T(8,128)(2,1)S(1)}, bf16[768,2304]{1,0:T(8,128)(2,1)S(1)}, u32[]{:S(2)}, u32[]{:S(2)}) collective-permute-start(bf16[768,2304]{1,0:T(8,128)(2,1)S(1)} %convolution_convert_fusion.3), channel_id=1, source_target_pairs={{0,1},{1,0},{2,3},{3,2},{4,5},{5,4},{6,7},{7,6},{8,9},{9,8},{10,11... | collective-permute-start | bytes 10616840 | tf_op jit(solution)/shard_map/ppermute | solution.py:535
  529.5 201.5 %collective-permute-start.10 = (bf16[768,2304]{1,0:T(8,128)(2,1)}, bf16[768,2304]{1,0:T(8,128)(2,1)}, u32[]{:S(2)}, u32[]{:S(2)}) collective-permute-start(bf16[768,2304]{1,0:T(8,128)(2,1)} %convolution_convert_fusion.1), channel_id=1, source_target_pairs={{0,1},{1,0},{2,3},{3,2},{4,5},{5,4},{6,7},{7,6},{8,9},{9,8},{10,11... | collective-permute-start | bytes 10616840 | tf_op jit(solution)/shard_map/ppermute | solution.py:535
  548.9 58.6 %collective-permute-start.6 = (bf16[384,2304]{1,0:T(8,128)(2,1)S(1)}, bf16[384,2304]{1,0:T(8,128)(2,1)}, u32[]{:S(2)}, u32[]{:S(2)}) collective-permute-start(bf16[384,2304]{1,0:T(8,128)(2,1)S(1)} %add_convert_fusion.8), channel_id=1, source_target_pairs={{0,8},{8,0},{16,24},{24,16},{1,9},{9,1},{17,25},{25,17},{2,10},{10... | collective-permute-start | bytes 5308424 | tf_op jit(solution)/shard_map/ppermute | solution.py:543
  554.5 56.7 %collective-permute-start.5 = (bf16[384,2304]{1,0:T(8,128)(2,1)}, bf16[384,2304]{1,0:T(8,128)(2,1)}, u32[]{:S(2)}, u32[]{:S(2)}) collective-permute-start(bf16[384,2304]{1,0:T(8,128)(2,1)} %add_convert_fusion.7), channel_id=1, source_target_pairs={{0,16},{8,24},{16,0},{24,8},{1,17},{9,25},{17,1},{25,9},{2,18},{10... | collective-permute-start | bytes 5308424 | tf_op jit(solution)/shard_map/ppermute | solution.py:544
  632.2 70.1 %collective-permute-start.16 = (bf16[512,384]{1,0:T(8,128)(2,1)}, bf16[512,384]{1,0:T(8,128)(2,1)S(1)}, u32[]{:S(2)}, u32[]{:S(2)}) collective-permute-start(bf16[512,384]{1,0:T(8,128)(2,1)} %add_convert_fusion.32), channel_id=1, source_target_pairs={{0,8},{8,0},{16,24},{24,16},{1,9},{9,1},{17,25},{25,17},{2,10},{10... | collective-permute-start | bytes 1179656 | tf_op jit(solution)/shard_map/ppermute | solution.py:543
  687.9 27.2 %collective-permute-start.19 = (bf16[768,512]{1,0:T(8,128)(2,1)S(1)}, bf16[768,512]{1,0:T(8,128)(2,1)S(1)}, u32[]{:S(2)}, u32[]{:S(2)}) collective-permute-start(bf16[768,512]{1,0:T(8,128)(2,1)S(1)} %convolution_convert_fusion.10), channel_id=1, source_target_pairs={{0,1},{1,0},{2,3},{3,2},{4,5},{5,4},{6,7},{7,6},{8,9},{9,8},{10,11... | collective-permute-start | bytes 2359304 | tf_op jit(solution)/shard_map/ppermute | solution.py:535
  688.1 27.8 %collective-permute-start.18 = (bf16[768,512]{1,0:T(8,128)(2,1)S(1)}, bf16[768,512]{1,0:T(8,128)(2,1)S(1)}, u32[]{:S(2)}, u32[]{:S(2)}) collective-permute-start(bf16[768,512]{1,0:T(8,128)(2,1)S(1)} %convolution_convert_fusion.11), channel_id=1, source_target_pairs={{0,1},{1,0},{2,3},{3,2},{4,5},{5,4},{6,7},{7,6},{8,9},{9,8},{10,11... | collective-permute-start | bytes 2359304 | tf_op jit(solution)/shard_map/ppermute | solution.py:535
  688.5 29.0 %collective-permute-start.17 = (bf16[768,512]{1,0:T(8,128)(2,1)S(1)}, bf16[768,512]{1,0:T(8,128)(2,1)S(1)}, u32[]{:S(2)}, u32[]{:S(2)}) collective-permute-start(bf16[768,512]{1,0:T(8,128)(2,1)S(1)} %convolution_convert_fusion.12), channel_id=1, source_target_pairs={{0,1},{1,0},{2,3},{3,2},{4,5},{5,4},{6,7},{7,6},{8,9},{9,8},{10,11... | collective-permute-start | bytes 2359304 | tf_op jit(solution)/shard_map/ppermute | solution.py:535
  713.7 41.9 %collective-permute-start.14 = (bf16[384,2304]{1,0:T(8,128)(2,1)}, bf16[384,2304]{1,0:T(8,128)(2,1)}, u32[]{:S(2)}, u32[]{:S(2)}) collective-permute-start(bf16[384,2304]{1,0:T(8,128)(2,1)} %add_convert_fusion.5), channel_id=1, source_target_pairs={{0,16},{8,24},{16,0},{24,8},{1,17},{9,25},{17,1},{25,9},{2,18},{10... | collective-permute-start | bytes 5308424 | tf_op jit(solution)/shard_map/ppermute | solution.py:546
  715.1 41.9 %collective-permute-start.11 = (bf16[384,2304]{1,0:T(8,128)(2,1)}, bf16[384,2304]{1,0:T(8,128)(2,1)}, u32[]{:S(2)}, u32[]{:S(2)}) collective-permute-start(bf16[384,2304]{1,0:T(8,128)(2,1)} %add_convert_fusion.6), channel_id=1, source_target_pairs={{0,8},{8,0},{16,24},{24,16},{1,9},{9,1},{17,25},{25,17},{2,10},{10... | collective-permute-start | bytes 5308424 | tf_op jit(solution)/shard_map/ppermute | solution.py:545
  716.0 76.0 %collective-permute-start.12 = (bf16[384,2304]{1,0:T(8,128)(2,1)S(1)}, bf16[384,2304]{1,0:T(8,128)(2,1)}, u32[]{:S(2)}, u32[]{:S(2)}) collective-permute-start(bf16[384,2304]{1,0:T(8,128)(2,1)S(1)} %add_convert_fusion.3), channel_id=1, source_target_pairs={{0,16},{8,24},{16,0},{24,8},{1,17},{9,25},{17,1},{25,9},{2,18},{10... | collective-permute-start | bytes 5308424 | tf_op jit(solution)/shard_map/ppermute | solution.py:561
  717.4 75.7 %collective-permute-start.13 = (bf16[384,2304]{1,0:T(8,128)(2,1)}, bf16[384,2304]{1,0:T(8,128)(2,1)}, u32[]{:S(2)}, u32[]{:S(2)}) collective-permute-start(bf16[384,2304]{1,0:T(8,128)(2,1)} %add_convert_fusion.4), channel_id=1, source_target_pairs={{0,8},{8,0},{16,24},{24,16},{1,9},{9,1},{17,25},{25,17},{2,10},{10... | collective-permute-start | bytes 5308424 | tf_op jit(solution)/shard_map/ppermute | solution.py:560
  884.1 260.3 %reduce-scatter.5.cloned.1.call-start = ((), (), s32[]{:S(2)}) async-start(), calls=%async_computation.8 | async-start | bytes 15925248 | tf_op jit(solution)/shard_map/reduce_scatter | solution.py:486
  884.9 387.1 %reduce-scatter.7.cloned.1.call-start = ((), (), s32[]{:S(2)}) async-start(), calls=%async_computation.9 | async-start | bytes 2211840 | tf_op jit(solution)/shard_map/reduce_scatter | solution.py:487
  908.9 22.2 %collective-permute-start.22 = (bf16[1024,384]{1,0:T(8,128)(2,1)S(1)}, bf16[1024,384]{1,0:T(8,128)(2,1)S(1)}, u32[]{:S(2)}, u32[]{:S(2)}) collective-permute-start(bf16[1024,384]{1,0:T(8,128)(2,1)S(1)} %convolution_convert_fusion.13), channel_id=1, source_target_pairs={{0,1},{1,0},{2,3},{3,2},{4,5},{5,4},{6,7},{7,6},{8,9},{9,8},{10,11... | collective-permute-start | bytes 2359304 | tf_op jit(solution)/shard_map/ppermute | solution.py:535
  910.7 20.5 %collective-permute-start.26 = (bf16[512,384]{1,0:T(8,128)(2,1)S(1)}, bf16[512,384]{1,0:T(8,128)(2,1)S(1)}, u32[]{:S(2)}, u32[]{:S(2)}) collective-permute-start(bf16[512,384]{1,0:T(8,128)(2,1)S(1)} %copy-done.97), channel_id=1, source_target_pairs={{0,16},{8,24},{16,0},{24,8},{1,17},{9,25},{17,1},{25,9},{2,18},{10... | collective-permute-start | bytes 1179656 | tf_op jit(solution)/shard_map/ppermute | solution.py:546
  911.4 19.8 %collective-permute-start.23 = (bf16[512,384]{1,0:T(8,128)(2,1)S(1)}, bf16[512,384]{1,0:T(8,128)(2,1)S(1)}, u32[]{:S(2)}, u32[]{:S(2)}) collective-permute-start(bf16[512,384]{1,0:T(8,128)(2,1)S(1)} %copy-done.98), channel_id=1, source_target_pairs={{0,8},{8,0},{16,24},{24,16},{1,9},{9,1},{17,25},{25,17},{2,10},{10... | collective-permute-start | bytes 1179656 | tf_op jit(solution)/shard_map/ppermute | solution.py:545
  931.2 231.1 %collective-permute-start.31 = (bf16[768,512]{1,0:T(8,128)(2,1)}, bf16[768,512]{1,0:T(8,128)(2,1)}, u32[]{:S(2)}, u32[]{:S(2)}) collective-permute-start(bf16[768,512]{1,0:T(8,128)(2,1)} %convolution_convert_fusion.6), channel_id=1, source_target_pairs={{0,1},{1,0},{2,3},{3,2},{4,5},{5,4},{6,7},{7,6},{8,9},{9,8},{10,11... | collective-permute-start | bytes 2359304 | tf_op jit(solution)/shard_map/ppermute | solution.py:535
  939.0 29.3 %collective-permute-start.50 = (bf16[256,384]{1,0:T(8,128)(2,1)S(1)}, bf16[256,384]{1,0:T(8,128)(2,1)S(1)}, u32[]{:S(2)}, u32[]{:S(2)}) collective-permute-start(bf16[256,384]{1,0:T(8,128)(2,1)S(1)} %get-tuple-element.123), channel_id=1, source_target_pairs={{0,4},{1,5},{2,6},{3,7},{4,0},{5,1},{6,2},{7,3},{8,12},{9,13},{10,... | collective-permute-start | bytes 589832 | tf_op jit(solution)/shard_map/ppermute | solution.py:577
  941.5 29.0 %collective-permute-start.49 = (bf16[256,384]{1,0:T(8,128)(2,1)S(1)}, bf16[256,384]{1,0:T(8,128)(2,1)S(1)}, u32[]{:S(2)}, u32[]{:S(2)}) collective-permute-start(bf16[256,384]{1,0:T(8,128)(2,1)S(1)} %get-tuple-element.124), channel_id=1, source_target_pairs={{0,2},{1,3},{2,4},{3,5},{4,6},{5,7},{6,0},{7,1},{8,10},{9,11},{10,... | collective-permute-start | bytes 589832 | tf_op jit(solution)/shard_map/ppermute | solution.py:577
  943.5 218.8 %collective-permute-start.35 = (bf16[384,512]{1,0:T(8,128)(2,1)}, bf16[384,512]{1,0:T(8,128)(2,1)}, u32[]{:S(2)}, u32[]{:S(2)}) collective-permute-start(bf16[384,512]{1,0:T(8,128)(2,1)} %add_convert_fusion.23), channel_id=1, source_target_pairs={{0,16},{8,24},{16,0},{24,8},{1,17},{9,25},{17,1},{25,9},{2,18},{10... | collective-permute-start | bytes 1179656 | tf_op jit(solution)/shard_map/ppermute | solution.py:546
  949.7 214.2 %collective-permute-start.32 = (bf16[384,512]{1,0:T(8,128)(2,1)}, bf16[384,512]{1,0:T(8,128)(2,1)}, u32[]{:S(2)}, u32[]{:S(2)}) collective-permute-start(bf16[384,512]{1,0:T(8,128)(2,1)} %add_convert_fusion.24), channel_id=1, source_target_pairs={{0,8},{8,0},{16,24},{24,16},{1,9},{9,1},{17,25},{25,17},{2,10},{10... | collective-permute-start | bytes 1179656 | tf_op jit(solution)/shard_map/ppermute | solution.py:545
  968.3 26.2 %collective-permute-start.21 = (bf16[384,512]{1,0:T(8,128)(2,1)}, bf16[384,512]{1,0:T(8,128)(2,1)S(1)}, u32[]{:S(2)}, u32[]{:S(2)}) collective-permute-start(bf16[384,512]{1,0:T(8,128)(2,1)} %add_convert_fusion.26), channel_id=1, source_target_pairs={{0,8},{8,0},{16,24},{24,16},{1,9},{9,1},{17,25},{25,17},{2,10},{10... | collective-permute-start | bytes 1179656 | tf_op jit(solution)/shard_map/ppermute | solution.py:543
  970.5 26.4 %collective-permute-start.20 = (bf16[384,512]{1,0:T(8,128)(2,1)}, bf16[384,512]{1,0:T(8,128)(2,1)}, u32[]{:S(2)}, u32[]{:S(2)}) collective-permute-start(bf16[384,512]{1,0:T(8,128)(2,1)} %add_convert_fusion.25), channel_id=1, source_target_pairs={{0,16},{8,24},{16,0},{24,8},{1,17},{9,25},{17,1},{25,9},{2,18},{10... | collective-permute-start | bytes 1179656 | tf_op jit(solution)/shard_map/ppermute | solution.py:544
  994.5 182.4 %collective-permute-start.54 = (bf16[192,2304]{1,0:T(8,128)(2,1)}, bf16[192,2304]{1,0:T(8,128)(2,1)}, u32[]{:S(2)}, u32[]{:S(2)}) collective-permute-start(bf16[192,2304]{1,0:T(8,128)(2,1)} %get-tuple-element.107), channel_id=1, source_target_pairs={{0,6},{1,7},{2,0},{3,1},{4,2},{5,3},{6,4},{7,5},{8,14},{9,15},{10,... | collective-permute-start | bytes 2654216 | tf_op jit(solution)/shard_map/ppermute | solution.py:577
  996.9 36.9 %collective-permute-start.27 = (bf16[2,3,2048]{2,1,0:T(4,128)(2,1)S(1)}, bf16[2,3,2048]{2,1,0:T(4,128)(2,1)S(1)}, u32[]{:S(2)}, u32[]{:S(2)}) collective-permute-start(bf16[2,3,2048]{2,1,0:T(4,128)(2,1)S(1)} %slice.1094), channel_id=1, source_target_pairs={{1,0},{2,1},{3,2},{4,3},{5,4},{6,5},{7,6},{9,8},{10,9},{11,10},{12... | collective-permute-start | bytes 73736 | tf_op jit(solution)/shard_map/ppermute | solution.py:25
  1033.8 144.9 %collective-permute-start.53 = (bf16[192,2304]{1,0:T(8,128)(2,1)}, bf16[192,2304]{1,0:T(8,128)(2,1)}, u32[]{:S(2)}, u32[]{:S(2)}) collective-permute-start(bf16[192,2304]{1,0:T(8,128)(2,1)} %get-tuple-element.108), channel_id=1, source_target_pairs={{0,4},{1,5},{2,6},{3,7},{4,0},{5,1},{6,2},{7,3},{8,12},{9,13},{10,... | collective-permute-start | bytes 2654216 | tf_op jit(solution)/shard_map/ppermute | solution.py:577
  1144.5 154.7 %all-gather.28.cloned.1.call-start = ((), (), s32[]{:S(2)}) async-start(), calls=%async_computation.11 | async-start | bytes 4423680 | tf_op jit(solution)/shard_map/all_gather | solution.py:587
  1162.3 30.9 %collective-permute-start.52 = (bf16[192,2304]{1,0:T(8,128)(2,1)S(1)}, bf16[192,2304]{1,0:T(8,128)(2,1)S(1)}, u32[]{:S(2)}, u32[]{:S(2)}) collective-permute-start(bf16[192,2304]{1,0:T(8,128)(2,1)S(1)} %copy-done.61), channel_id=1, source_target_pairs={{0,2},{1,3},{2,4},{3,5},{4,6},{5,7},{6,0},{7,1},{8,10},{9,11},{10,... | collective-permute-start | bytes 2654216 | tf_op jit(solution)/shard_map/ppermute | solution.py:577
  1174.5 45.9 %collective-permute-start.30 = (bf16[768,512]{1,0:T(8,128)(2,1)}, bf16[768,512]{1,0:T(8,128)(2,1)}, u32[]{:S(2)}, u32[]{:S(2)}) collective-permute-start(bf16[768,512]{1,0:T(8,128)(2,1)} %convolution_convert_fusion.7), channel_id=1, source_target_pairs={{0,1},{1,0},{2,3},{3,2},{4,5},{5,4},{6,7},{7,6},{8,9},{9,8},{10,11... | collective-permute-start | bytes 2359304 | tf_op jit(solution)/shard_map/ppermute | solution.py:535
  1174.5 48.5 %collective-permute-start.29 = (bf16[768,512]{1,0:T(8,128)(2,1)}, bf16[768,512]{1,0:T(8,128)(2,1)}, u32[]{:S(2)}, u32[]{:S(2)}) collective-permute-start(bf16[768,512]{1,0:T(8,128)(2,1)} %convolution_convert_fusion.8), channel_id=1, source_target_pairs={{0,1},{1,0},{2,3},{3,2},{4,5},{5,4},{6,7},{7,6},{8,9},{9,8},{10,11... | collective-permute-start | bytes 2359304 | tf_op jit(solution)/shard_map/ppermute | solution.py:535
  1176.9 19.4 %collective-permute-start.48 = (bf16[192,512]{1,0:T(8,128)(2,1)S(1)}, bf16[192,512]{1,0:T(8,128)(2,1)S(1)}, u32[]{:S(2)}, u32[]{:S(2)}) collective-permute-start(bf16[192,512]{1,0:T(8,128)(2,1)S(1)} %get-tuple-element.117), channel_id=1, source_target_pairs={{0,6},{1,7},{2,0},{3,1},{4,2},{5,3},{6,4},{7,5},{8,14},{9,15},{10,... | collective-permute-start | bytes 589832 | tf_op jit(solution)/shard_map/ppermute | solution.py:577
  1196.3 112.5 %all-gather.26.cloned.1.call-start = ((), (), s32[]{:S(2)}) async-start(), calls=%async_computation.10 | async-start | bytes 2211840 | tf_op jit(solution)/shard_map/all_gather | solution.py:488
  1196.4 68.3 %collective-permute-start.38 = (bf16[768,512]{1,0:T(8,128)(2,1)}, bf16[768,512]{1,0:T(8,128)(2,1)S(1)}, u32[]{:S(2)}, u32[]{:S(2)}) collective-permute-start(bf16[768,512]{1,0:T(8,128)(2,1)} %convolution_convert_fusion.5), channel_id=1, source_target_pairs={{0,1},{1,0},{2,3},{3,2},{4,5},{5,4},{6,7},{7,6},{8,9},{9,8},{10,11... | collective-permute-start | bytes 2359304 | tf_op jit(solution)/shard_map/ppermute | solution.py:535
  1196.5 30.0 %collective-permute-start.28 = (bf16[768,512]{1,0:T(8,128)(2,1)}, bf16[768,512]{1,0:T(8,128)(2,1)S(1)}, u32[]{:S(2)}, u32[]{:S(2)}) collective-permute-start(bf16[768,512]{1,0:T(8,128)(2,1)} %convolution_convert_fusion.9), channel_id=1, source_target_pairs={{0,1},{1,0},{2,3},{3,2},{4,5},{5,4},{6,7},{7,6},{8,9},{9,8},{10,11... | collective-permute-start | bytes 2359304 | tf_op jit(solution)/shard_map/ppermute | solution.py:535
  1222.5 42.2 %collective-permute-start.42 = (bf16[384,512]{1,0:T(8,128)(2,1)S(1)}, bf16[384,512]{1,0:T(8,128)(2,1)S(1)}, u32[]{:S(2)}, u32[]{:S(2)}) collective-permute-start(bf16[384,512]{1,0:T(8,128)(2,1)S(1)} %add_convert_fusion.15), channel_id=1, source_target_pairs={{0,16},{8,24},{16,0},{24,8},{1,17},{9,25},{17,1},{25,9},{2,18},{10... | collective-permute-start | bytes 1179656 | tf_op jit(solution)/shard_map/ppermute | solution.py:546
  1225.0 39.7 %collective-permute-start.39 = (bf16[384,512]{1,0:T(8,128)(2,1)S(1)}, bf16[384,512]{1,0:T(8,128)(2,1)S(1)}, u32[]{:S(2)}, u32[]{:S(2)}) collective-permute-start(bf16[384,512]{1,0:T(8,128)(2,1)S(1)} %add_convert_fusion.16), channel_id=1, source_target_pairs={{0,8},{8,0},{16,24},{24,16},{1,9},{9,1},{17,25},{25,17},{2,10},{10... | collective-permute-start | bytes 1179656 | tf_op jit(solution)/shard_map/ppermute | solution.py:545
  1228.3 31.9 %collective-permute-start.37 = (bf16[384,512]{1,0:T(8,128)(2,1)S(1)}, bf16[384,512]{1,0:T(8,128)(2,1)S(1)}, u32[]{:S(2)}, u32[]{:S(2)}) collective-permute-start(bf16[384,512]{1,0:T(8,128)(2,1)S(1)} %add_convert_fusion.18), channel_id=1, source_target_pairs={{0,8},{8,0},{16,24},{24,16},{1,9},{9,1},{17,25},{25,17},{2,10},{10... | collective-permute-start | bytes 1179656 | tf_op jit(solution)/shard_map/ppermute | solution.py:543
  1230.9 31.5 %collective-permute-start.36 = (bf16[384,512]{1,0:T(8,128)(2,1)S(1)}, bf16[384,512]{1,0:T(8,128)(2,1)S(1)}, u32[]{:S(2)}, u32[]{:S(2)}) collective-permute-start(bf16[384,512]{1,0:T(8,128)(2,1)S(1)} %add_convert_fusion.17), channel_id=1, source_target_pairs={{0,16},{8,24},{16,0},{24,8},{1,17},{9,25},{17,1},{25,9},{2,18},{10... | collective-permute-start | bytes 1179656 | tf_op jit(solution)/shard_map/ppermute | solution.py:544
  (123 other events, 1702.6 us)
Sparse Core Ops, SparseCore 0:
  11.5 96.4 all-gather.15
  109.6 21.0 all-gather.17
  133.7 68.8 all-gather.19
  205.9 167.7 all-gather.21
  377.1 101.3 all-gather.23
  884.2 41.7 all-reduce.4
  928.4 216.0 reduce-scatter.4
  1147.8 39.3 reduce-scatter.6
  1196.4 67.2 all-gather.27
  1272.1 35.7 all-gather.25

commit v4 on v3

--- a/solution.py
+++ b/solution.py
@@ -15,6 +15,8 @@
 CONV = 4
 CHUNKS = 8
 HALO = 8
+BACK = 8 * (CONV - 1)
+TAIL = 32
 F32 = jnp.float32
 BF16 = jnp.bfloat16
 
@@ -51,24 +53,40 @@
     return rate, inp, decay, root
 
 
+def shifted_group(group, step, fill):
+    row = lax.broadcasted_iota(jnp.int32, group.shape, 0)
+    edge = 0 if step == 1 else CHUNKS - 1
+    moved = pltpu.roll(group, step % CHUNKS, 0)
+    return jnp.where(row == edge, fill, moved)
+
+
+def extend_back(ext_s, u_ref, halo_ref, b):
+    rows = u_ref.shape[1]
+    ext_s[pl.ds(BACK, rows), :] = u_ref[b].astype(F32)
+    halo = halo_ref[b].astype(F32)
+    for m in range(CONV - 1):
+        group = ext_s[pl.ds(BACK + rows - BACK + 8 * m, 8), :]
+        fill = halo[HALO - CONV + 1 + m : HALO - CONV + 2 + m, :]
+        ext_s[pl.ds(8 * m, 8), :] = shifted_group(group, 1, fill)
+
+
 def mixer_forward_kernel(
     u_ref, halo_ref, dist_ref, gates_ref, taps_ref, soft_ref,
     c_ref, keep_ref, state_ref, prod_ref, chunk_ref,
     ext_s, c_s, rate_s, inp_s,
 ):
     seqs, rows, _ = u_ref.shape
-    step = rows // CHUNKS
     soft = soft_ref[...]
     for b in range(seqs):
-        ext_s[b, pl.ds(0, HALO), :] = halo_ref[b].astype(F32)
-        ext_s[b, pl.ds(HALO, rows), :] = u_ref[b].astype(F32)
+        extend_back(ext_s, u_ref, halo_ref, b)
 
         def conv_chunk(n, _):
             at = pl.multiple_of(n * 64, 64)
-            total = taps_ref[0:1, :] * ext_s[b, pl.ds(at + HALO, 64), :]
+            far = dist_ref[b, pl.ds(at, 64), :]
+            total = taps_ref[0:1, :] * ext_s[pl.ds(at + BACK, 64), :]
             for k in range(1, CONV):
-                same = (dist_ref[b, pl.ds(at, 64), :] >= float(k)).astype(F32)
-                total = total + taps_ref[k : k + 1, :] * ext_s[b, pl.ds(at + HALO - k, 64), :] * same
+                window = taps_ref[k : k + 1, :] * ext_s[pl.ds(at + BACK - 8 * k, 64), :]
+                total = total + jnp.where(far >= float(k), window, 0.0)
             low = total.astype(BF16)
             c_ref[b, pl.ds(at, 64), :] = low
             c_s[b, pl.ds(at, 64), :] = low.astype(F32)
@@ -82,10 +100,10 @@
     def scan_step(j, carry):
         new = []
         for b in range(seqs):
-            at = pl.ds(j, CHUNKS, stride=step)
+            at = pl.ds(pl.multiple_of(j * 8, 8), 8)
             state, prod = carry[b]
             _, inp, decay, root = drive_values(rate_s[b, at, :], inp_s[b, at, :], soft)
-            keep = decay * (dist_ref[b, at, :] >= 1.0).astype(F32)
+            keep = jnp.where(dist_ref[b, at, :] >= 1.0, decay, 0.0)
             state = keep * state + root * inp * c_s[b, at, :]
             prod = keep * prod
             keep_ref[b, at, :] = keep
@@ -95,46 +113,59 @@
         return tuple(new)
 
     zero, one = jnp.zeros((CHUNKS, HS), F32), jnp.ones((CHUNKS, HS), F32)
-    ends = lax.fori_loop(0, step, scan_step, ((zero, one),) * seqs, unroll=4)
+    ends = lax.fori_loop(0, rows // CHUNKS, scan_step, ((zero, one),) * seqs, unroll=8)
     for b in range(seqs):
         chunk_ref[b, 0] = ends[b][0]
         chunk_ref[b, 1] = ends[b][1]
 
 
+def branch_kernel(core_ref, state_ref, prod_ref, carry_ref, gate_ref, out_ref, branch_ref, split_ref):
+    del core_ref
+    seqs, rows, _ = state_ref.shape
+    for b in range(seqs):
+        carry = jnp.concatenate([carry_ref[b]] * 4, axis=0)
+
+        def point(n, _):
+            at = pl.ds(pl.multiple_of(n * 32, 32), 32)
+            state = state_ref[b, at, :] + prod_ref[b, at, :] * carry
+            out_ref[b, at, :] = state
+            low = (state * gelu_tanh(gate_ref[b, at, :])).astype(BF16)
+            branch_ref[b, at, :] = low
+            split_ref[0, b, at, :] = low
+            return 0
+
+        lax.fori_loop(0, rows // 32, point, 0, unroll=4)
+
+
 def reverse_kernel(
     grad_ref, gate_ref, keep_ref, state_ref,
     dg_ref, local_ref, prod_ref, chunk_ref,
-    dh_s,
 ):
     seqs, rows, _ = grad_ref.shape
-    step = rows // CHUNKS
-    for b in range(seqs):
-
-        def point(n, _):
-            at = pl.ds(pl.multiple_of(n * 64, 64), 64)
+    pairs = rows // 16
+
+    def scan_step(n, carry):
+        first = pl.multiple_of((pairs - 1 - n) * 16, 16)
+        at = pl.ds(first, 16)
+        new = []
+        for b in range(seqs):
+            pull, prod = carry[b]
             act, slope = gelu_parts(gate_ref[b, at, :])
             grad = grad_ref[b, at, :]
-            dh_s[b, at, :] = grad * act
             dg_ref[b, at, :] = (grad * state_ref[b, at, :] * slope).astype(BF16)
-            return 0
-
-        lax.fori_loop(0, rows // 64, point, 0)
-
-    def scan_step(n, carry):
-        j = step - 1 - n
-        new = []
-        for b in range(seqs):
-            at = pl.ds(j, CHUNKS, stride=step)
-            pull, prod = carry[b]
+            dh = grad * act
             keep = keep_ref[b, at, :]
-            local = dh_s[b, at, :] + pull
-            local_ref[b, at, :] = local
-            prod_ref[b, at, :] = prod
-            new.append((keep * local, keep * prod))
+            late = dh[8:] + pull
+            late_prod = prod
+            pull, prod = keep[8:] * late, keep[8:] * prod
+            early = dh[:8] + pull
+            local_ref[b, at, :] = jnp.concatenate([early, late], axis=0)
+            prod_ref[b, at, :] = jnp.concatenate([prod, late_prod], axis=0)
+            new.append((keep[:8] * early, keep[:8] * prod))
         return tuple(new)
 
     zero, one = jnp.zeros((CHUNKS, HS), F32), jnp.ones((CHUNKS, HS), F32)
-    ends = lax.fori_loop(0, step, scan_step, ((zero, one),) * seqs, unroll=4)
+    ends = lax.fori_loop(0, pairs, scan_step, ((zero, one),) * seqs, unroll=4)
     for b in range(seqs):
         chunk_ref[b, 0] = ends[b][0]
         chunk_ref[b, 1] = ends[b][1]
@@ -147,7 +178,6 @@
     q_s, dq_s, dc_s, h_s, ext_s, dist_s,
 ):
     seqs, rows, _ = local_ref.shape
-    step = rows // CHUNKS
     soft = soft_ref[...]
     ggate = jnp.zeros((HS, 2 * HS), F32)
     decay_sum = jnp.zeros((8, HS), F32)
@@ -158,38 +188,38 @@
 
     for b in range(seqs):
         q_s[...] = jnp.dot(c_ref[b], gates_ref[0], preferred_element_type=F32)
-        h_s[pl.ds(0, HALO), :] = before_ref[b]
-        h_s[pl.ds(HALO, rows), :] = state_ref[b]
+        h_s[pl.ds(0, 8), :] = before_ref[b]
+        h_s[pl.ds(8, rows), :] = state_ref[b]
+        carry = jnp.concatenate([carry_ref[b]] * 4, axis=0)
 
         def point(n, total):
-            at = pl.ds(pl.multiple_of(n * step, step), step)
-            lam = local_ref[b, at, :] + prod_ref[b, at, :] * carry_ref[b, pl.ds(n, 1), :]
+            first = pl.multiple_of(n * 32, 32)
+            at = pl.ds(first, 32)
+            lam = local_ref[b, at, :] + prod_ref[b, at, :] * carry
             rate, inp, decay, root = drive_values(q_s[at, :HS], q_s[at, HS:], soft)
             conv = c_ref[b, at, :].astype(F32)
-            is_open = (dist_ref[b, at, :] >= 1.0).astype(F32)
-            prev = h_s[pl.ds(pl.multiple_of(n * step, step) + HALO - 1, step), :]
+            kept = jnp.where(dist_ref[b, at, :] >= 1.0, h_s[at, :], 0.0)
             lam_root = lam * root
             lam_inp = lam * inp
-            grad_decay = lam * prev * is_open - lam_inp * conv * decay / root
-            grad_log = grad_decay * decay
-            rated = grad_log * rate
+            grad_decay = lam * kept - lam_inp * conv * decay / root
+            rated = grad_decay * decay * rate
             dq_s[at, :HS] = (-8.0 * soft * rated * (1.0 - rate)).astype(BF16)
             dq_s[at, HS:] = (lam_root * conv * inp * (1.0 - inp)).astype(BF16)
             dc_s[at, :] = lam_root * inp
             return total + fold(rated)
 
-        decay_sum = lax.fori_loop(0, CHUNKS, point, decay_sum)
+        decay_sum = lax.fori_loop(0, rows // 32, point, decay_sum, unroll=2)
         dc_s[pl.ds(0, rows), :] += lax.dot_general(
             dq_s[...], gates_ref[0], (((1,), (1,)), ((), ())), preferred_element_type=F32
         )
-        dc_s[pl.ds(rows, HALO), :] = jnp.zeros((HALO, HS), F32)
         ggate = ggate + lax.dot_general(
             c_ref[b], dq_s[...], (((0,), (0,)), ((), ())), preferred_element_type=F32
         )
-        ext_s[pl.ds(0, HALO), :] = halo_ref[b].astype(F32)
-        ext_s[pl.ds(HALO, rows), :] = u_ref[b].astype(F32)
+        extend_back(ext_s, u_ref, halo_ref, b)
         dist_s[pl.ds(0, rows), :] = dist_ref[b]
-        dist_s[pl.ds(rows, HALO), :] = jnp.zeros((HALO, HS), F32)
+        for m in range(CONV - 1):
+            for held in (dc_s, dist_s):
+                held[pl.ds(rows + 8 * m, 8), :] = shifted_group(held[pl.ds(8 * m, 8), :], -1, 0.0)
 
         def conv_chunk(n, totals):
             at = pl.multiple_of(n * 64, 64)
@@ -197,32 +227,31 @@
             far = dist_s[pl.ds(at, 64), :]
             out = taps_ref[0:1, :] * grad
             totals = list(totals)
-            totals[0] = totals[0] + fold(grad * ext_s[pl.ds(at + HALO, 64), :])
+            totals[0] = totals[0] + fold(grad * ext_s[pl.ds(at + BACK, 64), :])
             for k in range(1, CONV):
                 masked = jnp.where(far >= float(k), grad, 0.0)
-                totals[k] = totals[k] + fold(masked * ext_s[pl.ds(at + HALO - k, 64), :])
-                ahead = jnp.where(
-                    dist_s[pl.ds(at + k, 64), :] >= float(k), dc_s[pl.ds(at + k, 64), :], 0.0
-                )
-                out = out + taps_ref[k : k + 1, :] * ahead
+                totals[k] = totals[k] + fold(masked * ext_s[pl.ds(at + BACK - 8 * k, 64), :])
+                ahead = pl.ds(at + 8 * k, 64)
+                value = taps_ref[k : k + 1, :] * dc_s[ahead, :]
+                out = out + jnp.where(dist_s[ahead, :] >= float(k), value, 0.0)
             du_ref[b, pl.ds(at, 64), :] = out.astype(BF16)
 
             @pl.when(n == rows // 64 - 1)
             def _():
-                tail_ref[b] = out[64 - HALO :, :]
+                tail_ref[b] = out[64 - TAIL :, :]
 
             return tuple(totals)
 
         taps_sum = list(lax.fori_loop(0, rows // 64, conv_chunk, tuple(taps_sum)))
-        head = dc_s[pl.ds(0, HALO), :]
-        far = dist_s[pl.ds(0, HALO), :]
-        zeros = jnp.zeros((HALO, HS), F32)
-        edge = zeros
-        for k in range(1, CONV):
-            masked = jnp.where(far >= float(k), head, 0.0)
-            both = jnp.concatenate([zeros, masked], axis=0)
-            edge = edge + taps_ref[k : k + 1, :] * both[k : k + HALO, :]
-        edge_ref[b] = edge
+        edges = [jnp.zeros((HALO - CONV + 1, HS), F32)]
+        for m in range(CONV - 1, 0, -1):
+            edge = jnp.zeros((1, HS), F32)
+            for k in range(m, CONV):
+                at = pl.ds(8 * (k - m), 1)
+                masked = jnp.where(dist_s[at, :] >= float(k), dc_s[at, :], 0.0)
+                edge = edge + taps_ref[k : k + 1, :] * masked
+            edges.append(edge)
+        edge_ref[b] = jnp.concatenate(edges, axis=0)
     ggate_ref[0] = ggate
     gdecay_ref[...] = jnp.broadcast_to(
         8.0 * jnp.sum(decay_sum, axis=0, keepdims=True), (8, HS)
@@ -310,7 +339,7 @@
             jax.ShapeDtypeStruct((seqs, 2, CHUNKS, LRU), F32),
         ],
         scratch_shapes=[
-            pltpu.VMEM((seqs, rows + HALO, HS), F32),
+            pltpu.VMEM((rows + BACK, HS), F32),
             pltpu.VMEM((seqs, rows, HS), F32),
             pltpu.VMEM((seqs, rows, HS), F32),
             pltpu.VMEM((seqs, rows, HS), F32),
@@ -318,6 +347,36 @@
         compiler_params=PARAMS,
         name="mixer_forward",
     )(u, halo, dist, gates, taps, soft)
+
+
+def mixer_branch(state, prod, carry, gate, shards, core):
+    seqs, rows, _ = state.shape
+    per = HEADS // shards
+
+    def at(h, core_ref):
+        return (0, 0, h)
+
+    def split_at(h, core_ref):
+        shard = h // per
+        return ((shard % 2 + core_ref[0]) % 2, 0, 0, (shard // 2) * per + h % per)
+
+    full = pl.BlockSpec((seqs, rows, HS), at)
+    return pl.pallas_call(
+        branch_kernel,
+        grid_spec=pltpu.PrefetchScalarGridSpec(
+            num_scalar_prefetch=1,
+            grid=(HEADS,),
+            in_specs=[full, full, pl.BlockSpec((seqs, CHUNKS, HS), at), full],
+            out_specs=[full, full, pl.BlockSpec((1, seqs, rows, HS), split_at)],
+        ),
+        out_shape=[
+            jax.ShapeDtypeStruct((seqs, rows, LRU), F32),
+            jax.ShapeDtypeStruct((seqs, rows, LRU), BF16),
+            jax.ShapeDtypeStruct((2, seqs, rows, LRU // 2), BF16),
+        ],
+        compiler_params=PARAMS,
+        name="mixer_branch",
+    )(core.reshape(1), state, prod, carry, gate)
 
 
 def mixer_reverse(grad, gate, keep, state):
@@ -335,7 +394,6 @@
             wide,
             jax.ShapeDtypeStruct((seqs, 2, CHUNKS, LRU), F32),
         ],
-        scratch_shapes=[pltpu.VMEM((seqs, rows, HS), F32)],
         compiler_params=PARAMS,
         name="mixer_reverse",
     )(grad, gate, keep, state)
@@ -364,10 +422,10 @@
             pl.BlockSpec((CONV, HS), lambda h: (0, h)),
             pl.BlockSpec((1, HS), lambda h: (0, h)),
         ],
-        out_specs=[full, small, small, gate_block, row_block, row_block],
+        out_specs=[full, head_block(seqs, TAIL), small, gate_block, row_block, row_block],
         out_shape=[
             jax.ShapeDtypeStruct((seqs, rows, LRU), BF16),
-            jax.ShapeDtypeStruct((seqs, HALO, LRU), F32),
+            jax.ShapeDtypeStruct((seqs, TAIL, LRU), F32),
             jax.ShapeDtypeStruct((seqs, HALO, LRU), F32),
             jax.ShapeDtypeStruct((HEADS, HS, 2 * HS), F32),
             jax.ShapeDtypeStruct((8, LRU), F32),
@@ -376,10 +434,10 @@
         scratch_shapes=[
             pltpu.VMEM((rows, 2 * HS), F32),
             pltpu.VMEM((rows, 2 * HS), BF16),
-            pltpu.VMEM((rows + HALO, HS), F32),
-            pltpu.VMEM((rows + HALO, HS), F32),
-            pltpu.VMEM((rows + HALO, HS), F32),
-            pltpu.VMEM((rows + HALO, HS), F32),
+            pltpu.VMEM((rows + BACK, HS), F32),
+            pltpu.VMEM((rows + 8, HS), F32),
+            pltpu.VMEM((rows + BACK, HS), F32),
+            pltpu.VMEM((rows + BACK, HS), F32),
         ],
         compiler_params=PARAMS,
         name="mixer_backward",
@@ -492,13 +550,14 @@
     return lax.dot_general(a, b, (((1,), (1,)), ((), ())), preferred_element_type=F32)
 
 
-def split_cores(a, shards, core):
-    tokens, depth = a.shape
-    split = a.reshape(tokens, shards // 2, 2, depth // shards)
-    return tuple(
-        lax.dynamic_index_in_dim(split, c, 2, False).reshape(tokens, depth // 2)
-        for c in (core, 1 - core)
-    )
+def by_position(a):
+    seqs, rows = a.shape[:2]
+    return a.reshape(seqs, CHUNKS, rows // CHUNKS, *a.shape[2:]).swapaxes(1, 2).reshape(a.shape)
+
+
+def by_token(a):
+    seqs, rows = a.shape[:2]
+    return a.reshape(seqs, rows // CHUNKS, CHUNKS, *a.shape[2:]).swapaxes(1, 2).reshape(a.shape)
 
 
 class Reduction:
@@ -535,38 +594,47 @@
             self.far[k] = lax.ppermute(product, "seq", xor_pairs("seq", 1))
         half = self.half
         self.sent = (
-            self.own(3, 0).astype(BF16),
-            self.own(3, half).astype(BF16),
-            self.own(1, 0).astype(BF16),
-            self.own(2, half).astype(BF16),
+            self.own(3, 0, half).astype(BF16),
+            self.own(3, half, full).astype(BF16),
         )
         self.diag_a = lax.ppermute(self.sent[0], "grp", self.x)
         self.diag_b = lax.ppermute(self.sent[1], "grp", self.y)
-        self.x_a = lax.ppermute(self.sent[2], "grp", self.x)
-        self.y_b = lax.ppermute(self.sent[3], "grp", self.y)
-
-    def own(self, k, first):
-        last = first + self.half
+
+    def own(self, k, first, last):
         product = dot_rows(self.a_own[:, first:last], self.b[k])
         return product + self.far[k][first:last].astype(F32)
 
-    def second(self):
+    def second(self, *after):
         if self.simple:
             return ()
+        full, none = 2 * self.half, ((0, self.half), (0, 0))
+        diag_a, diag_b = self.diag_a, self.diag_b
+        if after:
+            diag_a, diag_b = tie((diag_a, diag_b), *after)
         sent = (
-            (self.own(1, self.half) + self.diag_b.astype(F32)).astype(BF16),
-            (self.own(2, 0) + self.diag_a.astype(F32)).astype(BF16),
+            (self.own(1, 0, full) + jnp.pad(diag_b.astype(F32), (none[0][::-1], (0, 0)))).astype(BF16),
+            (self.own(2, 0, full) + jnp.pad(diag_a.astype(F32), none)).astype(BF16),
         )
-        self.x_b = lax.ppermute(sent[0], "grp", self.x)
-        self.y_a = lax.ppermute(sent[1], "grp", self.y)
+        self.from_x = lax.ppermute(sent[0], "grp", self.x)
+        self.from_y = lax.ppermute(sent[1], "grp", self.y)
         return sent
 
-    def third(self):
+    def third(self, *after, offload=False):
         if self.simple:
             return ()
-        first = self.own(0, 0) + self.x_a.astype(F32) + self.y_a.astype(F32)
-        second = self.own(0, self.half) + self.x_b.astype(F32) + self.y_b.astype(F32)
-        mine = jnp.concatenate([first.astype(BF16), second.astype(BF16)], axis=0)
+        from_x, from_y = self.from_x, self.from_y
+        if after:
+            from_x, from_y = tie((from_x, from_y), *after)
+        mine = self.own(0, 0, 2 * self.half) + from_x.astype(F32) + from_y.astype(F32)
+        mine = mine.astype(BF16)
+        self.kept = None
+        if offload:
+            count = 2 * self.chips
+            cores = [list(range(c, count, 2)) for c in range(2)]
+            self.arrived = lax.psum_scatter(
+                mine, "seq", scatter_dimension=0, axis_index_groups=cores, tiled=True
+            )
+            return (mine,)
         mine = mine.reshape(self.chips, self.rows, self.width)
         self.kept = lax.dynamic_index_in_dim(mine, self.chip, 0, False)
         sent = tuple(
@@ -581,9 +649,11 @@
     def finish(self):
         if self.simple:
             return reduce_rows(self.product)
-        total = self.kept.astype(F32)
-        for part in self.arrived:
-            total = total + part.astype(F32)
+        total = self.arrived
+        if self.kept is not None:
+            total = self.kept.astype(F32)
+            for part in self.arrived:
+                total = total + part.astype(F32)
         parts = lax.all_gather(total.astype(BF16), "grp")
         return parts.transpose(1, 0, 2).reshape(self.rows, 4 * self.width).astype(F32)
 
@@ -656,48 +726,52 @@
     proj_up = gather_rows(up_proj)
     proj_down = gather_rows(down_proj)
 
+    tokens = by_position(tokens)
+    cotangent = by_position(cotangent)
     inputs = tokens.reshape(row_count, D).astype(F32)
     first_normed, first_own, first_far, first_scale = rms_norm(
         tokens.reshape(row_count, D), gain_one, last + 1, place % 2
     )
     first_scale = first_scale[:, :1]
+    wide = (seq_count, shard_len, LRU)
     inner_low = jnp.dot(first_normed, proj_in[:, :LRU], preferred_element_type=F32).astype(BF16)
-    inner_low = inner_low.reshape(seq_count, shard_len, LRU)
-    gate_pre = jnp.dot(first_normed, proj_in[:, LRU:], preferred_element_type=F32)
-
-    prev_inner = from_behind(inner_low[:, shard_len - HALO :], "seq", 1)
+    inner_low = inner_low.reshape(wide)
+
+    step = shard_len // CHUNKS
+    final = inner_low.reshape(seq_count, step, CHUNKS, LRU)[:, step - HALO :, CHUNKS - 1]
+    prev_inner = from_behind(final, "seq", 1)
     prev_ids = from_behind(seg_ids[:, shard_len - edge_len :], "seq", 1)
     prev_ids = jnp.where(place == 0, -1, prev_ids)
     ext_ids = jnp.concatenate([prev_ids, seg_ids], axis=1)
     dist = jnp.zeros((seq_count, shard_len), F32)
     for k in range(1, CONV):
         dist = dist + (ext_ids[:, edge_len - k : edge_len - k + shard_len] == seg_ids).astype(F32)
-    dist = jnp.broadcast_to(dist[:, :, None], (seq_count, shard_len, HS))
+    dist = jnp.broadcast_to(by_position(dist)[:, :, None], (seq_count, shard_len, HS))
     soft = jax.nn.softplus(-decay_float).reshape(1, LRU)
 
     conv_low, keep, state_part, prod_part, chunks = mixer_forward(
         inner_low, prev_inner, dist, gates_all, taps_all, soft
     )
     end_state, end_prod = chunk_ends(chunks, False)
+    gate_pre = jnp.dot(first_normed, proj_in[:, LRU:], preferred_element_type=F32).reshape(wide)
     carry_in = shard_carry(end_state, end_prod, False)
     carries = chunk_carries(chunks, carry_in, False)
-    chunked = (seq_count, CHUNKS, shard_len // CHUNKS, LRU)
-    state = (
-        state_part.reshape(chunked) + prod_part.reshape(chunked) * carries[:, :, None, :]
-    ).reshape(row_count, LRU)
-    branch = (state * gelu_tanh(gate_pre)).astype(BF16)
-    resid = inputs + jnp.dot(branch, proj_out, preferred_element_type=F32)
+    state, branch, branch_split = mixer_branch(
+        state_part, prod_part, carries, gate_pre, last + 1, place % 2
+    )
+    branch_split = branch_split.reshape(2, row_count, LRU // 2)
+    resid = inputs + jnp.dot(
+        branch.reshape(row_count, LRU), proj_out, preferred_element_type=F32
+    )
     second_normed, second_own, second_far, second_scale = rms_norm(
         resid, gain_two, last + 1, place % 2
     )
     second_scale = second_scale[:, :1]
     hidden, pull = ffn_forward(second_normed, proj_up)
-    ffn_out = jnp.dot(hidden, proj_down, preferred_element_type=F32)
-    block_out = (resid + ffn_out).astype(BF16).reshape(seq_count, shard_len, D)
 
     grad_out = cotangent.reshape(row_count, D)
     grad_down = dot_rows(hidden, grad_out).astype(BF16)
-    down_total = reduce_rows(grad_down)
+    down_part = lax.psum_scatter(grad_down, "seq", scatter_dimension=0, tiled=True)
     grad_expanded = ffn_backward(tie(grad_out, grad_down), proj_down, pull)
     quarter = FF // 2
 
@@ -712,82 +786,94 @@
     grad_second_normed = dot_far(grad_expanded[0], proj_up[:, :FF]) + dot_far(
         grad_expanded[1], proj_up[:, FF:]
     )
-    sent = up_sum.second()
+    sent = up_sum.second(grad_second_normed)
     grad_second_normed = tie(grad_second_normed, *sent)
     grad_resid = grad_out.astype(F32) + norm_back(
         resid, second_scale, gain_two, grad_second_normed
     )
     grad_mixer = grad_resid.astype(BF16)
     out_sum = Reduction(
-        *split_cores(branch, last + 1, place % 2),
+        branch_split[0],
+        branch_split[1],
         lambda n: lax.dynamic_slice_in_dim(grad_mixer, n * (D // 4), D // 4, 1),
         D // 4,
     )
     grad_branch = dot_far(tie(grad_mixer, *out_sum.sent), proj_out)
 
-    wide = (seq_count, shard_len, LRU)
     grad_gate, local, rev_prod, rev_chunks = mixer_reverse(
-        grad_branch.reshape(wide), gate_pre.reshape(wide), keep, state.reshape(wide)
-    )
+        grad_branch.reshape(wide), gate_pre, keep, state
+    )
+    head_pull, head_prod = chunk_ends(rev_chunks, True)
     grad_gate = grad_gate.reshape(row_count, LRU)
     width = LRU // 4
+    sent = (*out_sum.second(head_pull), *up_sum.third(head_pull, down_part, offload=True))
+    grad_gate = tie(grad_gate, *sent)
     in_gate_sum = Reduction(
         first_own,
         first_far,
         lambda n: lax.dynamic_slice_in_dim(grad_gate, n * width, width, 1),
         width,
     )
-    sent = (*up_sum.third(), *out_sum.second(), *in_gate_sum.sent)
-    local = tie(local, *sent)
-    head_pull, head_prod = chunk_ends(rev_chunks, True)
     rev_carry = shard_carry(head_pull, head_prod, True)
     rev_carries = chunk_carries(rev_chunks, rev_carry, True)
-    before = jnp.broadcast_to(carry_in[:, None], (seq_count, HALO, LRU))
+    local = tie(local, *in_gate_sum.sent)
     du, tail, edge, grad_gates, grad_taps, grad_decay = mixer_backward(
-        local, rev_prod, rev_carries, state.reshape(wide), before, conv_low, inner_low,
+        local, rev_prod, rev_carries, state, carries, conv_low, inner_low,
         prev_inner, dist, gates_all, taps_all, soft,
     )
-    grad_decay_row = grad_decay[0] * jax.nn.sigmoid(-decay_float)
-    flat = jnp.concatenate(
-        [
-            grad_gates.reshape(last + 1, -1),
-            grad_taps[:CONV].reshape(CONV, last + 1, n_lru).transpose(1, 0, 2).reshape(last + 1, -1),
-            grad_decay_row.reshape(last + 1, n_lru),
-        ],
-        axis=1,
-    ).astype(BF16)
-    flat = lax.psum_scatter(flat.reshape(-1, HS), "seq", scatter_dimension=0, tiled=True)
-    flat = lax.psum(flat, "grp").astype(F32).reshape(-1)
-    n_gates = flat.shape[0] - (CONV + 1) * n_lru
-    gates_total = flat[:n_gates].reshape(gate_heads.shape)
-    taps_total = flat[n_gates : n_gates + CONV * n_lru].reshape(CONV, n_lru)
-    decay_total = flat[n_gates + CONV * n_lru :]
-    sent = (*in_gate_sum.second(), *out_sum.third())
-    du = tie(du, *sent)
-    up_total = up_sum.finish()
     returned = from_behind(edge[:, HALO - edge_len :].astype(BF16), "seq", -1).astype(F32)
-    returned = jnp.pad(returned, ((0, 0), (HALO - edge_len, 0), (0, 0)))
+    sent = (*out_sum.third(edge), *in_gate_sum.second(edge))
+    gate_gate = tie(grad_gate, *sent)
+    first_grad = dot_far(gate_gate, proj_in[:, LRU:])
+    groups = TAIL // CHUNKS
+    padded = jnp.pad(
+        returned[:, :, None, :], ((0, 0), (groups - edge_len, 0), (CHUNKS - 1, 0), (0, 0))
+    ).reshape(seq_count, TAIL, LRU)
     grad_inner = lax.dynamic_update_slice(
-        du, (tail + returned).astype(BF16), (0, shard_len - HALO, 0)
-    )
-    grad_inner = grad_inner.reshape(row_count, LRU)
+        du, (tail + padded).astype(BF16), (0, shard_len - TAIL, 0)
+    )
+    grad_inner = tie(grad_inner, first_grad).reshape(row_count, LRU)
     in_value_sum = Reduction(
         first_own,
         first_far,
         lambda n: lax.dynamic_slice_in_dim(grad_inner, n * width, width, 1),
         width,
     )
-    grad_inner = tie(grad_inner, *in_value_sum.sent)
-    grad_first_normed = dot_far(grad_inner, proj_in[:, :LRU]) + dot_far(
-        grad_gate, proj_in[:, LRU:]
-    )
-    sent = (*in_gate_sum.third(), *in_value_sum.second())
-    grad_first_normed = tie(grad_first_normed, *sent)
+    grad_inner = tie(grad_inner, *in_value_sum.sent, *in_gate_sum.third())
+    first_grad = first_grad + dot_far(grad_inner, proj_in[:, :LRU])
+
+    shards = last + 1
+    grad_decay_row = grad_decay[0] * jax.nn.sigmoid(-decay_float)
+    flat = jnp.concatenate(
+        [
+            grad_gates.reshape(shards, -1, HS),
+            grad_taps[:CONV].reshape(CONV, shards, -1, HS).swapaxes(0, 1).reshape(shards, -1, HS),
+            grad_decay_row.reshape(shards, -1, HS),
+        ],
+        axis=1,
+    )
+    lines = flat.shape[1]
+    whole = 16 * lax.axis_size("grp")
+    flat = jnp.pad(flat, ((0, 0), (0, -lines % whole), (0, 0))).astype(BF16).reshape(-1, HS)
+    flat = lax.psum_scatter(flat, ("seq", "grp"), scatter_dimension=0, tiled=True)
+    flat = lax.all_gather(flat, "grp", axis=0, tiled=True)
+    flat = flat[:lines].astype(F32).reshape(-1)
+    n_gates = flat.shape[0] - (CONV + 1) * n_lru
+    gates_total = flat[:n_gates].reshape(gate_heads.shape)
+    taps_total = flat[n_gates : n_gates + CONV * n_lru].reshape(CONV, n_lru)
+    decay_total = flat[n_gates + CONV * n_lru :]
+
+    in_value_sum.second(first_grad)
     out_total = out_sum.finish()
-    grad_tokens = grad_resid + norm_back(inputs, first_scale, gain_one, grad_first_normed)
-    grad_tokens = grad_tokens.astype(BF16).reshape(seq_count, shard_len, D)
+    up_total = up_sum.finish()
+    down_part = lax.psum_scatter(tie(down_part, up_total), "grp", scatter_dimension=0, tiled=True)
+    down_total = lax.all_gather(down_part, "grp", axis=0, tiled=True).astype(F32)
     in_value_sum.third()
     in_total = jnp.concatenate([in_value_sum.finish(), in_gate_sum.finish()], axis=1)
+    ffn_out = jnp.dot(hidden, proj_down, preferred_element_type=F32)
+    block_out = by_token((resid + ffn_out).astype(BF16).reshape(tokens.shape))
+    grad_tokens = grad_resid + norm_back(inputs, first_scale, gain_one, first_grad)
+    grad_tokens = by_token(grad_tokens.astype(BF16).reshape(tokens.shape))
     first_total = gain_grad(in_proj, in_total, first_gain)
     second_total = gain_grad(up_proj, up_total, second_gain)
     return (

time: 1330 us -> 1110 us (0.83)
  waiting for transfers between devices: 488 us -> 378 us
  Pallas kernels: 219 us -> 182 us
  other arithmetic: 73 us -> 46.3 us
  local copies, waits for them, and re-layouts: 106 us -> 85.8 us
  blocking collectives: 102 us -> 86.9 us
    all_gather x4, waiting for transfers between devices: 185 us -> 255 us  [gather_rows(): return lax.all_gather(own, ('seq', 'grp'), axis=0, tiled=True)]
    ppermute x16 -> x8, waiting for transfers between devices: 78.7 us -> 29.1 us  [the longest x4 29 us: second(): self.from_x = lax.ppermute(sent[0], 'grp', self.x)]
    reduce_scatter x2 -> x4, waiting for transfers between devices: 110 us -> 64.8 us  [the longest x1 64.8 us: third(): lax.psum_scatter(mine, 'seq', scatter_dimension=0, axis_index_groups=core...]
    pallas_call x1, Pallas kernels: 63.2 us -> 28.1 us  [mixer_forward(): pl.pallas_call(mixer_forward_kernel, grid=(HEADS,), in_specs=[full, head_...]
    ppermute x3, waiting for transfers between devices: 32.6 us -> 0.01 us  [from_behind(): lax.ppermute(value, axis, [(source, source + steps) for source in range(f...]
    ppermute x12 -> x9, waiting for transfers between devices: 42 us -> 19.9 us  [third(): lax.ppermute(part, 'seq', ring_pairs(2 * j + 2))]
    convert_element_type x15 -> x7, other arithmetic: 39.8 us -> 20.7 us  [the longest x4 14.8 us: third(): mine = mine.astype(BF16)]
    unnamed x226 -> x173, local copies, waits for them, and re-layouts: 64.1 us -> 45.1 us
  transfers between devices with their start and end apart: 66 -> 55, of which waited for: 23 -> 16; matrix products, arithmetic and copies ran while one was open for 29% -> 30% of each run, Pallas kernels for 11% -> 17%
where the time goes in v4:
time: 1110 us; the launch traced here: 1100 us
  waiting for transfers between devices  378 us (34%)
  matrix products  257 us (23%)
  Pallas kernels  182 us (16%)
  blocking collectives  86.9 us (8%)
  local copies, waits for them, and re-layouts  85.8 us (8%)
  other arithmetic  46.3 us (4%)
  starting transfers between devices  46 us (4%)
  between operations  15.7 us (1%)
    all_gather x4, waiting for transfers between devices, gather_rows(): return lax.all_gather(own, ('seq', 'grp'), axis=0, tiled=True)  255 us
    dot_general x37, matrix products, dot_rows(): lax.dot_general(a, b, (((0,), (0,)), ((), ())), preferred_element_type=F32)  132 us
    dot_general x5, matrix products, dot_far(): lax.dot_general(a, b, (((1,), (1,)), ((), ())), preferred_element_type=F32)  74.7 us
    reduce_scatter x1, waiting for transfers between devices, third(): lax.psum_scatter(mine, 'seq', scatter_dimension=0, axis_index_groups=core...  64.8 us
    pallas_call x1, Pallas kernels, mixer_backward(): pl.pallas_call(mixer_backward_kernel, grid=(HEADS,), in_specs=[full, full...  46.7 us
    unnamed x173, local copies, waits for them, and re-layouts  45.1 us
    all_gather x3, blocking collectives, finish(): parts = lax.all_gather(total.astype(BF16), 'grp')  39 us
    pallas_call x1, Pallas kernels, ffn_forward(): pl.pallas_call(ffn_forward_kernel, grid=(steps,), in_specs=[pl.BlockSpec(...  37.6 us
  transfers between devices with their start and end apart: 55, of which 16 were waited for; matrix products, arithmetic and copies ran while one was open for 30% of the time, Pallas kernels for 17%

profile of v4, /device:TPU:18, one launch (start us, length us, event | category | flops | bytes accessed | tf_op | source)
XLA Modules:
  0.0 1098.2 jit_solution(5061834363767528758)
XLA Ops:
  17.0 12.2 %all-gather.7 = bf16[8,1,1664]{2,1,0:T(2,128)(2,1)S(1)} all-gather(bf16[1,1,1664]{2,1,0:T(2,128)(2,1)S(1)} %reshape.2494), channel_id=2, replica_groups=mesh['grp'=4,'seq'=8] {'seq'}, dimensions={0}, use_global_device_ids=true | all-gather | bytes 29952 | tf_op jit(solution)/shard_map/all_gather | solution.py:715
  30.2 5.3 copy.292
  35.5 5.3 copy.327
  48.0 60.1 %all-gather.16.cloned.1.call-done = bf16[1536,4096]{1,0:T(8,128)(2,1)} async-done(((bf16[48,4096]{1,0:T(8,128)(2,1)}), bf16[1536,4096]{1,0:T(8,128)(2,1)}) %all-gather.16.cloned.1.call-update) | async-done | bytes 12582928 | tf_op jit(solution)/shard_map/all_gather | solution.py:523
  108.1 10.4 fusion.49
  122.9 8.9 fusion.15
  135.7 28.1 %mixer_forward.1 = (bf16[2,512,2048]{2,1,0:T(8,128)(2,1)S(1)}, f32[2,512,2048]{2,1,0:T(8,128)}, f32[2,512,2048]{2,1,0:T(8,128)}, f32[2,512,2048]{2,1,0:T(8,128)}, f32[2,2,8,2048]{3,2,1,0:T(8,128)S(1)}) custom-call(bf16[2,512,2048]{2,1,0:T(8,128)(2,1)S(1)} %bitcast.784, bf16[2,8,2048]{2,1,0:T(8,128)(2,1)S(1)} %collective-permute-done.halo_ref, ...), custom_call_target="tpu_custom_call" | custom-call | tf_op jit(solution)/shard_map/mixer_forward/pallas_call | solution.py:322
  166.5 14.0 %all-gather.1 = f32[16,2,2048]{2,1,0:T(2,128)S(1)} all-gather(f32[2,2,2048]{2,1,0:T(2,128)S(1)} %copy.311), channel_id=3, replica_groups=mesh['grp'=4,'seq'=8] {'seq'}, dimensions={0}, use_global_device_ids=true | all-gather | bytes 294912 | tf_op jit(solution)/shard_map/all_gather | solution.py:664
  181.0 17.8 %mixer_branch.1 = (f32[2,512,2048]{2,1,0:T(8,128)}, bf16[2,512,2048]{2,1,0:T(8,128)(2,1)S(1)}, bf16[2,2,512,1024]{3,2,1,0:T(8,128)(2,1)S(1)}) custom-call(s32[1]{0:T(128)} %bitcast.3.core_ref, f32[2,512,2048]{2,1,0:T(8,128)} %get-tuple-element.62.state_ref, f32[2,512,2048]{2,1,0:T(8,128)} %get-tuple-element.63.prod_ref, ...), custom_call_target="tpu_custom_call" | custom-call | tf_op jit(solution)/shard_map/mixer_branch/pallas_call | solution.py:364
  203.3 10.5 convert_add_fusion.x_ref
  222.3 152.3 %all-gather.22.cloned.1.call-done.gate_ref.up_ref = bf16[1536,9216]{1,0:T(8,128)(2,1)} async-done(((bf16[48,9216]{1,0:T(8,128)(2,1)}), bf16[1536,9216]{1,0:T(8,128)(2,1)}) %all-gather.22.cloned.1.call-update) | async-done | bytes 28311568 | tf_op jit(solution)/shard_map/all_gather | solution.py:523
  376.5 37.6 %ffn_forward.1 = (bf16[1024,4608]{1,0:T(8,128)(2,1)S(1)}, bf16[2,1024,4608]{2,1,0:T(8,128)(2,1)}) custom-call(bf16[1024,1536]{1,0:T(8,128)(2,1)S(1)} %copy-done.19, bf16[1536,9216]{1,0:T(8,128)(2,1)} %all-gather.22.cloned.1.call-done.gate_ref.up_ref, bf16[1536,9216]{1,0:T(8,128)(2,1)} %all-gather.22.cloned.1.call-done.gate_ref.up_ref), custom_call_target="tpu_custom_call" | custom-call | tf_op jit(solution)/shard_map/ffn_forward/pallas_call | solution.py:481
  417.7 18.0 %convolution_convert_fusion = bf16[4608,1536]{1,0:T(8,128)(2,1)} fusion(bf16[1024,4608]{1,0:T(8,128)(2,1)S(1)} %get-tuple-element.67, bf16[1024,1536]{1,0:T(8,128)(2,1)S(1)} %bitcast.780), kind=kOutput, calls=%fused_computation | convolution fusion | flops 14502592512 | bytes 26738688 | tf_op jit(solution)/shard_map/dot_general | solution.py:540
  436.2 42.5 %all-gather.24.cloned.1.call-done.down_ref = bf16[4608,1536]{1,0:T(8,128)(2,1)} async-done(((bf16[144,1536]{1,0:T(8,128)(2,1)}), bf16[4608,1536]{1,0:T(8,128)(2,1)}) %all-gather.24.cloned.1.call-update) | async-done | bytes 14155792 | tf_op jit(solution)/shard_map/all_gather | solution.py:523
  480.6 26.2 %ffn_backward.1 = bf16[2,1024,4608]{2,1,0:T(8,128)(2,1)} custom-call(bf16[1024,1536]{1,0:T(8,128)(2,1)S(1)} %bitcast.781, bf16[4608,1536]{1,0:T(8,128)(2,1)} %all-gather.24.cloned.1.call-done.down_ref, bf16[2,1024,4608]{2,1,0:T(8,128)(2,1)} %get-tuple-element.70.pull_ref), custom_call_target="tpu_custom_call" | custom-call | tf_op jit(solution)/shard_map/ffn_backward/pallas_call | solution.py:504
  506.8 7.6 convolution_convert_fusion.4
  514.9 4.8 fusion.309
  519.8 7.8 convolution_convert_fusion.2
  529.0 5.4 convolution_convert_fusion.3
  534.8 4.8 add_convert_fusion.5
  539.8 4.8 add_convert_fusion.4
  546.3 21.9 %fusion = f32[1024,1536]{1,0:T(8,128)} fusion(bf16[1536,9216]{1,0:T(8,128)(2,1)} %all-gather.22.cloned.1.call-done.gate_ref.up_ref, bf16[2,1024,4608]{2,1,0:T(8,128)(2,1)} %ffn_backward.1), kind=kOutput, calls=%fused_computation.1 | convolution fusion | flops 14495514624 | bytes 29884416 | tf_op jit(solution)/shard_map/dot_general | solution.py:550
  568.2 22.4 %fusion.38 = f32[1024,1536]{1,0:T(8,128)} fusion(f32[1024,1536]{1,0:T(8,128)} %fusion, bf16[1536,9216]{1,0:T(8,128)(2,1)} %all-gather.22.cloned.1.call-done.gate_ref.up_ref, bf16[2,1024,4608]{2,1,0:T(8,128)(2,1)} %ffn_backward.1), kind=kOutput, calls=%fused_computation.52 | convolution fusion | flops 14497087488 | bytes 36175872 | tf_op jit(solution)/shard_map/dot_general | solution.py:550
  590.7 9.6 add_convert_fusion.1
  600.3 9.3 add_convert_fusion.2
  609.6 4.0 multiply_reduce_fusion.1
  613.6 5.9 fusion.302
  620.9 7.9 convolution_convert_fusion.1
  631.4 8.2 fusion.22
  642.6 9.0 fusion.312
  651.6 22.0 %mixer_reverse.1 = (bf16[2,512,2048]{2,1,0:T(8,128)(2,1)S(1)}, f32[2,512,2048]{2,1,0:T(8,128)S(1)}, f32[2,512,2048]{2,1,0:T(8,128)}, f32[2,2,8,2048]{3,2,1,0:T(8,128)S(1)}) custom-call(f32[2,512,2048]{2,1,0:T(8,128)} %bitcast.817, f32[2,512,2048]{2,1,0:T(8,128)} %bitcast.809, f32[2,512,2048]{2,1,0:T(8,128)} %get-tuple-element.80.keep_ref, ...), custom_call_target="tpu_custom_call" | custom-call | tf_op jit(solution)/shard_map/mixer_reverse/pallas_call | solution.py:386
  679.1 29.0 %collective-permute-done.13 = bf16[768,2304]{1,0:T(8,128)(2,1)} collective-permute-done((bf16[768,2304]{1,0:T(8,128)(2,1)}, bf16[768,2304]{1,0:T(8,128)(2,1)}, u32[]{:S(2)}, u32[]{:S(2)}) %collective-permute-start.13) | collective-permute-done | bytes 3538976 | tf_op jit(solution)/shard_map/ppermute | solution.py:618
  708.2 9.4 add_convert_fusion
  719.9 64.8 %reduce-scatter.9.cloned.1.call-done = bf16[192,2304]{1,0:T(8,128)(2,1)} async-done(((bf16[768,2304]{1,0:T(8,128)(2,1)}), bf16[192,2304]{1,0:T(8,128)(2,1)}) %reduce-scatter.9.cloned.1.call-update) | async-done | bytes 884752 | tf_op jit(solution)/shard_map/reduce_scatter | solution.py:634
  784.7 21.3 %add_convert_fusion.3 = bf16[1024,1536]{1,0:T(8,128)(2,1)S(1)} fusion(f32[1024,1536]{1,0:T(8,128)} %copy-done.2, bf16[1024,4608]{1,0:T(8,128)(2,1)} %copy-done.30, bf16[4608,1536]{1,0:T(8,128)(2,1)} %all-gather.24.cloned.1.call-done.down_ref), kind=kOutput, calls=%fused_computation.24 | convolution fusion | flops 14498660352 | bytes 33030144 | tf_op jit(solution)/shard_map/dot_general | solution.py:873
  821.6 12.4 %all-gather.2 = f32[16,2,2048]{2,1,0:T(2,128)S(1)} all-gather(f32[2,2,2048]{2,1,0:T(2,128)S(1)} %copy.344), channel_id=4, replica_groups=mesh['grp'=4,'seq'=8] {'seq'}, dimensions={0}, use_global_device_ids=true | all-gather | bytes 294912 | tf_op jit(solution)/shard_map/all_gather | solution.py:664
  834.6 5.1 collective-permute-done.9
  869.8 46.7 %mixer_backward.1 = (bf16[2,512,2048]{2,1,0:T(8,128)(2,1)S(1)}, f32[2,32,2048]{2,1,0:T(8,128)S(1)}, f32[2,8,2048]{2,1,0:T(8,128)S(1)}, f32[16,128,256]{2,1,0:T(8...) custom-call(f32[2,512,2048]{2,1,0:T(8,128)} %copy-done.10, f32[2,512,2048]{2,1,0:T(8,128)} %get-tuple-element.93.prod_ref, ...), custom_call_target="tpu_custom_call" | custom-call | tf_op jit(solution)/shard_map/mixer_backward/pallas_call | solution.py:408
  938.6 4.9 collective-permute-done.42
  943.5 4.0 collective-permute-start.41
  952.8 12.6 %all-gather.5 = bf16[1024,384]{1,0:T(8,128)(2,1)S(1)} all-gather(bf16[256,384]{1,0:T(8,128)(2,1)S(1)} %fusion.139), channel_id=7, replica_groups=mesh['grp'=4,'seq'=8] {'grp'}, dimensions={0}, use_global_device_ids=true | all-gather | bytes 983040 | tf_op jit(solution)/shard_map/all_gather | solution.py:657
  973.9 10.9 fusion.13
  997.2 10.4 fusion.12
  1008.5 4.1 collective-permute-start.39
  1029.5 14.9 %all-gather.4 = bf16[768,512]{1,0:T(8,128)(2,1)S(1)} all-gather(bf16[192,512]{1,0:T(8,128)(2,1)S(1)} %fusion.142), channel_id=6, replica_groups=mesh['grp'=4,'seq'=8] {'grp'}, dimensions={0}, use_global_device_ids=true | all-gather | bytes 983040 | tf_op jit(solution)/shard_map/all_gather | solution.py:657
  1045.1 9.3 all_gather.78
  1063.3 6.0 collective-permute-done.35
  1070.4 11.5 %all-gather.3 = bf16[768,512]{1,0:T(8,128)(2,1)S(1)} all-gather(bf16[192,512]{1,0:T(8,128)(2,1)S(1)} %fusion.145), channel_id=5, replica_groups=mesh['grp'=4,'seq'=8] {'grp'}, dimensions={0}, use_global_device_ids=true | all-gather | bytes 983040 | tf_op jit(solution)/shard_map/all_gather | solution.py:657
  (398 shorter events, 200.5 us)
Async XLA Ops:
  7.2 100.8 %all-gather.16.cloned.1.call-start = ((), (), s32[]{:S(2)}) async-start(), calls=%async_computation.4 | async-start | bytes 12976128 | tf_op jit(solution)/shard_map/all_gather | solution.py:523
  9.2 122.7 %all-gather.18.cloned.1.call-start = ((), (), s32[]{:S(2)}) async-start(), calls=%async_computation.5 | async-start | bytes 1179648 | tf_op jit(solution)/shard_map/all_gather | solution.py:724
  10.0 193.4 %all-gather.20.cloned.1.call-start = ((), (), s32[]{:S(2)}) async-start(), calls=%async_computation.6 | async-start | bytes 6488064 | tf_op jit(solution)/shard_map/all_gather | solution.py:523
  11.7 362.9 %all-gather.22.cloned.1.call-start = ((), (), s32[]{:S(2)}) async-start(), calls=%async_computation.7 | async-start | bytes 29196288 | tf_op jit(solution)/shard_map/all_gather | solution.py:523
  13.9 464.8 %all-gather.24.cloned.1.call-start = ((), (), s32[]{:S(2)}) async-start(), calls=%async_computation.8 | async-start | bytes 14598144 | tf_op jit(solution)/shard_map/all_gather | solution.py:523
  14.8 693.4 %reduce-scatter.5.cloned.1.call-start = ((), (), s32[]{:S(2)}) async-start(), calls=%async_computation.9 | async-start | bytes 15925248 | tf_op jit(solution)/shard_map/reduce_scatter | solution.py:774
  14.9 32.7 %collective-permute-start.1 = (s32[2,3]{1,0:T(2,128)S(1)}, s32[2,3]{1,0:T(2,128)S(1)}, u32[]{:S(2)}, u32[]{:S(2)}) collective-permute-start(s32[2,3]{1,0:T(2,128)S(1)} %slice.360), channel_id=1, source_target_pairs={{0,1},{1,2},{2,3},{3,4},{4,5},{5,6},{6,7},{8,9},{9,10},{10,11},{11... | collective-permute-start | bytes 80 | tf_op jit(solution)/shard_map/ppermute | solution.py:27
  120.7 11.1 %collective-permute-start = (bf16[2,8,2048]{2,1,0:T(8,128)(2,1)S(1)}, bf16[2,8,2048]{2,1,0:T(8,128)(2,1)S(1)}, u32[]{:S(2)}, u32[]{:S(2)}) collective-permute-start(bf16[2,8,2048]{2,1,0:T(8,128)(2,1)S(1)} %bitcast.855), channel_id=1, source_target_pairs={{0,1},{1,2},{2,3},{3,4},{4,5},{5,6},{6,7},{8,9},{9,10},{10,11},{11... | collective-permute-start | bytes 196616 | tf_op jit(solution)/shard_map/ppermute | solution.py:27
  435.7 349.0 %reduce-scatter.9.cloned.1.call-start = ((), (), s32[]{:S(2)}) async-start(), calls=%async_computation.11 | async-start | bytes 4423680 | tf_op jit(solution)/shard_map/reduce_scatter | solution.py:634
  514.4 20.4 %collective-permute-start.2 = (bf16[768,2304]{1,0:T(8,128)(2,1)}, bf16[768,2304]{1,0:T(8,128)(2,1)}, u32[]{:S(2)}, u32[]{:S(2)}) collective-permute-start(bf16[768,2304]{1,0:T(8,128)(2,1)} %convolution_convert_fusion.4), channel_id=1, source_target_pairs={{0,1},{1,0},{2,3},{3,2},{4,5},{5,4},{6,7},{7,6},{8,9},{9,8},{10,11... | collective-permute-start | bytes 10616840 | tf_op jit(solution)/shard_map/ppermute | solution.py:594
  527.6 63.0 %collective-permute-start.6 = (bf16[768,2304]{1,0:T(8,128)(2,1)}, bf16[768,2304]{1,0:T(8,128)(2,1)}, u32[]{:S(2)}, u32[]{:S(2)}) collective-permute-start(bf16[768,2304]{1,0:T(8,128)(2,1)} %convolution_convert_fusion.2), channel_id=1, source_target_pairs={{0,1},{1,0},{2,3},{3,2},{4,5},{5,4},{6,7},{7,6},{8,9},{9,8},{10,11... | collective-permute-start | bytes 10616840 | tf_op jit(solution)/shard_map/ppermute | solution.py:594
  534.4 65.9 %collective-permute-start.3 = (bf16[768,2304]{1,0:T(8,128)(2,1)}, bf16[768,2304]{1,0:T(8,128)(2,1)}, u32[]{:S(2)}, u32[]{:S(2)}) collective-permute-start(bf16[768,2304]{1,0:T(8,128)(2,1)} %convolution_convert_fusion.3), channel_id=1, source_target_pairs={{0,1},{1,0},{2,3},{3,2},{4,5},{5,4},{6,7},{7,6},{8,9},{9,8},{10,11... | collective-permute-start | bytes 10616840 | tf_op jit(solution)/shard_map/ppermute | solution.py:594
  539.6 51.0 %collective-permute-start.4 = (bf16[384,2304]{1,0:T(8,128)(2,1)}, bf16[384,2304]{1,0:T(8,128)(2,1)}, u32[]{:S(2)}, u32[]{:S(2)}) collective-permute-start(bf16[384,2304]{1,0:T(8,128)(2,1)} %add_convert_fusion.5), channel_id=1, source_target_pairs={{0,8},{8,0},{16,24},{24,16},{1,9},{9,1},{17,25},{25,17},{2,10},{10... | collective-permute-start | bytes 5308424 | tf_op jit(solution)/shard_map/ppermute | solution.py:600
  544.7 46.0 %collective-permute-start.5 = (bf16[384,2304]{1,0:T(8,128)(2,1)}, bf16[384,2304]{1,0:T(8,128)(2,1)S(1)}, u32[]{:S(2)}, u32[]{:S(2)}) collective-permute-start(bf16[384,2304]{1,0:T(8,128)(2,1)} %add_convert_fusion.4), channel_id=1, source_target_pairs={{0,16},{8,24},{16,0},{24,8},{1,17},{9,25},{17,1},{25,9},{2,18},{10... | collective-permute-start | bytes 5308424 | tf_op jit(solution)/shard_map/ppermute | solution.py:601
  620.8 18.8 %collective-permute-start.7 = (bf16[1024,384]{1,0:T(8,128)(2,1)S(1)}, bf16[1024,384]{1,0:T(8,128)(2,1)S(1)}, u32[]{:S(2)}, u32[]{:S(2)}) collective-permute-start(bf16[1024,384]{1,0:T(8,128)(2,1)S(1)} %convolution_convert_fusion.16), channel_id=1, source_target_pairs={{0,1},{1,0},{2,3},{3,2},{4,5},{5,4},{6,7},{7,6},{8,9},{9,8},{10,11... | collective-permute-start | bytes 2359304 | tf_op jit(solution)/shard_map/ppermute | solution.py:594
  628.8 79.4 %collective-permute-start.12 = (bf16[768,2304]{1,0:T(8,128)(2,1)}, bf16[768,2304]{1,0:T(8,128)(2,1)}, u32[]{:S(2)}, u32[]{:S(2)}) collective-permute-start(bf16[768,2304]{1,0:T(8,128)(2,1)} %convolution_convert_fusion.1), channel_id=1, source_target_pairs={{0,1},{1,0},{2,3},{3,2},{4,5},{5,4},{6,7},{7,6},{8,9},{9,8},{10,11... | collective-permute-start | bytes 10616840 | tf_op jit(solution)/shard_map/ppermute | solution.py:594
  629.3 78.8 %collective-permute-start.13 = (bf16[768,2304]{1,0:T(8,128)(2,1)}, bf16[768,2304]{1,0:T(8,128)(2,1)}, u32[]{:S(2)}, u32[]{:S(2)}) collective-permute-start(bf16[768,2304]{1,0:T(8,128)(2,1)} %add_convert_fusion.2), channel_id=1, source_target_pairs={{0,8},{8,0},{16,24},{24,16},{1,9},{9,1},{17,25},{25,17},{2,10},{10... | collective-permute-start | bytes 10616840 | tf_op jit(solution)/shard_map/ppermute | solution.py:618
  629.5 78.7 %collective-permute-start.14 = (bf16[768,2304]{1,0:T(8,128)(2,1)}, bf16[768,2304]{1,0:T(8,128)(2,1)}, u32[]{:S(2)}, u32[]{:S(2)}) collective-permute-start(bf16[768,2304]{1,0:T(8,128)(2,1)} %add_convert_fusion.1), channel_id=1, source_target_pairs={{0,16},{8,24},{16,0},{24,8},{1,17},{9,25},{17,1},{25,9},{2,18},{10... | collective-permute-start | bytes 10616840 | tf_op jit(solution)/shard_map/ppermute | solution.py:619
  717.6 124.6 %all-gather.28.cloned.1.call-start = ((), (), s32[]{:S(2)}) async-start(), calls=%async_computation.14 | async-start | bytes 4423680 | tf_op jit(solution)/shard_map/all_gather | solution.py:657
  784.7 239.8 %reduce-scatter.11.cloned.1.call-start = ((), (), s32[]{:S(2)}) async-start(), calls=%async_computation.12 | async-start | bytes 2211840 | tf_op jit(solution)/shard_map/reduce_scatter | solution.py:869
  811.9 112.6 %collective-permute-start.15 = (bf16[1024,384]{1,0:T(8,128)(2,1)}, bf16[1024,384]{1,0:T(8,128)(2,1)}, u32[]{:S(2)}, u32[]{:S(2)}) collective-permute-start(bf16[1024,384]{1,0:T(8,128)(2,1)} %convolution_convert_fusion.13), channel_id=1, source_target_pairs={{0,1},{1,0},{2,3},{3,2},{4,5},{5,4},{6,7},{7,6},{8,9},{9,8},{10,11... | collective-permute-start | bytes 2359304 | tf_op jit(solution)/shard_map/ppermute | solution.py:594
  814.1 38.9 %collective-permute-start.11 = (bf16[1024,384]{1,0:T(8,128)(2,1)}, bf16[1024,384]{1,0:T(8,128)(2,1)}, u32[]{:S(2)}, u32[]{:S(2)}) collective-permute-start(bf16[1024,384]{1,0:T(8,128)(2,1)} %convolution_convert_fusion.14), channel_id=1, source_target_pairs={{0,1},{1,0},{2,3},{3,2},{4,5},{5,4},{6,7},{7,6},{8,9},{9,8},{10,11... | collective-permute-start | bytes 2359304 | tf_op jit(solution)/shard_map/ppermute | solution.py:594
  816.8 32.0 %collective-permute-start.8 = (bf16[1024,384]{1,0:T(8,128)(2,1)}, bf16[1024,384]{1,0:T(8,128)(2,1)}, u32[]{:S(2)}, u32[]{:S(2)}) collective-permute-start(bf16[1024,384]{1,0:T(8,128)(2,1)} %convolution_convert_fusion.15), channel_id=1, source_target_pairs={{0,1},{1,0},{2,3},{3,2},{4,5},{5,4},{6,7},{7,6},{8,9},{9,8},{10,11... | collective-permute-start | bytes 2359304 | tf_op jit(solution)/shard_map/ppermute | solution.py:594
  819.2 20.4 %collective-permute-start.9 = (bf16[512,384]{1,0:T(8,128)(2,1)}, bf16[512,384]{1,0:T(8,128)(2,1)S(1)}, u32[]{:S(2)}, u32[]{:S(2)}) collective-permute-start(bf16[512,384]{1,0:T(8,128)(2,1)} %add_convert_fusion.18), channel_id=1, source_target_pairs={{0,8},{8,0},{16,24},{24,16},{1,9},{9,1},{17,25},{25,17},{2,10},{10... | collective-permute-start | bytes 1179656 | tf_op jit(solution)/shard_map/ppermute | solution.py:600
  819.8 20.4 %collective-permute-start.10 = (bf16[512,384]{1,0:T(8,128)(2,1)}, bf16[512,384]{1,0:T(8,128)(2,1)}, u32[]{:S(2)}, u32[]{:S(2)}) collective-permute-start(bf16[512,384]{1,0:T(8,128)(2,1)} %add_convert_fusion.17), channel_id=1, source_target_pairs={{0,16},{8,24},{16,0},{24,8},{1,17},{9,25},{17,1},{25,9},{2,18},{10... | collective-permute-start | bytes 1179656 | tf_op jit(solution)/shard_map/ppermute | solution.py:601
  848.5 196.6 %reduce-scatter.7.cloned.1.call-start = ((), (), s32[]{:S(2)}) async-start(), calls=%async_computation.10 | async-start | bytes 1216512 | tf_op jit(solution)/shard_map/reduce_scatter | solution.py:858
  852.4 68.1 %collective-permute-start.16 = (bf16[1024,384]{1,0:T(8,128)(2,1)S(1)}, bf16[1024,384]{1,0:T(8,128)(2,1)S(1)}, u32[]{:S(2)}, u32[]{:S(2)}) collective-permute-start(bf16[1024,384]{1,0:T(8,128)(2,1)S(1)} %add_convert_fusion.14), channel_id=1, source_target_pairs={{0,8},{8,0},{16,24},{24,16},{1,9},{9,1},{17,25},{25,17},{2,10},{10... | collective-permute-start | bytes 2359304 | tf_op jit(solution)/shard_map/ppermute | solution.py:618
  856.0 65.2 %collective-permute-start.17 = (bf16[1024,384]{1,0:T(8,128)(2,1)S(1)}, bf16[1024,384]{1,0:T(8,128)(2,1)S(1)}, u32[]{:S(2)}, u32[]{:S(2)}) collective-permute-start(bf16[1024,384]{1,0:T(8,128)(2,1)S(1)} %add_convert_fusion.13), channel_id=1, source_target_pairs={{0,16},{8,24},{16,0},{24,8},{1,17},{9,25},{17,1},{25,9},{2,18},{10... | collective-permute-start | bytes 2359304 | tf_op jit(solution)/shard_map/ppermute | solution.py:619
  859.3 108.0 %collective-permute-start.22 = (bf16[768,512]{1,0:T(8,128)(2,1)}, bf16[768,512]{1,0:T(8,128)(2,1)}, u32[]{:S(2)}, u32[]{:S(2)}) collective-permute-start(bf16[768,512]{1,0:T(8,128)(2,1)} %convolution_convert_fusion.10), channel_id=1, source_target_pairs={{0,1},{1,0},{2,3},{3,2},{4,5},{5,4},{6,7},{7,6},{8,9},{9,8},{10,11... | collective-permute-start | bytes 2359304 | tf_op jit(solution)/shard_map/ppermute | solution.py:594
  866.9 103.4 %collective-permute-start.19 = (bf16[768,512]{1,0:T(8,128)(2,1)}, bf16[768,512]{1,0:T(8,128)(2,1)}, u32[]{:S(2)}, u32[]{:S(2)}) collective-permute-start(bf16[768,512]{1,0:T(8,128)(2,1)} %convolution_convert_fusion.11), channel_id=1, source_target_pairs={{0,1},{1,0},{2,3},{3,2},{4,5},{5,4},{6,7},{7,6},{8,9},{9,8},{10,11... | collective-permute-start | bytes 2359304 | tf_op jit(solution)/shard_map/ppermute | solution.py:594
  920.5 46.8 %collective-permute-start.20 = (bf16[384,512]{1,0:T(8,128)(2,1)}, bf16[384,512]{1,0:T(8,128)(2,1)}, u32[]{:S(2)}, u32[]{:S(2)}) collective-permute-start(bf16[384,512]{1,0:T(8,128)(2,1)} %fusion.101), channel_id=1, source_target_pairs={{0,8},{8,0},{16,24},{24,16},{1,9},{9,1},{17,25},{25,17},{2,10},{10... | collective-permute-start | bytes 1179656 | tf_op jit(solution)/shard_map/ppermute | solution.py:600
  922.2 10.8 collective-permute-start.23
  933.0 154.6 %all-gather.26.cloned.1.call-start = ((), (), s32[]{:S(2)}) async-start(), calls=%async_computation.13 | async-start | bytes 2211840 | tf_op jit(solution)/shard_map/all_gather | solution.py:870
  937.2 30.0 %collective-permute-start.21 = (bf16[384,512]{1,0:T(8,128)(2,1)}, bf16[384,512]{1,0:T(8,128)(2,1)S(1)}, u32[]{:S(2)}, u32[]{:S(2)}) collective-permute-start(bf16[384,512]{1,0:T(8,128)(2,1)} %fusion.98), channel_id=1, source_target_pairs={{0,16},{8,24},{16,0},{24,8},{1,17},{9,25},{17,1},{25,9},{2,18},{10... | collective-permute-start | bytes 1179656 | tf_op jit(solution)/shard_map/ppermute | solution.py:601
  951.7 40.9 %collective-permute-start.25 = (bf16[768,512]{1,0:T(8,128)(2,1)}, bf16[768,512]{1,0:T(8,128)(2,1)S(1)}, u32[]{:S(2)}, u32[]{:S(2)}) collective-permute-start(bf16[768,512]{1,0:T(8,128)(2,1)} %convolution_convert_fusion.8), channel_id=1, source_target_pairs={{0,1},{1,0},{2,3},{3,2},{4,5},{5,4},{6,7},{7,6},{8,9},{9,8},{10,11... | collective-permute-start | bytes 2359304 | tf_op jit(solution)/shard_map/ppermute | solution.py:594
  969.6 23.1 %collective-permute-start.27 = (bf16[768,512]{1,0:T(8,128)(2,1)S(1)}, bf16[768,512]{1,0:T(8,128)(2,1)S(1)}, u32[]{:S(2)}, u32[]{:S(2)}) collective-permute-start(bf16[768,512]{1,0:T(8,128)(2,1)S(1)} %add_convert_fusion.10), channel_id=1, source_target_pairs={{0,16},{8,24},{16,0},{24,8},{1,17},{9,25},{17,1},{25,9},{2,18},{10... | collective-permute-start | bytes 2359304 | tf_op jit(solution)/shard_map/ppermute | solution.py:619
  972.6 20.6 %collective-permute-start.26 = (bf16[768,512]{1,0:T(8,128)(2,1)S(1)}, bf16[768,512]{1,0:T(8,128)(2,1)S(1)}, u32[]{:S(2)}, u32[]{:S(2)}) collective-permute-start(bf16[768,512]{1,0:T(8,128)(2,1)S(1)} %add_convert_fusion.11), channel_id=1, source_target_pairs={{0,8},{8,0},{16,24},{24,16},{1,9},{9,1},{17,25},{25,17},{2,10},{10... | collective-permute-start | bytes 2359304 | tf_op jit(solution)/shard_map/ppermute | solution.py:618
  989.9 22.7 %collective-permute-start.33 = (bf16[768,512]{1,0:T(8,128)(2,1)S(1)}, bf16[768,512]{1,0:T(8,128)(2,1)S(1)}, u32[]{:S(2)}, u32[]{:S(2)}) collective-permute-start(bf16[768,512]{1,0:T(8,128)(2,1)S(1)} %convolution_convert_fusion.5), channel_id=1, source_target_pairs={{0,1},{1,0},{2,3},{3,2},{4,5},{5,4},{6,7},{7,6},{8,9},{9,8},{10,11... | collective-permute-start | bytes 2359304 | tf_op jit(solution)/shard_map/ppermute | solution.py:594
  992.7 23.0 %collective-permute-start.29 = (bf16[768,512]{1,0:T(8,128)(2,1)S(1)}, bf16[768,512]{1,0:T(8,128)(2,1)S(1)}, u32[]{:S(2)}, u32[]{:S(2)}) collective-permute-start(bf16[768,512]{1,0:T(8,128)(2,1)S(1)} %convolution_convert_fusion.6), channel_id=1, source_target_pairs={{0,1},{1,0},{2,3},{3,2},{4,5},{5,4},{6,7},{7,6},{8,9},{9,8},{10,11... | collective-permute-start | bytes 2359304 | tf_op jit(solution)/shard_map/ppermute | solution.py:594
  992.7 63.2 %collective-permute-start.28 = (bf16[768,512]{1,0:T(8,128)(2,1)}, bf16[768,512]{1,0:T(8,128)(2,1)}, u32[]{:S(2)}, u32[]{:S(2)}) collective-permute-start(bf16[768,512]{1,0:T(8,128)(2,1)} %convolution_convert_fusion.7), channel_id=1, source_target_pairs={{0,1},{1,0},{2,3},{3,2},{4,5},{5,4},{6,7},{7,6},{8,9},{9,8},{10,11... | collective-permute-start | bytes 2359304 | tf_op jit(solution)/shard_map/ppermute | solution.py:594
  994.4 13.2 %collective-permute-start.30 = (bf16[384,512]{1,0:T(8,128)(2,1)S(1)}, bf16[384,512]{1,0:T(8,128)(2,1)S(1)}, u32[]{:S(2)}, u32[]{:S(2)}) collective-permute-start(bf16[384,512]{1,0:T(8,128)(2,1)S(1)} %add_convert_fusion.16), channel_id=1, source_target_pairs={{0,8},{8,0},{16,24},{24,16},{1,9},{9,1},{17,25},{25,17},{2,10},{10... | collective-permute-start | bytes 1179656 | tf_op jit(solution)/shard_map/ppermute | solution.py:600
  996.3 12.2 %collective-permute-start.31 = (bf16[384,512]{1,0:T(8,128)(2,1)S(1)}, bf16[384,512]{1,0:T(8,128)(2,1)S(1)}, u32[]{:S(2)}, u32[]{:S(2)}) collective-permute-start(bf16[384,512]{1,0:T(8,128)(2,1)S(1)} %add_convert_fusion.15), channel_id=1, source_target_pairs={{0,16},{8,24},{16,0},{24,8},{1,17},{9,25},{17,1},{25,9},{2,18},{10... | collective-permute-start | bytes 1179656 | tf_op jit(solution)/shard_map/ppermute | solution.py:601
  1007.7 11.1 %collective-permute-start.40 = (bf16[192,512]{1,0:T(8,128)(2,1)S(1)}, bf16[192,512]{1,0:T(8,128)(2,1)S(1)}, u32[]{:S(2)}, u32[]{:S(2)}) collective-permute-start(bf16[192,512]{1,0:T(8,128)(2,1)S(1)} %get-tuple-element.140), channel_id=1, source_target_pairs={{0,6},{1,7},{2,0},{3,1},{4,2},{5,3},{6,4},{7,5},{8,14},{9,15},{10,... | collective-permute-start | bytes 589832 | tf_op jit(solution)/shard_map/ppermute | solution.py:645
  1008.5 17.1 %collective-permute-start.39 = (bf16[192,512]{1,0:T(8,128)(2,1)S(1)}, bf16[192,512]{1,0:T(8,128)(2,1)S(1)}, u32[]{:S(2)}, u32[]{:S(2)}) collective-permute-start(bf16[192,512]{1,0:T(8,128)(2,1)S(1)} %get-tuple-element.141), channel_id=1, source_target_pairs={{0,4},{1,5},{2,6},{3,7},{4,0},{5,1},{6,2},{7,3},{8,12},{9,13},{10,... | collective-permute-start | bytes 589832 | tf_op jit(solution)/shard_map/ppermute | solution.py:645
  1012.6 16.8 %collective-permute-start.38 = (bf16[192,512]{1,0:T(8,128)(2,1)S(1)}, bf16[192,512]{1,0:T(8,128)(2,1)S(1)}, u32[]{:S(2)}, u32[]{:S(2)}) collective-permute-start(bf16[192,512]{1,0:T(8,128)(2,1)S(1)} %get-tuple-element.142), channel_id=1, source_target_pairs={{0,2},{1,3},{2,4},{3,5},{4,6},{5,7},{6,0},{7,1},{8,10},{9,11},{10,... | collective-permute-start | bytes 589832 | tf_op jit(solution)/shard_map/ppermute | solution.py:645
  1015.7 40.2 %collective-permute-start.34 = (bf16[768,512]{1,0:T(8,128)(2,1)}, bf16[768,512]{1,0:T(8,128)(2,1)}, u32[]{:S(2)}, u32[]{:S(2)}) collective-permute-start(bf16[768,512]{1,0:T(8,128)(2,1)} %add_convert_fusion.7), channel_id=1, source_target_pairs={{0,16},{8,24},{16,0},{24,8},{1,17},{9,25},{17,1},{25,9},{2,18},{10... | collective-permute-start | bytes 2359304 | tf_op jit(solution)/shard_map/ppermute | solution.py:619
  1018.8 37.1 %collective-permute-start.32 = (bf16[768,512]{1,0:T(8,128)(2,1)}, bf16[768,512]{1,0:T(8,128)(2,1)S(1)}, u32[]{:S(2)}, u32[]{:S(2)}) collective-permute-start(bf16[768,512]{1,0:T(8,128)(2,1)} %add_convert_fusion.8), channel_id=1, source_target_pairs={{0,8},{8,0},{16,24},{24,16},{1,9},{9,1},{17,25},{25,17},{2,10},{10... | collective-permute-start | bytes 2359304 | tf_op jit(solution)/shard_map/ppermute | solution.py:618
  1058.4 10.9 collective-permute-start.35
  (89 other events, 869.7 us)
Sparse Core Ops, SparseCore 0:
  11.5 96.4 all-gather.15
  109.7 20.8 all-gather.17
  134.0 69.2 all-gather.19
  206.7 167.8 all-gather.21
  377.3 101.3 all-gather.23
  480.9 140.6 reduce-scatter.4
  717.7 66.8 reduce-scatter.8
  786.5 55.6 all-gather.27
  848.7 41.9 reduce-scatter.10
  933.1 104.9 reduce-scatter.6
  1039.9 34.2 all-gather.25

commit v5 on v4

--- a/solution.py
+++ b/solution.py
@@ -558,6 +558,97 @@
 def by_token(a):
     seqs, rows = a.shape[:2]
     return a.reshape(seqs, rows // CHUNKS, CHUNKS, *a.shape[2:]).swapaxes(1, 2).reshape(a.shape)
+
+
+def place_kernel(where_ref, *refs):
+    *pieces, out_ref, sems = refs
+    own, far = pieces[:6], pieces[6:]
+    rows, columns = own[0].shape
+    width = columns // 4
+    depth = own[1].shape[0]
+    half = own[4].shape[0]
+    chips = depth // rows + 1
+    chip, core, group = where_ref[0], where_ref[1], where_ref[2]
+    copies = []
+
+    def copy(source, row, column, count, wide):
+        row, column = pl.multiple_of(row, 16), pl.multiple_of(column, 128)
+        target = out_ref.at[pl.ds(row, count), pl.ds(column, wide)]
+        copies.append(pltpu.make_async_copy(source, target, sems.at[len(copies)]))
+
+    for c, (shard, *parts) in enumerate((own, far)):
+        side = lax.rem(core + c, 2)
+        copy(shard, (chip * 2 + side) * rows, 0, rows, columns)
+        for j in range(1, chips):
+            start = (lax.rem(chip + chips - j, chips) * 2 + side) * rows
+            first = (j - 1) * rows
+            for k in range(3):
+                column = lax.bitwise_xor(group, k) * width
+                copy(parts[k].at[pl.ds(first, rows)], start, column, rows, width)
+            column = lax.bitwise_xor(group, 3) * width
+            for n in range(2):
+                low, high = max(first, n * half), min(first + rows, (n + 1) * half)
+                if low < high:
+                    source = parts[3 + n].at[pl.ds(low - n * half, high - low)]
+                    copy(source, start + low - first, column, high - low, width)
+    for one in copies:
+        one.start()
+    for one in copies:
+        one.wait()
+
+
+class Gather:
+    def __init__(self, shard):
+        self.shard = shard
+        self.chips = lax.axis_size("seq") // 2
+        half = (self.chips - 1) * shard.shape[0] // 2
+        self.simple = lax.axis_size("grp") != 4 or half % 16 != 0
+        if self.simple:
+            self.whole = gather_rows(shard)
+            return
+        group = lax.axis_index("grp")
+        width = shard.shape[1] // 4
+        own = lax.dynamic_slice_in_dim(shard, group * width, width, 1)
+        self.near = jnp.concatenate(
+            [lax.ppermute(own, "seq", ring_pairs(2 * j)) for j in range(1, self.chips)], axis=0
+        )
+        self.half = half
+
+    def first(self):
+        if self.simple:
+            return ()
+        self.from_x = lax.ppermute(self.near, "grp", xor_pairs("grp", 1))
+        self.from_y = lax.ppermute(self.near, "grp", xor_pairs("grp", 2))
+        return (self.near,)
+
+    def second(self, *after):
+        if self.simple:
+            return ()
+        self.from_x, self.from_y = tie((self.from_x, self.from_y), *after)
+        self.halves = (self.from_y[: self.half], self.from_x[self.half :])
+        return self.halves
+
+    def whole_weight(self):
+        if self.simple:
+            return self.whole
+        diag_a = lax.ppermute(self.halves[0], "grp", xor_pairs("grp", 1))
+        diag_b = lax.ppermute(self.halves[1], "grp", xor_pairs("grp", 2))
+        own = (self.shard, self.near, self.from_x, self.from_y, diag_a, diag_b)
+        far = tuple(lax.ppermute(piece, "seq", xor_pairs("seq", 1)) for piece in own)
+        place = lax.axis_index("seq")
+        where = jnp.stack([place // 2, place % 2, lax.axis_index("grp")]).astype(jnp.int32)
+        rows, columns = self.shard.shape
+        count = 2 * (1 + (self.chips - 1) * 5)
+        anywhere = pl.BlockSpec(memory_space=pl.ANY)
+        return pl.pallas_call(
+            place_kernel,
+            in_specs=[pl.BlockSpec(memory_space=pltpu.SMEM)] + [anywhere] * 12,
+            out_specs=anywhere,
+            out_shape=jax.ShapeDtypeStruct((2 * self.chips * rows, columns), BF16),
+            scratch_shapes=[pltpu.SemaphoreType.DMA((count,))],
+            compiler_params=PARAMS,
+            name="place_pieces",
+        )(where, *own, *far)
 
 
 class Reduction:
@@ -646,10 +737,12 @@
         ]
         return sent
 
-    def finish(self):
+    def finish(self, *after):
         if self.simple:
             return reduce_rows(self.product)
         total = self.arrived
+        if after:
+            total = tie(total, *after)
         if self.kept is not None:
             total = self.kept.astype(F32)
             for part in self.arrived:
@@ -723,7 +816,7 @@
     proj_in = gather_rows(in_proj)
     gates_all = lax.all_gather(gate_heads, "seq", axis=0, tiled=True)
     proj_out = gather_rows(out_proj)
-    proj_up = gather_rows(up_proj)
+    up_gather = Gather(up_proj)
     proj_down = gather_rows(down_proj)
 
     tokens = by_position(tokens)
@@ -734,6 +827,7 @@
     )
     first_scale = first_scale[:, :1]
     wide = (seq_count, shard_len, LRU)
+    first_normed = tie(first_normed, *up_gather.first())
     inner_low = jnp.dot(first_normed, proj_in[:, :LRU], preferred_element_type=F32).astype(BF16)
     inner_low = inner_low.reshape(wide)
 
@@ -757,7 +851,7 @@
     carry_in = shard_carry(end_state, end_prod, False)
     carries = chunk_carries(chunks, carry_in, False)
     state, branch, branch_split = mixer_branch(
-        state_part, prod_part, carries, gate_pre, last + 1, place % 2
+        tie(state_part, *up_gather.second(chunks)), prod_part, carries, gate_pre, last + 1, place % 2
     )
     branch_split = branch_split.reshape(2, row_count, LRU // 2)
     resid = inputs + jnp.dot(
@@ -767,6 +861,7 @@
         resid, gain_two, last + 1, place % 2
     )
     second_scale = second_scale[:, :1]
+    proj_up = up_gather.whole_weight()
     hidden, pull = ffn_forward(second_normed, proj_up)
 
     grad_out = cotangent.reshape(row_count, D)
@@ -863,14 +958,14 @@
     taps_total = flat[n_gates : n_gates + CONV * n_lru].reshape(CONV, n_lru)
     decay_total = flat[n_gates + CONV * n_lru :]
 
-    in_value_sum.second(first_grad)
+    sent = in_value_sum.second(first_grad)
     out_total = out_sum.finish()
-    up_total = up_sum.finish()
+    up_total = up_sum.finish(edge)
     down_part = lax.psum_scatter(tie(down_part, up_total), "grp", scatter_dimension=0, tiled=True)
     down_total = lax.all_gather(down_part, "grp", axis=0, tiled=True).astype(F32)
     in_value_sum.third()
     in_total = jnp.concatenate([in_value_sum.finish(), in_gate_sum.finish()], axis=1)
-    ffn_out = jnp.dot(hidden, proj_down, preferred_element_type=F32)
+    ffn_out = jnp.dot(tie(hidden, *sent), proj_down, preferred_element_type=F32)
     block_out = by_token((resid + ffn_out).astype(BF16).reshape(tokens.shape))
     grad_tokens = grad_resid + norm_back(inputs, first_scale, gain_one, first_grad)
     grad_tokens = by_token(grad_tokens.astype(BF16).reshape(tokens.shape))

time: 1110 us -> 1800 us (1.62)
  Pallas kernels: 182 us -> 1000 us
  waiting for transfers between devices: 378 us -> 120 us
  blocking collectives: 86.9 us -> 195 us
    pallas_call x0 -> x1, Pallas kernels: none -> 819 us  [whole_weight(): pl.pallas_call(place_kernel, in_specs=[pl.BlockSpec(memory_space=pltpu.SM...]
    all_gather x4 -> x3, waiting for transfers between devices: 255 us -> 0.02 us  [gather_rows(): return lax.all_gather(own, ('seq', 'grp'), axis=0, tiled=True)]
    all_gather x1, blocking collectives: 12.2 us -> 121 us  [body(): small_all = lax.all_gather(small, 'seq')]
    reduce_scatter x1, waiting for transfers between devices: 64.8 us -> 0.01 us  [third(): lax.psum_scatter(mine, 'seq', scatter_dimension=0, axis_index_groups=core...]
    all_gather x1, waiting for transfers between devices: 1.94 us -> 49.5 us  [finish(): parts = lax.all_gather(total.astype(BF16), 'grp')]
    unnamed x173 -> x201, local copies, waits for them, and re-layouts: 45.1 us -> 44.1 us
  transfers between devices with their start and end apart: 55 -> 67, of which waited for: 16 -> 12; matrix products, arithmetic and copies ran while one was open for 30% -> 19% of each run, Pallas kernels for 17% -> 56%
where the time goes in v5:
time: 1800 us; the launch traced here: 1780 us
  Pallas kernels  1000 us (56%)
  matrix products  269 us (15%)
  blocking collectives  195 us (11%)
  waiting for transfers between devices  120 us (7%)
  local copies, waits for them, and re-layouts  91.9 us (5%)
  starting transfers between devices  55.5 us (3%)
  other arithmetic  34.9 us (2%)
    pallas_call x1, Pallas kernels, whole_weight(): pl.pallas_call(place_kernel, in_specs=[pl.BlockSpec(memory_space=pltpu.SM...  819 us
    dot_general x37, matrix products, dot_rows(): lax.dot_general(a, b, (((0,), (0,)), ((), ())), preferred_element_type=F32)  142 us
    all_gather x1, blocking collectives, body(): small_all = lax.all_gather(small, 'seq')  121 us
    dot_general x5, matrix products, dot_far(): lax.dot_general(a, b, (((1,), (1,)), ((), ())), preferred_element_type=F32)  75.7 us
    all_gather x1, waiting for transfers between devices, finish(): parts = lax.all_gather(total.astype(BF16), 'grp')  49.5 us
    pallas_call x1, Pallas kernels, mixer_backward(): pl.pallas_call(mixer_backward_kernel, grid=(HEADS,), in_specs=[full, full...  46.7 us
    unnamed x201, local copies, waits for them, and re-layouts  44.1 us
    pallas_call x1, Pallas kernels, ffn_forward(): pl.pallas_call(ffn_forward_kernel, grid=(steps,), in_specs=[pl.BlockSpec(...  37.5 us
  transfers between devices with their start and end apart: 67, of which 12 were waited for; matrix products, arithmetic and copies ran while one was open for 19% of the time, Pallas kernels for 56%

profile of v5, /device:TPU:18, one launch (start us, length us, event | category | flops | bytes accessed | tf_op | source)
XLA Modules:
  0.0 1784.1 jit_solution(17339351284643559036)
XLA Ops:
  22.0 120.6 %all-gather.7 = bf16[8,1,1664]{2,1,0:T(2,128)(2,1)S(1)} all-gather(bf16[1,1,1664]{2,1,0:T(2,128)(2,1)S(1)} %reshape.2494), channel_id=2, replica_groups=mesh['grp'=4,'seq'=8] {'seq'}, dimensions={0}, use_global_device_ids=true | all-gather | bytes 29952 | tf_op jit(solution)/shard_map/all_gather | solution.py:808
  143.5 5.4 copy.292
  167.1 9.9 fusion.55
  181.7 8.8 fusion.15
  194.4 28.0 %mixer_forward.1 = (bf16[2,512,2048]{2,1,0:T(8,128)(2,1)S(1)}, f32[2,512,2048]{2,1,0:T(8,128)}, f32[2,512,2048]{2,1,0:T(8,128)}, f32[2,512,2048]{2,1,0:T(8,128)}, f32[2,2,8,2048]{3,2,1,0:T(8,128)S(1)}) custom-call(bf16[2,512,2048]{2,1,0:T(8,128)(2,1)S(1)} %bitcast.792, bf16[2,8,2048]{2,1,0:T(8,128)(2,1)S(1)} %collective-permute-done.3.halo_ref, ...), custom_call_target="tpu_custom_call" | custom-call | tf_op jit(solution)/shard_map/mixer_forward/pallas_call | solution.py:322
  222.7 6.4 collective-permute-done.6.refs_3_
  239.8 13.9 all-gather.1
  254.6 17.9 %mixer_branch.1 = (f32[2,512,2048]{2,1,0:T(8,128)}, bf16[2,512,2048]{2,1,0:T(8,128)(2,1)S(1)}, bf16[2,2,512,1024]{3,2,1,0:T(8,128)(2,1)S(1)}) custom-call(s32[1]{0:T(128)} %bitcast.3.core_ref, f32[2,512,2048]{2,1,0:T(8,128)} %get-tuple-element.73.state_ref, f32[2,512,2048]{2,1,0:T(8,128)} %get-tuple-element.74.prod_ref, ...), custom_call_target="tpu_custom_call" | custom-call | tf_op jit(solution)/shard_map/mixer_branch/pallas_call | solution.py:364
  277.6 10.9 convert_add_fusion.x_ref
  294.5 819.4 %place_pieces.1.gate_ref.up_ref = bf16[1536,9216]{1,0:T(8,128)(2,1)} custom-call(s32[3]{0:T(128)S(1)} %pad_add_fusion.1.where_ref, bf16[192,9216]{1,0:T(8,128)(2,1)} %refs_0_.1, bf16[576,2304]{1,0:T(8,128)(2,1)} %constant_dynamic-update-slice_fusion.refs_1_, bf16[576,2304]{1,0:T(8,128)(2,1)} %collective-permute-done.5.refs_2_, ...), custom_call_target="tpu_custom_call" | custom-call | tf_op jit(solution)/shard_map/place_pieces/pallas_call | solution.py:643
  1113.8 37.5 %ffn_forward.1 = (bf16[1024,4608]{1,0:T(8,128)(2,1)S(1)}, bf16[2,1024,4608]{2,1,0:T(8,128)(2,1)}) custom-call(bf16[1024,1536]{1,0:T(8,128)(2,1)S(1)} %get-tuple-element.76.n_ref, bf16[1536,9216]{1,0:T(8,128)(2,1)} %place_pieces.1.gate_ref.up_ref, bf16[1536,9216]{1,0:T(8,128)(2,1)} %place_pieces.1.gate_ref.up_ref), custom_call_target="tpu_custom_call" | custom-call | tf_op jit(solution)/shard_map/ffn_forward/pallas_call | solution.py:481
  1154.9 17.5 convolution_convert_fusion
  1174.6 25.8 %ffn_backward.1 = bf16[2,1024,4608]{2,1,0:T(8,128)(2,1)} custom-call(bf16[1024,1536]{1,0:T(8,128)(2,1)S(1)} %bitcast.789, bf16[4608,1536]{1,0:T(8,128)(2,1)} %all-gather.21.cloned.1.call-done.down_ref, bf16[2,1024,4608]{2,1,0:T(8,128)(2,1)} %get-tuple-element.81.pull_ref), custom_call_target="tpu_custom_call" | custom-call | tf_op jit(solution)/shard_map/ffn_backward/pallas_call | solution.py:504
  1200.4 7.7 convolution_convert_fusion.4
  1208.5 4.8 fusion.315
  1213.4 7.8 convolution_convert_fusion.2
  1222.6 5.4 convolution_convert_fusion.3
  1228.6 4.8 fusion.70
  1234.0 4.8 fusion.67
  1240.1 22.0 %fusion = f32[1024,1536]{1,0:T(8,128)} fusion(bf16[1536,9216]{1,0:T(8,128)(2,1)} %place_pieces.1.gate_ref.up_ref, bf16[2,1024,4608]{2,1,0:T(8,128)(2,1)} %ffn_backward.1), kind=kOutput, calls=%fused_computation.1 | convolution fusion | flops 14495514624 | bytes 29884416 | tf_op jit(solution)/shard_map/dot_general | solution.py:550
  1262.0 21.1 %fusion.38 = f32[1024,1536]{1,0:T(8,128)S(1)} fusion(f32[1024,1536]{1,0:T(8,128)} %fusion, bf16[1536,9216]{1,0:T(8,128)(2,1)} %place_pieces.1.gate_ref.up_ref, bf16[2,1024,4608]{2,1,0:T(8,128)(2,1)} %ffn_backward.1), kind=kOutput, calls=%fused_computation.52 | convolution fusion | flops 14497087488 | bytes 36175872 | tf_op jit(solution)/shard_map/dot_general | solution.py:550
  1283.2 9.1 add_convert_fusion.2
  1293.7 9.4 add_convert_fusion.1
  1305.1 4.4 fusion.308
  1310.9 8.2 convolution_convert_fusion.1
  1320.8 8.9 fusion.318
  1329.7 22.1 %mixer_reverse.1 = (bf16[2,512,2048]{2,1,0:T(8,128)(2,1)S(1)}, f32[2,512,2048]{2,1,0:T(8,128)S(1)}, f32[2,512,2048]{2,1,0:T(8,128)}, f32[2,2,8,2048]{3,2,1,0:T(8,128)S(1)}) custom-call(f32[2,512,2048]{2,1,0:T(8,128)} %bitcast.825, f32[2,512,2048]{2,1,0:T(8,128)} %bitcast.817, f32[2,512,2048]{2,1,0:T(8,128)} %get-tuple-element.90.keep_ref, ...), custom_call_target="tpu_custom_call" | custom-call | tf_op jit(solution)/shard_map/mixer_reverse/pallas_call | solution.py:386
  1357.1 13.4 collective-permute-done.26
  1370.5 10.6 collective-permute-done.27
  1381.1 11.2 add_convert_fusion
  1399.5 14.1 all-gather.2
  1430.5 46.7 %mixer_backward.1 = (bf16[2,512,2048]{2,1,0:T(8,128)(2,1)S(1)}, f32[2,32,2048]{2,1,0:T(8,128)S(1)}, f32[2,8,2048]{2,1,0:T(8,128)S(1)}, f32[16,128,256]{2,1,0:T(8...) custom-call(f32[2,512,2048]{2,1,0:T(8,128)} %copy-done.10, f32[2,512,2048]{2,1,0:T(8,128)} %get-tuple-element.102.prod_ref, ...), custom_call_target="tpu_custom_call" | custom-call | tf_op jit(solution)/shard_map/mixer_backward/pallas_call | solution.py:408
  1480.6 49.5 %all-gather.25.cloned.1.call-done = bf16[768,2304]{1,0:T(8,128)(2,1)} async-done(((bf16[192,2304]{1,0:T(8,128)(2,1)}), bf16[768,2304]{1,0:T(8,128)(2,1)}) %all-gather.25.cloned.1.call-update) | async-done | bytes 3538960 | tf_op jit(solution)/shard_map/all_gather | solution.py:750
  1532.7 3.7 copy.399
  1538.4 4.1 convolution_convert_fusion.13
  1542.5 3.9 fusion.129
  1557.5 16.1 collective-permute-done.31
  1593.7 4.7 collective-permute-done.55
  1607.3 13.3 all-gather.5
  1629.1 10.8 fusion.13
  1657.9 13.0 fusion.12
  1672.9 3.9 fusion.11
  1679.5 12.4 all-gather.4
  1700.7 21.8 %add_convert_fusion.3 = bf16[1024,1536]{1,0:T(8,128)(2,1)} fusion(f32[1024,1536]{1,0:T(8,128)} %copy-done.2, bf16[1024,4608]{1,0:T(8,128)(2,1)} %copy-done.33, bf16[4608,1536]{1,0:T(8,128)(2,1)} %all-gather.21.cloned.1.call-done.down_ref), kind=kOutput, calls=%fused_computation.22 | convolution fusion | flops 14498660352 | bytes 33030144 | tf_op jit(solution)/shard_map/dot_general | solution.py:968
  1722.5 9.5 all_gather.74
  1733.5 4.6 copy.359
  1746.0 9.2 collective-permute-done.48
  1756.0 11.7 all-gather.3
  (453 shorter events, 217.7 us)
Async XLA Ops:
  7.2 159.9 %all-gather.15.cloned.1.call-start = ((), (), s32[]{:S(2)}) async-start(), calls=%async_computation.4 | async-start | bytes 12976128 | tf_op jit(solution)/shard_map/all_gather | solution.py:523
  9.2 181.3 %all-gather.17.cloned.1.call-start = ((), (), s32[]{:S(2)}) async-start(), calls=%async_computation.5 | async-start | bytes 1179648 | tf_op jit(solution)/shard_map/all_gather | solution.py:817
  9.9 267.7 %all-gather.19.cloned.1.call-start = ((), (), s32[]{:S(2)}) async-start(), calls=%async_computation.6 | async-start | bytes 6488064 | tf_op jit(solution)/shard_map/all_gather | solution.py:523
  11.6 1161.1 %all-gather.21.cloned.1.call-start = ((), (), s32[]{:S(2)}) async-start(), calls=%async_computation.7 | async-start | bytes 14598144 | tf_op jit(solution)/shard_map/all_gather | solution.py:523
  12.5 1368.6 %reduce-scatter.5.cloned.1.call-start = ((), (), s32[]{:S(2)}) async-start(), calls=%async_computation.8 | async-start | bytes 15925248 | tf_op jit(solution)/shard_map/reduce_scatter | solution.py:869
  14.7 148.9 %collective-permute-start.2 = (bf16[192,2304]{1,0:T(8,128)(2,1)}, bf16[192,2304]{1,0:T(8,128)(2,1)S(1)}, u32[]{:S(2)}, u32[]{:S(2)}) collective-permute-start(bf16[192,2304]{1,0:T(8,128)(2,1)} %constant_dynamic-slice_fusion.3), channel_id=1, source_target_pairs={{0,6},{1,7},{2,0},{3,1},{4,2},{5,3},{6,4},{7,5},{8,14},{9,15},{10,... | collective-permute-start | bytes 2654216 | tf_op jit(solution)/shard_map/ppermute | solution.py:613
  15.2 147.4 %collective-permute-start.1 = (bf16[192,2304]{1,0:T(8,128)(2,1)}, bf16[192,2304]{1,0:T(8,128)(2,1)S(1)}, u32[]{:S(2)}, u32[]{:S(2)}) collective-permute-start(bf16[192,2304]{1,0:T(8,128)(2,1)} %constant_dynamic-slice_fusion.3), channel_id=1, source_target_pairs={{0,4},{1,5},{2,6},{3,7},{4,0},{5,1},{6,2},{7,3},{8,12},{9,13},{10,... | collective-permute-start | bytes 2654216 | tf_op jit(solution)/shard_map/ppermute | solution.py:613
  18.7 141.8 %collective-permute-start = (bf16[192,2304]{1,0:T(8,128)(2,1)}, bf16[192,2304]{1,0:T(8,128)(2,1)}, u32[]{:S(2)}, u32[]{:S(2)}) collective-permute-start(bf16[192,2304]{1,0:T(8,128)(2,1)} %constant_dynamic-slice_fusion.3), channel_id=1, source_target_pairs={{0,2},{1,3},{2,4},{3,5},{4,6},{5,7},{6,0},{7,1},{8,10},{9,11},{10,... | collective-permute-start | bytes 2654216 | tf_op jit(solution)/shard_map/ppermute | solution.py:613
  18.7 274.4 %collective-permute-start.9 = (bf16[192,9216]{1,0:T(8,128)(2,1)}, bf16[192,9216]{1,0:T(8,128)(2,1)}, u32[]{:S(2)}, u32[]{:S(2)}) collective-permute-start(bf16[192,9216]{1,0:T(8,128)(2,1)} %refs_0_.1), channel_id=1, source_target_pairs={{0,1},{1,0},{2,3},{3,2},{4,5},{5,4},{6,7},{7,6},{8,9},{9,8},{10,11... | collective-permute-start | bytes 10616840 | tf_op jit(solution)/shard_map/ppermute | solution.py:637
  18.7 141.3 %collective-permute-start.4 = (s32[2,3]{1,0:T(2,128)S(1)}, s32[2,3]{1,0:T(2,128)S(1)}, u32[]{:S(2)}, u32[]{:S(2)}) collective-permute-start(s32[2,3]{1,0:T(2,128)S(1)} %slice.366), channel_id=1, source_target_pairs={{0,1},{1,2},{2,3},{3,4},{4,5},{5,6},{6,7},{8,9},{9,10},{10,11},{11... | collective-permute-start | bytes 80 | tf_op jit(solution)/shard_map/ppermute | solution.py:27
  164.6 89.2 %collective-permute-start.10 = (bf16[576,2304]{1,0:T(8,128)(2,1)}, bf16[576,2304]{1,0:T(8,128)(2,1)}, u32[]{:S(2)}, u32[]{:S(2)}) collective-permute-start(bf16[576,2304]{1,0:T(8,128)(2,1)} %constant_dynamic-update-slice_fusion.refs_1_), channel_id=1, source_target_pairs={{0,1},{1,0},{2,3},{3,2},{4,5},{5,4},{6,7},{7,6},{8,9},{9,8},{10,11... | collective-permute-start | bytes 7962632 | tf_op jit(solution)/shard_map/ppermute | solution.py:637
  165.1 64.0 %collective-permute-start.6 = (bf16[576,2304]{1,0:T(8,128)(2,1)}, bf16[576,2304]{1,0:T(8,128)(2,1)}, u32[]{:S(2)}, u32[]{:S(2)}) collective-permute-start(bf16[576,2304]{1,0:T(8,128)(2,1)} %constant_dynamic-update-slice_fusion.refs_1_), channel_id=1, source_target_pairs={{0,16},{8,24},{16,0},{24,8},{1,17},{9,25},{17,1},{25,9},{2,18},{10... | collective-permute-start | bytes 7962632 | tf_op jit(solution)/shard_map/ppermute | solution.py:621
  165.8 66.5 %collective-permute-start.5 = (bf16[576,2304]{1,0:T(8,128)(2,1)}, bf16[576,2304]{1,0:T(8,128)(2,1)}, u32[]{:S(2)}, u32[]{:S(2)}) collective-permute-start(bf16[576,2304]{1,0:T(8,128)(2,1)} %constant_dynamic-update-slice_fusion.refs_1_), channel_id=1, source_target_pairs={{0,8},{8,0},{16,24},{24,16},{1,9},{9,1},{17,25},{25,17},{2,10},{10... | collective-permute-start | bytes 7962632 | tf_op jit(solution)/shard_map/ppermute | solution.py:620
  237.7 39.4 %collective-permute-start.8 = (bf16[288,2304]{1,0:T(8,128)(2,1)}, bf16[288,2304]{1,0:T(8,128)(2,1)S(1)}, u32[]{:S(2)}, u32[]{:S(2)}) collective-permute-start(bf16[288,2304]{1,0:T(8,128)(2,1)} %slice.373), channel_id=1, source_target_pairs={{0,16},{8,24},{16,0},{24,8},{1,17},{9,25},{17,1},{25,9},{2,18},{10... | collective-permute-start | bytes 3981320 | tf_op jit(solution)/shard_map/ppermute | solution.py:635
  238.7 38.4 %collective-permute-start.7 = (bf16[288,2304]{1,0:T(8,128)(2,1)}, bf16[288,2304]{1,0:T(8,128)(2,1)}, u32[]{:S(2)}, u32[]{:S(2)}) collective-permute-start(bf16[288,2304]{1,0:T(8,128)(2,1)} %slice.372), channel_id=1, source_target_pairs={{0,8},{8,0},{16,24},{24,16},{1,9},{9,1},{17,25},{25,17},{2,10},{10... | collective-permute-start | bytes 3981320 | tf_op jit(solution)/shard_map/ppermute | solution.py:634
  239.6 53.5 %collective-permute-start.12 = (bf16[576,2304]{1,0:T(8,128)(2,1)}, bf16[576,2304]{1,0:T(8,128)(2,1)}, u32[]{:S(2)}, u32[]{:S(2)}) collective-permute-start(bf16[576,2304]{1,0:T(8,128)(2,1)} %collective-permute-done.6.refs_3_), channel_id=1, source_target_pairs={{0,1},{1,0},{2,3},{3,2},{4,5},{5,4},{6,7},{7,6},{8,9},{9,8},{10,11... | collective-permute-start | bytes 7962632 | tf_op jit(solution)/shard_map/ppermute | solution.py:637
  253.7 39.4 %collective-permute-start.11 = (bf16[576,2304]{1,0:T(8,128)(2,1)}, bf16[576,2304]{1,0:T(8,128)(2,1)}, u32[]{:S(2)}, u32[]{:S(2)}) collective-permute-start(bf16[576,2304]{1,0:T(8,128)(2,1)} %collective-permute-done.5.refs_2_), channel_id=1, source_target_pairs={{0,1},{1,0},{2,3},{3,2},{4,5},{5,4},{6,7},{7,6},{8,9},{9,8},{10,11... | collective-permute-start | bytes 7962632 | tf_op jit(solution)/shard_map/ppermute | solution.py:637
  1172.4 308.1 %reduce-scatter.9.cloned.1.call-start = ((), (), s32[]{:S(2)}) async-start(), calls=%async_computation.10 | async-start | bytes 4423680 | tf_op jit(solution)/shard_map/reduce_scatter | solution.py:725
  1221.2 72.5 %collective-permute-start.19 = (bf16[768,2304]{1,0:T(8,128)(2,1)}, bf16[768,2304]{1,0:T(8,128)(2,1)}, u32[]{:S(2)}, u32[]{:S(2)}) collective-permute-start(bf16[768,2304]{1,0:T(8,128)(2,1)} %convolution_convert_fusion.2), channel_id=1, source_target_pairs={{0,1},{1,0},{2,3},{3,2},{4,5},{5,4},{6,7},{7,6},{8,9},{9,8},{10,11... | collective-permute-start | bytes 10616840 | tf_op jit(solution)/shard_map/ppermute | solution.py:685
  1228.0 55.2 %collective-permute-start.16 = (bf16[768,2304]{1,0:T(8,128)(2,1)}, bf16[768,2304]{1,0:T(8,128)(2,1)}, u32[]{:S(2)}, u32[]{:S(2)}) collective-permute-start(bf16[768,2304]{1,0:T(8,128)(2,1)} %convolution_convert_fusion.3), channel_id=1, source_target_pairs={{0,1},{1,0},{2,3},{3,2},{4,5},{5,4},{6,7},{7,6},{8,9},{9,8},{10,11... | collective-permute-start | bytes 10616840 | tf_op jit(solution)/shard_map/ppermute | solution.py:685
  1233.4 49.8 %collective-permute-start.17 = (bf16[384,2304]{1,0:T(8,128)(2,1)}, bf16[384,2304]{1,0:T(8,128)(2,1)}, u32[]{:S(2)}, u32[]{:S(2)}) collective-permute-start(bf16[384,2304]{1,0:T(8,128)(2,1)} %fusion.70), channel_id=1, source_target_pairs={{0,8},{8,0},{16,24},{24,16},{1,9},{9,1},{17,25},{25,17},{2,10},{10... | collective-permute-start | bytes 5308424 | tf_op jit(solution)/shard_map/ppermute | solution.py:691
  1238.8 44.4 %collective-permute-start.18 = (bf16[384,2304]{1,0:T(8,128)(2,1)}, bf16[384,2304]{1,0:T(8,128)(2,1)}, u32[]{:S(2)}, u32[]{:S(2)}) collective-permute-start(bf16[384,2304]{1,0:T(8,128)(2,1)} %fusion.67), channel_id=1, source_target_pairs={{0,16},{8,24},{16,0},{24,8},{1,17},{9,25},{17,1},{25,9},{2,18},{10... | collective-permute-start | bytes 5308424 | tf_op jit(solution)/shard_map/ppermute | solution.py:692
  1292.3 78.2 %collective-permute-start.26 = (bf16[768,2304]{1,0:T(8,128)(2,1)}, bf16[768,2304]{1,0:T(8,128)(2,1)}, u32[]{:S(2)}, u32[]{:S(2)}) collective-permute-start(bf16[768,2304]{1,0:T(8,128)(2,1)} %add_convert_fusion.2), channel_id=1, source_target_pairs={{0,8},{8,0},{16,24},{24,16},{1,9},{9,1},{17,25},{25,17},{2,10},{10... | collective-permute-start | bytes 10616840 | tf_op jit(solution)/shard_map/ppermute | solution.py:709
  1303.1 78.1 %collective-permute-start.27 = (bf16[768,2304]{1,0:T(8,128)(2,1)}, bf16[768,2304]{1,0:T(8,128)(2,1)}, u32[]{:S(2)}, u32[]{:S(2)}) collective-permute-start(bf16[768,2304]{1,0:T(8,128)(2,1)} %add_convert_fusion.1), channel_id=1, source_target_pairs={{0,16},{8,24},{16,0},{24,8},{1,17},{9,25},{17,1},{25,9},{2,18},{10... | collective-permute-start | bytes 10616840 | tf_op jit(solution)/shard_map/ppermute | solution.py:710
  1319.1 62.0 %collective-permute-start.25 = (bf16[768,2304]{1,0:T(8,128)(2,1)}, bf16[768,2304]{1,0:T(8,128)(2,1)}, u32[]{:S(2)}, u32[]{:S(2)}) collective-permute-start(bf16[768,2304]{1,0:T(8,128)(2,1)} %convolution_convert_fusion.1), channel_id=1, source_target_pairs={{0,1},{1,0},{2,3},{3,2},{4,5},{5,4},{6,7},{7,6},{8,9},{9,8},{10,11... | collective-permute-start | bytes 10616840 | tf_op jit(solution)/shard_map/ppermute | solution.py:685
  1392.3 137.7 %all-gather.25.cloned.1.call-start = ((), (), s32[]{:S(2)}) async-start(), calls=%async_computation.13 | async-start | bytes 4423680 | tf_op jit(solution)/shard_map/all_gather | solution.py:750
  1480.5 220.1 %reduce-scatter.11.cloned.1.call-start = ((), (), s32[]{:S(2)}) async-start(), calls=%async_computation.11 | async-start | bytes 2211840 | tf_op jit(solution)/shard_map/reduce_scatter | solution.py:964
  1536.5 186.1 %reduce-scatter.7.cloned.1.call-start = ((), (), s32[]{:S(2)}) async-start(), calls=%async_computation.9 | async-start | bytes 1216512 | tf_op jit(solution)/shard_map/reduce_scatter | solution.py:953
  1542.5 35.4 %collective-permute-start.30 = (bf16[1024,384]{1,0:T(8,128)(2,1)}, bf16[1024,384]{1,0:T(8,128)(2,1)}, u32[]{:S(2)}, u32[]{:S(2)}) collective-permute-start(bf16[1024,384]{1,0:T(8,128)(2,1)} %convolution_convert_fusion.13), channel_id=1, source_target_pairs={{0,1},{1,0},{2,3},{3,2},{4,5},{5,4},{6,7},{7,6},{8,9},{9,8},{10,11... | collective-permute-start | bytes 2359304 | tf_op jit(solution)/shard_map/ppermute | solution.py:685
  1546.5 27.1 %collective-permute-start.31 = (bf16[1024,384]{1,0:T(8,128)(2,1)S(1)}, bf16[1024,384]{1,0:T(8,128)(2,1)S(1)}, u32[]{:S(2)}, u32[]{:S(2)}) collective-permute-start(bf16[1024,384]{1,0:T(8,128)(2,1)S(1)} %copy-done.85), channel_id=1, source_target_pairs={{0,8},{8,0},{16,24},{24,16},{1,9},{9,1},{17,25},{25,17},{2,10},{10... | collective-permute-start | bytes 2359304 | tf_op jit(solution)/shard_map/ppermute | solution.py:709
  1547.0 28.0 %collective-permute-start.32 = (bf16[1024,384]{1,0:T(8,128)(2,1)S(1)}, bf16[1024,384]{1,0:T(8,128)(2,1)S(1)}, u32[]{:S(2)}, u32[]{:S(2)}) collective-permute-start(bf16[1024,384]{1,0:T(8,128)(2,1)S(1)} %copy-done.84), channel_id=1, source_target_pairs={{0,16},{8,24},{16,0},{24,8},{1,17},{9,25},{17,1},{25,9},{2,18},{10... | collective-permute-start | bytes 2359304 | tf_op jit(solution)/shard_map/ppermute | solution.py:710
  1550.4 72.0 %collective-permute-start.36 = (bf16[768,512]{1,0:T(8,128)(2,1)}, bf16[768,512]{1,0:T(8,128)(2,1)}, u32[]{:S(2)}, u32[]{:S(2)}) collective-permute-start(bf16[768,512]{1,0:T(8,128)(2,1)} %convolution_convert_fusion.10), channel_id=1, source_target_pairs={{0,1},{1,0},{2,3},{3,2},{4,5},{5,4},{6,7},{7,6},{8,9},{9,8},{10,11... | collective-permute-start | bytes 2359304 | tf_op jit(solution)/shard_map/ppermute | solution.py:685
  1552.4 73.0 %collective-permute-start.33 = (bf16[768,512]{1,0:T(8,128)(2,1)}, bf16[768,512]{1,0:T(8,128)(2,1)}, u32[]{:S(2)}, u32[]{:S(2)}) collective-permute-start(bf16[768,512]{1,0:T(8,128)(2,1)} %convolution_convert_fusion.11), channel_id=1, source_target_pairs={{0,1},{1,0},{2,3},{3,2},{4,5},{5,4},{6,7},{7,6},{8,9},{9,8},{10,11... | collective-permute-start | bytes 2359304 | tf_op jit(solution)/shard_map/ppermute | solution.py:685
  1573.6 48.9 %collective-permute-start.34 = (bf16[384,512]{1,0:T(8,128)(2,1)}, bf16[384,512]{1,0:T(8,128)(2,1)}, u32[]{:S(2)}, u32[]{:S(2)}) collective-permute-start(bf16[384,512]{1,0:T(8,128)(2,1)} %fusion.119), channel_id=1, source_target_pairs={{0,8},{8,0},{16,24},{24,16},{1,9},{9,1},{17,25},{25,17},{2,10},{10... | collective-permute-start | bytes 1179656 | tf_op jit(solution)/shard_map/ppermute | solution.py:691
  1587.9 185.5 %all-gather.23.cloned.1.call-start = ((), (), s32[]{:S(2)}) async-start(), calls=%async_computation.12 | async-start | bytes 2211840 | tf_op jit(solution)/shard_map/all_gather | solution.py:965
  1592.2 30.3 %collective-permute-start.35 = (bf16[384,512]{1,0:T(8,128)(2,1)}, bf16[384,512]{1,0:T(8,128)(2,1)S(1)}, u32[]{:S(2)}, u32[]{:S(2)}) collective-permute-start(bf16[384,512]{1,0:T(8,128)(2,1)} %fusion.116), channel_id=1, source_target_pairs={{0,16},{8,24},{16,0},{24,8},{1,17},{9,25},{17,1},{25,9},{2,18},{10... | collective-permute-start | bytes 1179656 | tf_op jit(solution)/shard_map/ppermute | solution.py:692
  1606.2 42.2 %collective-permute-start.41 = (bf16[768,512]{1,0:T(8,128)(2,1)}, bf16[768,512]{1,0:T(8,128)(2,1)S(1)}, u32[]{:S(2)}, u32[]{:S(2)}) collective-permute-start(bf16[768,512]{1,0:T(8,128)(2,1)} %convolution_convert_fusion.7), channel_id=1, source_target_pairs={{0,1},{1,0},{2,3},{3,2},{4,5},{5,4},{6,7},{7,6},{8,9},{9,8},{10,11... | collective-permute-start | bytes 2359304 | tf_op jit(solution)/shard_map/ppermute | solution.py:685
  1624.7 23.8 %collective-permute-start.43 = (bf16[768,512]{1,0:T(8,128)(2,1)S(1)}, bf16[768,512]{1,0:T(8,128)(2,1)S(1)}, u32[]{:S(2)}, u32[]{:S(2)}) collective-permute-start(bf16[768,512]{1,0:T(8,128)(2,1)S(1)} %add_convert_fusion.8), channel_id=1, source_target_pairs={{0,16},{8,24},{16,0},{24,8},{1,17},{9,25},{17,1},{25,9},{2,18},{10... | collective-permute-start | bytes 2359304 | tf_op jit(solution)/shard_map/ppermute | solution.py:710
  1645.8 47.8 %collective-permute-start.44 = (bf16[768,512]{1,0:T(8,128)(2,1)}, bf16[768,512]{1,0:T(8,128)(2,1)}, u32[]{:S(2)}, u32[]{:S(2)}) collective-permute-start(bf16[768,512]{1,0:T(8,128)(2,1)} %convolution_convert_fusion.6), channel_id=1, source_target_pairs={{0,1},{1,0},{2,3},{3,2},{4,5},{5,4},{6,7},{7,6},{8,9},{9,8},{10,11... | collective-permute-start | bytes 2359304 | tf_op jit(solution)/shard_map/ppermute | solution.py:685
  1648.5 49.2 %collective-permute-start.37 = (bf16[768,512]{1,0:T(8,128)(2,1)S(1)}, bf16[768,512]{1,0:T(8,128)(2,1)S(1)}, u32[]{:S(2)}, u32[]{:S(2)}) collective-permute-start(bf16[768,512]{1,0:T(8,128)(2,1)S(1)} %convolution_convert_fusion.9), channel_id=1, source_target_pairs={{0,1},{1,0},{2,3},{3,2},{4,5},{5,4},{6,7},{7,6},{8,9},{9,8},{10,11... | collective-permute-start | bytes 2359304 | tf_op jit(solution)/shard_map/ppermute | solution.py:685
  1649.1 21.7 %collective-permute-start.53 = (bf16[192,512]{1,0:T(8,128)(2,1)S(1)}, bf16[192,512]{1,0:T(8,128)(2,1)S(1)}, u32[]{:S(2)}, u32[]{:S(2)}) collective-permute-start(bf16[192,512]{1,0:T(8,128)(2,1)S(1)} %get-tuple-element.152), channel_id=1, source_target_pairs={{0,6},{1,7},{2,0},{3,1},{4,2},{5,3},{6,4},{7,5},{8,14},{9,15},{10,... | collective-permute-start | bytes 589832 | tf_op jit(solution)/shard_map/ppermute | solution.py:736
  1650.4 21.6 %collective-permute-start.52 = (bf16[192,512]{1,0:T(8,128)(2,1)S(1)}, bf16[192,512]{1,0:T(8,128)(2,1)S(1)}, u32[]{:S(2)}, u32[]{:S(2)}) collective-permute-start(bf16[192,512]{1,0:T(8,128)(2,1)S(1)} %get-tuple-element.153), channel_id=1, source_target_pairs={{0,4},{1,5},{2,6},{3,7},{4,0},{5,1},{6,2},{7,3},{8,12},{9,13},{10,... | collective-permute-start | bytes 589832 | tf_op jit(solution)/shard_map/ppermute | solution.py:736
  1654.0 25.4 %collective-permute-start.51 = (bf16[192,512]{1,0:T(8,128)(2,1)S(1)}, bf16[192,512]{1,0:T(8,128)(2,1)S(1)}, u32[]{:S(2)}, u32[]{:S(2)}) collective-permute-start(bf16[192,512]{1,0:T(8,128)(2,1)S(1)} %get-tuple-element.154), channel_id=1, source_target_pairs={{0,2},{1,3},{2,4},{3,5},{4,6},{5,7},{6,0},{7,1},{8,10},{9,11},{10,... | collective-permute-start | bytes 589832 | tf_op jit(solution)/shard_map/ppermute | solution.py:736
  1670.8 22.8 %collective-permute-start.39 = (bf16[384,512]{1,0:T(8,128)(2,1)}, bf16[384,512]{1,0:T(8,128)(2,1)S(1)}, u32[]{:S(2)}, u32[]{:S(2)}) collective-permute-start(bf16[384,512]{1,0:T(8,128)(2,1)} %add_convert_fusion.14), channel_id=1, source_target_pairs={{0,8},{8,0},{16,24},{24,16},{1,9},{9,1},{17,25},{25,17},{2,10},{10... | collective-permute-start | bytes 1179656 | tf_op jit(solution)/shard_map/ppermute | solution.py:691
  1672.0 21.7 %collective-permute-start.40 = (bf16[384,512]{1,0:T(8,128)(2,1)S(1)}, bf16[384,512]{1,0:T(8,128)(2,1)S(1)}, u32[]{:S(2)}, u32[]{:S(2)}) collective-permute-start(bf16[384,512]{1,0:T(8,128)(2,1)S(1)} %add_convert_fusion.13), channel_id=1, source_target_pairs={{0,16},{8,24},{16,0},{24,8},{1,17},{9,25},{17,1},{25,9},{2,18},{10... | collective-permute-start | bytes 1179656 | tf_op jit(solution)/shard_map/ppermute | solution.py:692
  1679.4 58.7 %collective-permute-start.45 = (bf16[768,512]{1,0:T(8,128)(2,1)}, bf16[768,512]{1,0:T(8,128)(2,1)}, u32[]{:S(2)}, u32[]{:S(2)}) collective-permute-start(bf16[768,512]{1,0:T(8,128)(2,1)} %convolution_convert_fusion.5), channel_id=1, source_target_pairs={{0,1},{1,0},{2,3},{3,2},{4,5},{5,4},{6,7},{7,6},{8,9},{9,8},{10,11... | collective-permute-start | bytes 2359304 | tf_op jit(solution)/shard_map/ppermute | solution.py:685
  1696.7 41.4 %collective-permute-start.47 = (bf16[768,512]{1,0:T(8,128)(2,1)}, bf16[768,512]{1,0:T(8,128)(2,1)S(1)}, u32[]{:S(2)}, u32[]{:S(2)}) collective-permute-start(bf16[768,512]{1,0:T(8,128)(2,1)} %add_convert_fusion.5), channel_id=1, source_target_pairs={{0,16},{8,24},{16,0},{24,8},{1,17},{9,25},{17,1},{25,9},{2,18},{10... | collective-permute-start | bytes 2359304 | tf_op jit(solution)/shard_map/ppermute | solution.py:710
  1699.6 39.4 %collective-permute-start.46 = (bf16[768,512]{1,0:T(8,128)(2,1)}, bf16[768,512]{1,0:T(8,128)(2,1)S(1)}, u32[]{:S(2)}, u32[]{:S(2)}) collective-permute-start(bf16[768,512]{1,0:T(8,128)(2,1)} %add_convert_fusion.6), channel_id=1, source_target_pairs={{0,8},{8,0},{16,24},{24,16},{1,9},{9,1},{17,25},{25,17},{2,10},{10... | collective-permute-start | bytes 2359304 | tf_op jit(solution)/shard_map/ppermute | solution.py:709
  (114 other events, 1155.9 us)
Sparse Core Ops, SparseCore 0:
  11.5 143.5 all-gather.14
  156.7 23.8 all-gather.16
  184.1 84.8 all-gather.18
  271.7 101.2 all-gather.20
  1172.6 141.6 reduce-scatter.4
  1392.5 68.9 reduce-scatter.8
  1480.7 49.3 all-gather.24
  1536.6 40.7 reduce-scatter.10
  1588.0 104.7 reduce-scatter.6
  1700.8 37.1 all-gather.22

commit v6 on v5

--- a/solution.py
+++ b/solution.py
@@ -473,6 +473,7 @@
 
 
 FF_TILE = 512
+GATHER_TILE = 768
 
 
 def ffn_forward(normed, proj_up):
@@ -560,45 +561,72 @@
     return a.reshape(seqs, rows // CHUNKS, CHUNKS, *a.shape[2:]).swapaxes(1, 2).reshape(a.shape)
 
 
-def place_kernel(where_ref, *refs):
-    *pieces, out_ref, sems = refs
+def gathered_ffn_kernel(where_ref, n_ref, *refs):
+    pieces, (hidden_ref, pull_ref, gate_ref, up_ref, held, sems) = refs[:12], refs[12:]
     own, far = pieces[:6], pieces[6:]
+    step, steps = pl.program_id(0), pl.num_programs(0)
     rows, columns = own[0].shape
     width = columns // 4
-    depth = own[1].shape[0]
-    half = own[4].shape[0]
+    tile = hidden_ref.shape[1]
+    depth, half = own[1].shape[0], own[4].shape[0]
     chips = depth // rows + 1
     chip, core, group = where_ref[0], where_ref[1], where_ref[2]
-    copies = []
-
-    def copy(source, row, column, count, wide):
-        row, column = pl.multiple_of(row, 16), pl.multiple_of(column, 128)
-        target = out_ref.at[pl.ds(row, count), pl.ds(column, wide)]
-        copies.append(pltpu.make_async_copy(source, target, sems.at[len(copies)]))
-
-    for c, (shard, *parts) in enumerate((own, far)):
-        side = lax.rem(core + c, 2)
-        copy(shard, (chip * 2 + side) * rows, 0, rows, columns)
-        for j in range(1, chips):
-            start = (lax.rem(chip + chips - j, chips) * 2 + side) * rows
-            first = (j - 1) * rows
-            for k in range(3):
-                column = lax.bitwise_xor(group, k) * width
-                copy(parts[k].at[pl.ds(first, rows)], start, column, rows, width)
-            column = lax.bitwise_xor(group, 3) * width
-            for n in range(2):
-                low, high = max(first, n * half), min(first + rows, (n + 1) * half)
-                if low < high:
-                    source = parts[3 + n].at[pl.ds(low - n * half, high - low)]
-                    copy(source, start + low - first, column, high - low, width)
-    for one in copies:
-        one.start()
-    for one in copies:
-        one.wait()
+
+    def fetch(n, slot):
+        for side in range(2):
+            start = n * tile + side * (columns // 2)
+            quarter = start // width
+            offset = pl.multiple_of(start - quarter * width, 128)
+            start = pl.multiple_of(start, 128)
+            relation = lax.bitwise_xor(group, quarter)
+            target, sem = held.at[slot, side], sems.at[slot, side]
+
+            def copy(source, row, count):
+                place = target.at[pl.ds(pl.multiple_of(row, 16), count), :]
+                pltpu.make_async_copy(source, place, sem).start()
+
+            for c, (shard, *parts) in enumerate((own, far)):
+                other = lax.rem(core + c, 2)
+                copy(shard.at[:, pl.ds(start, tile)], (chip * 2 + other) * rows, rows)
+                for j in range(1, chips):
+                    row = (lax.rem(chip + chips - j, chips) * 2 + other) * rows
+                    first = (j - 1) * rows
+                    for k in range(3):
+
+                        @pl.when(relation == k)
+                        def _():
+                            source = parts[k].at[pl.ds(first, rows), pl.ds(offset, tile)]
+                            copy(source, row, rows)
+
+                    @pl.when(relation == 3)
+                    def _():
+                        for m in range(2):
+                            low, high = max(first, m * half), min(first + rows, (m + 1) * half)
+                            if low < high:
+                                at = pl.ds(low - m * half, high - low)
+                                source = parts[3 + m].at[at, pl.ds(offset, tile)]
+                                copy(source, row + (low - first), high - low)
+
+    slot = lax.rem(step, 2)
+
+    @pl.when(step == 0)
+    def _():
+        fetch(step, slot)
+
+    @pl.when(step + 1 < steps)
+    def _():
+        fetch(step + 1, 1 - slot)
+
+    for side in range(2):
+        whole = held.at[slot, side]
+        pltpu.make_async_copy(whole, whole, sems.at[slot, side]).wait()
+    gate_ref[...] = held[slot, 0]
+    up_ref[...] = held[slot, 1]
+    ffn_forward_kernel(n_ref, gate_ref, up_ref, hidden_ref, pull_ref)
 
 
 class Gather:
-    def __init__(self, shard):
+    def __init__(self, shard, *after):
         self.shard = shard
         self.chips = lax.axis_size("seq") // 2
         half = (self.chips - 1) * shard.shape[0] // 2
@@ -608,7 +636,7 @@
             return
         group = lax.axis_index("grp")
         width = shard.shape[1] // 4
-        own = lax.dynamic_slice_in_dim(shard, group * width, width, 1)
+        own = tie(lax.dynamic_slice_in_dim(shard, group * width, width, 1), *after)
         self.near = jnp.concatenate(
             [lax.ppermute(own, "seq", ring_pairs(2 * j)) for j in range(1, self.chips)], axis=0
         )
@@ -628,27 +656,46 @@
         self.halves = (self.from_y[: self.half], self.from_x[self.half :])
         return self.halves
 
-    def whole_weight(self):
+    def ffn_forward(self, normed):
         if self.simple:
-            return self.whole
+            hidden, pull = ffn_forward(normed, self.whole)
+            return hidden, pull, self.whole[:, :FF], self.whole[:, FF:]
         diag_a = lax.ppermute(self.halves[0], "grp", xor_pairs("grp", 1))
         diag_b = lax.ppermute(self.halves[1], "grp", xor_pairs("grp", 2))
         own = (self.shard, self.near, self.from_x, self.from_y, diag_a, diag_b)
         far = tuple(lax.ppermute(piece, "seq", xor_pairs("seq", 1)) for piece in own)
         place = lax.axis_index("seq")
         where = jnp.stack([place // 2, place % 2, lax.axis_index("grp")]).astype(jnp.int32)
-        rows, columns = self.shard.shape
-        count = 2 * (1 + (self.chips - 1) * 5)
-        anywhere = pl.BlockSpec(memory_space=pl.ANY)
+        rows = normed.shape[0]
+        tile = GATHER_TILE
+        weight = pl.BlockSpec((D, tile), lambda n: (0, n))
         return pl.pallas_call(
-            place_kernel,
-            in_specs=[pl.BlockSpec(memory_space=pltpu.SMEM)] + [anywhere] * 12,
-            out_specs=anywhere,
-            out_shape=jax.ShapeDtypeStruct((2 * self.chips * rows, columns), BF16),
-            scratch_shapes=[pltpu.SemaphoreType.DMA((count,))],
-            compiler_params=PARAMS,
-            name="place_pieces",
-        )(where, *own, *far)
+            gathered_ffn_kernel,
+            grid=(FF // tile,),
+            in_specs=[
+                pl.BlockSpec(memory_space=pltpu.SMEM),
+                pl.BlockSpec((rows, D), lambda n: (0, 0)),
+            ]
+            + [pl.BlockSpec(memory_space=pl.ANY)] * 12,
+            out_specs=[
+                pl.BlockSpec((rows, tile), lambda n: (0, n)),
+                pl.BlockSpec((2, rows, tile), lambda n: (0, 0, n)),
+                weight,
+                weight,
+            ],
+            out_shape=[
+                jax.ShapeDtypeStruct((rows, FF), BF16),
+                jax.ShapeDtypeStruct((2, rows, FF), BF16),
+                jax.ShapeDtypeStruct((D, FF), BF16),
+                jax.ShapeDtypeStruct((D, FF), BF16),
+            ],
+            scratch_shapes=[
+                pltpu.VMEM((2, 2, D, tile), BF16),
+                pltpu.SemaphoreType.DMA((2, 2)),
+            ],
+            compiler_params=pltpu.CompilerParams(vmem_limit_bytes=56 * 1024 * 1024),
+            name="gathered_ffn",
+        )(where, normed, *own, *far)
 
 
 class Reduction:
@@ -674,6 +721,7 @@
                 axis=1,
             )
             self.product = cores.reshape(2 * full, 4 * width).astype(BF16)
+            self.arrived = self.product
             self.sent = (self.product,)
             return
         group = lax.axis_index("grp")
@@ -710,23 +758,15 @@
         self.from_y = lax.ppermute(sent[1], "grp", self.y)
         return sent
 
-    def third(self, *after, offload=False):
-        if self.simple:
-            return ()
+    def mine(self, *after):
         from_x, from_y = self.from_x, self.from_y
         if after:
             from_x, from_y = tie((from_x, from_y), *after)
         mine = self.own(0, 0, 2 * self.half) + from_x.astype(F32) + from_y.astype(F32)
-        mine = mine.astype(BF16)
-        self.kept = None
-        if offload:
-            count = 2 * self.chips
-            cores = [list(range(c, count, 2)) for c in range(2)]
-            self.arrived = lax.psum_scatter(
-                mine, "seq", scatter_dimension=0, axis_index_groups=cores, tiled=True
-            )
-            return (mine,)
-        mine = mine.reshape(self.chips, self.rows, self.width)
+        return mine.astype(BF16)
+
+    def along_z(self, mine):
+        mine = mine.reshape(self.chips, self.rows, -1)
         self.kept = lax.dynamic_index_in_dim(mine, self.chip, 0, False)
         sent = tuple(
             lax.dynamic_index_in_dim(mine, (self.chip + j) % self.chips, 0, False)
@@ -737,18 +777,54 @@
         ]
         return sent
 
+    def third(self, *after, offload=False):
+        if self.simple:
+            return ()
+        mine = self.mine(*after)
+        if not offload:
+            return self.along_z(mine)
+        count = 2 * self.chips
+        cores = [list(range(c, count, 2)) for c in range(2)]
+        self.kept = None
+        self.arrived = lax.psum_scatter(
+            mine, "seq", scatter_dimension=0, axis_index_groups=cores, tiled=True
+        )
+        return (mine,)
+
+    def total(self):
+        if self.kept is None:
+            return self.arrived
+        total = self.kept.astype(F32)
+        for part in self.arrived:
+            total = total + part.astype(F32)
+        return total
+
     def finish(self, *after):
         if self.simple:
             return reduce_rows(self.product)
-        total = self.arrived
+        total = self.total()
         if after:
             total = tie(total, *after)
-        if self.kept is not None:
-            total = self.kept.astype(F32)
-            for part in self.arrived:
-                total = total + part.astype(F32)
         parts = lax.all_gather(total.astype(BF16), "grp")
         return parts.transpose(1, 0, 2).reshape(self.rows, 4 * self.width).astype(F32)
+
+
+def gather_parts(lines, sums):
+    if sums[0].simple:
+        return lax.all_gather(lines, "grp", axis=0, tiled=True), [one.finish() for one in sums]
+    pieces = [lines]
+    for one in sums:
+        total = one.total().astype(BF16)
+        pieces += [total[:, n : n + HS] for n in range(0, one.width, HS)]
+    parts = lax.all_gather(jnp.concatenate(pieces, axis=0), "grp")
+    at = lines.shape[0]
+    found = []
+    for one in sums:
+        blocks = one.width // HS
+        part = parts[:, at : at + blocks * one.rows].reshape(4, blocks, one.rows, HS)
+        found.append(part.transpose(2, 0, 1, 3).reshape(one.rows, 4 * one.width).astype(F32))
+        at += blocks * one.rows
+    return parts[:, : lines.shape[0]].reshape(-1, HS), found
 
 
 def shard_carry(ends, prods, reverse):
@@ -816,7 +892,6 @@
     proj_in = gather_rows(in_proj)
     gates_all = lax.all_gather(gate_heads, "seq", axis=0, tiled=True)
     proj_out = gather_rows(out_proj)
-    up_gather = Gather(up_proj)
     proj_down = gather_rows(down_proj)
 
     tokens = by_position(tokens)
@@ -827,7 +902,7 @@
     )
     first_scale = first_scale[:, :1]
     wide = (seq_count, shard_len, LRU)
-    first_normed = tie(first_normed, *up_gather.first())
+    up_gather = Gather(up_proj, first_normed)
     inner_low = jnp.dot(first_normed, proj_in[:, :LRU], preferred_element_type=F32).astype(BF16)
     inner_low = inner_low.reshape(wide)
 
@@ -844,14 +919,14 @@
     soft = jax.nn.softplus(-decay_float).reshape(1, LRU)
 
     conv_low, keep, state_part, prod_part, chunks = mixer_forward(
-        inner_low, prev_inner, dist, gates_all, taps_all, soft
+        tie(inner_low, *up_gather.first()), prev_inner, dist, gates_all, taps_all, soft
     )
     end_state, end_prod = chunk_ends(chunks, False)
     gate_pre = jnp.dot(first_normed, proj_in[:, LRU:], preferred_element_type=F32).reshape(wide)
     carry_in = shard_carry(end_state, end_prod, False)
     carries = chunk_carries(chunks, carry_in, False)
     state, branch, branch_split = mixer_branch(
-        tie(state_part, *up_gather.second(chunks)), prod_part, carries, gate_pre, last + 1, place % 2
+        tie(state_part, *up_gather.second(carries)), prod_part, carries, gate_pre, last + 1, place % 2
     )
     branch_split = branch_split.reshape(2, row_count, LRU // 2)
     resid = inputs + jnp.dot(
@@ -861,12 +936,12 @@
         resid, gain_two, last + 1, place % 2
     )
     second_scale = second_scale[:, :1]
-    proj_up = up_gather.whole_weight()
-    hidden, pull = ffn_forward(second_normed, proj_up)
+    hidden, pull, proj_gate, proj_up = up_gather.ffn_forward(second_normed)
 
     grad_out = cotangent.reshape(row_count, D)
     grad_down = dot_rows(hidden, grad_out).astype(BF16)
-    down_part = lax.psum_scatter(grad_down, "seq", scatter_dimension=0, tiled=True)
+    down_sum = lax.psum_scatter(grad_down, "seq", scatter_dimension=0, tiled=True)
+    down_sum = lax.psum(down_sum, "grp")
     grad_expanded = ffn_backward(tie(grad_out, grad_down), proj_down, pull)
     quarter = FF // 2
 
@@ -878,8 +953,8 @@
 
     up_sum = Reduction(second_own, second_far, up_columns, quarter)
     grad_expanded = tie(grad_expanded, *up_sum.sent)
-    grad_second_normed = dot_far(grad_expanded[0], proj_up[:, :FF]) + dot_far(
-        grad_expanded[1], proj_up[:, FF:]
+    grad_second_normed = dot_far(grad_expanded[0], proj_gate) + dot_far(
+        grad_expanded[1], proj_up
     )
     sent = up_sum.second(grad_second_normed)
     grad_second_normed = tie(grad_second_normed, *sent)
@@ -901,8 +976,7 @@
     head_pull, head_prod = chunk_ends(rev_chunks, True)
     grad_gate = grad_gate.reshape(row_count, LRU)
     width = LRU // 4
-    sent = (*out_sum.second(head_pull), *up_sum.third(head_pull, down_part, offload=True))
-    grad_gate = tie(grad_gate, *sent)
+    grad_gate = tie(grad_gate, *out_sum.second(head_pull))
     in_gate_sum = Reduction(
         first_own,
         first_far,
@@ -911,15 +985,15 @@
     )
     rev_carry = shard_carry(head_pull, head_prod, True)
     rev_carries = chunk_carries(rev_chunks, rev_carry, True)
-    local = tie(local, *in_gate_sum.sent)
+    sent = up_sum.third(rev_carry, down_sum, *in_gate_sum.sent, offload=True)
+    local = tie(local, *in_gate_sum.sent, *sent)
     du, tail, edge, grad_gates, grad_taps, grad_decay = mixer_backward(
         local, rev_prod, rev_carries, state, carries, conv_low, inner_low,
         prev_inner, dist, gates_all, taps_all, soft,
     )
     returned = from_behind(edge[:, HALO - edge_len :].astype(BF16), "seq", -1).astype(F32)
-    sent = (*out_sum.third(edge), *in_gate_sum.second(edge))
-    gate_gate = tie(grad_gate, *sent)
-    first_grad = dot_far(gate_gate, proj_in[:, LRU:])
+    grad_gate = tie(grad_gate, *out_sum.third(edge), *in_gate_sum.second(edge))
+    first_grad = dot_far(grad_gate, proj_in[:, LRU:])
     groups = TAIL // CHUNKS
     padded = jnp.pad(
         returned[:, :, None, :], ((0, 0), (groups - edge_len, 0), (CHUNKS - 1, 0), (0, 0))
@@ -934,8 +1008,7 @@
         lambda n: lax.dynamic_slice_in_dim(grad_inner, n * width, width, 1),
         width,
     )
-    grad_inner = tie(grad_inner, *in_value_sum.sent, *in_gate_sum.third())
-    first_grad = first_grad + dot_far(grad_inner, proj_in[:, :LRU])
+    grad_inner = tie(grad_inner, *in_value_sum.sent)
 
     shards = last + 1
     grad_decay_row = grad_decay[0] * jax.nn.sigmoid(-decay_float)
@@ -951,20 +1024,32 @@
     whole = 16 * lax.axis_size("grp")
     flat = jnp.pad(flat, ((0, 0), (0, -lines % whole), (0, 0))).astype(BF16).reshape(-1, HS)
     flat = lax.psum_scatter(flat, ("seq", "grp"), scatter_dimension=0, tiled=True)
-    flat = lax.all_gather(flat, "grp", axis=0, tiled=True)
+    flat, (out_total,) = gather_parts(flat, [out_sum])
     flat = flat[:lines].astype(F32).reshape(-1)
     n_gates = flat.shape[0] - (CONV + 1) * n_lru
     gates_total = flat[:n_gates].reshape(gate_heads.shape)
     taps_total = flat[n_gates : n_gates + CONV * n_lru].reshape(CONV, n_lru)
     decay_total = flat[n_gates + CONV * n_lru :]
 
-    sent = in_value_sum.second(first_grad)
-    out_total = out_sum.finish()
+    first_grad = first_grad + dot_far(grad_inner, proj_in[:, :LRU])
+    sent = in_value_sum.second(first_grad, up_sum.arrived)
     up_total = up_sum.finish(edge)
-    down_part = lax.psum_scatter(tie(down_part, up_total), "grp", scatter_dimension=0, tiled=True)
-    down_total = lax.all_gather(down_part, "grp", axis=0, tiled=True).astype(F32)
-    in_value_sum.third()
-    in_total = jnp.concatenate([in_value_sum.finish(), in_gate_sum.finish()], axis=1)
+    down_total = down_sum.astype(F32)
+    if in_value_sum.simple:
+        in_total = jnp.concatenate([in_value_sum.finish(), in_gate_sum.finish()], axis=1)
+    else:
+        both = jnp.concatenate([in_value_sum.mine(), in_gate_sum.mine()], axis=1)
+        in_value_sum.along_z(both)
+        both = in_value_sum.total().astype(BF16)
+        in_total = jnp.concatenate(
+            [
+                lax.all_gather(both[:, n * width : (n + 1) * width], "grp")
+                .transpose(1, 0, 2)
+                .reshape(-1, LRU)
+                for n in range(2)
+            ],
+            axis=1,
+        ).astype(F32)
     ffn_out = jnp.dot(tie(hidden, *sent), proj_down, preferred_element_type=F32)
     block_out = by_token((resid + ffn_out).astype(BF16).reshape(tokens.shape))
     grad_tokens = grad_resid + norm_back(inputs, first_scale, gain_one, first_grad)

time: 1800 us -> 1080 us (0.60)
  Pallas kernels: 1000 us -> 183 us
  waiting for transfers between devices: 120 us -> 331 us
  blocking collectives: 195 us -> 95.2 us
    pallas_call x2 -> x1, Pallas kernels: 857 us -> 39.9 us  [ffn_forward(): pl.pallas_call(gathered_ffn_kernel, grid=(FF // tile,), in_specs=[pl.Bloc...]
    ppermute x3, waiting for transfers between devices: 0.01 us -> 116 us  [from_behind(): lax.ppermute(value, axis, [(source, source + steps) for source in range(f...]
    all_gather x1, blocking collectives: 121 us -> 12.2 us  [body(): small_all = lax.all_gather(small, 'seq')]
    ppermute x4, waiting for transfers between devices: 0.01 us -> 63.1 us  [__init__(): self.diag_a = lax.ppermute(self.sent[0], 'grp', self.x)]
    reduce_scatter x1, waiting for transfers between devices: 0.01 us -> 52.2 us  [third(): lax.psum_scatter(mine, 'seq', scatter_dimension=0, axis_index_groups=core...]
    all_gather x1, waiting for transfers between devices: 49.5 us -> 0.01 us  [finish(): parts = lax.all_gather(total.astype(BF16), 'grp')]
    psum x0 -> x1, waiting for transfers between devices: none -> 47.8 us  [body(): down_sum = lax.psum(down_sum, 'grp')]
    ppermute x4, waiting for transfers between devices: 29.5 us -> 3.07 us  [second(): self.from_x = lax.ppermute(sent[0], 'grp', self.x)]
  transfers between devices with their start and end apart: 67 -> 63, of which waited for: 12 -> 16; matrix products, arithmetic and copies ran while one was open for 19% -> 32% of each run, Pallas kernels for 56% -> 13%
where the time goes in v6:
time: 1080 us; the launch traced here: 1070 us
  waiting for transfers between devices  331 us (31%)
  matrix products  280 us (26%)
  Pallas kernels  183 us (17%)
  blocking collectives  95.2 us (9%)
  local copies, waits for them, and re-layouts  87.1 us (8%)
  starting transfers between devices  42.6 us (4%)
  other arithmetic  35.4 us (3%)
  between operations  15.7 us (1%)
    dot_general x37, matrix products, dot_rows(): lax.dot_general(a, b, (((0,), (0,)), ((), ())), preferred_element_type=F32)  151 us
    ppermute x3, waiting for transfers between devices, from_behind(): lax.ppermute(value, axis, [(source, source + steps) for source in range(f...  116 us
    dot_general x5, matrix products, dot_far(): lax.dot_general(a, b, (((1,), (1,)), ((), ())), preferred_element_type=F32)  77.3 us
    ppermute x4, waiting for transfers between devices, __init__(): self.diag_a = lax.ppermute(self.sent[0], 'grp', self.x)  63.1 us
    reduce_scatter x1, waiting for transfers between devices, third(): lax.psum_scatter(mine, 'seq', scatter_dimension=0, axis_index_groups=core...  52.2 us
    psum x1, waiting for transfers between devices, body(): down_sum = lax.psum(down_sum, 'grp')  47.8 us
    pallas_call x1, Pallas kernels, mixer_backward(): pl.pallas_call(mixer_backward_kernel, grid=(HEADS,), in_specs=[full, full...  46.7 us
    unnamed x191, local copies, waits for them, and re-layouts  46.2 us
  transfers between devices with their start and end apart: 63, of which 16 were waited for; matrix products, arithmetic and copies ran while one was open for 32% of the time, Pallas kernels for 13%

profile of v6, /device:TPU:18, one launch (start us, length us, event | category | flops | bytes accessed | tf_op | source)
XLA Modules:
  0.0 1070.6 jit_solution(14160300521290822279)
XLA Ops:
  12.8 12.2 %all-gather.7 = bf16[8,1,1664]{2,1,0:T(2,128)(2,1)S(1)} all-gather(bf16[1,1,1664]{2,1,0:T(2,128)(2,1)S(1)} %reshape.2483), channel_id=2, replica_groups=mesh['grp'=4,'seq'=8] {'seq'}, dimensions={0}, use_global_device_ids=true | all-gather | bytes 29952 | tf_op jit(solution)/shard_map/all_gather | solution.py:884
  46.4 5.3 copy.336
  52.3 115.5 %collective-permute-done.4 = s32[2,3]{1,0:T(2,128)S(1)} collective-permute-done((s32[2,3]{1,0:T(2,128)S(1)}, s32[2,3]{1,0:T(2,128)S(1)}, u32[]{:S(2)}, u32[]{:S(2)}) %collective-permute-start.4) | collective-permute-done | bytes 56 | tf_op jit(solution)/shard_map/ppermute | solution.py:27
  176.5 9.8 fusion.63
  190.9 4.4 all-gather.16.cloned.1.call-done.gates_ref
  198.9 28.0 %mixer_forward.1 = (bf16[2,512,2048]{2,1,0:T(8,128)(2,1)S(1)}, f32[2,512,2048]{2,1,0:T(8,128)}, f32[2,512,2048]{2,1,0:T(8,128)}, f32[2,512,2048]{2,1,0:T(8,128)}, f32[2,2,8,2048]{3,2,1,0:T(8,128)S(1)}) custom-call(bf16[2,512,2048]{2,1,0:T(8,128)(2,1)S(1)} %bitcast.790, bf16[2,8,2048]{2,1,0:T(8,128)(2,1)S(1)} %collective-permute-done.3.halo_ref, ...), custom_call_target="tpu_custom_call" | custom-call | tf_op jit(solution)/shard_map/mixer_forward/pallas_call | solution.py:322
  229.4 13.7 %all-gather.1 = f32[16,2,2048]{2,1,0:T(2,128)S(1)} all-gather(f32[2,2,2048]{2,1,0:T(2,128)S(1)} %copy.321), channel_id=3, replica_groups=mesh['grp'=4,'seq'=8] {'seq'}, dimensions={0}, use_global_device_ids=true | all-gather | bytes 294912 | tf_op jit(solution)/shard_map/all_gather | solution.py:833
  248.5 11.2 %fusion.13 = f32[1024,2048]{1,0:T(8,128)} fusion(bf16[1024,1536]{1,0:T(8,128)(2,1)S(1)} %copy-done.37, bf16[1536,4096]{1,0:T(8,128)(2,1)} %all-gather.14.cloned.1.call-done), kind=kOutput, calls=%fused_computation.25 | convolution fusion | flops 6442450944 | bytes 17825792 | tf_op jit(solution)/shard_map/dot_general | solution.py:925
  259.6 17.3 %mixer_branch.1 = (f32[2,512,2048]{2,1,0:T(8,128)}, bf16[2,512,2048]{2,1,0:T(8,128)(2,1)S(1)}, bf16[2,2,512,1024]{3,2,1,0:T(8,128)(2,1)S(1)}) custom-call(s32[1]{0:T(128)} %bitcast.3.core_ref, f32[2,512,2048]{2,1,0:T(8,128)} %get-tuple-element.76.state_ref, f32[2,512,2048]{2,1,0:T(8,128)} %get-tuple-element.77.prod_ref, ...), custom_call_target="tpu_custom_call" | custom-call | tf_op jit(solution)/shard_map/mixer_branch/pallas_call | solution.py:364
  281.0 9.1 collective-permute-done.8.refs_5_
  290.6 10.1 convert_add_fusion.x_ref
  308.1 39.9 %gathered_ffn.1 = (bf16[1024,4608]{1,0:T(8,128)(2,1)}, bf16[2,1024,4608]{2,1,0:T(8,128)(2,1)}, bf16[1536,4608]{1,0:T(8,128)(2,1)}, bf16[1536,4608]{1,0:T(8,128)(2,1)}) custom-call(s32[3]{0:T(128)} %pad_add_fusion.1.where_ref, bf16[1024,1536]{1,0:T(8,128)(2,1)} %copy-done.16, bf16[192,9216]{1,0:T(8,128)(2,1)} %refs_0_.1, ...), custom_call_target="tpu_custom_call" | custom-call | tf_op jit(solution)/shard_map/gathered_ffn/pallas_call | solution.py:672
  348.0 21.5 %convolution_convert_fusion = bf16[4608,1536]{1,0:T(8,128)(2,1)} fusion(bf16[1024,4608]{1,0:T(8,128)(2,1)} %get-tuple-element.121, bf16[1024,1536]{1,0:T(8,128)(2,1)S(1)} %bitcast.786), kind=kOutput, calls=%fused_computation | convolution fusion | flops 14502592512 | bytes 26738688 | tf_op jit(solution)/shard_map/dot_general | solution.py:541
  369.7 17.9 %all-gather.20.cloned.1.call-done.down_ref = bf16[4608,1536]{1,0:T(8,128)(2,1)} async-done(((bf16[144,1536]{1,0:T(8,128)(2,1)}), bf16[4608,1536]{1,0:T(8,128)(2,1)}) %all-gather.20.cloned.1.call-update) | async-done | bytes 14155792 | tf_op jit(solution)/shard_map/all_gather | solution.py:524
  387.6 25.1 %ffn_backward.1 = bf16[2,1024,4608]{2,1,0:T(8,128)(2,1)} custom-call(bf16[1024,1536]{1,0:T(8,128)(2,1)S(1)} %bitcast.787, bf16[4608,1536]{1,0:T(8,128)(2,1)} %all-gather.20.cloned.1.call-done.down_ref, bf16[2,1024,4608]{2,1,0:T(8,128)(2,1)} %get-tuple-element.84.pull_ref), custom_call_target="tpu_custom_call" | custom-call | tf_op jit(solution)/shard_map/ffn_backward/pallas_call | solution.py:505
  412.7 7.6 convolution_convert_fusion.4
  424.9 4.8 fusion.308
  429.7 7.8 convolution_convert_fusion.2
  439.0 5.8 convolution_convert_fusion.3
  444.9 4.8 fusion.54
  450.1 4.9 fusion.51
  456.5 21.8 %fusion = f32[1024,1536]{1,0:T(8,128)} fusion(bf16[1536,4608]{1,0:T(8,128)(2,1)} %get-tuple-element.89, bf16[2,1024,4608]{2,1,0:T(8,128)(2,1)} %ffn_backward.1), kind=kOutput, calls=%fused_computation.4 | convolution fusion | flops 14495514624 | bytes 29884416 | tf_op jit(solution)/shard_map/dot_general | solution.py:551
  478.3 22.5 %fusion.33 = f32[1024,1536]{1,0:T(8,128)} fusion(f32[1024,1536]{1,0:T(8,128)} %fusion, bf16[1536,4608]{1,0:T(8,128)(2,1)} %get-tuple-element.88, bf16[2,1024,4608]{2,1,0:T(8,128)(2,1)} %ffn_backward.1), kind=kOutput, calls=%fused_computation.49 | convolution fusion | flops 14497087488 | bytes 36175872 | tf_op jit(solution)/shard_map/dot_general | solution.py:551
  500.8 9.5 add_convert_fusion.1
  510.4 9.5 add_convert_fusion.2
  520.6 3.9 fusion.301
  525.9 7.7 convolution_convert_fusion.1
  543.6 9.1 fusion.313
  552.7 22.0 %mixer_reverse.1 = (bf16[2,512,2048]{2,1,0:T(8,128)(2,1)S(1)}, f32[2,512,2048]{2,1,0:T(8,128)S(1)}, f32[2,512,2048]{2,1,0:T(8,128)}, f32[2,2,8,2048]{3,2,1,0:T(8,128)S(1)}) custom-call(f32[2,512,2048]{2,1,0:T(8,128)} %bitcast.823, f32[2,512,2048]{2,1,0:T(8,128)} %bitcast.815, f32[2,512,2048]{2,1,0:T(8,128)} %get-tuple-element.95.keep_ref, ...), custom_call_target="tpu_custom_call" | custom-call | tf_op jit(solution)/shard_map/mixer_reverse/pallas_call | solution.py:386
  580.2 41.1 %collective-permute-done.22 = bf16[512,384]{1,0:T(8,128)(2,1)S(1)} collective-permute-done((bf16[512,384]{1,0:T(8,128)(2,1)S(1)}, bf16[512,384]{1,0:T(8,128)(2,1)S(1)}, u32[]{:S(2)}, u32[]{:S(2)}) %collective-permute-start.22) | collective-permute-done | bytes 393248 | tf_op jit(solution)/shard_map/ppermute | solution.py:739
  621.9 15.1 %all-gather.2 = f32[16,2,2048]{2,1,0:T(2,128)} all-gather(f32[2,2,2048]{2,1,0:T(2,128)S(1)} %copy.353), channel_id=4, replica_groups=mesh['grp'=4,'seq'=8] {'seq'}, dimensions={0}, use_global_device_ids=true | all-gather | bytes 294912 | tf_op jit(solution)/shard_map/all_gather | solution.py:833
  639.4 4.4 add_convert_fusion.12
  656.0 47.8 %all-reduce.12.cloned.1.call-done = bf16[576,1536]{1,0:T(8,128)(2,1)} async-done(((bf16[576,1536]{1,0:T(8,128)(2,1)}), bf16[576,1536]{1,0:T(8,128)(2,1)}) %all-reduce.12.cloned.1.call-update) | async-done | bytes 1769488 | tf_op jit(solution)/shard_map/psum | solution.py:944
  703.8 11.7 %add_convert_fusion = bf16[768,2304]{1,0:T(8,128)(2,1)} fusion(bf16[768,2304]{1,0:T(8,128)(2,1)} %collective-permute-done.28, bf16[768,2304]{1,0:T(8,128)(2,1)} %collective-permute-done.27, bf16[768,2304]{1,0:T(8,128)(2,1)} %collective-permute-done.26, bf16[1024,768]{1,0:T(8,128)(2,1)S(1)} %copy-done.20, bf16[2,1024,4608]{2,1,0:T(8,128)(2,1)} %ffn_backward.1, ...), kind=kOutput, calls=%fused_computation.12 | convolution fusion | flops 3636264960 | bytes 20447240 | tf_op jit(solution)/shard_map/dot_general | solution.py:541
  717.7 46.7 %mixer_backward.1 = (bf16[2,512,2048]{2,1,0:T(8,128)(2,1)S(1)}, f32[2,32,2048]{2,1,0:T(8,128)S(1)}, f32[2,8,2048]{2,1,0:T(8,128)S(1)}, f32[16,128,256]{2,1,0:T(8...) custom-call(f32[2,512,2048]{2,1,0:T(8,128)} %copy-done.8, f32[2,512,2048]{2,1,0:T(8,128)} %get-tuple-element.106.prod_ref, ...), custom_call_target="tpu_custom_call" | custom-call | tf_op jit(solution)/shard_map/mixer_backward/pallas_call | solution.py:408
  771.3 4.1 convolution_convert_fusion.13
  775.4 3.7 fusion.128
  785.5 22.0 %collective-permute-done.34 = bf16[384,512]{1,0:T(8,128)(2,1)S(1)} collective-permute-done((bf16[384,512]{1,0:T(8,128)(2,1)S(1)}, bf16[384,512]{1,0:T(8,128)(2,1)S(1)}, u32[]{:S(2)}, u32[]{:S(2)}) %collective-permute-start.34) | collective-permute-done | bytes 393248 | tf_op jit(solution)/shard_map/ppermute | solution.py:739
  812.2 6.0 collective-permute-done.35
  833.3 10.9 %fusion.11 = f32[1024,1536]{1,0:T(8,128)} fusion(bf16[1024,2048]{1,0:T(8,128)(2,1)S(1)} %bitcast.802, bf16[1536,4096]{1,0:T(8,128)(2,1)} %all-gather.14.cloned.1.call-done), kind=kOutput, calls=%fused_computation.23 | convolution fusion | flops 6442450944 | bytes 16777216 | tf_op jit(solution)/shard_map/dot_general | solution.py:551
  857.3 3.8 collective-permute-done.51
  871.7 13.0 %fusion.10 = (f32[1024]{0:T(1024)S(1)}, f32[1024,1536]{1,0:T(8,128)}) fusion(f32[1536]{0:T(1024)S(1)} %copy-done.60, bf16[2,8,64,1536]{3,1,2,0:T(8,128)(2,1)S(1)} %copy-done.4, f32[1024,1536]{1,0:T(8,128)} %fusion.11, bf16[1024,2048]{1,0:T(8,128)(2,1)S(1)} %bitcast.810, bf16[1536,4096]{1,0:T(8,128)(2,1)} %all-gather.14.cloned.1.call-done), kind=kOutput, calls=%fused_computation.19 | convolution fusion | flops 6450314240 | bytes 26224640 | tf_op jit(solution)/shard_map/dot_general | solution.py:551
  884.8 3.8 fusion.9
  892.0 52.2 %reduce-scatter.6.cloned.1.call-done = bf16[192,2304]{1,0:T(8,128)(2,1)} async-done(((bf16[768,2304]{1,0:T(8,128)(2,1)}), bf16[192,2304]{1,0:T(8,128)(2,1)}) %reduce-scatter.6.cloned.1.call-update) | async-done | bytes 884752 | tf_op jit(solution)/shard_map/reduce_scatter | solution.py:789
  953.1 26.5 %all-gather.5 = bf16[3648,128]{1,0:T(8,128)(2,1)S(1)} all-gather(bf16[912,128]{1,0:T(8,128)(2,1)S(1)} %pad_maximum_fusion.1), channel_id=7, replica_groups=mesh['grp'=4,'seq'=8] {'grp'}, dimensions={0}, use_global_device_ids=true | all-gather | bytes 1167360 | tf_op jit(solution)/shard_map/all_gather | solution.py:819
  995.9 21.1 %add_convert_fusion.3 = bf16[1024,1536]{1,0:T(8,128)(2,1)S(1)} fusion(f32[1024,1536]{1,0:T(8,128)S(1)} %bitcast.783, bf16[1024,4608]{1,0:T(8,128)(2,1)} %get-tuple-element.121, bf16[4608,1536]{1,0:T(8,128)(2,1)} %all-gather.20.cloned.1.call-done.down_ref), kind=kOutput, calls=%fused_computation.20 | convolution fusion | flops 14498660352 | bytes 33030144 | tf_op jit(solution)/shard_map/dot_general | solution.py:1053
  1025.0 17.3 %all-gather.3 = bf16[768,512]{1,0:T(8,128)(2,1)S(1)} all-gather(bf16[192,512]{1,0:T(8,128)(2,1)S(1)} %get-tuple-element.203), channel_id=5, replica_groups=mesh['grp'=4,'seq'=8] {'grp'}, dimensions={0}, use_global_device_ids=true | all-gather | bytes 983040 | tf_op jit(solution)/shard_map/all_gather | solution.py:1046
  1043.2 10.3 all-gather.4
  (438 shorter events, 210.8 us)
Async XLA Ops:
  7.2 169.3 %all-gather.14.cloned.1.call-start = ((), (), s32[]{:S(2)}) async-start(), calls=%async_computation.3 | async-start | bytes 12976128 | tf_op jit(solution)/shard_map/all_gather | solution.py:524
  9.2 186.1 %all-gather.16.cloned.1.call-start = ((), (), s32[]{:S(2)}) async-start(), calls=%async_computation.4 | async-start | bytes 1179648 | tf_op jit(solution)/shard_map/all_gather | solution.py:893
  9.9 280.6 %all-gather.18.cloned.1.call-start = ((), (), s32[]{:S(2)}) async-start(), calls=%async_computation.5 | async-start | bytes 6488064 | tf_op jit(solution)/shard_map/all_gather | solution.py:524
  11.6 376.0 %all-gather.20.cloned.1.call-start = ((), (), s32[]{:S(2)}) async-start(), calls=%async_computation.6 | async-start | bytes 14598144 | tf_op jit(solution)/shard_map/all_gather | solution.py:524
  12.5 626.8 %reduce-scatter.4.cloned.1.call-start = ((), (), s32[]{:S(2)}) async-start(), calls=%async_computation.7 | async-start | bytes 15925248 | tf_op jit(solution)/shard_map/reduce_scatter | solution.py:943
  12.6 235.3 %collective-permute-start.9 = (bf16[192,9216]{1,0:T(8,128)(2,1)}, bf16[192,9216]{1,0:T(8,128)(2,1)}, u32[]{:S(2)}, u32[]{:S(2)}) collective-permute-start(bf16[192,9216]{1,0:T(8,128)(2,1)} %refs_0_.1), channel_id=1, source_target_pairs={{0,1},{1,0},{2,3},{3,2},{4,5},{5,4},{6,7},{7,6},{8,9},{9,8},{10,11... | collective-permute-start | bytes 10616840 | tf_op jit(solution)/shard_map/ppermute | solution.py:666
  37.9 134.4 %collective-permute-start.2 = (bf16[192,2304]{1,0:T(8,128)(2,1)}, bf16[192,2304]{1,0:T(8,128)(2,1)}, u32[]{:S(2)}, u32[]{:S(2)}) collective-permute-start(bf16[192,2304]{1,0:T(8,128)(2,1)} %constant_dynamic-slice_fusion.2), channel_id=1, source_target_pairs={{0,6},{1,7},{2,0},{3,1},{4,2},{5,3},{6,4},{7,5},{8,14},{9,15},{10,... | collective-permute-start | bytes 2654216 | tf_op jit(solution)/shard_map/ppermute | solution.py:641
  40.3 129.9 %collective-permute-start.1 = (bf16[192,2304]{1,0:T(8,128)(2,1)}, bf16[192,2304]{1,0:T(8,128)(2,1)}, u32[]{:S(2)}, u32[]{:S(2)}) collective-permute-start(bf16[192,2304]{1,0:T(8,128)(2,1)} %constant_dynamic-slice_fusion.2), channel_id=1, source_target_pairs={{0,4},{1,5},{2,6},{3,7},{4,0},{5,1},{6,2},{7,3},{8,12},{9,13},{10,... | collective-permute-start | bytes 2654216 | tf_op jit(solution)/shard_map/ppermute | solution.py:641
  43.6 124.4 %collective-permute-start = (bf16[192,2304]{1,0:T(8,128)(2,1)}, bf16[192,2304]{1,0:T(8,128)(2,1)}, u32[]{:S(2)}, u32[]{:S(2)}) collective-permute-start(bf16[192,2304]{1,0:T(8,128)(2,1)} %constant_dynamic-slice_fusion.2), channel_id=1, source_target_pairs={{0,2},{1,3},{2,4},{3,5},{4,6},{5,7},{6,0},{7,1},{8,10},{9,11},{10,... | collective-permute-start | bytes 2654216 | tf_op jit(solution)/shard_map/ppermute | solution.py:641
  43.7 124.1 %collective-permute-start.4 = (s32[2,3]{1,0:T(2,128)S(1)}, s32[2,3]{1,0:T(2,128)S(1)}, u32[]{:S(2)}, u32[]{:S(2)}) collective-permute-start(s32[2,3]{1,0:T(2,128)S(1)} %slice.381), channel_id=1, source_target_pairs={{0,1},{1,2},{2,3},{3,4},{4,5},{5,6},{6,7},{8,9},{9,10},{10,11},{11... | collective-permute-start | bytes 80 | tf_op jit(solution)/shard_map/ppermute | solution.py:27
  174.5 69.2 %collective-permute-start.6 = (bf16[576,2304]{1,0:T(8,128)(2,1)}, bf16[576,2304]{1,0:T(8,128)(2,1)}, u32[]{:S(2)}, u32[]{:S(2)}) collective-permute-start(bf16[576,2304]{1,0:T(8,128)(2,1)} %constant_dynamic-update-slice_fusion.refs_1_), channel_id=1, source_target_pairs={{0,16},{8,24},{16,0},{24,8},{1,17},{9,25},{17,1},{25,9},{2,18},{10... | collective-permute-start | bytes 7962632 | tf_op jit(solution)/shard_map/ppermute | solution.py:649
  176.0 67.8 %collective-permute-start.5 = (bf16[576,2304]{1,0:T(8,128)(2,1)}, bf16[576,2304]{1,0:T(8,128)(2,1)}, u32[]{:S(2)}, u32[]{:S(2)}) collective-permute-start(bf16[576,2304]{1,0:T(8,128)(2,1)} %constant_dynamic-update-slice_fusion.refs_1_), channel_id=1, source_target_pairs={{0,8},{8,0},{16,24},{24,16},{1,9},{9,1},{17,25},{25,17},{2,10},{10... | collective-permute-start | bytes 7962632 | tf_op jit(solution)/shard_map/ppermute | solution.py:648
  190.8 116.5 %collective-permute-start.10 = (bf16[576,2304]{1,0:T(8,128)(2,1)}, bf16[576,2304]{1,0:T(8,128)(2,1)}, u32[]{:S(2)}, u32[]{:S(2)}) collective-permute-start(bf16[576,2304]{1,0:T(8,128)(2,1)} %constant_dynamic-update-slice_fusion.refs_1_), channel_id=1, source_target_pairs={{0,1},{1,0},{2,3},{3,2},{4,5},{5,4},{6,7},{7,6},{8,9},{9,8},{10,11... | collective-permute-start | bytes 7962632 | tf_op jit(solution)/shard_map/ppermute | solution.py:666
  245.3 62.1 %collective-permute-start.12 = (bf16[576,2304]{1,0:T(8,128)(2,1)}, bf16[576,2304]{1,0:T(8,128)(2,1)}, u32[]{:S(2)}, u32[]{:S(2)}) collective-permute-start(bf16[576,2304]{1,0:T(8,128)(2,1)} %collective-permute-done.6.refs_3_), channel_id=1, source_target_pairs={{0,1},{1,0},{2,3},{3,2},{4,5},{5,4},{6,7},{7,6},{8,9},{9,8},{10,11... | collective-permute-start | bytes 7962632 | tf_op jit(solution)/shard_map/ppermute | solution.py:666
  247.1 60.3 %collective-permute-start.11 = (bf16[576,2304]{1,0:T(8,128)(2,1)}, bf16[576,2304]{1,0:T(8,128)(2,1)}, u32[]{:S(2)}, u32[]{:S(2)}) collective-permute-start(bf16[576,2304]{1,0:T(8,128)(2,1)} %collective-permute-done.5.refs_2_), channel_id=1, source_target_pairs={{0,1},{1,0},{2,3},{3,2},{4,5},{5,4},{6,7},{7,6},{8,9},{9,8},{10,11... | collective-permute-start | bytes 7962632 | tf_op jit(solution)/shard_map/ppermute | solution.py:666
  247.3 42.7 %collective-permute-start.8 = (bf16[288,2304]{1,0:T(8,128)(2,1)S(1)}, bf16[288,2304]{1,0:T(8,128)(2,1)}, u32[]{:S(2)}, u32[]{:S(2)}) collective-permute-start(bf16[288,2304]{1,0:T(8,128)(2,1)S(1)} %slice.418), channel_id=1, source_target_pairs={{0,16},{8,24},{16,0},{24,8},{1,17},{9,25},{17,1},{25,9},{2,18},{10... | collective-permute-start | bytes 3981320 | tf_op jit(solution)/shard_map/ppermute | solution.py:664
  247.9 42.2 %collective-permute-start.7 = (bf16[288,2304]{1,0:T(8,128)(2,1)S(1)}, bf16[288,2304]{1,0:T(8,128)(2,1)}, u32[]{:S(2)}, u32[]{:S(2)}) collective-permute-start(bf16[288,2304]{1,0:T(8,128)(2,1)S(1)} %slice.417), channel_id=1, source_target_pairs={{0,8},{8,0},{16,24},{24,16},{1,9},{9,1},{17,25},{25,17},{2,10},{10... | collective-permute-start | bytes 3981320 | tf_op jit(solution)/shard_map/ppermute | solution.py:663
  369.6 334.2 %all-reduce.12.cloned.1.call-start = ((), (), s32[]{:S(2)}) async-start(), calls=%async_computation.8 | async-start | bytes 3538944 | tf_op jit(solution)/shard_map/psum | solution.py:944
  437.5 63.3 %collective-permute-start.19 = (bf16[768,2304]{1,0:T(8,128)(2,1)}, bf16[768,2304]{1,0:T(8,128)(2,1)}, u32[]{:S(2)}, u32[]{:S(2)}) collective-permute-start(bf16[768,2304]{1,0:T(8,128)(2,1)} %convolution_convert_fusion.2), channel_id=1, source_target_pairs={{0,1},{1,0},{2,3},{3,2},{4,5},{5,4},{6,7},{7,6},{8,9},{9,8},{10,11... | collective-permute-start | bytes 10616840 | tf_op jit(solution)/shard_map/ppermute | solution.py:733
  444.7 65.6 %collective-permute-start.16 = (bf16[768,2304]{1,0:T(8,128)(2,1)}, bf16[768,2304]{1,0:T(8,128)(2,1)}, u32[]{:S(2)}, u32[]{:S(2)}) collective-permute-start(bf16[768,2304]{1,0:T(8,128)(2,1)} %convolution_convert_fusion.3), channel_id=1, source_target_pairs={{0,1},{1,0},{2,3},{3,2},{4,5},{5,4},{6,7},{7,6},{8,9},{9,8},{10,11... | collective-permute-start | bytes 10616840 | tf_op jit(solution)/shard_map/ppermute | solution.py:733
  449.7 51.1 %collective-permute-start.17 = (bf16[384,2304]{1,0:T(8,128)(2,1)}, bf16[384,2304]{1,0:T(8,128)(2,1)}, u32[]{:S(2)}, u32[]{:S(2)}) collective-permute-start(bf16[384,2304]{1,0:T(8,128)(2,1)} %fusion.54), channel_id=1, source_target_pairs={{0,8},{8,0},{16,24},{24,16},{1,9},{9,1},{17,25},{25,17},{2,10},{10... | collective-permute-start | bytes 5308424 | tf_op jit(solution)/shard_map/ppermute | solution.py:739
  455.0 45.8 %collective-permute-start.18 = (bf16[384,2304]{1,0:T(8,128)(2,1)}, bf16[384,2304]{1,0:T(8,128)(2,1)S(1)}, u32[]{:S(2)}, u32[]{:S(2)}) collective-permute-start(bf16[384,2304]{1,0:T(8,128)(2,1)} %fusion.51), channel_id=1, source_target_pairs={{0,16},{8,24},{16,0},{24,8},{1,17},{9,25},{17,1},{25,9},{2,18},{10... | collective-permute-start | bytes 5308424 | tf_op jit(solution)/shard_map/ppermute | solution.py:740
  533.6 170.2 %collective-permute-start.26 = (bf16[768,2304]{1,0:T(8,128)(2,1)}, bf16[768,2304]{1,0:T(8,128)(2,1)}, u32[]{:S(2)}, u32[]{:S(2)}) collective-permute-start(bf16[768,2304]{1,0:T(8,128)(2,1)} %convolution_convert_fusion.1), channel_id=1, source_target_pairs={{0,1},{1,0},{2,3},{3,2},{4,5},{5,4},{6,7},{7,6},{8,9},{9,8},{10,11... | collective-permute-start | bytes 10616840 | tf_op jit(solution)/shard_map/ppermute | solution.py:733
  534.2 121.8 %collective-permute-start.27 = (bf16[768,2304]{1,0:T(8,128)(2,1)}, bf16[768,2304]{1,0:T(8,128)(2,1)}, u32[]{:S(2)}, u32[]{:S(2)}) collective-permute-start(bf16[768,2304]{1,0:T(8,128)(2,1)} %add_convert_fusion.2), channel_id=1, source_target_pairs={{0,8},{8,0},{16,24},{24,16},{1,9},{9,1},{17,25},{25,17},{2,10},{10... | collective-permute-start | bytes 10616840 | tf_op jit(solution)/shard_map/ppermute | solution.py:757
  534.7 121.2 %collective-permute-start.28 = (bf16[768,2304]{1,0:T(8,128)(2,1)}, bf16[768,2304]{1,0:T(8,128)(2,1)}, u32[]{:S(2)}, u32[]{:S(2)}) collective-permute-start(bf16[768,2304]{1,0:T(8,128)(2,1)} %add_convert_fusion.1), channel_id=1, source_target_pairs={{0,16},{8,24},{16,0},{24,8},{1,17},{9,25},{17,1},{25,9},{2,18},{10... | collective-permute-start | bytes 10616840 | tf_op jit(solution)/shard_map/ppermute | solution.py:758
  540.7 80.5 %collective-permute-start.22 = (bf16[512,384]{1,0:T(8,128)(2,1)S(1)}, bf16[512,384]{1,0:T(8,128)(2,1)S(1)}, u32[]{:S(2)}, u32[]{:S(2)}) collective-permute-start(bf16[512,384]{1,0:T(8,128)(2,1)S(1)} %add_convert_fusion.16), channel_id=1, source_target_pairs={{0,8},{8,0},{16,24},{24,16},{1,9},{9,1},{17,25},{25,17},{2,10},{10... | collective-permute-start | bytes 1179656 | tf_op jit(solution)/shard_map/ppermute | solution.py:739
  542.2 79.3 %collective-permute-start.23 = (bf16[512,384]{1,0:T(8,128)(2,1)S(1)}, bf16[512,384]{1,0:T(8,128)(2,1)S(1)}, u32[]{:S(2)}, u32[]{:S(2)}) collective-permute-start(bf16[512,384]{1,0:T(8,128)(2,1)S(1)} %add_convert_fusion.15), channel_id=1, source_target_pairs={{0,16},{8,24},{16,0},{24,8},{1,17},{9,25},{17,1},{25,9},{2,18},{10... | collective-permute-start | bytes 1179656 | tf_op jit(solution)/shard_map/ppermute | solution.py:740
  639.4 251.8 %reduce-scatter.8.cloned.1.call-start = ((), (), s32[]{:S(2)}) async-start(), calls=%async_computation.10 | async-start | bytes 1216512 | tf_op jit(solution)/shard_map/reduce_scatter | solution.py:1026
  771.2 173.0 %reduce-scatter.6.cloned.1.call-start = ((), (), s32[]{:S(2)}) async-start(), calls=%async_computation.9 | async-start | bytes 4423680 | tf_op jit(solution)/shard_map/reduce_scatter | solution.py:789
  775.4 46.6 %collective-permute-start.30 = (bf16[1024,384]{1,0:T(8,128)(2,1)}, bf16[1024,384]{1,0:T(8,128)(2,1)}, u32[]{:S(2)}, u32[]{:S(2)}) collective-permute-start(bf16[1024,384]{1,0:T(8,128)(2,1)} %convolution_convert_fusion.13), channel_id=1, source_target_pairs={{0,1},{1,0},{2,3},{3,2},{4,5},{5,4},{6,7},{7,6},{8,9},{9,8},{10,11... | collective-permute-start | bytes 2359304 | tf_op jit(solution)/shard_map/ppermute | solution.py:733
  779.1 39.1 %collective-permute-start.31 = (bf16[1024,384]{1,0:T(8,128)(2,1)S(1)}, bf16[1024,384]{1,0:T(8,128)(2,1)}, u32[]{:S(2)}, u32[]{:S(2)}) collective-permute-start(bf16[1024,384]{1,0:T(8,128)(2,1)S(1)} %copy-done.72), channel_id=1, source_target_pairs={{0,8},{8,0},{16,24},{24,16},{1,9},{9,1},{17,25},{25,17},{2,10},{10... | collective-permute-start | bytes 2359304 | tf_op jit(solution)/shard_map/ppermute | solution.py:757
  779.7 39.3 %collective-permute-start.32 = (bf16[1024,384]{1,0:T(8,128)(2,1)S(1)}, bf16[1024,384]{1,0:T(8,128)(2,1)}, u32[]{:S(2)}, u32[]{:S(2)}) collective-permute-start(bf16[1024,384]{1,0:T(8,128)(2,1)S(1)} %copy-done.71), channel_id=1, source_target_pairs={{0,16},{8,24},{16,0},{24,8},{1,17},{9,25},{17,1},{25,9},{2,18},{10... | collective-permute-start | bytes 2359304 | tf_op jit(solution)/shard_map/ppermute | solution.py:758
  781.0 26.5 %collective-permute-start.34 = (bf16[384,512]{1,0:T(8,128)(2,1)S(1)}, bf16[384,512]{1,0:T(8,128)(2,1)S(1)}, u32[]{:S(2)}, u32[]{:S(2)}) collective-permute-start(bf16[384,512]{1,0:T(8,128)(2,1)S(1)} %copy-done.76), channel_id=1, source_target_pairs={{0,8},{8,0},{16,24},{24,16},{1,9},{9,1},{17,25},{25,17},{2,10},{10... | collective-permute-start | bytes 1179656 | tf_op jit(solution)/shard_map/ppermute | solution.py:739
  783.6 41.5 %collective-permute-start.36 = (bf16[768,512]{1,0:T(8,128)(2,1)}, bf16[768,512]{1,0:T(8,128)(2,1)}, u32[]{:S(2)}, u32[]{:S(2)}) collective-permute-start(bf16[768,512]{1,0:T(8,128)(2,1)} %convolution_convert_fusion.10), channel_id=1, source_target_pairs={{0,1},{1,0},{2,3},{3,2},{4,5},{5,4},{6,7},{7,6},{8,9},{9,8},{10,11... | collective-permute-start | bytes 2359304 | tf_op jit(solution)/shard_map/ppermute | solution.py:733
  818.2 43.1 %collective-permute-start.45 = (bf16[768,512]{1,0:T(8,128)(2,1)}, bf16[768,512]{1,0:T(8,128)(2,1)S(1)}, u32[]{:S(2)}, u32[]{:S(2)}) collective-permute-start(bf16[768,512]{1,0:T(8,128)(2,1)} %convolution_convert_fusion.5), channel_id=1, source_target_pairs={{0,1},{1,0},{2,3},{3,2},{4,5},{5,4},{6,7},{7,6},{8,9},{9,8},{10,11... | collective-permute-start | bytes 2359304 | tf_op jit(solution)/shard_map/ppermute | solution.py:733
  819.0 237.3 %all-gather.22.cloned.1.call-start = ((), (), s32[]{:S(2)}) async-start(), calls=%async_computation.11 | async-start | bytes 4423680 | tf_op jit(solution)/shard_map/all_gather | solution.py:808
  819.1 27.4 %collective-permute-start.29 = (bf16[2,3,2048]{2,1,0:T(4,128)(2,1)S(1)}, bf16[2,3,2048]{2,1,0:T(4,128)(2,1)S(1)}, u32[]{:S(2)}, u32[]{:S(2)}) collective-permute-start(bf16[2,3,2048]{2,1,0:T(4,128)(2,1)S(1)} %slice.764), channel_id=1, source_target_pairs={{1,0},{2,1},{3,2},{4,3},{5,4},{6,5},{7,6},{9,8},{10,9},{11,10},{12... | collective-permute-start | bytes 73736 | tf_op jit(solution)/shard_map/ppermute | solution.py:27
  824.4 30.9 %collective-permute-start.53 = (bf16[256,384]{1,0:T(8,128)(2,1)S(1)}, bf16[256,384]{1,0:T(8,128)(2,1)S(1)}, u32[]{:S(2)}, u32[]{:S(2)}) collective-permute-start(bf16[256,384]{1,0:T(8,128)(2,1)S(1)} %get-tuple-element.200), channel_id=1, source_target_pairs={{0,6},{1,7},{2,0},{3,1},{4,2},{5,3},{6,4},{7,5},{8,14},{9,15},{10,... | collective-permute-start | bytes 589832 | tf_op jit(solution)/shard_map/ppermute | solution.py:776
  825.1 32.2 %collective-permute-start.52 = (bf16[256,384]{1,0:T(8,128)(2,1)S(1)}, bf16[256,384]{1,0:T(8,128)(2,1)S(1)}, u32[]{:S(2)}, u32[]{:S(2)}) collective-permute-start(bf16[256,384]{1,0:T(8,128)(2,1)S(1)} %get-tuple-element.201), channel_id=1, source_target_pairs={{0,4},{1,5},{2,6},{3,7},{4,0},{5,1},{6,2},{7,3},{8,12},{9,13},{10,... | collective-permute-start | bytes 589832 | tf_op jit(solution)/shard_map/ppermute | solution.py:776
  830.5 31.4 %collective-permute-start.47 = (bf16[768,512]{1,0:T(8,128)(2,1)S(1)}, bf16[768,512]{1,0:T(8,128)(2,1)S(1)}, u32[]{:S(2)}, u32[]{:S(2)}) collective-permute-start(bf16[768,512]{1,0:T(8,128)(2,1)S(1)} %add_convert_fusion.8), channel_id=1, source_target_pairs={{0,16},{8,24},{16,0},{24,8},{1,17},{9,25},{17,1},{25,9},{2,18},{10... | collective-permute-start | bytes 2359304 | tf_op jit(solution)/shard_map/ppermute | solution.py:758
  857.3 131.8 %collective-permute-start.42 = (bf16[768,512]{1,0:T(8,128)(2,1)}, bf16[768,512]{1,0:T(8,128)(2,1)}, u32[]{:S(2)}, u32[]{:S(2)}) collective-permute-start(bf16[768,512]{1,0:T(8,128)(2,1)} %convolution_convert_fusion.6), channel_id=1, source_target_pairs={{0,1},{1,0},{2,3},{3,2},{4,5},{5,4},{6,7},{7,6},{8,9},{9,8},{10,11... | collective-permute-start | bytes 2359304 | tf_op jit(solution)/shard_map/ppermute | solution.py:733
  861.3 82.9 %collective-permute-start.41 = (bf16[768,512]{1,0:T(8,128)(2,1)}, bf16[768,512]{1,0:T(8,128)(2,1)}, u32[]{:S(2)}, u32[]{:S(2)}) collective-permute-start(bf16[768,512]{1,0:T(8,128)(2,1)} %convolution_convert_fusion.7), channel_id=1, source_target_pairs={{0,1},{1,0},{2,3},{3,2},{4,5},{5,4},{6,7},{7,6},{8,9},{9,8},{10,11... | collective-permute-start | bytes 2359304 | tf_op jit(solution)/shard_map/ppermute | solution.py:733
  861.9 87.3 %collective-permute-start.37 = (bf16[768,512]{1,0:T(8,128)(2,1)}, bf16[768,512]{1,0:T(8,128)(2,1)}, u32[]{:S(2)}, u32[]{:S(2)}) collective-permute-start(bf16[768,512]{1,0:T(8,128)(2,1)} %convolution_convert_fusion.9), channel_id=1, source_target_pairs={{0,1},{1,0},{2,3},{3,2},{4,5},{5,4},{6,7},{7,6},{8,9},{9,8},{10,11... | collective-permute-start | bytes 2359304 | tf_op jit(solution)/shard_map/ppermute | solution.py:733
  947.7 41.5 %collective-permute-start.44 = (bf16[768,512]{1,0:T(8,128)(2,1)}, bf16[768,512]{1,0:T(8,128)(2,1)}, u32[]{:S(2)}, u32[]{:S(2)}) collective-permute-start(bf16[768,512]{1,0:T(8,128)(2,1)} %add_convert_fusion.6), channel_id=1, source_target_pairs={{0,16},{8,24},{16,0},{24,8},{1,17},{9,25},{17,1},{25,9},{2,18},{10... | collective-permute-start | bytes 2359304 | tf_op jit(solution)/shard_map/ppermute | solution.py:758
  952.5 36.7 %collective-permute-start.43 = (bf16[768,512]{1,0:T(8,128)(2,1)}, bf16[768,512]{1,0:T(8,128)(2,1)}, u32[]{:S(2)}, u32[]{:S(2)}) collective-permute-start(bf16[768,512]{1,0:T(8,128)(2,1)} %add_convert_fusion.7), channel_id=1, source_target_pairs={{0,8},{8,0},{16,24},{24,16},{1,9},{9,1},{17,25},{25,17},{2,10},{10... | collective-permute-start | bytes 2359304 | tf_op jit(solution)/shard_map/ppermute | solution.py:757
  992.2 29.0 %collective-permute-start.48 = (bf16[192,1024]{1,0:T(8,128)(2,1)S(1)}, bf16[192,1024]{1,0:T(8,128)(2,1)S(1)}, u32[]{:S(2)}, u32[]{:S(2)}) collective-permute-start(bf16[192,1024]{1,0:T(8,128)(2,1)S(1)} %get-tuple-element.197), channel_id=1, source_target_pairs={{0,2},{1,3},{2,4},{3,5},{4,6},{5,7},{6,0},{7,1},{8,10},{9,11},{10,... | collective-permute-start | bytes 1179656 | tf_op jit(solution)/shard_map/ppermute | solution.py:776
  992.7 28.5 %collective-permute-start.50 = (bf16[192,1024]{1,0:T(8,128)(2,1)S(1)}, bf16[192,1024]{1,0:T(8,128)(2,1)S(1)}, u32[]{:S(2)}, u32[]{:S(2)}) collective-permute-start(bf16[192,1024]{1,0:T(8,128)(2,1)S(1)} %get-tuple-element.198), channel_id=1, source_target_pairs={{0,6},{1,7},{2,0},{3,1},{4,2},{5,3},{6,4},{7,5},{8,14},{9,15},{10,... | collective-permute-start | bytes 1179656 | tf_op jit(solution)/shard_map/ppermute | solution.py:776
  994.3 30.4 %collective-permute-start.49 = (bf16[192,1024]{1,0:T(8,128)(2,1)S(1)}, bf16[192,1024]{1,0:T(8,128)(2,1)S(1)}, u32[]{:S(2)}, u32[]{:S(2)}) collective-permute-start(bf16[192,1024]{1,0:T(8,128)(2,1)S(1)} %get-tuple-element.199), channel_id=1, source_target_pairs={{0,4},{1,5},{2,6},{3,7},{4,0},{5,1},{6,2},{7,3},{8,12},{9,13},{10,... | collective-permute-start | bytes 1179656 | tf_op jit(solution)/shard_map/ppermute | solution.py:776
  (105 other events, 1836.6 us)
Sparse Core Ops, SparseCore 0:
  11.5 154.8 all-gather.13
  168.0 27.1 all-gather.15
  198.7 84.6 all-gather.17
  286.2 101.3 all-gather.19
  389.8 140.5 reduce-scatter.3
  639.5 64.2 all-reduce.11
  771.3 103.8 reduce-scatter.7
  877.5 66.6 reduce-scatter.5
  989.3 51.7 all-gather.21

commit v7 on v6

--- a/solution.py
+++ b/solution.py
@@ -474,6 +474,7 @@
 
 FF_TILE = 512
 GATHER_TILE = 768
+DOT_TILE = 512
 
 
 def ffn_forward(normed, proj_up):
@@ -537,6 +538,11 @@
     return [(i, (i + steps) % count) for i in range(count)]
 
 
+def same_cores():
+    count = lax.axis_size("seq")
+    return [list(range(core, count, 2)) for core in range(2)]
+
+
 def dot_rows(a, b):
     return lax.dot_general(a, b, (((0,), (0,)), ((), ())), preferred_element_type=F32)
 
@@ -561,52 +567,46 @@
     return a.reshape(seqs, rows // CHUNKS, CHUNKS, *a.shape[2:]).swapaxes(1, 2).reshape(a.shape)
 
 
-def gathered_ffn_kernel(where_ref, n_ref, *refs):
-    pieces, (hidden_ref, pull_ref, gate_ref, up_ref, held, sems) = refs[:12], refs[12:]
+def fetch_columns(where_ref, pieces, start, target, sem):
     own, far = pieces[:6], pieces[6:]
-    step, steps = pl.program_id(0), pl.num_programs(0)
     rows, columns = own[0].shape
-    width = columns // 4
-    tile = hidden_ref.shape[1]
+    width, tile = columns // 4, target.shape[1]
     depth, half = own[1].shape[0], own[4].shape[0]
     chips = depth // rows + 1
     chip, core, group = where_ref[0], where_ref[1], where_ref[2]
-
-    def fetch(n, slot):
-        for side in range(2):
-            start = n * tile + side * (columns // 2)
-            quarter = start // width
-            offset = pl.multiple_of(start - quarter * width, 128)
-            start = pl.multiple_of(start, 128)
-            relation = lax.bitwise_xor(group, quarter)
-            target, sem = held.at[slot, side], sems.at[slot, side]
-
-            def copy(source, row, count):
-                place = target.at[pl.ds(pl.multiple_of(row, 16), count), :]
-                pltpu.make_async_copy(source, place, sem).start()
-
-            for c, (shard, *parts) in enumerate((own, far)):
-                other = lax.rem(core + c, 2)
-                copy(shard.at[:, pl.ds(start, tile)], (chip * 2 + other) * rows, rows)
-                for j in range(1, chips):
-                    row = (lax.rem(chip + chips - j, chips) * 2 + other) * rows
-                    first = (j - 1) * rows
-                    for k in range(3):
-
-                        @pl.when(relation == k)
-                        def _():
-                            source = parts[k].at[pl.ds(first, rows), pl.ds(offset, tile)]
-                            copy(source, row, rows)
-
-                    @pl.when(relation == 3)
-                    def _():
-                        for m in range(2):
-                            low, high = max(first, m * half), min(first + rows, (m + 1) * half)
-                            if low < high:
-                                at = pl.ds(low - m * half, high - low)
-                                source = parts[3 + m].at[at, pl.ds(offset, tile)]
-                                copy(source, row + (low - first), high - low)
-
+    quarter = start // width
+    offset = pl.multiple_of(start - quarter * width, 128)
+    start = pl.multiple_of(start, 128)
+    relation = lax.bitwise_xor(group, quarter)
+
+    def copy(source, row, count):
+        place = target.at[pl.ds(pl.multiple_of(row, 16), count), :]
+        pltpu.make_async_copy(source, place, sem).start()
+
+    for c, (shard, *parts) in enumerate((own, far)):
+        other = lax.rem(core + c, 2)
+        copy(shard.at[:, pl.ds(start, tile)], (chip * 2 + other) * rows, rows)
+        for j in range(1, chips):
+            row = (lax.rem(chip + j, chips) * 2 + other) * rows
+            first = (j - 1) * rows
+            for k in range(3):
+
+                @pl.when(relation == k)
+                def _():
+                    copy(parts[k].at[pl.ds(first, rows), pl.ds(offset, tile)], row, rows)
+
+            @pl.when(relation == 3)
+            def _():
+                for m in range(2):
+                    low, high = max(first, m * half), min(first + rows, (m + 1) * half)
+                    if low < high:
+                        at = pl.ds(low - m * half, high - low)
+                        source = parts[3 + m].at[at, pl.ds(offset, tile)]
+                        copy(source, row + (low - first), high - low)
+
+
+def gathered_tiles(fetch, held, sems):
+    step, steps = pl.program_id(0), pl.num_programs(0)
     slot = lax.rem(step, 2)
 
     @pl.when(step == 0)
@@ -617,16 +617,44 @@
     def _():
         fetch(step + 1, 1 - slot)
 
-    for side in range(2):
+    for side in range(held.shape[1]):
         whole = held.at[slot, side]
         pltpu.make_async_copy(whole, whole, sems.at[slot, side]).wait()
+    return slot
+
+
+def gathered_ffn_kernel(where_ref, n_ref, *refs):
+    pieces, (hidden_ref, pull_ref, gate_ref, up_ref, held, sems) = refs[:12], refs[12:]
+    tile = hidden_ref.shape[1]
+
+    def fetch(n, slot):
+        for side in range(2):
+            start = n * tile + side * (pieces[0].shape[1] // 2)
+            fetch_columns(where_ref, pieces, start, held.at[slot, side], sems.at[slot, side])
+
+    slot = gathered_tiles(fetch, held, sems)
     gate_ref[...] = held[slot, 0]
     up_ref[...] = held[slot, 1]
     ffn_forward_kernel(n_ref, gate_ref, up_ref, hidden_ref, pull_ref)
 
 
+def gathered_dot_kernel(base, where_ref, n_ref, *refs):
+    pieces, (out_ref, weight_ref, held, sems) = refs[:12], refs[12:]
+    tile = out_ref.shape[1]
+
+    def fetch(n, slot):
+        start = base + n * tile
+        fetch_columns(where_ref, pieces, start, held.at[slot, 0], sems.at[slot, 0])
+
+    slot = gathered_tiles(fetch, held, sems)
+    weight_ref[...] = held[slot, 0]
+    out_ref[...] = jnp.dot(n_ref[...], weight_ref[...], preferred_element_type=F32).astype(
+        out_ref.dtype
+    )
+
+
 class Gather:
-    def __init__(self, shard, *after):
+    def __init__(self, shard, offload=False):
         self.shard = shard
         self.chips = lax.axis_size("seq") // 2
         half = (self.chips - 1) * shard.shape[0] // 2
@@ -636,10 +664,17 @@
             return
         group = lax.axis_index("grp")
         width = shard.shape[1] // 4
-        own = tie(lax.dynamic_slice_in_dim(shard, group * width, width, 1), *after)
-        self.near = jnp.concatenate(
-            [lax.ppermute(own, "seq", ring_pairs(2 * j)) for j in range(1, self.chips)], axis=0
-        )
+        own = lax.dynamic_slice_in_dim(shard, group * width, width, 1)
+        others = range(1, self.chips)
+        if offload:
+            slabs = lax.all_gather(own, "seq", axis_index_groups=same_cores())
+            chip = lax.axis_index("seq") // 2
+            slabs = [
+                lax.dynamic_index_in_dim(slabs, (chip + j) % self.chips, 0, False) for j in others
+            ]
+        else:
+            slabs = [lax.ppermute(own, "seq", ring_pairs(-2 * j)) for j in others]
+        self.near = jnp.concatenate(slabs, axis=0)
         self.half = half
 
     def first(self):
@@ -652,54 +687,86 @@
     def second(self, *after):
         if self.simple:
             return ()
-        self.from_x, self.from_y = tie((self.from_x, self.from_y), *after)
+        if after:
+            self.from_x, self.from_y = tie((self.from_x, self.from_y), *after)
         self.halves = (self.from_y[: self.half], self.from_x[self.half :])
         return self.halves
 
-    def ffn_forward(self, normed):
+    def third(self):
         if self.simple:
-            hidden, pull = ffn_forward(normed, self.whole)
-            return hidden, pull, self.whole[:, :FF], self.whole[:, FF:]
+            return
         diag_a = lax.ppermute(self.halves[0], "grp", xor_pairs("grp", 1))
         diag_b = lax.ppermute(self.halves[1], "grp", xor_pairs("grp", 2))
         own = (self.shard, self.near, self.from_x, self.from_y, diag_a, diag_b)
         far = tuple(lax.ppermute(piece, "seq", xor_pairs("seq", 1)) for piece in own)
         place = lax.axis_index("seq")
         where = jnp.stack([place // 2, place % 2, lax.axis_index("grp")]).astype(jnp.int32)
-        rows = normed.shape[0]
-        tile = GATHER_TILE
-        weight = pl.BlockSpec((D, tile), lambda n: (0, n))
+        self.pieces = (where, own, far)
+
+    def call(self, kernel, normed, steps, tile, weights, out_specs, out_shape, name):
+        where, own, far = self.pieces
+        rows, depth = normed.shape
         return pl.pallas_call(
-            gathered_ffn_kernel,
-            grid=(FF // tile,),
+            kernel,
+            grid=(steps,),
             in_specs=[
                 pl.BlockSpec(memory_space=pltpu.SMEM),
-                pl.BlockSpec((rows, D), lambda n: (0, 0)),
+                pl.BlockSpec((rows, depth), lambda n: (0, 0)),
             ]
             + [pl.BlockSpec(memory_space=pl.ANY)] * 12,
-            out_specs=[
+            out_specs=out_specs + [pl.BlockSpec((depth, tile), lambda n: (0, n))] * weights,
+            out_shape=out_shape + [jax.ShapeDtypeStruct((depth, steps * tile), BF16)] * weights,
+            scratch_shapes=[
+                pltpu.VMEM((2, weights, depth, tile), BF16),
+                pltpu.SemaphoreType.DMA((2, weights)),
+            ],
+            compiler_params=pltpu.CompilerParams(vmem_limit_bytes=56 * 1024 * 1024),
+            name=name,
+        )(where, normed, *own, *far)
+
+    def dot(self, normed, half, dtype):
+        columns = self.shard.shape[1] // 2
+        base = half * columns
+        if self.simple:
+            weight = self.whole[:, base : base + columns]
+            return jnp.dot(normed, weight, preferred_element_type=F32).astype(dtype), weight
+        rows, tile = normed.shape[0], DOT_TILE
+        return self.call(
+            functools.partial(gathered_dot_kernel, base),
+            normed,
+            columns // tile,
+            tile,
+            1,
+            [pl.BlockSpec((rows, tile), lambda n: (0, n))],
+            [jax.ShapeDtypeStruct((rows, columns), dtype)],
+            "gathered_dot",
+        )
+
+    def ffn_forward(self, normed):
+        if self.simple:
+            hidden, pull = ffn_forward(normed, self.whole)
+            return hidden, pull, self.whole[:, :FF], self.whole[:, FF:]
+        rows, tile = normed.shape[0], GATHER_TILE
+        return self.call(
+            gathered_ffn_kernel,
+            normed,
+            FF // tile,
+            tile,
+            2,
+            [
                 pl.BlockSpec((rows, tile), lambda n: (0, n)),
                 pl.BlockSpec((2, rows, tile), lambda n: (0, 0, n)),
-                weight,
-                weight,
             ],
-            out_shape=[
+            [
                 jax.ShapeDtypeStruct((rows, FF), BF16),
                 jax.ShapeDtypeStruct((2, rows, FF), BF16),
-                jax.ShapeDtypeStruct((D, FF), BF16),
-                jax.ShapeDtypeStruct((D, FF), BF16),
             ],
-            scratch_shapes=[
-                pltpu.VMEM((2, 2, D, tile), BF16),
-                pltpu.SemaphoreType.DMA((2, 2)),
-            ],
-            compiler_params=pltpu.CompilerParams(vmem_limit_bytes=56 * 1024 * 1024),
-            name="gathered_ffn",
-        )(where, normed, *own, *far)
+            "gathered_ffn",
+        )
 
 
 class Reduction:
-    def __init__(self, a_own, a_far, columns, width):
+    def __init__(self, a_own, a_far, columns, width, fused=False):
         self.simple = lax.axis_size("grp") != 4
         count = lax.axis_size("seq")
         place = lax.axis_index("seq")
@@ -728,9 +795,15 @@
         self.x, self.y = xor_pairs("grp", 1), xor_pairs("grp", 2)
         self.b = [columns(group ^ k) for k in range(4)]
         self.far = [None] * 4
-        for k in (3, 1, 2, 0):
+        self.product = None
+        other = xor_pairs("seq", 1)
+        if fused:
+            b_all = jnp.concatenate(self.b, axis=1)
+            far = lax.ppermute(dot_rows(a_far, b_all).astype(BF16), "seq", other)
+            self.product = (dot_rows(a_own, b_all) + far.astype(F32)).astype(BF16)
+        for k in () if fused else (3, 1, 2, 0):
             product = dot_rows(a_far, self.b[k]).astype(BF16)
-            self.far[k] = lax.ppermute(product, "seq", xor_pairs("seq", 1))
+            self.far[k] = lax.ppermute(product, "seq", other)
         half = self.half
         self.sent = (
             self.own(3, 0, half).astype(BF16),
@@ -740,6 +813,9 @@
         self.diag_b = lax.ppermute(self.sent[1], "grp", self.y)
 
     def own(self, k, first, last):
+        if self.product is not None:
+            left = k * self.width
+            return self.product[first:last, left : left + self.width].astype(F32)
         product = dot_rows(self.a_own[:, first:last], self.b[k])
         return product + self.far[k][first:last].astype(F32)
 
@@ -783,11 +859,9 @@
         mine = self.mine(*after)
         if not offload:
             return self.along_z(mine)
-        count = 2 * self.chips
-        cores = [list(range(c, count, 2)) for c in range(2)]
         self.kept = None
         self.arrived = lax.psum_scatter(
-            mine, "seq", scatter_dimension=0, axis_index_groups=cores, tiled=True
+            mine, "seq", scatter_dimension=0, axis_index_groups=same_cores(), tiled=True
         )
         return (mine,)
 
@@ -889,7 +963,11 @@
     taps_all = (
         small_all[:, 2 * n_gain + n_lru :].reshape(-1, CONV, n_lru).transpose(1, 0, 2)
     ).reshape(CONV, LRU).astype(F32)
-    proj_in = gather_rows(in_proj)
+    in_gather = Gather(in_proj)
+    up_gather = Gather(up_proj, offload=True)
+    in_gather.first()
+    in_gather.second()
+    in_gather.third()
     gates_all = lax.all_gather(gate_heads, "seq", axis=0, tiled=True)
     proj_out = gather_rows(out_proj)
     proj_down = gather_rows(down_proj)
@@ -902,8 +980,7 @@
     )
     first_scale = first_scale[:, :1]
     wide = (seq_count, shard_len, LRU)
-    up_gather = Gather(up_proj, first_normed)
-    inner_low = jnp.dot(first_normed, proj_in[:, :LRU], preferred_element_type=F32).astype(BF16)
+    inner_low, in_value = in_gather.dot(first_normed, 0, BF16)
     inner_low = inner_low.reshape(wide)
 
     step = shard_len // CHUNKS
@@ -922,7 +999,8 @@
         tie(inner_low, *up_gather.first()), prev_inner, dist, gates_all, taps_all, soft
     )
     end_state, end_prod = chunk_ends(chunks, False)
-    gate_pre = jnp.dot(first_normed, proj_in[:, LRU:], preferred_element_type=F32).reshape(wide)
+    gate_pre, in_gate = in_gather.dot(first_normed, 1, F32)
+    gate_pre = gate_pre.reshape(wide)
     carry_in = shard_carry(end_state, end_prod, False)
     carries = chunk_carries(chunks, carry_in, False)
     state, branch, branch_split = mixer_branch(
@@ -936,12 +1014,13 @@
         resid, gain_two, last + 1, place % 2
     )
     second_scale = second_scale[:, :1]
+    up_gather.third()
     hidden, pull, proj_gate, proj_up = up_gather.ffn_forward(second_normed)
 
     grad_out = cotangent.reshape(row_count, D)
     grad_down = dot_rows(hidden, grad_out).astype(BF16)
-    down_sum = lax.psum_scatter(grad_down, "seq", scatter_dimension=0, tiled=True)
-    down_sum = lax.psum(down_sum, "grp")
+    down_part = lax.psum_scatter(grad_down, "seq", scatter_dimension=0, tiled=True)
+    down_sum = lax.psum(down_part, "grp")
     grad_expanded = ffn_backward(tie(grad_out, grad_down), proj_down, pull)
     quarter = FF // 2
 
@@ -962,38 +1041,41 @@
         resid, second_scale, gain_two, grad_second_normed
     )
     grad_mixer = grad_resid.astype(BF16)
+    grad_branch = dot_far(grad_mixer, proj_out)
+
+    grad_gate, local, rev_prod, rev_chunks = mixer_reverse(
+        tie(grad_branch, down_part).reshape(wide), gate_pre, keep, state
+    )
+    head_pull, head_prod = chunk_ends(rev_chunks, True)
+    grad_gate = grad_gate.reshape(row_count, LRU)
+    width = LRU // 4
+    rev_carry = shard_carry(head_pull, head_prod, True)
+    rev_carries = chunk_carries(rev_chunks, rev_carry, True)
+    grad_mixer, grad_gate = tie((grad_mixer, grad_gate), rev_carry)
     out_sum = Reduction(
         branch_split[0],
         branch_split[1],
         lambda n: lax.dynamic_slice_in_dim(grad_mixer, n * (D // 4), D // 4, 1),
         D // 4,
-    )
-    grad_branch = dot_far(tie(grad_mixer, *out_sum.sent), proj_out)
-
-    grad_gate, local, rev_prod, rev_chunks = mixer_reverse(
-        grad_branch.reshape(wide), gate_pre, keep, state
-    )
-    head_pull, head_prod = chunk_ends(rev_chunks, True)
-    grad_gate = grad_gate.reshape(row_count, LRU)
-    width = LRU // 4
-    grad_gate = tie(grad_gate, *out_sum.second(head_pull))
+        True,
+    )
     in_gate_sum = Reduction(
         first_own,
         first_far,
         lambda n: lax.dynamic_slice_in_dim(grad_gate, n * width, width, 1),
         width,
-    )
-    rev_carry = shard_carry(head_pull, head_prod, True)
-    rev_carries = chunk_carries(rev_chunks, rev_carry, True)
-    sent = up_sum.third(rev_carry, down_sum, *in_gate_sum.sent, offload=True)
-    local = tie(local, *in_gate_sum.sent, *sent)
+        True,
+    )
+    sent = (*out_sum.sent, *in_gate_sum.sent)
+    sent = up_sum.third(*sent)
+    local = tie(local, down_sum, *sent)
     du, tail, edge, grad_gates, grad_taps, grad_decay = mixer_backward(
         local, rev_prod, rev_carries, state, carries, conv_low, inner_low,
         prev_inner, dist, gates_all, taps_all, soft,
     )
     returned = from_behind(edge[:, HALO - edge_len :].astype(BF16), "seq", -1).astype(F32)
-    grad_gate = tie(grad_gate, *out_sum.third(edge), *in_gate_sum.second(edge))
-    first_grad = dot_far(grad_gate, proj_in[:, LRU:])
+    grad_gate = tie(grad_gate, *out_sum.second(edge), *in_gate_sum.second(edge))
+    first_grad = dot_far(grad_gate, in_gate)
     groups = TAIL // CHUNKS
     padded = jnp.pad(
         returned[:, :, None, :], ((0, 0), (groups - edge_len, 0), (CHUNKS - 1, 0), (0, 0))
@@ -1007,8 +1089,9 @@
         first_far,
         lambda n: lax.dynamic_slice_in_dim(grad_inner, n * width, width, 1),
         width,
-    )
-    grad_inner = tie(grad_inner, *in_value_sum.sent)
+        True,
+    )
+    grad_inner = tie(grad_inner, *in_value_sum.sent, *out_sum.third())
 
     shards = last + 1
     grad_decay_row = grad_decay[0] * jax.nn.sigmoid(-decay_float)
@@ -1031,8 +1114,8 @@
     taps_total = flat[n_gates : n_gates + CONV * n_lru].reshape(CONV, n_lru)
     decay_total = flat[n_gates + CONV * n_lru :]
 
-    first_grad = first_grad + dot_far(grad_inner, proj_in[:, :LRU])
-    sent = in_value_sum.second(first_grad, up_sum.arrived)
+    first_grad = first_grad + dot_far(grad_inner, in_value)
+    sent = in_value_sum.second(first_grad)
     up_total = up_sum.finish(edge)
     down_total = down_sum.astype(F32)
     if in_value_sum.simple:

time: 1080 us -> 989 us (0.916)
  waiting for transfers between devices: 331 us -> 251 us
  matrix products: 280 us -> 239 us
  Pallas kernels: 183 us -> 210 us
  blocking collectives: 95.2 us -> 80.2 us
    ppermute x3, waiting for transfers between devices: 116 us -> 4.3 us  [from_behind(): lax.ppermute(value, axis, [(source, source + steps) for source in range(f...]
    ppermute x27 -> x26, waiting for transfers between devices: 11 us -> 85.7 us  [the longest x3 73.9 us: __init__(): slabs = [lax.ppermute(own, 'seq', ring_pairs(-2 * j)) for j in others]]
    ppermute x4, waiting for transfers between devices: 63.1 us -> 0.38 us  [__init__(): self.diag_a = lax.ppermute(self.sent[0], 'grp', self.x)]
    ppermute x6 -> x9, waiting for transfers between devices: 8.94 us -> 68.6 us  [along_z(): lax.ppermute(part, 'seq', ring_pairs(2 * j + 2))]
    reduce_scatter x1 -> x0, waiting for transfers between devices: 52.2 us -> none  [third(): lax.psum_scatter(mine, 'seq', scatter_dimension=0, axis_index_groups=core...]
    ppermute x4, waiting for transfers between devices: 0.01 us -> 28 us  [second(): self.from_y = lax.ppermute(sent[1], 'grp', self.y)]
    pallas_call x1 -> x3, Pallas kernels: 39.9 us -> 66.6 us  [call(): pl.pallas_call(kernel, grid=(steps,), in_specs=[pl.BlockSpec(memory_space...]
    dot_general x2 -> x0, matrix products: 21 us -> none  [the longest x1 11.2 us: body(): jnp.dot(first_normed, proj_in[:, LRU:], preferred_element_type=F32)]
  transfers between devices with their start and end apart: 63 -> 66, of which waited for: 16 -> 21; matrix products, arithmetic and copies ran while one was open for 32% -> 33% of each run, Pallas kernels for 13% -> 21%
where the time goes in v7:
time: 989 us; the launch traced here: 982 us
  waiting for transfers between devices  251 us (25%)
  matrix products  239 us (24%)
  Pallas kernels  210 us (21%)
  local copies, waits for them, and re-layouts  93.8 us (9%)
  blocking collectives  80.2 us (8%)
  starting transfers between devices  46.3 us (5%)
  other arithmetic  44.2 us (4%)
  between operations  16.1 us (2%)
    dot_general x16, matrix products, dot_rows(): lax.dot_general(a, b, (((0,), (0,)), ((), ())), preferred_element_type=F32)  132 us
    dot_general x5, matrix products, dot_far(): lax.dot_general(a, b, (((1,), (1,)), ((), ())), preferred_element_type=F32)  76.6 us
    ppermute x3, waiting for transfers between devices, __init__(): slabs = [lax.ppermute(own, 'seq', ring_pairs(-2 * j)) for j in others]  73.9 us
    ppermute x9, waiting for transfers between devices, along_z(): lax.ppermute(part, 'seq', ring_pairs(2 * j + 2))  68.6 us
    pallas_call x3, Pallas kernels, call(): pl.pallas_call(kernel, grid=(steps,), in_specs=[pl.BlockSpec(memory_space...  66.6 us
    pallas_call x1, Pallas kernels, mixer_backward(): pl.pallas_call(mixer_backward_kernel, grid=(HEADS,), in_specs=[full, full...  46.7 us
    psum x1, waiting for transfers between devices, body(): down_sum = lax.psum(down_part, 'grp')  41.5 us
    unnamed x192, local copies, waits for them, and re-layouts  41.3 us
  transfers between devices with their start and end apart: 66, of which 21 were waited for; matrix products, arithmetic and copies ran while one was open for 33% of the time, Pallas kernels for 21%

profile of v7, /device:TPU:18, one launch (start us, length us, event | category | flops | bytes accessed | tf_op | source)
XLA Modules:
  0.0 981.6 jit_solution(11785140398148982289)
XLA Ops:
  18.0 18.2 %collective-permute-done = bf16[192,1024]{1,0:T(8,128)(2,1)S(1)} collective-permute-done((bf16[192,1024]{1,0:T(8,128)(2,1)S(1)}, bf16[192,1024]{1,0:T(8,128)(2,1)S(1)}, u32[]{:S(2)}, u32[]{:S(2)}) %collective-permute-start) | collective-permute-done | bytes 393248 | tf_op jit(solution)/shard_map/ppermute | solution.py:676
  36.3 42.6 %collective-permute-done.1 = bf16[192,1024]{1,0:T(8,128)(2,1)S(1)} collective-permute-done((bf16[192,1024]{1,0:T(8,128)(2,1)S(1)}, bf16[192,1024]{1,0:T(8,128)(2,1)S(1)}, u32[]{:S(2)}, u32[]{:S(2)}) %collective-permute-start.1) | collective-permute-done | bytes 393248 | tf_op jit(solution)/shard_map/ppermute | solution.py:676
  78.9 13.1 %collective-permute-done.2 = bf16[192,1024]{1,0:T(8,128)(2,1)S(1)} collective-permute-done((bf16[192,1024]{1,0:T(8,128)(2,1)S(1)}, bf16[192,1024]{1,0:T(8,128)(2,1)S(1)}, u32[]{:S(2)}, u32[]{:S(2)}) %collective-permute-start.2) | collective-permute-done | bytes 393248 | tf_op jit(solution)/shard_map/ppermute | solution.py:676
  94.8 12.3 %all-gather.8 = bf16[8,1,1664]{2,1,0:T(2,128)(2,1)S(1)} all-gather(bf16[1,1,1664]{2,1,0:T(2,128)(2,1)S(1)} %reshape.2491), channel_id=2, replica_groups=mesh['grp'=4,'seq'=8] {'seq'}, dimensions={0}, use_global_device_ids=true | all-gather | bytes 29952 | tf_op jit(solution)/shard_map/all_gather | solution.py:958
  107.7 7.4 collective-permute-done.4.refs_3_
  130.9 8.2 collective-permute-done.6.refs_5_
  153.5 12.0 %gathered_dot.2 = (bf16[1024,2048]{1,0:T(8,128)(2,1)}, bf16[1536,2048]{1,0:T(8,128)(2,1)}) custom-call(s32[3]{0:T(128)} %pad_add_fusion.1.where_ref, bf16[1024,1536]{1,0:T(8,128)(2,1)} %copy-done.7, bf16[192,4096]{1,0:T(8,128)(2,1)} %refs_0_.4, bf16[576,1024]{1,0:T(8,128)(2,1)} %copy-done.52, bf16[576,1024]{1,0:T(8,128)(2,1)} %collective-permute-done.3.refs_2_, ...), custom_call_target="tpu_custom_call" | custom-call | tf_op jit(solution)/shard_map/gathered_dot/pallas_call | solution.py:709
  175.9 28.0 %mixer_forward.1 = (bf16[2,512,2048]{2,1,0:T(8,128)(2,1)S(1)}, f32[2,512,2048]{2,1,0:T(8,128)}, f32[2,512,2048]{2,1,0:T(8,128)}, f32[2,512,2048]{2,1,0:T(8,128)}, f32[2,2,8,2048]{3,2,1,0:T(8,128)S(1)}) custom-call(bf16[2,512,2048]{2,1,0:T(8,128)(2,1)S(1)} %bitcast.791, bf16[2,8,2048]{2,1,0:T(8,128)(2,1)S(1)} %collective-permute-done.13.halo_ref, ...), custom_call_target="tpu_custom_call" | custom-call | tf_op jit(solution)/shard_map/mixer_forward/pallas_call | solution.py:322
  206.5 13.5 %all-gather.2 = f32[16,2,2048]{2,1,0:T(2,128)S(1)} all-gather(f32[2,2,2048]{2,1,0:T(2,128)S(1)} %copy.313), channel_id=4, replica_groups=mesh['grp'=4,'seq'=8] {'seq'}, dimensions={0}, use_global_device_ids=true | all-gather | bytes 294912 | tf_op jit(solution)/shard_map/all_gather | solution.py:907
  229.3 5.3 copy.328
  234.6 12.8 %gathered_dot.3 = (f32[1024,2048]{1,0:T(8,128)}, bf16[1536,2048]{1,0:T(8,128)(2,1)}) custom-call(s32[3]{0:T(128)} %pad_add_fusion.1.where_ref, bf16[1024,1536]{1,0:T(8,128)(2,1)} %copy-done.7, bf16[192,4096]{1,0:T(8,128)(2,1)} %refs_0_.4, bf16[576,1024]{1,0:T(8,128)(2,1)} %copy-done.52, bf16[576,1024]{1,0:T(8,128)(2,1)} %collective-permute-done.3.refs_2_, ...), custom_call_target="tpu_custom_call" | custom-call | tf_op jit(solution)/shard_map/gathered_dot/pallas_call | solution.py:709
  247.4 17.8 %mixer_branch.1 = (f32[2,512,2048]{2,1,0:T(8,128)}, bf16[2,512,2048]{2,1,0:T(8,128)(2,1)S(1)}, bf16[2,2,512,1024]{3,2,1,0:T(8,128)(2,1)S(1)}) custom-call(s32[1]{0:T(128)} %bitcast.3.core_ref, f32[2,512,2048]{2,1,0:T(8,128)} %get-tuple-element.78.state_ref, f32[2,512,2048]{2,1,0:T(8,128)} %get-tuple-element.79.prod_ref, ...), custom_call_target="tpu_custom_call" | custom-call | tf_op jit(solution)/shard_map/mixer_branch/pallas_call | solution.py:364
  269.8 10.0 %convert_add_fusion.x_ref = f32[1024,1536]{1,0:T(8,128)S(1)} fusion(bf16[1024,1536]{1,0:T(8,128)(2,1)S(1)} %bitcast.786, bf16[1024,2048]{1,0:T(8,128)(2,1)} %bitcast.798, bf16[2048,1536]{1,0:T(8,128)(2,1)} %all-gather.17.cloned.1.call-done), kind=kOutput, calls=%fused_computation.3 | convolution fusion | flops 6445596672 | bytes 19922944 | tf_op jit(solution)/shard_map/dot_general | solution.py:1010
  289.3 41.8 %gathered_ffn.1 = (bf16[1024,4608]{1,0:T(8,128)(2,1)}, bf16[2,1024,4608]{2,1,0:T(8,128)(2,1)}, bf16[1536,4608]{1,0:T(8,128)(2,1)}, bf16[1536,4608]{1,0:T(8,128)(2,1)}) custom-call(s32[3]{0:T(128)} %pad_add_fusion.1.where_ref, bf16[1024,1536]{1,0:T(8,128)(2,1)} %copy-done.21, bf16[192,9216]{1,0:T(8,128)(2,1)} %refs_0_.5, ...), custom_call_target="tpu_custom_call" | custom-call | tf_op jit(solution)/shard_map/gathered_ffn/pallas_call | solution.py:709
  331.1 31.7 %convolution_convert_fusion = bf16[4608,1536]{1,0:T(8,128)(2,1)} fusion(bf16[1024,4608]{1,0:T(8,128)(2,1)} %get-tuple-element.125, bf16[1024,1536]{1,0:T(8,128)(2,1)S(1)} %bitcast.787), kind=kOutput, calls=%fused_computation | convolution fusion | flops 14502592512 | bytes 26738688 | tf_op jit(solution)/shard_map/dot_general | solution.py:547
  363.0 25.1 %ffn_backward.1 = bf16[2,1024,4608]{2,1,0:T(8,128)(2,1)} custom-call(bf16[1024,1536]{1,0:T(8,128)(2,1)S(1)} %bitcast.788, bf16[4608,1536]{1,0:T(8,128)(2,1)} %all-gather.19.cloned.1.call-done.down_ref, bf16[2,1024,4608]{2,1,0:T(8,128)(2,1)} %get-tuple-element.87.pull_ref), custom_call_target="tpu_custom_call" | custom-call | tf_op jit(solution)/shard_map/ffn_backward/pallas_call | solution.py:506
  388.0 7.7 convolution_convert_fusion.4
  402.3 7.9 convolution_convert_fusion.1
  411.6 5.3 convolution_convert_fusion.2
  416.9 5.8 convolution_convert_fusion.3
  433.8 21.8 %fusion = f32[1024,1536]{1,0:T(8,128)} fusion(bf16[1536,4608]{1,0:T(8,128)(2,1)} %get-tuple-element.92, bf16[2,1024,4608]{2,1,0:T(8,128)(2,1)} %ffn_backward.1), kind=kOutput, calls=%fused_computation.4 | convolution fusion | flops 14495514624 | bytes 29884416 | tf_op jit(solution)/shard_map/dot_general | solution.py:557
  455.6 22.5 %fusion.25 = f32[1024,1536]{1,0:T(8,128)} fusion(f32[1024,1536]{1,0:T(8,128)} %fusion, bf16[1536,4608]{1,0:T(8,128)(2,1)} %get-tuple-element.91, bf16[2,1024,4608]{2,1,0:T(8,128)(2,1)} %ffn_backward.1), kind=kOutput, calls=%fused_computation.43 | convolution fusion | flops 14497087488 | bytes 36175872 | tf_op jit(solution)/shard_map/dot_general | solution.py:557
  478.1 9.1 add_convert_fusion.2
  489.0 9.3 add_convert_fusion.1
  506.1 11.0 %fusion.198 = f32[1024,2048]{1,0:T(8,128)} fusion(bf16[1024,1536]{1,0:T(8,128)(2,1)S(1)} %get-tuple-element.102, bf16[2048,1536]{1,0:T(8,128)(2,1)} %all-gather.17.cloned.1.call-done), kind=kOutput, calls=%fused_computation.350 | convolution fusion | flops 6442450944 | bytes 17825792 | tf_op jit(solution)/shard_map/dot_general | solution.py:557
  517.0 22.2 %mixer_reverse.1 = (bf16[2,512,2048]{2,1,0:T(8,128)(2,1)S(1)}, f32[2,512,2048]{2,1,0:T(8,128)S(1)}, f32[2,512,2048]{2,1,0:T(8,128)}, f32[2,2,8,2048]{3,2,1,0:T(8,128)S(1)}) custom-call(f32[2,512,2048]{2,1,0:T(8,128)} %bitcast.811, f32[2,512,2048]{2,1,0:T(8,128)} %bitcast.800, f32[2,512,2048]{2,1,0:T(8,128)} %get-tuple-element.97.keep_ref, ...), custom_call_target="tpu_custom_call" | custom-call | tf_op jit(solution)/shard_map/mixer_reverse/pallas_call | solution.py:386
  542.3 5.5 convolution_convert_fusion.5
  549.3 5.5 convolution_convert_fusion.7
  555.2 13.7 %all-gather.3 = f32[16,2,2048]{2,1,0:T(2,128)S(1)} all-gather(f32[2,2,2048]{2,1,0:T(2,128)S(1)} %copy.345), channel_id=5, replica_groups=mesh['grp'=4,'seq'=8] {'seq'}, dimensions={0}, use_global_device_ids=true | all-gather | bytes 294912 | tf_op jit(solution)/shard_map/all_gather | solution.py:907
  569.6 7.1 add_convert_fusion.6
  579.0 5.7 add_convert_fusion.5
  588.7 10.1 %add_convert_fusion = bf16[768,2304]{1,0:T(8,128)(2,1)S(1)} fusion(bf16[768,2304]{1,0:T(8,128)(2,1)} %collective-permute-done.32, bf16[768,2304]{1,0:T(8,128)(2,1)} %collective-permute-done.31, bf16[768,2304]{1,0:T(8,128)(2,1)} %collective-permute-done.30, bf16[1024,768]{1,0:T(8,128)(2,1)S(1)} %copy-done.25, bf16[2,1024,4608]{2,1,0:T(8,128)(2,1)} %ffn_backward.1, ...), kind=kOutput, calls=%fused_computation.11 | convolution fusion | flops 3636264960 | bytes 20447240 | tf_op jit(solution)/shard_map/dot_general | solution.py:547
  602.1 41.5 %all-reduce.12.cloned.1.call-done = bf16[576,1536]{1,0:T(8,128)(2,1)} async-done(((bf16[576,1536]{1,0:T(8,128)(2,1)}), bf16[576,1536]{1,0:T(8,128)(2,1)}) %all-reduce.12.cloned.1.call-update) | async-done | bytes 1769488 | tf_op jit(solution)/shard_map/psum | solution.py:1023
  645.8 46.7 %mixer_backward.1 = (bf16[2,512,2048]{2,1,0:T(8,128)(2,1)S(1)}, f32[2,32,2048]{2,1,0:T(8,128)S(1)}, f32[2,8,2048]{2,1,0:T(8,128)S(1)}, f32[16,128,256]{2,1,0:T(8...) custom-call(f32[2,512,2048]{2,1,0:T(8,128)} %copy-done.8, f32[2,512,2048]{2,1,0:T(8,128)} %get-tuple-element.108.prod_ref, ...), custom_call_target="tpu_custom_call" | custom-call | tf_op jit(solution)/shard_map/mixer_backward/pallas_call | solution.py:408
  712.4 10.8 %fusion.199 = f32[1024,1536]{1,0:T(8,128)} fusion(bf16[1024,2048]{1,0:T(8,128)(2,1)S(1)} %bitcast.793, bf16[1536,2048]{1,0:T(8,128)(2,1)} %get-tuple-element.119), kind=kOutput, calls=%fused_computation.351 | convolution fusion | flops 6442450944 | bytes 16777216 | tf_op jit(solution)/shard_map/dot_general | solution.py:557
  724.7 5.3 convolution_convert_fusion.6
  734.6 47.7 %collective-permute-done.56 = bf16[192,2304]{1,0:T(8,128)(2,1)S(1)} collective-permute-done((bf16[192,2304]{1,0:T(8,128)(2,1)}, bf16[192,2304]{1,0:T(8,128)(2,1)S(1)}, u32[]{:S(2)}, u32[]{:S(2)}) %collective-permute-start.56) | collective-permute-done | bytes 884768 | tf_op jit(solution)/shard_map/ppermute | solution.py:852
  789.2 13.5 %collective-permute-done.44 = bf16[1024,384]{1,0:T(8,128)(2,1)S(1)} collective-permute-done((bf16[1024,384]{1,0:T(8,128)(2,1)}, bf16[1024,384]{1,0:T(8,128)(2,1)S(1)}, u32[]{:S(2)}, u32[]{:S(2)}) %collective-permute-start.44) | collective-permute-done | bytes 786464 | tf_op jit(solution)/shard_map/ppermute | solution.py:834
  812.1 9.9 %collective-permute-done.54 = bf16[256,384]{1,0:T(8,128)(2,1)S(1)} collective-permute-done((bf16[256,384]{1,0:T(8,128)(2,1)S(1)}, bf16[256,384]{1,0:T(8,128)(2,1)S(1)}, u32[]{:S(2)}, u32[]{:S(2)}) %collective-permute-start.54) | collective-permute-done | bytes 196640 | tf_op jit(solution)/shard_map/ppermute | solution.py:852
  825.9 17.7 %all-gather.6 = bf16[3648,128]{1,0:T(8,128)(2,1)S(1)} all-gather(bf16[912,128]{1,0:T(8,128)(2,1)S(1)} %pad_maximum_fusion.17), channel_id=8, replica_groups=mesh['grp'=4,'seq'=8] {'grp'}, dimensions={0}, use_global_device_ids=true | all-gather | bytes 1167360 | tf_op jit(solution)/shard_map/all_gather | solution.py:893
  850.5 6.8 add_convert_fusion.4
  859.0 10.6 %fusion.10 = (f32[1024]{0:T(1024)S(1)}, f32[1024,1536]{1,0:T(8,128)S(1)}) fusion(f32[1536]{0:T(1024)S(1)} %copy-done.73, bf16[2,8,64,1536]{3,1,2,0:T(8,128)(2,1)S(1)} %copy-done.4, f32[1024,1536]{1,0:T(8,128)} %fusion.199, bf16[1024,2048]{1,0:T(8,128)(2,1)S(1)} %bitcast.795, bf16[1536,2048]{1,0:T(8,128)(2,1)} %get-tuple-element.122), kind=kOutput, calls=%fused_computation.18 | convolution fusion | flops 6450314240 | bytes 26224640 | tf_op jit(solution)/shard_map/dot_general | solution.py:557
  869.6 6.7 collective-permute-done.42
  885.4 14.4 %collective-permute-done.46 = bf16[768,512]{1,0:T(8,128)(2,1)S(1)} collective-permute-done((bf16[768,512]{1,0:T(8,128)(2,1)S(1)}, bf16[768,512]{1,0:T(8,128)(2,1)S(1)}, u32[]{:S(2)}, u32[]{:S(2)}) %collective-permute-start.46) | collective-permute-done | bytes 786464 | tf_op jit(solution)/shard_map/ppermute | solution.py:834
  906.2 20.2 %add_convert_fusion.3 = bf16[1024,1536]{1,0:T(8,128)(2,1)S(1)} fusion(f32[1024,1536]{1,0:T(8,128)S(1)} %bitcast.784, bf16[1024,4608]{1,0:T(8,128)(2,1)} %get-tuple-element.125, bf16[4608,1536]{1,0:T(8,128)(2,1)} %all-gather.19.cloned.1.call-done.down_ref), kind=kOutput, calls=%fused_computation.19 | convolution fusion | flops 14498660352 | bytes 33030144 | tf_op jit(solution)/shard_map/dot_general | solution.py:1136
  934.4 10.9 %all-gather.4 = bf16[768,512]{1,0:T(8,128)(2,1)S(1)} all-gather(bf16[192,512]{1,0:T(8,128)(2,1)S(1)} %get-tuple-element.237), channel_id=6, replica_groups=mesh['grp'=4,'seq'=8] {'grp'}, dimensions={0}, use_global_device_ids=true | all-gather | bytes 983040 | tf_op jit(solution)/shard_map/all_gather | solution.py:1129
  946.1 12.0 %all-gather.5 = bf16[768,512]{1,0:T(8,128)(2,1)S(1)} all-gather(bf16[192,512]{1,0:T(8,128)(2,1)S(1)} %get-tuple-element.238), channel_id=7, replica_groups=mesh['grp'=4,'seq'=8] {'grp'}, dimensions={0}, use_global_device_ids=true | all-gather | bytes 983040 | tf_op jit(solution)/shard_map/all_gather | solution.py:1129
  968.5 5.5 multiply_reduce_fusion
  (436 shorter events, 215.3 us)
Async XLA Ops:
  7.2 121.8 %all-gather.21.cloned.1.call-start = ((), (), s32[]{:S(2)}) async-start(), calls=%async_computation.8 | async-start | bytes 4423680 | tf_op jit(solution)/shard_map/all_gather | solution.py:670
  9.6 159.4 %all-gather.15.cloned.1.call-start = ((), (), s32[]{:S(2)}) async-start(), calls=%async_computation.2 | async-start | bytes 1179648 | tf_op jit(solution)/shard_map/all_gather | solution.py:971
  10.3 259.5 %all-gather.17.cloned.1.call-start = ((), (), s32[]{:S(2)}) async-start(), calls=%async_computation.3 | async-start | bytes 6488064 | tf_op jit(solution)/shard_map/all_gather | solution.py:525
  12.0 350.9 %all-gather.19.cloned.1.call-start = ((), (), s32[]{:S(2)}) async-start(), calls=%async_computation.4 | async-start | bytes 14598144 | tf_op jit(solution)/shard_map/all_gather | solution.py:525
  12.9 504.1 %reduce-scatter.3.cloned.1.call-start = ((), (), s32[]{:S(2)}) async-start(), calls=%async_computation.5 | async-start | bytes 15925248 | tf_op jit(solution)/shard_map/reduce_scatter | solution.py:1022
  14.0 22.2 %collective-permute-start = (bf16[192,1024]{1,0:T(8,128)(2,1)S(1)}, bf16[192,1024]{1,0:T(8,128)(2,1)S(1)}, u32[]{:S(2)}, u32[]{:S(2)}) collective-permute-start(bf16[192,1024]{1,0:T(8,128)(2,1)S(1)} %constant_dynamic-slice_fusion.15), channel_id=1, source_target_pairs={{0,6},{1,7},{2,0},{3,1},{4,2},{5,3},{6,4},{7,5},{8,14},{9,15},{10,... | collective-permute-start | bytes 1179656 | tf_op jit(solution)/shard_map/ppermute | solution.py:676
  14.5 64.3 %collective-permute-start.1 = (bf16[192,1024]{1,0:T(8,128)(2,1)S(1)}, bf16[192,1024]{1,0:T(8,128)(2,1)S(1)}, u32[]{:S(2)}, u32[]{:S(2)}) collective-permute-start(bf16[192,1024]{1,0:T(8,128)(2,1)S(1)} %constant_dynamic-slice_fusion.15), channel_id=1, source_target_pairs={{0,4},{1,5},{2,6},{3,7},{4,0},{5,1},{6,2},{7,3},{8,12},{9,13},{10,... | collective-permute-start | bytes 1179656 | tf_op jit(solution)/shard_map/ppermute | solution.py:676
  18.0 74.0 %collective-permute-start.2 = (bf16[192,1024]{1,0:T(8,128)(2,1)S(1)}, bf16[192,1024]{1,0:T(8,128)(2,1)S(1)}, u32[]{:S(2)}, u32[]{:S(2)}) collective-permute-start(bf16[192,1024]{1,0:T(8,128)(2,1)S(1)} %constant_dynamic-slice_fusion.15), channel_id=1, source_target_pairs={{0,2},{1,3},{2,4},{3,5},{4,6},{5,7},{6,0},{7,1},{8,10},{9,11},{10,... | collective-permute-start | bytes 1179656 | tf_op jit(solution)/shard_map/ppermute | solution.py:676
  92.0 23.0 %collective-permute-start.4 = (bf16[576,1024]{1,0:T(8,128)(2,1)S(1)}, bf16[576,1024]{1,0:T(8,128)(2,1)S(1)}, u32[]{:S(2)}, u32[]{:S(2)}) collective-permute-start(bf16[576,1024]{1,0:T(8,128)(2,1)S(1)} %constant_dynamic-update-slice_fusion.refs_1_), channel_id=1, source_target_pairs={{0,16},{8,24},{16,0},{24,8},{1,17},{9,25},{17,1},{25,9},{2,18},{10... | collective-permute-start | bytes 3538952 | tf_op jit(solution)/shard_map/ppermute | solution.py:684
  93.6 27.0 %collective-permute-start.3 = (bf16[576,1024]{1,0:T(8,128)(2,1)S(1)}, bf16[576,1024]{1,0:T(8,128)(2,1)}, u32[]{:S(2)}, u32[]{:S(2)}) collective-permute-start(bf16[576,1024]{1,0:T(8,128)(2,1)S(1)} %constant_dynamic-update-slice_fusion.refs_1_), channel_id=1, source_target_pairs={{0,8},{8,0},{16,24},{24,16},{1,9},{9,1},{17,25},{25,17},{2,10},{10... | collective-permute-start | bytes 3538952 | tf_op jit(solution)/shard_map/ppermute | solution.py:683
  94.1 31.4 %collective-permute-start.8 = (bf16[576,1024]{1,0:T(8,128)(2,1)S(1)}, bf16[576,1024]{1,0:T(8,128)(2,1)}, u32[]{:S(2)}, u32[]{:S(2)}) collective-permute-start(bf16[576,1024]{1,0:T(8,128)(2,1)S(1)} %constant_dynamic-update-slice_fusion.refs_1_), channel_id=1, source_target_pairs={{0,1},{1,0},{2,3},{3,2},{4,5},{5,4},{6,7},{7,6},{8,9},{9,8},{10,11... | collective-permute-start | bytes 3538952 | tf_op jit(solution)/shard_map/ppermute | solution.py:701
  94.1 46.7 %collective-permute-start.7 = (bf16[192,4096]{1,0:T(8,128)(2,1)}, bf16[192,4096]{1,0:T(8,128)(2,1)}, u32[]{:S(2)}, u32[]{:S(2)}) collective-permute-start(bf16[192,4096]{1,0:T(8,128)(2,1)} %refs_0_.4), channel_id=1, source_target_pairs={{0,1},{1,0},{2,3},{3,2},{4,5},{5,4},{6,7},{7,6},{8,9},{9,8},{10,11... | collective-permute-start | bytes 4718600 | tf_op jit(solution)/shard_map/ppermute | solution.py:701
  115.8 25.9 %collective-permute-start.10 = (bf16[576,1024]{1,0:T(8,128)(2,1)S(1)}, bf16[576,1024]{1,0:T(8,128)(2,1)}, u32[]{:S(2)}, u32[]{:S(2)}) collective-permute-start(bf16[576,1024]{1,0:T(8,128)(2,1)S(1)} %collective-permute-done.4.refs_3_), channel_id=1, source_target_pairs={{0,1},{1,0},{2,3},{3,2},{4,5},{5,4},{6,7},{7,6},{8,9},{9,8},{10,11... | collective-permute-start | bytes 3538952 | tf_op jit(solution)/shard_map/ppermute | solution.py:701
  125.5 27.9 %collective-permute-start.9 = (bf16[576,1024]{1,0:T(8,128)(2,1)}, bf16[576,1024]{1,0:T(8,128)(2,1)}, u32[]{:S(2)}, u32[]{:S(2)}) collective-permute-start(bf16[576,1024]{1,0:T(8,128)(2,1)} %collective-permute-done.3.refs_2_), channel_id=1, source_target_pairs={{0,1},{1,0},{2,3},{3,2},{4,5},{5,4},{6,7},{7,6},{8,9},{9,8},{10,11... | collective-permute-start | bytes 3538952 | tf_op jit(solution)/shard_map/ppermute | solution.py:701
  140.8 88.4 %collective-permute-start.19 = (bf16[192,9216]{1,0:T(8,128)(2,1)}, bf16[192,9216]{1,0:T(8,128)(2,1)}, u32[]{:S(2)}, u32[]{:S(2)}) collective-permute-start(bf16[192,9216]{1,0:T(8,128)(2,1)} %refs_0_.5), channel_id=1, source_target_pairs={{0,1},{1,0},{2,3},{3,2},{4,5},{5,4},{6,7},{7,6},{8,9},{9,8},{10,11... | collective-permute-start | bytes 10616840 | tf_op jit(solution)/shard_map/ppermute | solution.py:701
  141.3 79.2 %collective-permute-start.16 = (bf16[576,2304]{1,0:T(8,128)(2,1)}, bf16[576,2304]{1,0:T(8,128)(2,1)}, u32[]{:S(2)}, u32[]{:S(2)}) collective-permute-start(bf16[576,2304]{1,0:T(8,128)(2,1)} %pad_maximum_fusion.3.refs_1_), channel_id=1, source_target_pairs={{0,16},{8,24},{16,0},{24,8},{1,17},{9,25},{17,1},{25,9},{2,18},{10... | collective-permute-start | bytes 7962632 | tf_op jit(solution)/shard_map/ppermute | solution.py:684
  141.6 78.9 %collective-permute-start.15 = (bf16[576,2304]{1,0:T(8,128)(2,1)}, bf16[576,2304]{1,0:T(8,128)(2,1)}, u32[]{:S(2)}, u32[]{:S(2)}) collective-permute-start(bf16[576,2304]{1,0:T(8,128)(2,1)} %pad_maximum_fusion.3.refs_1_), channel_id=1, source_target_pairs={{0,8},{8,0},{16,24},{24,16},{1,9},{9,1},{17,25},{25,17},{2,10},{10... | collective-permute-start | bytes 7962632 | tf_op jit(solution)/shard_map/ppermute | solution.py:683
  223.0 46.1 %collective-permute-start.18 = (bf16[288,2304]{1,0:T(8,128)(2,1)}, bf16[288,2304]{1,0:T(8,128)(2,1)}, u32[]{:S(2)}, u32[]{:S(2)}) collective-permute-start(bf16[288,2304]{1,0:T(8,128)(2,1)} %slice.430), channel_id=1, source_target_pairs={{0,16},{8,24},{16,0},{24,8},{1,17},{9,25},{17,1},{25,9},{2,18},{10... | collective-permute-start | bytes 3981320 | tf_op jit(solution)/shard_map/ppermute | solution.py:699
  227.1 42.6 %collective-permute-start.17 = (bf16[288,2304]{1,0:T(8,128)(2,1)}, bf16[288,2304]{1,0:T(8,128)(2,1)}, u32[]{:S(2)}, u32[]{:S(2)}) collective-permute-start(bf16[288,2304]{1,0:T(8,128)(2,1)} %slice.429), channel_id=1, source_target_pairs={{0,8},{8,0},{16,24},{24,16},{1,9},{9,1},{17,25},{25,17},{2,10},{10... | collective-permute-start | bytes 3981320 | tf_op jit(solution)/shard_map/ppermute | solution.py:698
  228.7 60.5 %collective-permute-start.20 = (bf16[576,2304]{1,0:T(8,128)(2,1)}, bf16[576,2304]{1,0:T(8,128)(2,1)}, u32[]{:S(2)}, u32[]{:S(2)}) collective-permute-start(bf16[576,2304]{1,0:T(8,128)(2,1)} %pad_maximum_fusion.3.refs_1_), channel_id=1, source_target_pairs={{0,1},{1,0},{2,3},{3,2},{4,5},{5,4},{6,7},{7,6},{8,9},{9,8},{10,11... | collective-permute-start | bytes 7962632 | tf_op jit(solution)/shard_map/ppermute | solution.py:701
  228.7 60.5 %collective-permute-start.22 = (bf16[576,2304]{1,0:T(8,128)(2,1)}, bf16[576,2304]{1,0:T(8,128)(2,1)}, u32[]{:S(2)}, u32[]{:S(2)}) collective-permute-start(bf16[576,2304]{1,0:T(8,128)(2,1)} %collective-permute-done.16.refs_3_), channel_id=1, source_target_pairs={{0,1},{1,0},{2,3},{3,2},{4,5},{5,4},{6,7},{7,6},{8,9},{9,8},{10,11... | collective-permute-start | bytes 7962632 | tf_op jit(solution)/shard_map/ppermute | solution.py:701
  229.2 60.0 %collective-permute-start.21 = (bf16[576,2304]{1,0:T(8,128)(2,1)}, bf16[576,2304]{1,0:T(8,128)(2,1)}, u32[]{:S(2)}, u32[]{:S(2)}) collective-permute-start(bf16[576,2304]{1,0:T(8,128)(2,1)} %collective-permute-done.15.refs_2_), channel_id=1, source_target_pairs={{0,1},{1,0},{2,3},{3,2},{4,5},{5,4},{6,7},{7,6},{8,9},{9,8},{10,11... | collective-permute-start | bytes 7962632 | tf_op jit(solution)/shard_map/ppermute | solution.py:701
  362.9 280.8 %all-reduce.12.cloned.1.call-start = ((), (), s32[]{:S(2)}) async-start(), calls=%async_computation.6 | async-start | bytes 3538944 | tf_op jit(solution)/shard_map/psum | solution.py:1023
  395.7 27.5 %collective-permute-start.25 = (bf16[768,2304]{1,0:T(8,128)(2,1)}, bf16[768,2304]{1,0:T(8,128)(2,1)}, u32[]{:S(2)}, u32[]{:S(2)}) collective-permute-start(bf16[768,2304]{1,0:T(8,128)(2,1)} %convolution_convert_fusion.4), channel_id=1, source_target_pairs={{0,1},{1,0},{2,3},{3,2},{4,5},{5,4},{6,7},{7,6},{8,9},{9,8},{10,11... | collective-permute-start | bytes 10616840 | tf_op jit(solution)/shard_map/ppermute | solution.py:806
  410.2 178.5 %collective-permute-start.30 = (bf16[768,2304]{1,0:T(8,128)(2,1)}, bf16[768,2304]{1,0:T(8,128)(2,1)}, u32[]{:S(2)}, u32[]{:S(2)}) collective-permute-start(bf16[768,2304]{1,0:T(8,128)(2,1)} %convolution_convert_fusion.1), channel_id=1, source_target_pairs={{0,1},{1,0},{2,3},{3,2},{4,5},{5,4},{6,7},{7,6},{8,9},{9,8},{10,11... | collective-permute-start | bytes 10616840 | tf_op jit(solution)/shard_map/ppermute | solution.py:806
  416.9 72.1 %collective-permute-start.29 = (bf16[768,2304]{1,0:T(8,128)(2,1)}, bf16[768,2304]{1,0:T(8,128)(2,1)}, u32[]{:S(2)}, u32[]{:S(2)}) collective-permute-start(bf16[768,2304]{1,0:T(8,128)(2,1)} %convolution_convert_fusion.2), channel_id=1, source_target_pairs={{0,1},{1,0},{2,3},{3,2},{4,5},{5,4},{6,7},{7,6},{8,9},{9,8},{10,11... | collective-permute-start | bytes 10616840 | tf_op jit(solution)/shard_map/ppermute | solution.py:806
  422.7 55.4 %collective-permute-start.26 = (bf16[768,2304]{1,0:T(8,128)(2,1)}, bf16[768,2304]{1,0:T(8,128)(2,1)}, u32[]{:S(2)}, u32[]{:S(2)}) collective-permute-start(bf16[768,2304]{1,0:T(8,128)(2,1)} %convolution_convert_fusion.3), channel_id=1, source_target_pairs={{0,1},{1,0},{2,3},{3,2},{4,5},{5,4},{6,7},{7,6},{8,9},{9,8},{10,11... | collective-permute-start | bytes 10616840 | tf_op jit(solution)/shard_map/ppermute | solution.py:806
  428.1 50.0 %collective-permute-start.27 = (bf16[384,2304]{1,0:T(8,128)(2,1)}, bf16[384,2304]{1,0:T(8,128)(2,1)S(1)}, u32[]{:S(2)}, u32[]{:S(2)}) collective-permute-start(bf16[384,2304]{1,0:T(8,128)(2,1)} %fusion.43), channel_id=1, source_target_pairs={{0,8},{8,0},{16,24},{24,16},{1,9},{9,1},{17,25},{25,17},{2,10},{10... | collective-permute-start | bytes 5308424 | tf_op jit(solution)/shard_map/ppermute | solution.py:812
  433.2 44.9 %collective-permute-start.28 = (bf16[384,2304]{1,0:T(8,128)(2,1)}, bf16[384,2304]{1,0:T(8,128)(2,1)}, u32[]{:S(2)}, u32[]{:S(2)}) collective-permute-start(bf16[384,2304]{1,0:T(8,128)(2,1)} %fusion.40), channel_id=1, source_target_pairs={{0,16},{8,24},{16,0},{24,8},{1,17},{9,25},{17,1},{25,9},{2,18},{10... | collective-permute-start | bytes 5308424 | tf_op jit(solution)/shard_map/ppermute | solution.py:813
  487.3 98.5 %collective-permute-start.31 = (bf16[768,2304]{1,0:T(8,128)(2,1)}, bf16[768,2304]{1,0:T(8,128)(2,1)}, u32[]{:S(2)}, u32[]{:S(2)}) collective-permute-start(bf16[768,2304]{1,0:T(8,128)(2,1)} %add_convert_fusion.2), channel_id=1, source_target_pairs={{0,8},{8,0},{16,24},{24,16},{1,9},{9,1},{17,25},{25,17},{2,10},{10... | collective-permute-start | bytes 10616840 | tf_op jit(solution)/shard_map/ppermute | solution.py:833
  498.4 89.3 %collective-permute-start.32 = (bf16[768,2304]{1,0:T(8,128)(2,1)}, bf16[768,2304]{1,0:T(8,128)(2,1)}, u32[]{:S(2)}, u32[]{:S(2)}) collective-permute-start(bf16[768,2304]{1,0:T(8,128)(2,1)} %add_convert_fusion.1), channel_id=1, source_target_pairs={{0,16},{8,24},{16,0},{24,8},{1,17},{9,25},{17,1},{25,9},{2,18},{10... | collective-permute-start | bytes 10616840 | tf_op jit(solution)/shard_map/ppermute | solution.py:834
  547.9 21.7 %collective-permute-start.33 = (bf16[1024,1536]{1,0:T(8,128)(2,1)}, bf16[1024,1536]{1,0:T(8,128)(2,1)}, u32[]{:S(2)}, u32[]{:S(2)}) collective-permute-start(bf16[1024,1536]{1,0:T(8,128)(2,1)} %convolution_convert_fusion.5), channel_id=1, source_target_pairs={{0,1},{1,0},{2,3},{3,2},{4,5},{5,4},{6,7},{7,6},{8,9},{9,8},{10,11... | collective-permute-start | bytes 9437192 | tf_op jit(solution)/shard_map/ppermute | solution.py:802
  554.8 23.2 %collective-permute-start.34 = (bf16[768,2048]{1,0:T(8,128)(2,1)}, bf16[768,2048]{1,0:T(8,128)(2,1)}, u32[]{:S(2)}, u32[]{:S(2)}) collective-permute-start(bf16[768,2048]{1,0:T(8,128)(2,1)} %convolution_convert_fusion.7), channel_id=1, source_target_pairs={{0,1},{1,0},{2,3},{3,2},{4,5},{5,4},{6,7},{7,6},{8,9},{9,8},{10,11... | collective-permute-start | bytes 9437192 | tf_op jit(solution)/shard_map/ppermute | solution.py:802
  569.5 255.6 %reduce-scatter.5.cloned.1.call-start = ((), (), s32[]{:S(2)}) async-start(), calls=%async_computation.7 | async-start | bytes 1216512 | tf_op jit(solution)/shard_map/reduce_scatter | solution.py:1109
  577.8 129.0 %collective-permute-start.37 = (bf16[512,384]{1,0:T(8,128)(2,1)}, bf16[512,384]{1,0:T(8,128)(2,1)}, u32[]{:S(2)}, u32[]{:S(2)}) collective-permute-start(bf16[512,384]{1,0:T(8,128)(2,1)} %get-tuple-element.225), channel_id=1, source_target_pairs={{0,16},{8,24},{16,0},{24,8},{1,17},{9,25},{17,1},{25,9},{2,18},{10... | collective-permute-start | bytes 1179656 | tf_op jit(solution)/shard_map/ppermute | solution.py:813
  578.0 128.8 %collective-permute-start.36 = (bf16[512,384]{1,0:T(8,128)(2,1)}, bf16[512,384]{1,0:T(8,128)(2,1)}, u32[]{:S(2)}, u32[]{:S(2)}) collective-permute-start(bf16[512,384]{1,0:T(8,128)(2,1)} %get-tuple-element.226), channel_id=1, source_target_pairs={{0,8},{8,0},{16,24},{24,16},{1,9},{9,1},{17,25},{25,17},{2,10},{10... | collective-permute-start | bytes 1179656 | tf_op jit(solution)/shard_map/ppermute | solution.py:812
  585.8 117.7 %collective-permute-start.39 = (bf16[384,512]{1,0:T(8,128)(2,1)}, bf16[384,512]{1,0:T(8,128)(2,1)}, u32[]{:S(2)}, u32[]{:S(2)}) collective-permute-start(bf16[384,512]{1,0:T(8,128)(2,1)} %get-tuple-element.223), channel_id=1, source_target_pairs={{0,16},{8,24},{16,0},{24,8},{1,17},{9,25},{17,1},{25,9},{2,18},{10... | collective-permute-start | bytes 1179656 | tf_op jit(solution)/shard_map/ppermute | solution.py:813
  587.6 119.1 %collective-permute-start.38 = (bf16[384,512]{1,0:T(8,128)(2,1)}, bf16[384,512]{1,0:T(8,128)(2,1)}, u32[]{:S(2)}, u32[]{:S(2)}) collective-permute-start(bf16[384,512]{1,0:T(8,128)(2,1)} %get-tuple-element.224), channel_id=1, source_target_pairs={{0,8},{8,0},{16,24},{24,16},{1,9},{9,1},{17,25},{25,17},{2,10},{10... | collective-permute-start | bytes 1179656 | tf_op jit(solution)/shard_map/ppermute | solution.py:812
  701.3 261.2 %all-gather.23.cloned.1.call-start = ((), (), s32[]{:S(2)}) async-start(), calls=%async_computation.9 | async-start | bytes 4423680 | tf_op jit(solution)/shard_map/all_gather | solution.py:882
  701.3 31.9 %collective-permute-start.57 = (bf16[192,2304]{1,0:T(8,128)(2,1)}, bf16[192,2304]{1,0:T(8,128)(2,1)S(1)}, u32[]{:S(2)}, u32[]{:S(2)}) collective-permute-start(bf16[192,2304]{1,0:T(8,128)(2,1)} %get-tuple-element.209), channel_id=1, source_target_pairs={{0,6},{1,7},{2,0},{3,1},{4,2},{5,3},{6,4},{7,5},{8,14},{9,15},{10,... | collective-permute-start | bytes 2654216 | tf_op jit(solution)/shard_map/ppermute | solution.py:852
  703.5 78.8 %collective-permute-start.56 = (bf16[192,2304]{1,0:T(8,128)(2,1)}, bf16[192,2304]{1,0:T(8,128)(2,1)S(1)}, u32[]{:S(2)}, u32[]{:S(2)}) collective-permute-start(bf16[192,2304]{1,0:T(8,128)(2,1)} %get-tuple-element.210), channel_id=1, source_target_pairs={{0,4},{1,5},{2,6},{3,7},{4,0},{5,1},{6,2},{7,3},{8,12},{9,13},{10,... | collective-permute-start | bytes 2654216 | tf_op jit(solution)/shard_map/ppermute | solution.py:852
  706.8 79.2 %collective-permute-start.55 = (bf16[192,2304]{1,0:T(8,128)(2,1)S(1)}, bf16[192,2304]{1,0:T(8,128)(2,1)S(1)}, u32[]{:S(2)}, u32[]{:S(2)}) collective-permute-start(bf16[192,2304]{1,0:T(8,128)(2,1)S(1)} %copy-done.68), channel_id=1, source_target_pairs={{0,2},{1,3},{2,4},{3,5},{4,6},{5,7},{6,0},{7,1},{8,10},{9,11},{10,... | collective-permute-start | bytes 2654216 | tf_op jit(solution)/shard_map/ppermute | solution.py:852
  730.0 120.5 %collective-permute-start.40 = (bf16[768,2048]{1,0:T(8,128)(2,1)}, bf16[768,2048]{1,0:T(8,128)(2,1)}, u32[]{:S(2)}, u32[]{:S(2)}) collective-permute-start(bf16[768,2048]{1,0:T(8,128)(2,1)} %convolution_convert_fusion.6), channel_id=1, source_target_pairs={{0,1},{1,0},{2,3},{3,2},{4,5},{5,4},{6,7},{7,6},{8,9},{9,8},{10,11... | collective-permute-start | bytes 9437192 | tf_op jit(solution)/shard_map/ppermute | solution.py:802
  732.7 75.1 %collective-permute-start.48 = (bf16[768,512]{1,0:T(8,128)(2,1)}, bf16[768,512]{1,0:T(8,128)(2,1)S(1)}, u32[]{:S(2)}, u32[]{:S(2)}) collective-permute-start(bf16[768,512]{1,0:T(8,128)(2,1)} %get-tuple-element.219), channel_id=1, source_target_pairs={{0,16},{8,24},{16,0},{24,8},{1,17},{9,25},{17,1},{25,9},{2,18},{10... | collective-permute-start | bytes 2359304 | tf_op jit(solution)/shard_map/ppermute | solution.py:834
  733.3 76.5 %collective-permute-start.47 = (bf16[768,512]{1,0:T(8,128)(2,1)}, bf16[768,512]{1,0:T(8,128)(2,1)S(1)}, u32[]{:S(2)}, u32[]{:S(2)}) collective-permute-start(bf16[768,512]{1,0:T(8,128)(2,1)} %get-tuple-element.220), channel_id=1, source_target_pairs={{0,8},{8,0},{16,24},{24,16},{1,9},{9,1},{17,25},{25,17},{2,10},{10... | collective-permute-start | bytes 2359304 | tf_op jit(solution)/shard_map/ppermute | solution.py:833
  901.6 28.9 %collective-permute-start.49 = (bf16[192,1024]{1,0:T(8,128)(2,1)S(1)}, bf16[192,1024]{1,0:T(8,128)(2,1)S(1)}, u32[]{:S(2)}, u32[]{:S(2)}) collective-permute-start(bf16[192,1024]{1,0:T(8,128)(2,1)S(1)} %get-tuple-element.231), channel_id=1, source_target_pairs={{0,2},{1,3},{2,4},{3,5},{4,6},{5,7},{6,0},{7,1},{8,10},{9,11},{10,... | collective-permute-start | bytes 1179656 | tf_op jit(solution)/shard_map/ppermute | solution.py:852
  901.7 28.8 %collective-permute-start.51 = (bf16[192,1024]{1,0:T(8,128)(2,1)S(1)}, bf16[192,1024]{1,0:T(8,128)(2,1)S(1)}, u32[]{:S(2)}, u32[]{:S(2)}) collective-permute-start(bf16[192,1024]{1,0:T(8,128)(2,1)S(1)} %get-tuple-element.232), channel_id=1, source_target_pairs={{0,6},{1,7},{2,0},{3,1},{4,2},{5,3},{6,4},{7,5},{8,14},{9,15},{10,... | collective-permute-start | bytes 1179656 | tf_op jit(solution)/shard_map/ppermute | solution.py:852
  903.9 30.2 %collective-permute-start.50 = (bf16[192,1024]{1,0:T(8,128)(2,1)S(1)}, bf16[192,1024]{1,0:T(8,128)(2,1)S(1)}, u32[]{:S(2)}, u32[]{:S(2)}) collective-permute-start(bf16[192,1024]{1,0:T(8,128)(2,1)S(1)} %get-tuple-element.233), channel_id=1, source_target_pairs={{0,4},{1,5},{2,6},{3,7},{4,0},{5,1},{6,2},{7,3},{8,12},{9,13},{10,... | collective-permute-start | bytes 1179656 | tf_op jit(solution)/shard_map/ppermute | solution.py:852
  (108 other events, 1867.7 us)
Sparse Core Ops, SparseCore 0:
  10.2 95.4 all-gather.20
  107.3 26.0 all-gather.14
  136.8 85.7 all-gather.16
  225.3 110.0 all-gather.18
  363.0 142.8 reduce-scatter.2
  569.6 73.9 all-reduce.11
  701.4 118.8 reduce-scatter.4
  822.1 66.4 all-gather.22

commit v8 on v7

--- a/solution.py
+++ b/solution.py
@@ -654,7 +654,7 @@
 
 
 class Gather:
-    def __init__(self, shard, offload=False):
+    def __init__(self, shard, *after, offload=False):
         self.shard = shard
         self.chips = lax.axis_size("seq") // 2
         half = (self.chips - 1) * shard.shape[0] // 2
@@ -665,6 +665,8 @@
         group = lax.axis_index("grp")
         width = shard.shape[1] // 4
         own = lax.dynamic_slice_in_dim(shard, group * width, width, 1)
+        if after:
+            own = tie(own, *after)
         others = range(1, self.chips)
         if offload:
             slabs = lax.all_gather(own, "seq", axis_index_groups=same_cores())
@@ -964,11 +966,11 @@
         small_all[:, 2 * n_gain + n_lru :].reshape(-1, CONV, n_lru).transpose(1, 0, 2)
     ).reshape(CONV, LRU).astype(F32)
     in_gather = Gather(in_proj)
-    up_gather = Gather(up_proj, offload=True)
-    in_gather.first()
+    near = in_gather.first()
     in_gather.second()
     in_gather.third()
     gates_all = lax.all_gather(gate_heads, "seq", axis=0, tiled=True)
+    up_gather = Gather(up_proj, gates_all, *near, offload=True)
     proj_out = gather_rows(out_proj)
     proj_down = gather_rows(down_proj)
 
@@ -1019,8 +1021,8 @@
 
     grad_out = cotangent.reshape(row_count, D)
     grad_down = dot_rows(hidden, grad_out).astype(BF16)
-    down_part = lax.psum_scatter(grad_down, "seq", scatter_dimension=0, tiled=True)
-    down_sum = lax.psum(down_part, "grp")
+    down_part = lax.psum_scatter(grad_down, ("seq", "grp"), scatter_dimension=0, tiled=True)
+    down_sum = lax.all_gather(down_part, "grp", axis=0, tiled=True)
     grad_expanded = ffn_backward(tie(grad_out, grad_down), proj_down, pull)
     quarter = FF // 2
 
@@ -1067,8 +1069,8 @@
         True,
     )
     sent = (*out_sum.sent, *in_gate_sum.sent)
-    sent = up_sum.third(*sent)
-    local = tie(local, down_sum, *sent)
+    sent = up_sum.third(down_sum, *sent, offload=True)
+    local = tie(local, *sent)
     du, tail, edge, grad_gates, grad_taps, grad_decay = mixer_backward(
         local, rev_prod, rev_carries, state, carries, conv_low, inner_low,
         prev_inner, dist, gates_all, taps_all, soft,
@@ -1091,7 +1093,7 @@
         width,
         True,
     )
-    grad_inner = tie(grad_inner, *in_value_sum.sent, *out_sum.third())
+    grad_inner = tie(grad_inner, *in_value_sum.sent)
 
     shards = last + 1
     grad_decay_row = grad_decay[0] * jax.nn.sigmoid(-decay_float)
@@ -1107,6 +1109,9 @@
     whole = 16 * lax.axis_size("grp")
     flat = jnp.pad(flat, ((0, 0), (0, -lines % whole), (0, 0))).astype(BF16).reshape(-1, HS)
     flat = lax.psum_scatter(flat, ("seq", "grp"), scatter_dimension=0, tiled=True)
+    first_grad = first_grad + dot_far(grad_inner, in_value)
+    sent = in_value_sum.second(first_grad)
+    out_sum.third(*sent)
     flat, (out_total,) = gather_parts(flat, [out_sum])
     flat = flat[:lines].astype(F32).reshape(-1)
     n_gates = flat.shape[0] - (CONV + 1) * n_lru
@@ -1114,8 +1119,6 @@
     taps_total = flat[n_gates : n_gates + CONV * n_lru].reshape(CONV, n_lru)
     decay_total = flat[n_gates + CONV * n_lru :]
 
-    first_grad = first_grad + dot_far(grad_inner, in_value)
-    sent = in_value_sum.second(first_grad)
     up_total = up_sum.finish(edge)
     down_total = down_sum.astype(F32)
     if in_value_sum.simple:

time: 989 us -> 952 us (0.963)
  waiting for transfers between devices: 251 us -> 200 us
    reduce_scatter x1 -> x2, waiting for transfers between devices: 0.01 us -> 66.2 us  [the longest x1 66.2 us: body(): lax.psum_scatter(grad_down, ('seq', 'grp'), scatter_dimension=0, tiled=True)]
    ppermute x9 -> x6, waiting for transfers between devices: 68.6 us -> 15.3 us  [along_z(): lax.ppermute(part, 'seq', ring_pairs(2 * j + 2))]
    psum x1 -> x0, waiting for transfers between devices: 41.5 us -> none  [body(): down_sum = lax.psum(down_part, 'grp')]
    ppermute x3, waiting for transfers between devices: 73.9 us -> 35 us  [__init__(): slabs = [lax.ppermute(own, 'seq', ring_pairs(-2 * j)) for j in others]]
    reduce_scatter x1, waiting for transfers between devices: 0.02 us -> 29 us  [body(): lax.psum_scatter(flat, ('seq', 'grp'), scatter_dimension=0, tiled=True)]
    all_gather x1, waiting for transfers between devices: 0.01 us -> 27.8 us  [__init__(): slabs = lax.all_gather(own, 'seq', axis_index_groups=same_cores())]
    ppermute x4, waiting for transfers between devices: 28 us -> 7.99 us  [second(): self.from_y = lax.ppermute(sent[1], 'grp', self.y)]
    unnamed x192 -> x191, local copies, waits for them, and re-layouts: 41.3 us -> 41.5 us
  transfers between devices with their start and end apart: 66 -> 64, of which waited for: 21 -> 14; matrix products, arithmetic and copies ran while one was open for 33% -> 36% of each run, Pallas kernels for 21% -> 22%
where the time goes in v8:
time: 952 us; the launch traced here: 942 us
  matrix products  240 us (25%)
  Pallas kernels  211 us (22%)
  waiting for transfers between devices  200 us (21%)
  local copies, waits for them, and re-layouts  93.8 us (10%)
  blocking collectives  82.6 us (9%)
  starting transfers between devices  53.2 us (6%)
  other arithmetic  45.9 us (5%)
  between operations  15.8 us (2%)
    dot_general x16, matrix products, dot_rows(): lax.dot_general(a, b, (((0,), (0,)), ((), ())), preferred_element_type=F32)  135 us
    dot_general x5, matrix products, dot_far(): lax.dot_general(a, b, (((1,), (1,)), ((), ())), preferred_element_type=F32)  73 us
    reduce_scatter x1, waiting for transfers between devices, body(): lax.psum_scatter(grad_down, ('seq', 'grp'), scatter_dimension=0, tiled=True)  66.2 us
    pallas_call x3, Pallas kernels, call(): pl.pallas_call(kernel, grid=(steps,), in_specs=[pl.BlockSpec(memory_space...  65.9 us
    pallas_call x1, Pallas kernels, mixer_backward(): pl.pallas_call(mixer_backward_kernel, grid=(HEADS,), in_specs=[full, full...  47.2 us
    unnamed x191, local copies, waits for them, and re-layouts  41.5 us
    ppermute x3, waiting for transfers between devices, __init__(): slabs = [lax.ppermute(own, 'seq', ring_pairs(-2 * j)) for j in others]  35 us
    reduce_scatter x1, waiting for transfers between devices, body(): lax.psum_scatter(flat, ('seq', 'grp'), scatter_dimension=0, tiled=True)  29 us
  transfers between devices with their start and end apart: 64, of which 14 were waited for; matrix products, arithmetic and copies ran while one was open for 36% of the time, Pallas kernels for 22%

profile of v8, /device:TPU:18, one launch (start us, length us, event | category | flops | bytes accessed | tf_op | source)
XLA Modules:
  0.0 942.2 jit_solution(16359263694027147174)
XLA Ops:
  16.1 7.5 collective-permute-done
  25.4 27.5 %collective-permute-done.1 = bf16[192,1024]{1,0:T(8,128)(2,1)} collective-permute-done((bf16[192,1024]{1,0:T(8,128)(2,1)}, bf16[192,1024]{1,0:T(8,128)(2,1)}, u32[]{:S(2)}, u32[]{:S(2)}) %collective-permute-start.1) | collective-permute-done | bytes 393248 | tf_op jit(solution)/shard_map/ppermute | solution.py:678
  61.8 15.9 %all-gather.8 = bf16[8,1,1664]{2,1,0:T(2,128)(2,1)S(1)} all-gather(bf16[1,1,1664]{2,1,0:T(2,128)(2,1)S(1)} %reshape.2484), channel_id=2, replica_groups=mesh['grp'=4,'seq'=8] {'seq'}, dimensions={0}, use_global_device_ids=true | all-gather | bytes 29952 | tf_op jit(solution)/shard_map/all_gather | solution.py:960
  78.4 7.8 collective-permute-done.4.refs_3_
  100.8 27.8 %all-gather.24.cloned.1.call-done = bf16[768,2304]{1,0:T(8,128)(2,1)} async-done(((bf16[192,2304]{1,0:T(8,128)(2,1)}), bf16[768,2304]{1,0:T(8,128)(2,1)}) %all-gather.24.cloned.1.call-update) | async-done | bytes 3538960 | tf_op jit(solution)/shard_map/all_gather | solution.py:672
  147.6 12.0 %gathered_dot.2 = (bf16[1024,2048]{1,0:T(8,128)(2,1)}, bf16[1536,2048]{1,0:T(8,128)(2,1)}) custom-call(s32[3]{0:T(128)} %pad_add_fusion.1.where_ref, bf16[1024,1536]{1,0:T(8,128)(2,1)} %copy-done.9, bf16[192,4096]{1,0:T(8,128)(2,1)} %refs_0_.4, bf16[576,1024]{1,0:T(8,128)(2,1)} %constant_dynamic-update-slice_fusion.refs_1_, ...), custom_call_target="tpu_custom_call" | custom-call | tf_op jit(solution)/shard_map/gathered_dot/pallas_call | solution.py:711
  169.6 28.0 %mixer_forward.1 = (bf16[2,512,2048]{2,1,0:T(8,128)(2,1)S(1)}, f32[2,512,2048]{2,1,0:T(8,128)}, f32[2,512,2048]{2,1,0:T(8,128)}, f32[2,512,2048]{2,1,0:T(8,128)}, f32[2,2,8,2048]{3,2,1,0:T(8,128)S(1)}) custom-call(bf16[2,512,2048]{2,1,0:T(8,128)(2,1)S(1)} %bitcast.780, bf16[2,8,2048]{2,1,0:T(8,128)(2,1)S(1)} %collective-permute-done.13.halo_ref, ...), custom_call_target="tpu_custom_call" | custom-call | tf_op jit(solution)/shard_map/mixer_forward/pallas_call | solution.py:322
  200.1 13.4 %all-gather.2 = f32[16,2,2048]{2,1,0:T(2,128)S(1)} all-gather(f32[2,2,2048]{2,1,0:T(2,128)S(1)} %copy.313), channel_id=4, replica_groups=mesh['grp'=4,'seq'=8] {'seq'}, dimensions={0}, use_global_device_ids=true | all-gather | bytes 294912 | tf_op jit(solution)/shard_map/all_gather | solution.py:909
  220.4 5.3 copy.328
  225.7 12.7 %gathered_dot.3 = (f32[1024,2048]{1,0:T(8,128)}, bf16[1536,2048]{1,0:T(8,128)(2,1)}) custom-call(s32[3]{0:T(128)} %pad_add_fusion.1.where_ref, bf16[1024,1536]{1,0:T(8,128)(2,1)} %copy-done.9, bf16[192,4096]{1,0:T(8,128)(2,1)} %refs_0_.4, bf16[576,1024]{1,0:T(8,128)(2,1)} %constant_dynamic-update-slice_fusion.refs_1_, ...), custom_call_target="tpu_custom_call" | custom-call | tf_op jit(solution)/shard_map/gathered_dot/pallas_call | solution.py:711
  238.4 17.9 %mixer_branch.1 = (f32[2,512,2048]{2,1,0:T(8,128)}, bf16[2,512,2048]{2,1,0:T(8,128)(2,1)S(1)}, bf16[2,2,512,1024]{3,2,1,0:T(8,128)(2,1)S(1)}) custom-call(s32[1]{0:T(128)} %bitcast.3.core_ref, f32[2,512,2048]{2,1,0:T(8,128)} %get-tuple-element.82.state_ref, f32[2,512,2048]{2,1,0:T(8,128)} %get-tuple-element.83.prod_ref, ...), custom_call_target="tpu_custom_call" | custom-call | tf_op jit(solution)/shard_map/mixer_branch/pallas_call | solution.py:364
  261.0 10.5 %convert_add_fusion.x_ref = f32[1024,1536]{1,0:T(8,128)S(1)} fusion(bf16[1024,1536]{1,0:T(8,128)(2,1)} %bitcast.775, bf16[1024,2048]{1,0:T(8,128)(2,1)} %bitcast.787, bf16[2048,1536]{1,0:T(8,128)(2,1)} %all-gather.18.cloned.1.call-done), kind=kOutput, calls=%fused_computation.3 | convolution fusion | flops 6445596672 | bytes 19922944 | tf_op jit(solution)/shard_map/dot_general | solution.py:1012
  278.8 41.1 %gathered_ffn.1 = (bf16[1024,4608]{1,0:T(8,128)(2,1)}, bf16[2,1024,4608]{2,1,0:T(8,128)(2,1)}, bf16[1536,4608]{1,0:T(8,128)(2,1)}, bf16[1536,4608]{1,0:T(8,128)(2,1)}) custom-call(s32[3]{0:T(128)} %pad_add_fusion.1.where_ref, bf16[1024,1536]{1,0:T(8,128)(2,1)} %copy-done.22, bf16[192,9216]{1,0:T(8,128)(2,1)} %refs_0_.5, ...), custom_call_target="tpu_custom_call" | custom-call | tf_op jit(solution)/shard_map/gathered_ffn/pallas_call | solution.py:711
  319.9 31.8 %convolution_convert_fusion = bf16[4608,1536]{1,0:T(8,128)(2,1)} fusion(bf16[1024,4608]{1,0:T(8,128)(2,1)} %get-tuple-element.129, bf16[1024,1536]{1,0:T(8,128)(2,1)S(1)} %bitcast.776), kind=kOutput, calls=%fused_computation | convolution fusion | flops 14502592512 | bytes 26738688 | tf_op jit(solution)/shard_map/dot_general | solution.py:547
  353.8 25.8 %ffn_backward.1 = bf16[2,1024,4608]{2,1,0:T(8,128)(2,1)} custom-call(bf16[1024,1536]{1,0:T(8,128)(2,1)S(1)} %bitcast.777, bf16[4608,1536]{1,0:T(8,128)(2,1)} %all-gather.20.cloned.1.call-done.down_ref, bf16[2,1024,4608]{2,1,0:T(8,128)(2,1)} %get-tuple-element.91.pull_ref), custom_call_target="tpu_custom_call" | custom-call | tf_op jit(solution)/shard_map/ffn_backward/pallas_call | solution.py:506
  379.6 7.9 convolution_convert_fusion.4
  389.8 5.1 fusion.188
  395.2 8.1 convolution_convert_fusion.1
  405.5 5.3 convolution_convert_fusion.2
  410.8 5.8 convolution_convert_fusion.3
  417.1 5.3 fusion.43
  422.8 4.8 fusion.40
  428.9 18.9 %fusion = f32[1024,1536]{1,0:T(8,128)S(1)} fusion(bf16[1536,4608]{1,0:T(8,128)(2,1)} %get-tuple-element.96, bf16[2,1024,4608]{2,1,0:T(8,128)(2,1)} %ffn_backward.1), kind=kOutput, calls=%fused_computation.4 | convolution fusion | flops 14495514624 | bytes 29884416 | tf_op jit(solution)/shard_map/dot_general | solution.py:557
  447.7 22.1 %fusion.25 = f32[1024,1536]{1,0:T(8,128)} fusion(f32[1024,1536]{1,0:T(8,128)S(1)} %fusion, bf16[1536,4608]{1,0:T(8,128)(2,1)} %get-tuple-element.95, bf16[2,1024,4608]{2,1,0:T(8,128)(2,1)} %ffn_backward.1), kind=kOutput, calls=%fused_computation.44 | convolution fusion | flops 14497087488 | bytes 36175872 | tf_op jit(solution)/shard_map/dot_general | solution.py:557
  469.8 66.2 %reduce-scatter.4.cloned.1.call-done = bf16[144,1536]{1,0:T(8,128)(2,1)} async-done(((bf16[4608,1536]{1,0:T(8,128)(2,1)}), bf16[144,1536]{1,0:T(8,128)(2,1)}) %reduce-scatter.4.cloned.1.call-update) | async-done | bytes 442384 | tf_op jit(solution)/shard_map/reduce_scatter | solution.py:1024
  536.2 9.1 add_convert_fusion.2
  546.0 9.9 %add_convert_fusion.1 = bf16[768,2304]{1,0:T(8,128)(2,1)} fusion(bf16[768,2304]{1,0:T(8,128)(2,1)} %collective-permute-done.29, bf16[1024,768]{1,0:T(8,128)(2,1)S(1)} %get-tuple-element.92, bf16[2,1024,4608]{2,1,0:T(8,128)(2,1)} %ffn_backward.1, s32[]{:T(128)S(6)} %select_n.801, s32[]{:T(128)S(6)} %select_n.803, bf16[384,2304]{1,0:T(8,128)(2,1)} %collective-permute-done.27), kind=kOutput, calls=%fused_computation.13 | convolution fusion | flops 3632726016 | bytes 15138824 | tf_op jit(solution)/shard_map/dot_general | solution.py:547
  562.0 10.9 %fusion.196 = f32[1024,2048]{1,0:T(8,128)} fusion(bf16[1024,1536]{1,0:T(8,128)(2,1)S(1)} %get-tuple-element.106, bf16[2048,1536]{1,0:T(8,128)(2,1)} %all-gather.18.cloned.1.call-done), kind=kOutput, calls=%fused_computation.345 | convolution fusion | flops 6442450944 | bytes 17825792 | tf_op jit(solution)/shard_map/dot_general | solution.py:557
  572.9 22.0 %mixer_reverse.1 = (bf16[2,512,2048]{2,1,0:T(8,128)(2,1)S(1)}, f32[2,512,2048]{2,1,0:T(8,128)S(1)}, f32[2,512,2048]{2,1,0:T(8,128)}, f32[2,2,8,2048]{3,2,1,0:T(8,128)S(1)}) custom-call(f32[2,512,2048]{2,1,0:T(8,128)} %bitcast.797, f32[2,512,2048]{2,1,0:T(8,128)} %bitcast.789, f32[2,512,2048]{2,1,0:T(8,128)} %get-tuple-element.101.keep_ref, ...), custom_call_target="tpu_custom_call" | custom-call | tf_op jit(solution)/shard_map/mixer_reverse/pallas_call | solution.py:386
  598.0 5.5 convolution_convert_fusion.5
  604.9 5.5 convolution_convert_fusion.7
  610.9 13.4 %all-gather.3 = f32[16,2,2048]{2,1,0:T(2,128)S(1)} all-gather(f32[2,2,2048]{2,1,0:T(2,128)S(1)} %copy.345), channel_id=5, replica_groups=mesh['grp'=4,'seq'=8] {'seq'}, dimensions={0}, use_global_device_ids=true | all-gather | bytes 294912 | tf_op jit(solution)/shard_map/all_gather | solution.py:909
  624.8 7.1 add_convert_fusion.6
  636.7 5.6 add_convert_fusion.5
  646.2 11.4 %add_convert_fusion = bf16[768,2304]{1,0:T(8,128)(2,1)} fusion(bf16[768,2304]{1,0:T(8,128)(2,1)} %collective-permute-done.32, bf16[768,2304]{1,0:T(8,128)(2,1)} %collective-permute-done.31, bf16[768,2304]{1,0:T(8,128)(2,1)} %collective-permute-done.30, bf16[1024,768]{1,0:T(8,128)(2,1)S(1)} %get-tuple-element.92, bf16[2,1024,4608]{2,1,0:T(8,128)(2,1)} %ffn_backward.1, ...), kind=kOutput, calls=%fused_computation.12 | convolution fusion | flops 3636264960 | bytes 20447240 | tf_op jit(solution)/shard_map/dot_general | solution.py:547
  660.9 47.2 %mixer_backward.1 = (bf16[2,512,2048]{2,1,0:T(8,128)(2,1)S(1)}, f32[2,32,2048]{2,1,0:T(8,128)S(1)}, f32[2,8,2048]{2,1,0:T(8,128)S(1)}, f32[16,128,256]{2,1,0:T(8...) custom-call(f32[2,512,2048]{2,1,0:T(8,128)} %copy-done.10, f32[2,512,2048]{2,1,0:T(8,128)} %get-tuple-element.112.prod_ref, ...), custom_call_target="tpu_custom_call" | custom-call | tf_op jit(solution)/shard_map/mixer_backward/pallas_call | solution.py:408
  715.7 10.5 %fusion.197 = f32[1024,1536]{1,0:T(8,128)} fusion(bf16[1024,2048]{1,0:T(8,128)(2,1)S(1)} %bitcast.782, bf16[1536,2048]{1,0:T(8,128)(2,1)} %get-tuple-element.123), kind=kOutput, calls=%fused_computation.346 | convolution fusion | flops 6442450944 | bytes 16777216 | tf_op jit(solution)/shard_map/dot_general | solution.py:557
  729.2 5.3 convolution_convert_fusion.6
  748.8 6.9 collective-permute-done.46
  759.1 6.8 add_convert_fusion.4
  767.8 10.6 %fusion.10 = (f32[1024]{0:T(1024)S(1)}, f32[1024,1536]{1,0:T(8,128)S(1)}) fusion(f32[1536]{0:T(1024)S(1)} %reshape.2468, bf16[2,8,64,1536]{3,1,2,0:T(8,128)(2,1)S(1)} %copy-done.4, f32[1024,1536]{1,0:T(8,128)} %fusion.197, bf16[1024,2048]{1,0:T(8,128)(2,1)S(1)} %bitcast.784, bf16[1536,2048]{1,0:T(8,128)(2,1)} %get-tuple-element.126), kind=kOutput, calls=%fused_computation.19 | convolution fusion | flops 6450314240 | bytes 26224640 | tf_op jit(solution)/shard_map/dot_general | solution.py:557
  794.6 21.1 %add_convert_fusion.3 = bf16[1024,1536]{1,0:T(8,128)(2,1)S(1)} fusion(f32[1024,1536]{1,0:T(8,128)} %copy-done.2, bf16[1024,4608]{1,0:T(8,128)(2,1)} %get-tuple-element.129, bf16[4608,1536]{1,0:T(8,128)(2,1)} %all-gather.20.cloned.1.call-done.down_ref), kind=kOutput, calls=%fused_computation.20 | convolution fusion | flops 14498660352 | bytes 33030144 | tf_op jit(solution)/shard_map/dot_general | solution.py:1139
  818.4 29.0 %reduce-scatter.6.cloned.1.call-done = bf16[144,128]{1,0:T(8,128)(2,1)} async-done(((bf16[4608,128]{1,0:T(8,128)(2,1)}), bf16[144,128]{1,0:T(8,128)(2,1)}) %reduce-scatter.6.cloned.1.call-update) | async-done | bytes 36880 | tf_op jit(solution)/shard_map/reduce_scatter | solution.py:1111
  848.2 17.8 %all-gather.6 = bf16[3648,128]{1,0:T(8,128)(2,1)S(1)} all-gather(bf16[912,128]{1,0:T(8,128)(2,1)S(1)} %pad_maximum_fusion.17), channel_id=8, replica_groups=mesh['grp'=4,'seq'=8] {'grp'}, dimensions={0}, use_global_device_ids=true | all-gather | bytes 1167360 | tf_op jit(solution)/shard_map/all_gather | solution.py:895
  883.0 11.8 %collective-permute-done.47 = bf16[192,1024]{1,0:T(8,128)(2,1)} collective-permute-done((bf16[192,1024]{1,0:T(8,128)(2,1)}, bf16[192,1024]{1,0:T(8,128)(2,1)}, u32[]{:S(2)}, u32[]{:S(2)}) %collective-permute-start.47) | collective-permute-done | bytes 393248 | tf_op jit(solution)/shard_map/ppermute | solution.py:854
  899.9 12.0 %all-gather.4 = bf16[768,512]{1,0:T(8,128)(2,1)S(1)} all-gather(bf16[192,512]{1,0:T(8,128)(2,1)S(1)} %get-tuple-element.240), channel_id=6, replica_groups=mesh['grp'=4,'seq'=8] {'grp'}, dimensions={0}, use_global_device_ids=true | all-gather | bytes 983040 | tf_op jit(solution)/shard_map/all_gather | solution.py:1132
  912.6 10.2 %all-gather.5 = bf16[768,512]{1,0:T(8,128)(2,1)S(1)} all-gather(bf16[192,512]{1,0:T(8,128)(2,1)S(1)} %get-tuple-element.241), channel_id=7, replica_groups=mesh['grp'=4,'seq'=8] {'grp'}, dimensions={0}, use_global_device_ids=true | all-gather | bytes 983040 | tf_op jit(solution)/shard_map/all_gather | solution.py:1132
  929.3 5.5 multiply_reduce_fusion
  (430 shorter events, 196.7 us)
Async XLA Ops:
  7.3 49.2 %all-gather.16.cloned.1.call-start = ((), (), s32[]{:S(2)}) async-start(), calls=%async_computation.3 | async-start | bytes 1179648 | tf_op jit(solution)/shard_map/all_gather | solution.py:972
  8.0 120.6 %all-gather.24.cloned.1.call-start = ((), (), s32[]{:S(2)}) async-start(), calls=%async_computation.10 | async-start | bytes 4423680 | tf_op jit(solution)/shard_map/all_gather | solution.py:672
  10.5 44.2 %collective-permute-start.2 = (bf16[192,1024]{1,0:T(8,128)(2,1)}, bf16[192,1024]{1,0:T(8,128)(2,1)}, u32[]{:S(2)}, u32[]{:S(2)}) collective-permute-start(bf16[192,1024]{1,0:T(8,128)(2,1)} %constant_dynamic-slice_fusion.15), channel_id=1, source_target_pairs={{0,2},{1,3},{2,4},{3,5},{4,6},{5,7},{6,0},{7,1},{8,10},{9,11},{10,... | collective-permute-start | bytes 1179656 | tf_op jit(solution)/shard_map/ppermute | solution.py:678
  12.0 40.8 %collective-permute-start.1 = (bf16[192,1024]{1,0:T(8,128)(2,1)}, bf16[192,1024]{1,0:T(8,128)(2,1)}, u32[]{:S(2)}, u32[]{:S(2)}) collective-permute-start(bf16[192,1024]{1,0:T(8,128)(2,1)} %constant_dynamic-slice_fusion.15), channel_id=1, source_target_pairs={{0,4},{1,5},{2,6},{3,7},{4,0},{5,1},{6,2},{7,3},{8,12},{9,13},{10,... | collective-permute-start | bytes 1179656 | tf_op jit(solution)/shard_map/ppermute | solution.py:678
  56.4 204.6 %all-gather.18.cloned.1.call-start = ((), (), s32[]{:S(2)}) async-start(), calls=%async_computation.4 | async-start | bytes 6488064 | tf_op jit(solution)/shard_map/all_gather | solution.py:525
  58.1 293.7 %all-gather.20.cloned.1.call-start = ((), (), s32[]{:S(2)}) async-start(), calls=%async_computation.5 | async-start | bytes 14598144 | tf_op jit(solution)/shard_map/all_gather | solution.py:525
  59.0 477.0 %reduce-scatter.4.cloned.1.call-start = ((), (), s32[]{:S(2)}) async-start(), calls=%async_computation.6 | async-start | bytes 14598144 | tf_op jit(solution)/shard_map/reduce_scatter | solution.py:1024
  59.1 27.1 %collective-permute-start.4 = (bf16[576,1024]{1,0:T(8,128)(2,1)}, bf16[576,1024]{1,0:T(8,128)(2,1)S(1)}, u32[]{:S(2)}, u32[]{:S(2)}) collective-permute-start(bf16[576,1024]{1,0:T(8,128)(2,1)} %constant_dynamic-update-slice_fusion.refs_1_), channel_id=1, source_target_pairs={{0,16},{8,24},{16,0},{24,8},{1,17},{9,25},{17,1},{25,9},{2,18},{10... | collective-permute-start | bytes 3538952 | tf_op jit(solution)/shard_map/ppermute | solution.py:686
  60.6 27.3 %collective-permute-start.3 = (bf16[576,1024]{1,0:T(8,128)(2,1)}, bf16[576,1024]{1,0:T(8,128)(2,1)}, u32[]{:S(2)}, u32[]{:S(2)}) collective-permute-start(bf16[576,1024]{1,0:T(8,128)(2,1)} %constant_dynamic-update-slice_fusion.refs_1_), channel_id=1, source_target_pairs={{0,8},{8,0},{16,24},{24,16},{1,9},{9,1},{17,25},{25,17},{2,10},{10... | collective-permute-start | bytes 3538952 | tf_op jit(solution)/shard_map/ppermute | solution.py:685
  61.2 33.2 %collective-permute-start.8 = (bf16[576,1024]{1,0:T(8,128)(2,1)}, bf16[576,1024]{1,0:T(8,128)(2,1)}, u32[]{:S(2)}, u32[]{:S(2)}) collective-permute-start(bf16[576,1024]{1,0:T(8,128)(2,1)} %constant_dynamic-update-slice_fusion.refs_1_), channel_id=1, source_target_pairs={{0,1},{1,0},{2,3},{3,2},{4,5},{5,4},{6,7},{7,6},{8,9},{9,8},{10,11... | collective-permute-start | bytes 3538952 | tf_op jit(solution)/shard_map/ppermute | solution.py:703
  61.2 71.0 %collective-permute-start.7 = (bf16[192,4096]{1,0:T(8,128)(2,1)S(1)}, bf16[192,4096]{1,0:T(8,128)(2,1)}, u32[]{:S(2)}, u32[]{:S(2)}) collective-permute-start(bf16[192,4096]{1,0:T(8,128)(2,1)S(1)} %copy-done.46), channel_id=1, source_target_pairs={{0,1},{1,0},{2,3},{3,2},{4,5},{5,4},{6,7},{7,6},{8,9},{9,8},{10,11... | collective-permute-start | bytes 4718600 | tf_op jit(solution)/shard_map/ppermute | solution.py:703
  87.7 46.4 %collective-permute-start.10 = (bf16[576,1024]{1,0:T(8,128)(2,1)S(1)}, bf16[576,1024]{1,0:T(8,128)(2,1)}, u32[]{:S(2)}, u32[]{:S(2)}) collective-permute-start(bf16[576,1024]{1,0:T(8,128)(2,1)S(1)} %collective-permute-done.4.refs_3_), channel_id=1, source_target_pairs={{0,1},{1,0},{2,3},{3,2},{4,5},{5,4},{6,7},{7,6},{8,9},{9,8},{10,11... | collective-permute-start | bytes 3538952 | tf_op jit(solution)/shard_map/ppermute | solution.py:703
  92.8 37.6 %collective-permute-start.6 = (bf16[288,1024]{1,0:T(8,128)(2,1)}, bf16[288,1024]{1,0:T(8,128)(2,1)}, u32[]{:S(2)}, u32[]{:S(2)}) collective-permute-start(bf16[288,1024]{1,0:T(8,128)(2,1)} %slice.504), channel_id=1, source_target_pairs={{0,16},{8,24},{16,0},{24,8},{1,17},{9,25},{17,1},{25,9},{2,18},{10... | collective-permute-start | bytes 1769480 | tf_op jit(solution)/shard_map/ppermute | solution.py:701
  94.4 53.2 %collective-permute-start.9 = (bf16[576,1024]{1,0:T(8,128)(2,1)}, bf16[576,1024]{1,0:T(8,128)(2,1)}, u32[]{:S(2)}, u32[]{:S(2)}) collective-permute-start(bf16[576,1024]{1,0:T(8,128)(2,1)} %collective-permute-done.3.refs_2_), channel_id=1, source_target_pairs={{0,1},{1,0},{2,3},{3,2},{4,5},{5,4},{6,7},{7,6},{8,9},{9,8},{10,11... | collective-permute-start | bytes 3538952 | tf_op jit(solution)/shard_map/ppermute | solution.py:703
  100.8 31.9 %collective-permute-start.11 = (bf16[288,1024]{1,0:T(8,128)(2,1)}, bf16[288,1024]{1,0:T(8,128)(2,1)}, u32[]{:S(2)}, u32[]{:S(2)}) collective-permute-start(bf16[288,1024]{1,0:T(8,128)(2,1)} %collective-permute-done.5.refs_4_), channel_id=1, source_target_pairs={{0,1},{1,0},{2,3},{3,2},{4,5},{5,4},{6,7},{7,6},{8,9},{9,8},{10,11... | collective-permute-start | bytes 1769480 | tf_op jit(solution)/shard_map/ppermute | solution.py:703
  132.2 88.1 %collective-permute-start.19 = (bf16[192,9216]{1,0:T(8,128)(2,1)}, bf16[192,9216]{1,0:T(8,128)(2,1)}, u32[]{:S(2)}, u32[]{:S(2)}) collective-permute-start(bf16[192,9216]{1,0:T(8,128)(2,1)} %refs_0_.5), channel_id=1, source_target_pairs={{0,1},{1,0},{2,3},{3,2},{4,5},{5,4},{6,7},{7,6},{8,9},{9,8},{10,11... | collective-permute-start | bytes 10616840 | tf_op jit(solution)/shard_map/ppermute | solution.py:703
  132.7 81.3 %collective-permute-start.16 = (bf16[576,2304]{1,0:T(8,128)(2,1)}, bf16[576,2304]{1,0:T(8,128)(2,1)}, u32[]{:S(2)}, u32[]{:S(2)}) collective-permute-start(bf16[576,2304]{1,0:T(8,128)(2,1)} %pad_maximum_fusion.3.refs_1_), channel_id=1, source_target_pairs={{0,16},{8,24},{16,0},{24,8},{1,17},{9,25},{17,1},{25,9},{2,18},{10... | collective-permute-start | bytes 7962632 | tf_op jit(solution)/shard_map/ppermute | solution.py:686
  134.1 80.0 %collective-permute-start.15 = (bf16[576,2304]{1,0:T(8,128)(2,1)}, bf16[576,2304]{1,0:T(8,128)(2,1)}, u32[]{:S(2)}, u32[]{:S(2)}) collective-permute-start(bf16[576,2304]{1,0:T(8,128)(2,1)} %pad_maximum_fusion.3.refs_1_), channel_id=1, source_target_pairs={{0,8},{8,0},{16,24},{24,16},{1,9},{9,1},{17,25},{25,17},{2,10},{10... | collective-permute-start | bytes 7962632 | tf_op jit(solution)/shard_map/ppermute | solution.py:685
  216.6 43.7 %collective-permute-start.18 = (bf16[288,2304]{1,0:T(8,128)(2,1)}, bf16[288,2304]{1,0:T(8,128)(2,1)}, u32[]{:S(2)}, u32[]{:S(2)}) collective-permute-start(bf16[288,2304]{1,0:T(8,128)(2,1)} %slice.430), channel_id=1, source_target_pairs={{0,16},{8,24},{16,0},{24,8},{1,17},{9,25},{17,1},{25,9},{2,18},{10... | collective-permute-start | bytes 3981320 | tf_op jit(solution)/shard_map/ppermute | solution.py:701
  218.7 42.3 %collective-permute-start.17 = (bf16[288,2304]{1,0:T(8,128)(2,1)S(1)}, bf16[288,2304]{1,0:T(8,128)(2,1)}, u32[]{:S(2)}, u32[]{:S(2)}) collective-permute-start(bf16[288,2304]{1,0:T(8,128)(2,1)S(1)} %slice.429), channel_id=1, source_target_pairs={{0,8},{8,0},{16,24},{24,16},{1,9},{9,1},{17,25},{25,17},{2,10},{10... | collective-permute-start | bytes 3981320 | tf_op jit(solution)/shard_map/ppermute | solution.py:700
  219.8 58.9 %collective-permute-start.20 = (bf16[576,2304]{1,0:T(8,128)(2,1)}, bf16[576,2304]{1,0:T(8,128)(2,1)}, u32[]{:S(2)}, u32[]{:S(2)}) collective-permute-start(bf16[576,2304]{1,0:T(8,128)(2,1)} %pad_maximum_fusion.3.refs_1_), channel_id=1, source_target_pairs={{0,1},{1,0},{2,3},{3,2},{4,5},{5,4},{6,7},{7,6},{8,9},{9,8},{10,11... | collective-permute-start | bytes 7962632 | tf_op jit(solution)/shard_map/ppermute | solution.py:703
  219.8 58.9 %collective-permute-start.22 = (bf16[576,2304]{1,0:T(8,128)(2,1)}, bf16[576,2304]{1,0:T(8,128)(2,1)}, u32[]{:S(2)}, u32[]{:S(2)}) collective-permute-start(bf16[576,2304]{1,0:T(8,128)(2,1)} %collective-permute-done.16.refs_3_), channel_id=1, source_target_pairs={{0,1},{1,0},{2,3},{3,2},{4,5},{5,4},{6,7},{7,6},{8,9},{9,8},{10,11... | collective-permute-start | bytes 7962632 | tf_op jit(solution)/shard_map/ppermute | solution.py:703
  220.3 58.4 %collective-permute-start.21 = (bf16[576,2304]{1,0:T(8,128)(2,1)}, bf16[576,2304]{1,0:T(8,128)(2,1)}, u32[]{:S(2)}, u32[]{:S(2)}) collective-permute-start(bf16[576,2304]{1,0:T(8,128)(2,1)} %collective-permute-done.15.refs_2_), channel_id=1, source_target_pairs={{0,1},{1,0},{2,3},{3,2},{4,5},{5,4},{6,7},{7,6},{8,9},{9,8},{10,11... | collective-permute-start | bytes 7962632 | tf_op jit(solution)/shard_map/ppermute | solution.py:703
  351.7 294.4 %all-gather.22.cloned.1.call-start = ((), (), s32[]{:S(2)}) async-start(), calls=%async_computation.7 | async-start | bytes 2211840 | tf_op jit(solution)/shard_map/all_gather | solution.py:1025
  387.5 29.6 %collective-permute-start.25 = (bf16[768,2304]{1,0:T(8,128)(2,1)}, bf16[768,2304]{1,0:T(8,128)(2,1)}, u32[]{:S(2)}, u32[]{:S(2)}) collective-permute-start(bf16[768,2304]{1,0:T(8,128)(2,1)} %convolution_convert_fusion.4), channel_id=1, source_target_pairs={{0,1},{1,0},{2,3},{3,2},{4,5},{5,4},{6,7},{7,6},{8,9},{9,8},{10,11... | collective-permute-start | bytes 10616840 | tf_op jit(solution)/shard_map/ppermute | solution.py:808
  403.3 242.8 %collective-permute-start.30 = (bf16[768,2304]{1,0:T(8,128)(2,1)}, bf16[768,2304]{1,0:T(8,128)(2,1)}, u32[]{:S(2)}, u32[]{:S(2)}) collective-permute-start(bf16[768,2304]{1,0:T(8,128)(2,1)} %convolution_convert_fusion.1), channel_id=1, source_target_pairs={{0,1},{1,0},{2,3},{3,2},{4,5},{5,4},{6,7},{7,6},{8,9},{9,8},{10,11... | collective-permute-start | bytes 10616840 | tf_op jit(solution)/shard_map/ppermute | solution.py:808
  410.8 135.2 %collective-permute-start.29 = (bf16[768,2304]{1,0:T(8,128)(2,1)}, bf16[768,2304]{1,0:T(8,128)(2,1)}, u32[]{:S(2)}, u32[]{:S(2)}) collective-permute-start(bf16[768,2304]{1,0:T(8,128)(2,1)} %convolution_convert_fusion.2), channel_id=1, source_target_pairs={{0,1},{1,0},{2,3},{3,2},{4,5},{5,4},{6,7},{7,6},{8,9},{9,8},{10,11... | collective-permute-start | bytes 10616840 | tf_op jit(solution)/shard_map/ppermute | solution.py:808
  416.6 119.6 %collective-permute-start.26 = (bf16[768,2304]{1,0:T(8,128)(2,1)}, bf16[768,2304]{1,0:T(8,128)(2,1)}, u32[]{:S(2)}, u32[]{:S(2)}) collective-permute-start(bf16[768,2304]{1,0:T(8,128)(2,1)} %convolution_convert_fusion.3), channel_id=1, source_target_pairs={{0,1},{1,0},{2,3},{3,2},{4,5},{5,4},{6,7},{7,6},{8,9},{9,8},{10,11... | collective-permute-start | bytes 10616840 | tf_op jit(solution)/shard_map/ppermute | solution.py:808
  422.5 113.7 %collective-permute-start.27 = (bf16[384,2304]{1,0:T(8,128)(2,1)}, bf16[384,2304]{1,0:T(8,128)(2,1)}, u32[]{:S(2)}, u32[]{:S(2)}) collective-permute-start(bf16[384,2304]{1,0:T(8,128)(2,1)} %fusion.43), channel_id=1, source_target_pairs={{0,8},{8,0},{16,24},{24,16},{1,9},{9,1},{17,25},{25,17},{2,10},{10... | collective-permute-start | bytes 5308424 | tf_op jit(solution)/shard_map/ppermute | solution.py:814
  427.6 108.5 %collective-permute-start.28 = (bf16[384,2304]{1,0:T(8,128)(2,1)}, bf16[384,2304]{1,0:T(8,128)(2,1)}, u32[]{:S(2)}, u32[]{:S(2)}) collective-permute-start(bf16[384,2304]{1,0:T(8,128)(2,1)} %fusion.40), channel_id=1, source_target_pairs={{0,16},{8,24},{16,0},{24,8},{1,17},{9,25},{17,1},{25,9},{2,18},{10... | collective-permute-start | bytes 5308424 | tf_op jit(solution)/shard_map/ppermute | solution.py:815
  536.1 258.5 %reduce-scatter.8.cloned.1.call-start = ((), (), s32[]{:S(2)}) async-start(), calls=%async_computation.9 | async-start | bytes 4423680 | tf_op jit(solution)/shard_map/reduce_scatter | solution.py:865
  545.3 98.1 %collective-permute-start.31 = (bf16[768,2304]{1,0:T(8,128)(2,1)}, bf16[768,2304]{1,0:T(8,128)(2,1)}, u32[]{:S(2)}, u32[]{:S(2)}) collective-permute-start(bf16[768,2304]{1,0:T(8,128)(2,1)} %add_convert_fusion.2), channel_id=1, source_target_pairs={{0,8},{8,0},{16,24},{24,16},{1,9},{9,1},{17,25},{25,17},{2,10},{10... | collective-permute-start | bytes 10616840 | tf_op jit(solution)/shard_map/ppermute | solution.py:835
  555.9 89.3 %collective-permute-start.32 = (bf16[768,2304]{1,0:T(8,128)(2,1)}, bf16[768,2304]{1,0:T(8,128)(2,1)}, u32[]{:S(2)}, u32[]{:S(2)}) collective-permute-start(bf16[768,2304]{1,0:T(8,128)(2,1)} %add_convert_fusion.1), channel_id=1, source_target_pairs={{0,16},{8,24},{16,0},{24,8},{1,17},{9,25},{17,1},{25,9},{2,18},{10... | collective-permute-start | bytes 10616840 | tf_op jit(solution)/shard_map/ppermute | solution.py:836
  610.4 25.3 %collective-permute-start.34 = (bf16[768,2048]{1,0:T(8,128)(2,1)}, bf16[768,2048]{1,0:T(8,128)(2,1)}, u32[]{:S(2)}, u32[]{:S(2)}) collective-permute-start(bf16[768,2048]{1,0:T(8,128)(2,1)} %convolution_convert_fusion.7), channel_id=1, source_target_pairs={{0,1},{1,0},{2,3},{3,2},{4,5},{5,4},{6,7},{7,6},{8,9},{9,8},{10,11... | collective-permute-start | bytes 9437192 | tf_op jit(solution)/shard_map/ppermute | solution.py:804
  634.5 73.7 %collective-permute-start.37 = (bf16[512,384]{1,0:T(8,128)(2,1)}, bf16[512,384]{1,0:T(8,128)(2,1)}, u32[]{:S(2)}, u32[]{:S(2)}) collective-permute-start(bf16[512,384]{1,0:T(8,128)(2,1)} %get-tuple-element.228), channel_id=1, source_target_pairs={{0,16},{8,24},{16,0},{24,8},{1,17},{9,25},{17,1},{25,9},{2,18},{10... | collective-permute-start | bytes 1179656 | tf_op jit(solution)/shard_map/ppermute | solution.py:815
  635.7 72.5 %collective-permute-start.36 = (bf16[512,384]{1,0:T(8,128)(2,1)}, bf16[512,384]{1,0:T(8,128)(2,1)}, u32[]{:S(2)}, u32[]{:S(2)}) collective-permute-start(bf16[512,384]{1,0:T(8,128)(2,1)} %get-tuple-element.229), channel_id=1, source_target_pairs={{0,8},{8,0},{16,24},{24,16},{1,9},{9,1},{17,25},{25,17},{2,10},{10... | collective-permute-start | bytes 1179656 | tf_op jit(solution)/shard_map/ppermute | solution.py:814
  643.4 67.2 %collective-permute-start.39 = (bf16[384,512]{1,0:T(8,128)(2,1)}, bf16[384,512]{1,0:T(8,128)(2,1)}, u32[]{:S(2)}, u32[]{:S(2)}) collective-permute-start(bf16[384,512]{1,0:T(8,128)(2,1)} %get-tuple-element.226), channel_id=1, source_target_pairs={{0,16},{8,24},{16,0},{24,8},{1,17},{9,25},{17,1},{25,9},{2,18},{10... | collective-permute-start | bytes 1179656 | tf_op jit(solution)/shard_map/ppermute | solution.py:815
  645.2 65.4 %collective-permute-start.38 = (bf16[384,512]{1,0:T(8,128)(2,1)}, bf16[384,512]{1,0:T(8,128)(2,1)}, u32[]{:S(2)}, u32[]{:S(2)}) collective-permute-start(bf16[384,512]{1,0:T(8,128)(2,1)} %get-tuple-element.227), channel_id=1, source_target_pairs={{0,8},{8,0},{16,24},{24,16},{1,9},{9,1},{17,25},{25,17},{2,10},{10... | collective-permute-start | bytes 1179656 | tf_op jit(solution)/shard_map/ppermute | solution.py:814
  657.5 189.9 %reduce-scatter.6.cloned.1.call-start = ((), (), s32[]{:S(2)}) async-start(), calls=%async_computation.8 | async-start | bytes 1216512 | tf_op jit(solution)/shard_map/reduce_scatter | solution.py:1111
  741.6 45.5 %collective-permute-start.51 = (bf16[1024,384]{1,0:T(8,128)(2,1)}, bf16[1024,384]{1,0:T(8,128)(2,1)}, u32[]{:S(2)}, u32[]{:S(2)}) collective-permute-start(bf16[1024,384]{1,0:T(8,128)(2,1)} %get-tuple-element.224), channel_id=1, source_target_pairs={{0,16},{8,24},{16,0},{24,8},{1,17},{9,25},{17,1},{25,9},{2,18},{10... | collective-permute-start | bytes 2359304 | tf_op jit(solution)/shard_map/ppermute | solution.py:836
  742.3 44.8 %collective-permute-start.50 = (bf16[1024,384]{1,0:T(8,128)(2,1)}, bf16[1024,384]{1,0:T(8,128)(2,1)}, u32[]{:S(2)}, u32[]{:S(2)}) collective-permute-start(bf16[1024,384]{1,0:T(8,128)(2,1)} %get-tuple-element.225), channel_id=1, source_target_pairs={{0,8},{8,0},{16,24},{24,16},{1,9},{9,1},{17,25},{25,17},{2,10},{10... | collective-permute-start | bytes 2359304 | tf_op jit(solution)/shard_map/ppermute | solution.py:835
  748.6 177.2 %all-gather.26.cloned.1.call-start = ((), (), s32[]{:S(2)}) async-start(), calls=%async_computation.11 | async-start | bytes 4423680 | tf_op jit(solution)/shard_map/all_gather | solution.py:884
  784.7 83.7 %collective-permute-start.44 = (bf16[768,512]{1,0:T(8,128)(2,1)}, bf16[768,512]{1,0:T(8,128)(2,1)}, u32[]{:S(2)}, u32[]{:S(2)}) collective-permute-start(bf16[768,512]{1,0:T(8,128)(2,1)} %get-tuple-element.218), channel_id=1, source_target_pairs={{0,16},{8,24},{16,0},{24,8},{1,17},{9,25},{17,1},{25,9},{2,18},{10... | collective-permute-start | bytes 2359304 | tf_op jit(solution)/shard_map/ppermute | solution.py:836
  786.1 82.3 %collective-permute-start.43 = (bf16[768,512]{1,0:T(8,128)(2,1)}, bf16[768,512]{1,0:T(8,128)(2,1)}, u32[]{:S(2)}, u32[]{:S(2)}) collective-permute-start(bf16[768,512]{1,0:T(8,128)(2,1)} %get-tuple-element.219), channel_id=1, source_target_pairs={{0,8},{8,0},{16,24},{24,16},{1,9},{9,1},{17,25},{25,17},{2,10},{10... | collective-permute-start | bytes 2359304 | tf_op jit(solution)/shard_map/ppermute | solution.py:835
  789.1 29.2 %collective-permute-start.52 = (bf16[256,384]{1,0:T(8,128)(2,1)S(1)}, bf16[256,384]{1,0:T(8,128)(2,1)S(1)}, u32[]{:S(2)}, u32[]{:S(2)}) collective-permute-start(bf16[256,384]{1,0:T(8,128)(2,1)S(1)} %get-tuple-element.237), channel_id=1, source_target_pairs={{0,2},{1,3},{2,4},{3,5},{4,6},{5,7},{6,0},{7,1},{8,10},{9,11},{10,... | collective-permute-start | bytes 589832 | tf_op jit(solution)/shard_map/ppermute | solution.py:854
  790.2 28.1 %collective-permute-start.54 = (bf16[256,384]{1,0:T(8,128)(2,1)S(1)}, bf16[256,384]{1,0:T(8,128)(2,1)S(1)}, u32[]{:S(2)}, u32[]{:S(2)}) collective-permute-start(bf16[256,384]{1,0:T(8,128)(2,1)S(1)} %get-tuple-element.238), channel_id=1, source_target_pairs={{0,6},{1,7},{2,0},{3,1},{4,2},{5,3},{6,4},{7,5},{8,14},{9,15},{10,... | collective-permute-start | bytes 589832 | tf_op jit(solution)/shard_map/ppermute | solution.py:854
  791.4 26.9 %collective-permute-start.53 = (bf16[256,384]{1,0:T(8,128)(2,1)S(1)}, bf16[256,384]{1,0:T(8,128)(2,1)S(1)}, u32[]{:S(2)}, u32[]{:S(2)}) collective-permute-start(bf16[256,384]{1,0:T(8,128)(2,1)S(1)} %get-tuple-element.239), channel_id=1, source_target_pairs={{0,4},{1,5},{2,6},{3,7},{4,0},{5,1},{6,2},{7,3},{8,12},{9,13},{10,... | collective-permute-start | bytes 589832 | tf_op jit(solution)/shard_map/ppermute | solution.py:854
  873.7 24.6 %collective-permute-start.48 = (bf16[192,1024]{1,0:T(8,128)(2,1)}, bf16[192,1024]{1,0:T(8,128)(2,1)}, u32[]{:S(2)}, u32[]{:S(2)}) collective-permute-start(bf16[192,1024]{1,0:T(8,128)(2,1)} %get-tuple-element.236), channel_id=1, source_target_pairs={{0,4},{1,5},{2,6},{3,7},{4,0},{5,1},{6,2},{7,3},{8,12},{9,13},{10,... | collective-permute-start | bytes 1179656 | tf_op jit(solution)/shard_map/ppermute | solution.py:854
  (106 other events, 1669.7 us)
Sparse Core Ops, SparseCore 0:
  9.7 38.9 all-gather.15
  56.6 71.9 all-gather.23
  132.0 85.7 all-gather.17
  220.6 106.1 all-gather.19
  351.9 184.1 reduce-scatter.3
  537.7 46.9 all-gather.21
  657.7 67.3 reduce-scatter.7
  748.7 98.6 reduce-scatter.5
  849.3 48.2 all-gather.25

commit v9 on v8

--- a/solution.py
+++ b/solution.py
@@ -667,21 +667,25 @@
         own = lax.dynamic_slice_in_dim(shard, group * width, width, 1)
         if after:
             own = tie(own, *after)
-        others = range(1, self.chips)
         if offload:
-            slabs = lax.all_gather(own, "seq", axis_index_groups=same_cores())
+            self.slabs = lax.all_gather(own, "seq", axis_index_groups=same_cores())
+        else:
+            self.slabs = [
+                lax.ppermute(own, "seq", ring_pairs(-2 * j)) for j in range(1, self.chips)
+            ]
+        self.half = half
+
+    def first(self, *after):
+        if self.simple:
+            return ()
+        slabs = tie(self.slabs, *after) if after else self.slabs
+        if not isinstance(slabs, list):
             chip = lax.axis_index("seq") // 2
             slabs = [
-                lax.dynamic_index_in_dim(slabs, (chip + j) % self.chips, 0, False) for j in others
+                lax.dynamic_index_in_dim(slabs, (chip + j) % self.chips, 0, False)
+                for j in range(1, self.chips)
             ]
-        else:
-            slabs = [lax.ppermute(own, "seq", ring_pairs(-2 * j)) for j in others]
         self.near = jnp.concatenate(slabs, axis=0)
-        self.half = half
-
-    def first(self):
-        if self.simple:
-            return ()
         self.from_x = lax.ppermute(self.near, "grp", xor_pairs("grp", 1))
         self.from_y = lax.ppermute(self.near, "grp", xor_pairs("grp", 2))
         return (self.near,)
@@ -885,24 +889,6 @@
         return parts.transpose(1, 0, 2).reshape(self.rows, 4 * self.width).astype(F32)
 
 
-def gather_parts(lines, sums):
-    if sums[0].simple:
-        return lax.all_gather(lines, "grp", axis=0, tiled=True), [one.finish() for one in sums]
-    pieces = [lines]
-    for one in sums:
-        total = one.total().astype(BF16)
-        pieces += [total[:, n : n + HS] for n in range(0, one.width, HS)]
-    parts = lax.all_gather(jnp.concatenate(pieces, axis=0), "grp")
-    at = lines.shape[0]
-    found = []
-    for one in sums:
-        blocks = one.width // HS
-        part = parts[:, at : at + blocks * one.rows].reshape(4, blocks, one.rows, HS)
-        found.append(part.transpose(2, 0, 1, 3).reshape(one.rows, 4 * one.width).astype(F32))
-        at += blocks * one.rows
-    return parts[:, : lines.shape[0]].reshape(-1, HS), found
-
-
 def shard_carry(ends, prods, reverse):
     count = lax.axis_size("seq")
     place = lax.axis_index("seq")
@@ -998,7 +984,7 @@
     soft = jax.nn.softplus(-decay_float).reshape(1, LRU)
 
     conv_low, keep, state_part, prod_part, chunks = mixer_forward(
-        tie(inner_low, *up_gather.first()), prev_inner, dist, gates_all, taps_all, soft
+        tie(inner_low, *up_gather.first(inner_low)), prev_inner, dist, gates_all, taps_all, soft
     )
     end_state, end_prod = chunk_ends(chunks, False)
     gate_pre, in_gate = in_gather.dot(first_normed, 1, F32)
@@ -1022,7 +1008,6 @@
     grad_out = cotangent.reshape(row_count, D)
     grad_down = dot_rows(hidden, grad_out).astype(BF16)
     down_part = lax.psum_scatter(grad_down, ("seq", "grp"), scatter_dimension=0, tiled=True)
-    down_sum = lax.all_gather(down_part, "grp", axis=0, tiled=True)
     grad_expanded = ffn_backward(tie(grad_out, grad_down), proj_down, pull)
     quarter = FF // 2
 
@@ -1046,8 +1031,9 @@
     grad_branch = dot_far(grad_mixer, proj_out)
 
     grad_gate, local, rev_prod, rev_chunks = mixer_reverse(
-        tie(grad_branch, down_part).reshape(wide), gate_pre, keep, state
-    )
+        grad_branch.reshape(wide), gate_pre, keep, state
+    )
+    down_sum = lax.all_gather(tie(down_part, rev_chunks), "grp", axis=0, tiled=True)
     head_pull, head_prod = chunk_ends(rev_chunks, True)
     grad_gate = grad_gate.reshape(row_count, LRU)
     width = LRU // 4
@@ -1106,14 +1092,13 @@
         axis=1,
     )
     lines = flat.shape[1]
-    whole = 16 * lax.axis_size("grp")
-    flat = jnp.pad(flat, ((0, 0), (0, -lines % whole), (0, 0))).astype(BF16).reshape(-1, HS)
-    flat = lax.psum_scatter(flat, ("seq", "grp"), scatter_dimension=0, tiled=True)
+    flat = jnp.pad(flat, ((0, 0), (0, -lines % 16), (0, 0))).astype(BF16).reshape(-1, HS)
+    flat = lax.psum_scatter(flat, "seq", scatter_dimension=0, tiled=True)
     first_grad = first_grad + dot_far(grad_inner, in_value)
     sent = in_value_sum.second(first_grad)
     out_sum.third(*sent)
-    flat, (out_total,) = gather_parts(flat, [out_sum])
-    flat = flat[:lines].astype(F32).reshape(-1)
+    flat = lax.all_gather(tie(flat, *sent), "grp").astype(F32)
+    flat = jnp.sum(flat, axis=0)[:lines].reshape(-1)
     n_gates = flat.shape[0] - (CONV + 1) * n_lru
     gates_total = flat[:n_gates].reshape(gate_heads.shape)
     taps_total = flat[n_gates : n_gates + CONV * n_lru].reshape(CONV, n_lru)
@@ -1123,9 +1108,10 @@
     down_total = down_sum.astype(F32)
     if in_value_sum.simple:
         in_total = jnp.concatenate([in_value_sum.finish(), in_gate_sum.finish()], axis=1)
+        last_sent = ()
     else:
         both = jnp.concatenate([in_value_sum.mine(), in_gate_sum.mine()], axis=1)
-        in_value_sum.along_z(both)
+        last_sent = in_value_sum.along_z(both)
         both = in_value_sum.total().astype(BF16)
         in_total = jnp.concatenate(
             [
@@ -1136,6 +1122,7 @@
             ],
             axis=1,
         ).astype(F32)
+    out_total = out_sum.finish(*last_sent)
     ffn_out = jnp.dot(tie(hidden, *sent), proj_down, preferred_element_type=F32)
     block_out = by_token((resid + ffn_out).astype(BF16).reshape(tokens.shape))
     grad_tokens = grad_resid + norm_back(inputs, first_scale, gain_one, first_grad)

time: 952 us -> 868 us (0.912)
  waiting for transfers between devices: 200 us -> 109 us
    reduce_scatter x1, waiting for transfers between devices: 66.2 us -> 0.01 us  [body(): lax.psum_scatter(grad_down, ('seq', 'grp'), scatter_dimension=0, tiled=True)]
    ppermute x2, waiting for transfers between devices: 7.79 us -> 43 us  [first(): self.from_y = lax.ppermute(self.near, 'grp', xor_pairs('grp', 2))]
    reduce_scatter x1, waiting for transfers between devices: 29 us -> 0.01 us  [body(): flat = lax.psum_scatter(flat, 'seq', scatter_dimension=0, tiled=True)]
    all_gather x2, waiting for transfers between devices: 27.8 us -> 0.02 us  [the longest x1 0.02 us: __init__(): self.slabs = lax.all_gather(own, 'seq', axis_index_groups=same_cores())]
    ppermute x6, waiting for transfers between devices: 15.3 us -> 3.15 us  [along_z(): lax.ppermute(part, 'seq', ring_pairs(2 * j + 2))]
    ppermute x4, waiting for transfers between devices: 0.01 us -> 11.2 us  [__init__(): self.diag_a = lax.ppermute(self.sent[0], 'grp', self.x)]
    all_gather x1 -> x2, blocking collectives: 17.8 us -> 24.9 us  [the longest x1 14.2 us: body(): flat = lax.all_gather(tie(flat, *sent), 'grp').astype(F32)]
    unnamed x191 -> x199, local copies, waits for them, and re-layouts: 41.5 us -> 44.2 us
  transfers between devices with their start and end apart: 64 -> 64, of which waited for: 14 -> 12; matrix products, arithmetic and copies ran while one was open for 36% -> 40% of each run, Pallas kernels for 22% -> 25%
where the time goes in v9:
time: 868 us; the launch traced here: 860 us
  matrix products  244 us (28%)
  Pallas kernels  212 us (24%)
  waiting for transfers between devices  109 us (13%)
  local copies, waits for them, and re-layouts  99.2 us (11%)
  blocking collectives  89.1 us (10%)
  starting transfers between devices  50.2 us (6%)
  other arithmetic  41.3 us (5%)
  between operations  15.5 us (2%)
    dot_general x16, matrix products, dot_rows(): lax.dot_general(a, b, (((0,), (0,)), ((), ())), preferred_element_type=F32)  135 us
    dot_general x5, matrix products, dot_far(): lax.dot_general(a, b, (((1,), (1,)), ((), ())), preferred_element_type=F32)  77 us
    pallas_call x3, Pallas kernels, call(): pl.pallas_call(kernel, grid=(steps,), in_specs=[pl.BlockSpec(memory_space...  66.3 us
    pallas_call x1, Pallas kernels, mixer_backward(): pl.pallas_call(mixer_backward_kernel, grid=(HEADS,), in_specs=[full, full...  46.8 us
    unnamed x199, local copies, waits for them, and re-layouts  44.2 us
    ppermute x2, waiting for transfers between devices, first(): self.from_y = lax.ppermute(self.near, 'grp', xor_pairs('grp', 2))  43 us
    ppermute x3, waiting for transfers between devices, __init__(): lax.ppermute(own, 'seq', ring_pairs(-2 * j))  35 us
    pallas_call x1, Pallas kernels, mixer_forward(): pl.pallas_call(mixer_forward_kernel, grid=(HEADS,), in_specs=[full, head_...  28 us
  transfers between devices with their start and end apart: 64, of which 12 were waited for; matrix products, arithmetic and copies ran while one was open for 40% of the time, Pallas kernels for 25%

profile of v9, /device:TPU:18, one launch (start us, length us, event | category | flops | bytes accessed | tf_op | source)
XLA Modules:
  0.0 859.6 jit_solution(5611880747125547794)
XLA Ops:
  16.1 7.5 collective-permute-done
  25.3 27.5 %collective-permute-done.1 = bf16[192,1024]{1,0:T(8,128)(2,1)} collective-permute-done((bf16[192,1024]{1,0:T(8,128)(2,1)}, bf16[192,1024]{1,0:T(8,128)(2,1)}, u32[]{:S(2)}, u32[]{:S(2)}) %collective-permute-start.1) | collective-permute-done | bytes 393248 | tf_op jit(solution)/shard_map/ppermute | solution.py:674
  61.7 24.6 %collective-permute-done.4.refs_3_ = bf16[576,1024]{1,0:T(8,128)(2,1)} collective-permute-done((bf16[576,1024]{1,0:T(8,128)(2,1)}, bf16[576,1024]{1,0:T(8,128)(2,1)}, u32[]{:S(2)}, u32[]{:S(2)}) %collective-permute-start.4) | collective-permute-done | bytes 1179680 | tf_op jit(solution)/shard_map/ppermute | solution.py:690
  92.0 15.3 %all-gather.9 = bf16[8,1,1664]{2,1,0:T(2,128)(2,1)S(1)} all-gather(bf16[1,1,1664]{2,1,0:T(2,128)(2,1)S(1)} %reshape.2479), channel_id=2, replica_groups=mesh['grp'=4,'seq'=8] {'seq'}, dimensions={0}, use_global_device_ids=true | all-gather | bytes 29952 | tf_op jit(solution)/shard_map/all_gather | solution.py:946
  108.7 5.3 copy.292
  124.8 12.0 %gathered_dot.2 = (bf16[1024,2048]{1,0:T(8,128)(2,1)}, bf16[1536,2048]{1,0:T(8,128)(2,1)}) custom-call(s32[3]{0:T(128)} %pad_add_fusion.1.where_ref, bf16[1024,1536]{1,0:T(8,128)(2,1)} %copy-done.9, bf16[192,4096]{1,0:T(8,128)(2,1)} %refs_0_.4, bf16[576,1024]{1,0:T(8,128)(2,1)} %constant_dynamic-update-slice_fusion.refs_1_, ...), custom_call_target="tpu_custom_call" | custom-call | tf_op jit(solution)/shard_map/gathered_dot/pallas_call | solution.py:715
  151.8 28.0 %mixer_forward.1 = (bf16[2,512,2048]{2,1,0:T(8,128)(2,1)S(1)}, f32[2,512,2048]{2,1,0:T(8,128)}, f32[2,512,2048]{2,1,0:T(8,128)}, f32[2,512,2048]{2,1,0:T(8,128)}, f32[2,2,8,2048]{3,2,1,0:T(8,128)S(1)}) custom-call(bf16[2,512,2048]{2,1,0:T(8,128)(2,1)S(1)} %bitcast.780, bf16[2,8,2048]{2,1,0:T(8,128)(2,1)S(1)} %collective-permute-done.13.halo_ref, ...), custom_call_target="tpu_custom_call" | custom-call | tf_op jit(solution)/shard_map/mixer_forward/pallas_call | solution.py:322
  182.4 13.9 %all-gather.2 = f32[16,2,2048]{2,1,0:T(2,128)S(1)} all-gather(f32[2,2,2048]{2,1,0:T(2,128)S(1)} %copy.311), channel_id=4, replica_groups=mesh['grp'=4,'seq'=8] {'seq'}, dimensions={0}, use_global_device_ids=true | all-gather | bytes 294912 | tf_op jit(solution)/shard_map/all_gather | solution.py:895
  196.8 18.5 %collective-permute-done.16.refs_3_ = bf16[576,2304]{1,0:T(8,128)(2,1)} collective-permute-done((bf16[576,2304]{1,0:T(8,128)(2,1)}, bf16[576,2304]{1,0:T(8,128)(2,1)}, u32[]{:S(2)}, u32[]{:S(2)}) %collective-permute-start.16) | collective-permute-done | bytes 2654240 | tf_op jit(solution)/shard_map/ppermute | solution.py:690
  225.2 5.3 copy.326
  230.5 12.6 %gathered_dot.3 = (f32[1024,2048]{1,0:T(8,128)}, bf16[1536,2048]{1,0:T(8,128)(2,1)}) custom-call(s32[3]{0:T(128)} %pad_add_fusion.1.where_ref, bf16[1024,1536]{1,0:T(8,128)(2,1)} %copy-done.9, bf16[192,4096]{1,0:T(8,128)(2,1)} %refs_0_.4, bf16[576,1024]{1,0:T(8,128)(2,1)} %constant_dynamic-update-slice_fusion.refs_1_, ...), custom_call_target="tpu_custom_call" | custom-call | tf_op jit(solution)/shard_map/gathered_dot/pallas_call | solution.py:715
  243.1 17.7 %mixer_branch.1 = (f32[2,512,2048]{2,1,0:T(8,128)}, bf16[2,512,2048]{2,1,0:T(8,128)(2,1)S(1)}, bf16[2,2,512,1024]{3,2,1,0:T(8,128)(2,1)S(1)}) custom-call(s32[1]{0:T(128)} %bitcast.3.core_ref, f32[2,512,2048]{2,1,0:T(8,128)} %get-tuple-element.86.state_ref, f32[2,512,2048]{2,1,0:T(8,128)} %get-tuple-element.87.prod_ref, ...), custom_call_target="tpu_custom_call" | custom-call | tf_op jit(solution)/shard_map/mixer_branch/pallas_call | solution.py:364
  265.3 10.5 %convert_add_fusion.x_ref = f32[1024,1536]{1,0:T(8,128)S(1)} fusion(bf16[1024,1536]{1,0:T(8,128)(2,1)} %bitcast.774, bf16[1024,2048]{1,0:T(8,128)(2,1)} %bitcast.787, bf16[2048,1536]{1,0:T(8,128)(2,1)} %all-gather.19.cloned.1.call-done), kind=kOutput, calls=%fused_computation.3 | convolution fusion | flops 6445596672 | bytes 19922944 | tf_op jit(solution)/shard_map/dot_general | solution.py:998
  283.0 41.7 %gathered_ffn.1 = (bf16[1024,4608]{1,0:T(8,128)(2,1)}, bf16[2,1024,4608]{2,1,0:T(8,128)(2,1)}, bf16[1536,4608]{1,0:T(8,128)(2,1)}, bf16[1536,4608]{1,0:T(8,128)(2,1)}) custom-call(s32[3]{0:T(128)} %pad_add_fusion.1.where_ref, bf16[1024,1536]{1,0:T(8,128)(2,1)} %copy-done.23, bf16[192,9216]{1,0:T(8,128)(2,1)} %refs_0_.5, ...), custom_call_target="tpu_custom_call" | custom-call | tf_op jit(solution)/shard_map/gathered_ffn/pallas_call | solution.py:715
  324.8 31.8 %convolution_convert_fusion = bf16[4608,1536]{1,0:T(8,128)(2,1)} fusion(bf16[1024,4608]{1,0:T(8,128)(2,1)} %get-tuple-element.133, bf16[1024,1536]{1,0:T(8,128)(2,1)S(1)} %bitcast.776), kind=kOutput, calls=%fused_computation | convolution fusion | flops 14502592512 | bytes 26738688 | tf_op jit(solution)/shard_map/dot_general | solution.py:547
  358.6 27.1 %ffn_backward.1 = bf16[2,1024,4608]{2,1,0:T(8,128)(2,1)} custom-call(bf16[1024,1536]{1,0:T(8,128)(2,1)S(1)} %bitcast.777, bf16[4608,1536]{1,0:T(8,128)(2,1)} %all-gather.21.cloned.1.call-done.down_ref, bf16[2,1024,4608]{2,1,0:T(8,128)(2,1)} %get-tuple-element.95.pull_ref), custom_call_target="tpu_custom_call" | custom-call | tf_op jit(solution)/shard_map/ffn_backward/pallas_call | solution.py:506
  385.7 8.0 convolution_convert_fusion.4
  393.7 5.1 fusion.187
  399.2 7.9 convolution_convert_fusion.1
  408.9 5.3 convolution_convert_fusion.2
  415.0 5.6 convolution_convert_fusion.3
  420.7 5.3 fusion.43
  426.4 4.8 fusion.40
  431.1 21.8 %fusion = f32[1024,1536]{1,0:T(8,128)} fusion(bf16[1536,4608]{1,0:T(8,128)(2,1)} %get-tuple-element.100, bf16[2,1024,4608]{2,1,0:T(8,128)(2,1)} %ffn_backward.1), kind=kOutput, calls=%fused_computation.4 | convolution fusion | flops 14495514624 | bytes 29884416 | tf_op jit(solution)/shard_map/dot_general | solution.py:557
  453.0 21.5 %fusion.25 = f32[1024,1536]{1,0:T(8,128)S(1)} fusion(f32[1024,1536]{1,0:T(8,128)} %fusion, bf16[1536,4608]{1,0:T(8,128)(2,1)} %get-tuple-element.99, bf16[2,1024,4608]{2,1,0:T(8,128)(2,1)} %ffn_backward.1), kind=kOutput, calls=%fused_computation.44 | convolution fusion | flops 14497087488 | bytes 36175872 | tf_op jit(solution)/shard_map/dot_general | solution.py:557
  474.4 11.2 %collective-permute-done.27 = bf16[384,2304]{1,0:T(8,128)(2,1)} collective-permute-done((bf16[384,2304]{1,0:T(8,128)(2,1)}, bf16[384,2304]{1,0:T(8,128)(2,1)}, u32[]{:S(2)}, u32[]{:S(2)}) %collective-permute-start.27) | collective-permute-done | bytes 1769504 | tf_op jit(solution)/shard_map/ppermute | solution.py:818
  486.5 9.0 %add_convert_fusion.2 = bf16[768,2304]{1,0:T(8,128)(2,1)} fusion(bf16[768,2304]{1,0:T(8,128)(2,1)} %collective-permute-done.26, bf16[1024,768]{1,0:T(8,128)(2,1)S(1)} %get-tuple-element.96, bf16[2,1024,4608]{2,1,0:T(8,128)(2,1)} %ffn_backward.1, s32[]{:T(128)S(6)} %select_n.797, s32[]{:T(128)S(6)} %select_n.799, bf16[384,2304]{1,0:T(8,128)(2,1)} %collective-permute-done.28), kind=kOutput, calls=%fused_computation.14 | convolution fusion | flops 3632726016 | bytes 15138824 | tf_op jit(solution)/shard_map/dot_general | solution.py:547
  496.2 10.0 %add_convert_fusion.1 = bf16[768,2304]{1,0:T(8,128)(2,1)} fusion(bf16[768,2304]{1,0:T(8,128)(2,1)} %collective-permute-done.29, bf16[1024,768]{1,0:T(8,128)(2,1)S(1)} %get-tuple-element.96, bf16[2,1024,4608]{2,1,0:T(8,128)(2,1)} %ffn_backward.1, s32[]{:T(128)S(6)} %select_n.801, s32[]{:T(128)S(6)} %select_n.803, bf16[384,2304]{1,0:T(8,128)(2,1)} %collective-permute-done.27), kind=kOutput, calls=%fused_computation.13 | convolution fusion | flops 3632726016 | bytes 15138824 | tf_op jit(solution)/shard_map/dot_general | solution.py:547
  508.2 3.9 fusion.180
  512.1 12.1 %fusion.194 = f32[1024,2048]{1,0:T(8,128)} fusion(bf16[1024,1536]{1,0:T(8,128)(2,1)S(1)} %get-tuple-element.111, bf16[2048,1536]{1,0:T(8,128)(2,1)} %all-gather.19.cloned.1.call-done), kind=kOutput, calls=%fused_computation.341 | convolution fusion | flops 6442450944 | bytes 17825792 | tf_op jit(solution)/shard_map/dot_general | solution.py:557
  524.2 21.8 %mixer_reverse.1 = (bf16[2,512,2048]{2,1,0:T(8,128)(2,1)S(1)}, f32[2,512,2048]{2,1,0:T(8,128)S(1)}, f32[2,512,2048]{2,1,0:T(8,128)}, f32[2,2,8,2048]{3,2,1,0:T(8,128)S(1)}) custom-call(f32[2,512,2048]{2,1,0:T(8,128)} %bitcast.795, f32[2,512,2048]{2,1,0:T(8,128)} %bitcast.789, f32[2,512,2048]{2,1,0:T(8,128)} %get-tuple-element.104.keep_ref, ...), custom_call_target="tpu_custom_call" | custom-call | tf_op jit(solution)/shard_map/mixer_reverse/pallas_call | solution.py:386
  556.0 5.7 convolution_convert_fusion.5
  563.2 5.3 convolution_convert_fusion.7
  569.1 12.4 %all-gather.3 = f32[16,2,2048]{2,1,0:T(2,128)S(1)} all-gather(f32[2,2,2048]{2,1,0:T(2,128)S(1)} %copy.343), channel_id=5, replica_groups=mesh['grp'=4,'seq'=8] {'seq'}, dimensions={0}, use_global_device_ids=true | all-gather | bytes 294912 | tf_op jit(solution)/shard_map/all_gather | solution.py:895
  582.1 7.1 add_convert_fusion.6
  594.0 5.8 add_convert_fusion.5
  605.1 11.2 %add_convert_fusion = bf16[768,2304]{1,0:T(8,128)(2,1)} fusion(bf16[768,2304]{1,0:T(8,128)(2,1)} %collective-permute-done.32, bf16[768,2304]{1,0:T(8,128)(2,1)} %collective-permute-done.31, bf16[768,2304]{1,0:T(8,128)(2,1)} %collective-permute-done.30, bf16[1024,768]{1,0:T(8,128)(2,1)S(1)} %get-tuple-element.96, bf16[2,1024,4608]{2,1,0:T(8,128)(2,1)} %ffn_backward.1, ...), kind=kOutput, calls=%fused_computation.12 | convolution fusion | flops 3636264960 | bytes 20447240 | tf_op jit(solution)/shard_map/dot_general | solution.py:547
  619.7 46.8 %mixer_backward.1 = (bf16[2,512,2048]{2,1,0:T(8,128)(2,1)S(1)}, f32[2,32,2048]{2,1,0:T(8,128)S(1)}, f32[2,8,2048]{2,1,0:T(8,128)S(1)}, f32[16,128,256]{2,1,0:T(8...) custom-call(f32[2,512,2048]{2,1,0:T(8,128)} %copy-done.10, f32[2,512,2048]{2,1,0:T(8,128)} %get-tuple-element.117.prod_ref, ...), custom_call_target="tpu_custom_call" | custom-call | tf_op jit(solution)/shard_map/mixer_backward/pallas_call | solution.py:408
  674.2 10.9 %fusion.195 = f32[1024,1536]{1,0:T(8,128)} fusion(bf16[1024,2048]{1,0:T(8,128)(2,1)S(1)} %bitcast.782, bf16[1536,2048]{1,0:T(8,128)(2,1)} %get-tuple-element.127), kind=kOutput, calls=%fused_computation.342 | convolution fusion | flops 6442450944 | bytes 16777216 | tf_op jit(solution)/shard_map/dot_general | solution.py:557
  688.1 5.3 convolution_convert_fusion.6
  707.5 7.0 collective-permute-done.46
  717.1 6.8 add_convert_fusion.4
  727.0 10.8 %fusion.10 = (f32[1024]{0:T(1024)S(1)}, f32[1024,1536]{1,0:T(8,128)S(1)}) fusion(f32[1536]{0:T(1024)S(1)} %reshape.2461, bf16[2,8,64,1536]{3,1,2,0:T(8,128)(2,1)S(1)} %copy-done.4, f32[1024,1536]{1,0:T(8,128)} %fusion.195, bf16[1024,2048]{1,0:T(8,128)(2,1)S(1)} %bitcast.784, bf16[1536,2048]{1,0:T(8,128)(2,1)} %get-tuple-element.130), kind=kOutput, calls=%fused_computation.19 | convolution fusion | flops 6450314240 | bytes 26224640 | tf_op jit(solution)/shard_map/dot_general | solution.py:557
  752.8 21.8 %add_convert_fusion.3 = bf16[1024,1536]{1,0:T(8,128)(2,1)} fusion(f32[1024,1536]{1,0:T(8,128)} %copy-done.2, bf16[1024,4608]{1,0:T(8,128)(2,1)} %get-tuple-element.133, bf16[4608,1536]{1,0:T(8,128)(2,1)} %all-gather.21.cloned.1.call-done.down_ref), kind=kOutput, calls=%fused_computation.20 | convolution fusion | flops 14498660352 | bytes 33030144 | tf_op jit(solution)/shard_map/dot_general | solution.py:1126
  774.7 14.2 %all-gather.6 = bf16[2112,128]{1,0:T(8,128)(2,1)S(1)} all-gather(bf16[528,128]{1,0:T(8,128)(2,1)} %reduce-scatter.6.cloned.1.call-done), channel_id=8, replica_groups=mesh['grp'=4,'seq'=8] {'grp'}, dimensions={0}, use_global_device_ids=true | all-gather | bytes 675840 | tf_op jit(solution)/shard_map/all_gather | solution.py:1100
  801.9 10.8 %all-gather.7 = bf16[1024,384]{1,0:T(8,128)(2,1)S(1)} all-gather(bf16[256,384]{1,0:T(8,128)(2,1)S(1)} %fusion.72), channel_id=9, replica_groups=mesh['grp'=4,'seq'=8] {'grp'}, dimensions={0}, use_global_device_ids=true | all-gather | bytes 983040 | tf_op jit(solution)/shard_map/all_gather | solution.py:888
  819.3 12.2 %all-gather.4 = bf16[768,512]{1,0:T(8,128)(2,1)S(1)} all-gather(bf16[192,512]{1,0:T(8,128)(2,1)S(1)} %get-tuple-element.202), channel_id=6, replica_groups=mesh['grp'=4,'seq'=8] {'grp'}, dimensions={0}, use_global_device_ids=true | all-gather | bytes 983040 | tf_op jit(solution)/shard_map/all_gather | solution.py:1118
  832.2 10.5 %all-gather.5 = bf16[768,512]{1,0:T(8,128)(2,1)S(1)} all-gather(bf16[192,512]{1,0:T(8,128)(2,1)S(1)} %get-tuple-element.203), channel_id=7, replica_groups=mesh['grp'=4,'seq'=8] {'grp'}, dimensions={0}, use_global_device_ids=true | all-gather | bytes 983040 | tf_op jit(solution)/shard_map/all_gather | solution.py:1118
  (435 shorter events, 187.2 us)
Async XLA Ops:
  7.2 49.2 %all-gather.17.cloned.1.call-start = ((), (), s32[]{:S(2)}) async-start(), calls=%async_computation.3 | async-start | bytes 1179648 | tf_op jit(solution)/shard_map/all_gather | solution.py:958
  7.9 128.8 %all-gather.25.cloned.1.call-start = ((), (), s32[]{:S(2)}) async-start(), calls=%async_computation.10 | async-start | bytes 4423680 | tf_op jit(solution)/shard_map/all_gather | solution.py:671
  10.4 44.2 %collective-permute-start.2 = (bf16[192,1024]{1,0:T(8,128)(2,1)}, bf16[192,1024]{1,0:T(8,128)(2,1)}, u32[]{:S(2)}, u32[]{:S(2)}) collective-permute-start(bf16[192,1024]{1,0:T(8,128)(2,1)} %constant_dynamic-slice_fusion.15), channel_id=1, source_target_pairs={{0,2},{1,3},{2,4},{3,5},{4,6},{5,7},{6,0},{7,1},{8,10},{9,11},{10,... | collective-permute-start | bytes 1179656 | tf_op jit(solution)/shard_map/ppermute | solution.py:674
  12.0 40.8 %collective-permute-start.1 = (bf16[192,1024]{1,0:T(8,128)(2,1)}, bf16[192,1024]{1,0:T(8,128)(2,1)}, u32[]{:S(2)}, u32[]{:S(2)}) collective-permute-start(bf16[192,1024]{1,0:T(8,128)(2,1)} %constant_dynamic-slice_fusion.15), channel_id=1, source_target_pairs={{0,4},{1,5},{2,6},{3,7},{4,0},{5,1},{6,2},{7,3},{8,12},{9,13},{10,... | collective-permute-start | bytes 1179656 | tf_op jit(solution)/shard_map/ppermute | solution.py:674
  56.4 208.9 %all-gather.19.cloned.1.call-start = ((), (), s32[]{:S(2)}) async-start(), calls=%async_computation.4 | async-start | bytes 6488064 | tf_op jit(solution)/shard_map/all_gather | solution.py:525
  58.1 298.6 %all-gather.21.cloned.1.call-start = ((), (), s32[]{:S(2)}) async-start(), calls=%async_computation.5 | async-start | bytes 14598144 | tf_op jit(solution)/shard_map/all_gather | solution.py:525
  59.0 493.4 %reduce-scatter.4.cloned.1.call-start = ((), (), s32[]{:S(2)}) async-start(), calls=%async_computation.6 | async-start | bytes 14598144 | tf_op jit(solution)/shard_map/reduce_scatter | solution.py:1010
  59.0 27.2 %collective-permute-start.4 = (bf16[576,1024]{1,0:T(8,128)(2,1)}, bf16[576,1024]{1,0:T(8,128)(2,1)}, u32[]{:S(2)}, u32[]{:S(2)}) collective-permute-start(bf16[576,1024]{1,0:T(8,128)(2,1)} %constant_dynamic-update-slice_fusion.refs_1_), channel_id=1, source_target_pairs={{0,16},{8,24},{16,0},{24,8},{1,17},{9,25},{17,1},{25,9},{2,18},{10... | collective-permute-start | bytes 3538952 | tf_op jit(solution)/shard_map/ppermute | solution.py:690
  60.6 27.3 %collective-permute-start.3 = (bf16[576,1024]{1,0:T(8,128)(2,1)}, bf16[576,1024]{1,0:T(8,128)(2,1)}, u32[]{:S(2)}, u32[]{:S(2)}) collective-permute-start(bf16[576,1024]{1,0:T(8,128)(2,1)} %constant_dynamic-update-slice_fusion.refs_1_), channel_id=1, source_target_pairs={{0,8},{8,0},{16,24},{24,16},{1,9},{9,1},{17,25},{25,17},{2,10},{10... | collective-permute-start | bytes 3538952 | tf_op jit(solution)/shard_map/ppermute | solution.py:689
  61.1 30.3 %collective-permute-start.8 = (bf16[576,1024]{1,0:T(8,128)(2,1)}, bf16[576,1024]{1,0:T(8,128)(2,1)S(1)}, u32[]{:S(2)}, u32[]{:S(2)}) collective-permute-start(bf16[576,1024]{1,0:T(8,128)(2,1)} %constant_dynamic-update-slice_fusion.refs_1_), channel_id=1, source_target_pairs={{0,1},{1,0},{2,3},{3,2},{4,5},{5,4},{6,7},{7,6},{8,9},{9,8},{10,11... | collective-permute-start | bytes 3538952 | tf_op jit(solution)/shard_map/ppermute | solution.py:707
  61.1 61.1 %collective-permute-start.7 = (bf16[192,4096]{1,0:T(8,128)(2,1)S(1)}, bf16[192,4096]{1,0:T(8,128)(2,1)}, u32[]{:S(2)}, u32[]{:S(2)}) collective-permute-start(bf16[192,4096]{1,0:T(8,128)(2,1)S(1)} %copy-done.48), channel_id=1, source_target_pairs={{0,1},{1,0},{2,3},{3,2},{4,5},{5,4},{6,7},{7,6},{8,9},{9,8},{10,11... | collective-permute-start | bytes 4718600 | tf_op jit(solution)/shard_map/ppermute | solution.py:707
  91.4 33.4 %collective-permute-start.10 = (bf16[576,1024]{1,0:T(8,128)(2,1)}, bf16[576,1024]{1,0:T(8,128)(2,1)}, u32[]{:S(2)}, u32[]{:S(2)}) collective-permute-start(bf16[576,1024]{1,0:T(8,128)(2,1)} %collective-permute-done.4.refs_3_), channel_id=1, source_target_pairs={{0,1},{1,0},{2,3},{3,2},{4,5},{5,4},{6,7},{7,6},{8,9},{9,8},{10,11... | collective-permute-start | bytes 3538952 | tf_op jit(solution)/shard_map/ppermute | solution.py:707
  91.4 33.4 %collective-permute-start.9 = (bf16[576,1024]{1,0:T(8,128)(2,1)}, bf16[576,1024]{1,0:T(8,128)(2,1)}, u32[]{:S(2)}, u32[]{:S(2)}) collective-permute-start(bf16[576,1024]{1,0:T(8,128)(2,1)} %collective-permute-done.3.refs_2_), channel_id=1, source_target_pairs={{0,1},{1,0},{2,3},{3,2},{4,5},{5,4},{6,7},{7,6},{8,9},{9,8},{10,11... | collective-permute-start | bytes 3538952 | tf_op jit(solution)/shard_map/ppermute | solution.py:707
  122.3 102.5 %collective-permute-start.19 = (bf16[192,9216]{1,0:T(8,128)(2,1)}, bf16[192,9216]{1,0:T(8,128)(2,1)}, u32[]{:S(2)}, u32[]{:S(2)}) collective-permute-start(bf16[192,9216]{1,0:T(8,128)(2,1)} %refs_0_.5), channel_id=1, source_target_pairs={{0,1},{1,0},{2,3},{3,2},{4,5},{5,4},{6,7},{7,6},{8,9},{9,8},{10,11... | collective-permute-start | bytes 10616840 | tf_op jit(solution)/shard_map/ppermute | solution.py:707
  140.4 74.9 %collective-permute-start.16 = (bf16[576,2304]{1,0:T(8,128)(2,1)}, bf16[576,2304]{1,0:T(8,128)(2,1)}, u32[]{:S(2)}, u32[]{:S(2)}) collective-permute-start(bf16[576,2304]{1,0:T(8,128)(2,1)} %pad_maximum_fusion.3.refs_1_), channel_id=1, source_target_pairs={{0,16},{8,24},{16,0},{24,8},{1,17},{9,25},{17,1},{25,9},{2,18},{10... | collective-permute-start | bytes 7962632 | tf_op jit(solution)/shard_map/ppermute | solution.py:690
  141.1 76.7 %collective-permute-start.15 = (bf16[576,2304]{1,0:T(8,128)(2,1)}, bf16[576,2304]{1,0:T(8,128)(2,1)}, u32[]{:S(2)}, u32[]{:S(2)}) collective-permute-start(bf16[576,2304]{1,0:T(8,128)(2,1)} %pad_maximum_fusion.3.refs_1_), channel_id=1, source_target_pairs={{0,8},{8,0},{16,24},{24,16},{1,9},{9,1},{17,25},{25,17},{2,10},{10... | collective-permute-start | bytes 7962632 | tf_op jit(solution)/shard_map/ppermute | solution.py:689
  220.3 44.4 %collective-permute-start.18 = (bf16[288,2304]{1,0:T(8,128)(2,1)}, bf16[288,2304]{1,0:T(8,128)(2,1)}, u32[]{:S(2)}, u32[]{:S(2)}) collective-permute-start(bf16[288,2304]{1,0:T(8,128)(2,1)} %slice.416), channel_id=1, source_target_pairs={{0,16},{8,24},{16,0},{24,8},{1,17},{9,25},{17,1},{25,9},{2,18},{10... | collective-permute-start | bytes 3981320 | tf_op jit(solution)/shard_map/ppermute | solution.py:705
  222.8 42.0 %collective-permute-start.17 = (bf16[288,2304]{1,0:T(8,128)(2,1)S(1)}, bf16[288,2304]{1,0:T(8,128)(2,1)}, u32[]{:S(2)}, u32[]{:S(2)}) collective-permute-start(bf16[288,2304]{1,0:T(8,128)(2,1)S(1)} %slice.415), channel_id=1, source_target_pairs={{0,8},{8,0},{16,24},{24,16},{1,9},{9,1},{17,25},{25,17},{2,10},{10... | collective-permute-start | bytes 3981320 | tf_op jit(solution)/shard_map/ppermute | solution.py:704
  224.3 58.7 %collective-permute-start.20 = (bf16[576,2304]{1,0:T(8,128)(2,1)}, bf16[576,2304]{1,0:T(8,128)(2,1)}, u32[]{:S(2)}, u32[]{:S(2)}) collective-permute-start(bf16[576,2304]{1,0:T(8,128)(2,1)} %pad_maximum_fusion.3.refs_1_), channel_id=1, source_target_pairs={{0,1},{1,0},{2,3},{3,2},{4,5},{5,4},{6,7},{7,6},{8,9},{9,8},{10,11... | collective-permute-start | bytes 7962632 | tf_op jit(solution)/shard_map/ppermute | solution.py:707
  224.7 58.4 %collective-permute-start.22 = (bf16[576,2304]{1,0:T(8,128)(2,1)}, bf16[576,2304]{1,0:T(8,128)(2,1)}, u32[]{:S(2)}, u32[]{:S(2)}) collective-permute-start(bf16[576,2304]{1,0:T(8,128)(2,1)} %collective-permute-done.16.refs_3_), channel_id=1, source_target_pairs={{0,1},{1,0},{2,3},{3,2},{4,5},{5,4},{6,7},{7,6},{8,9},{9,8},{10,11... | collective-permute-start | bytes 7962632 | tf_op jit(solution)/shard_map/ppermute | solution.py:707
  224.8 58.2 %collective-permute-start.21 = (bf16[576,2304]{1,0:T(8,128)(2,1)}, bf16[576,2304]{1,0:T(8,128)(2,1)}, u32[]{:S(2)}, u32[]{:S(2)}) collective-permute-start(bf16[576,2304]{1,0:T(8,128)(2,1)} %collective-permute-done.15.refs_2_), channel_id=1, source_target_pairs={{0,1},{1,0},{2,3},{3,2},{4,5},{5,4},{6,7},{7,6},{8,9},{9,8},{10,11... | collective-permute-start | bytes 7962632 | tf_op jit(solution)/shard_map/ppermute | solution.py:707
  356.6 248.5 %all-gather.23.cloned.1.call-start = ((), (), s32[]{:S(2)}) async-start(), calls=%async_computation.7 | async-start | bytes 2211840 | tf_op jit(solution)/shard_map/all_gather | solution.py:1036
  393.6 27.1 %collective-permute-start.25 = (bf16[768,2304]{1,0:T(8,128)(2,1)}, bf16[768,2304]{1,0:T(8,128)(2,1)}, u32[]{:S(2)}, u32[]{:S(2)}) collective-permute-start(bf16[768,2304]{1,0:T(8,128)(2,1)} %convolution_convert_fusion.4), channel_id=1, source_target_pairs={{0,1},{1,0},{2,3},{3,2},{4,5},{5,4},{6,7},{7,6},{8,9},{9,8},{10,11... | collective-permute-start | bytes 10616840 | tf_op jit(solution)/shard_map/ppermute | solution.py:812
  407.0 198.0 %collective-permute-start.30 = (bf16[768,2304]{1,0:T(8,128)(2,1)}, bf16[768,2304]{1,0:T(8,128)(2,1)}, u32[]{:S(2)}, u32[]{:S(2)}) collective-permute-start(bf16[768,2304]{1,0:T(8,128)(2,1)} %convolution_convert_fusion.1), channel_id=1, source_target_pairs={{0,1},{1,0},{2,3},{3,2},{4,5},{5,4},{6,7},{7,6},{8,9},{9,8},{10,11... | collective-permute-start | bytes 10616840 | tf_op jit(solution)/shard_map/ppermute | solution.py:812
  414.2 82.0 %collective-permute-start.29 = (bf16[768,2304]{1,0:T(8,128)(2,1)}, bf16[768,2304]{1,0:T(8,128)(2,1)}, u32[]{:S(2)}, u32[]{:S(2)}) collective-permute-start(bf16[768,2304]{1,0:T(8,128)(2,1)} %convolution_convert_fusion.2), channel_id=1, source_target_pairs={{0,1},{1,0},{2,3},{3,2},{4,5},{5,4},{6,7},{7,6},{8,9},{9,8},{10,11... | collective-permute-start | bytes 10616840 | tf_op jit(solution)/shard_map/ppermute | solution.py:812
  420.6 65.9 %collective-permute-start.26 = (bf16[768,2304]{1,0:T(8,128)(2,1)}, bf16[768,2304]{1,0:T(8,128)(2,1)}, u32[]{:S(2)}, u32[]{:S(2)}) collective-permute-start(bf16[768,2304]{1,0:T(8,128)(2,1)} %convolution_convert_fusion.3), channel_id=1, source_target_pairs={{0,1},{1,0},{2,3},{3,2},{4,5},{5,4},{6,7},{7,6},{8,9},{9,8},{10,11... | collective-permute-start | bytes 10616840 | tf_op jit(solution)/shard_map/ppermute | solution.py:812
  426.0 59.6 %collective-permute-start.27 = (bf16[384,2304]{1,0:T(8,128)(2,1)}, bf16[384,2304]{1,0:T(8,128)(2,1)}, u32[]{:S(2)}, u32[]{:S(2)}) collective-permute-start(bf16[384,2304]{1,0:T(8,128)(2,1)} %fusion.43), channel_id=1, source_target_pairs={{0,8},{8,0},{16,24},{24,16},{1,9},{9,1},{17,25},{25,17},{2,10},{10... | collective-permute-start | bytes 5308424 | tf_op jit(solution)/shard_map/ppermute | solution.py:818
  431.1 55.4 %collective-permute-start.28 = (bf16[384,2304]{1,0:T(8,128)(2,1)}, bf16[384,2304]{1,0:T(8,128)(2,1)}, u32[]{:S(2)}, u32[]{:S(2)}) collective-permute-start(bf16[384,2304]{1,0:T(8,128)(2,1)} %fusion.40), channel_id=1, source_target_pairs={{0,16},{8,24},{16,0},{24,8},{1,17},{9,25},{17,1},{25,9},{2,18},{10... | collective-permute-start | bytes 5308424 | tf_op jit(solution)/shard_map/ppermute | solution.py:819
  495.5 105.3 %collective-permute-start.31 = (bf16[768,2304]{1,0:T(8,128)(2,1)}, bf16[768,2304]{1,0:T(8,128)(2,1)}, u32[]{:S(2)}, u32[]{:S(2)}) collective-permute-start(bf16[768,2304]{1,0:T(8,128)(2,1)} %add_convert_fusion.2), channel_id=1, source_target_pairs={{0,8},{8,0},{16,24},{24,16},{1,9},{9,1},{17,25},{25,17},{2,10},{10... | collective-permute-start | bytes 10616840 | tf_op jit(solution)/shard_map/ppermute | solution.py:839
  506.3 98.1 %collective-permute-start.32 = (bf16[768,2304]{1,0:T(8,128)(2,1)}, bf16[768,2304]{1,0:T(8,128)(2,1)}, u32[]{:S(2)}, u32[]{:S(2)}) collective-permute-start(bf16[768,2304]{1,0:T(8,128)(2,1)} %add_convert_fusion.1), channel_id=1, source_target_pairs={{0,16},{8,24},{16,0},{24,8},{1,17},{9,25},{17,1},{25,9},{2,18},{10... | collective-permute-start | bytes 10616840 | tf_op jit(solution)/shard_map/ppermute | solution.py:840
  552.4 200.5 %reduce-scatter.8.cloned.1.call-start = ((), (), s32[]{:S(2)}) async-start(), calls=%async_computation.9 | async-start | bytes 4423680 | tf_op jit(solution)/shard_map/reduce_scatter | solution.py:869
  568.5 24.8 %collective-permute-start.34 = (bf16[768,2048]{1,0:T(8,128)(2,1)}, bf16[768,2048]{1,0:T(8,128)(2,1)}, u32[]{:S(2)}, u32[]{:S(2)}) collective-permute-start(bf16[768,2048]{1,0:T(8,128)(2,1)} %convolution_convert_fusion.7), channel_id=1, source_target_pairs={{0,1},{1,0},{2,3},{3,2},{4,5},{5,4},{6,7},{7,6},{8,9},{9,8},{10,11... | collective-permute-start | bytes 9437192 | tf_op jit(solution)/shard_map/ppermute | solution.py:808
  591.9 74.7 %collective-permute-start.37 = (bf16[512,384]{1,0:T(8,128)(2,1)}, bf16[512,384]{1,0:T(8,128)(2,1)}, u32[]{:S(2)}, u32[]{:S(2)}) collective-permute-start(bf16[512,384]{1,0:T(8,128)(2,1)} %get-tuple-element.190), channel_id=1, source_target_pairs={{0,16},{8,24},{16,0},{24,8},{1,17},{9,25},{17,1},{25,9},{2,18},{10... | collective-permute-start | bytes 1179656 | tf_op jit(solution)/shard_map/ppermute | solution.py:819
  593.2 73.4 %collective-permute-start.36 = (bf16[512,384]{1,0:T(8,128)(2,1)}, bf16[512,384]{1,0:T(8,128)(2,1)}, u32[]{:S(2)}, u32[]{:S(2)}) collective-permute-start(bf16[512,384]{1,0:T(8,128)(2,1)} %get-tuple-element.191), channel_id=1, source_target_pairs={{0,8},{8,0},{16,24},{24,16},{1,9},{9,1},{17,25},{25,17},{2,10},{10... | collective-permute-start | bytes 1179656 | tf_op jit(solution)/shard_map/ppermute | solution.py:818
  600.9 68.1 %collective-permute-start.39 = (bf16[384,512]{1,0:T(8,128)(2,1)}, bf16[384,512]{1,0:T(8,128)(2,1)}, u32[]{:S(2)}, u32[]{:S(2)}) collective-permute-start(bf16[384,512]{1,0:T(8,128)(2,1)} %get-tuple-element.188), channel_id=1, source_target_pairs={{0,16},{8,24},{16,0},{24,8},{1,17},{9,25},{17,1},{25,9},{2,18},{10... | collective-permute-start | bytes 1179656 | tf_op jit(solution)/shard_map/ppermute | solution.py:819
  604.3 64.6 %collective-permute-start.38 = (bf16[384,512]{1,0:T(8,128)(2,1)}, bf16[384,512]{1,0:T(8,128)(2,1)}, u32[]{:S(2)}, u32[]{:S(2)}) collective-permute-start(bf16[384,512]{1,0:T(8,128)(2,1)} %get-tuple-element.189), channel_id=1, source_target_pairs={{0,8},{8,0},{16,24},{24,16},{1,9},{9,1},{17,25},{25,17},{2,10},{10... | collective-permute-start | bytes 1179656 | tf_op jit(solution)/shard_map/ppermute | solution.py:818
  616.3 158.4 %reduce-scatter.6.cloned.1.call-start = ((), (), s32[]{:S(2)}) async-start(), calls=%async_computation.8 | async-start | bytes 1216512 | tf_op jit(solution)/shard_map/reduce_scatter | solution.py:1096
  693.4 23.6 %collective-permute-start.40 = (bf16[768,2048]{1,0:T(8,128)(2,1)}, bf16[768,2048]{1,0:T(8,128)(2,1)}, u32[]{:S(2)}, u32[]{:S(2)}) collective-permute-start(bf16[768,2048]{1,0:T(8,128)(2,1)} %convolution_convert_fusion.6), channel_id=1, source_target_pairs={{0,1},{1,0},{2,3},{3,2},{4,5},{5,4},{6,7},{7,6},{8,9},{9,8},{10,11... | collective-permute-start | bytes 9437192 | tf_op jit(solution)/shard_map/ppermute | solution.py:808
  699.9 45.7 %collective-permute-start.51 = (bf16[1024,384]{1,0:T(8,128)(2,1)}, bf16[1024,384]{1,0:T(8,128)(2,1)}, u32[]{:S(2)}, u32[]{:S(2)}) collective-permute-start(bf16[1024,384]{1,0:T(8,128)(2,1)} %get-tuple-element.186), channel_id=1, source_target_pairs={{0,16},{8,24},{16,0},{24,8},{1,17},{9,25},{17,1},{25,9},{2,18},{10... | collective-permute-start | bytes 2359304 | tf_op jit(solution)/shard_map/ppermute | solution.py:840
  701.5 44.1 %collective-permute-start.50 = (bf16[1024,384]{1,0:T(8,128)(2,1)}, bf16[1024,384]{1,0:T(8,128)(2,1)}, u32[]{:S(2)}, u32[]{:S(2)}) collective-permute-start(bf16[1024,384]{1,0:T(8,128)(2,1)} %get-tuple-element.187), channel_id=1, source_target_pairs={{0,8},{8,0},{16,24},{24,16},{1,9},{9,1},{17,25},{25,17},{2,10},{10... | collective-permute-start | bytes 2359304 | tf_op jit(solution)/shard_map/ppermute | solution.py:839
  707.4 138.2 %all-gather.27.cloned.1.call-start = ((), (), s32[]{:S(2)}) async-start(), calls=%async_computation.11 | async-start | bytes 4423680 | tf_op jit(solution)/shard_map/all_gather | solution.py:888
  744.1 44.9 %collective-permute-start.44 = (bf16[768,512]{1,0:T(8,128)(2,1)}, bf16[768,512]{1,0:T(8,128)(2,1)S(1)}, u32[]{:S(2)}, u32[]{:S(2)}) collective-permute-start(bf16[768,512]{1,0:T(8,128)(2,1)} %get-tuple-element.180), channel_id=1, source_target_pairs={{0,16},{8,24},{16,0},{24,8},{1,17},{9,25},{17,1},{25,9},{2,18},{10... | collective-permute-start | bytes 2359304 | tf_op jit(solution)/shard_map/ppermute | solution.py:840
  744.5 44.4 %collective-permute-start.43 = (bf16[768,512]{1,0:T(8,128)(2,1)}, bf16[768,512]{1,0:T(8,128)(2,1)}, u32[]{:S(2)}, u32[]{:S(2)}) collective-permute-start(bf16[768,512]{1,0:T(8,128)(2,1)} %get-tuple-element.181), channel_id=1, source_target_pairs={{0,8},{8,0},{16,24},{24,16},{1,9},{9,1},{17,25},{25,17},{2,10},{10... | collective-permute-start | bytes 2359304 | tf_op jit(solution)/shard_map/ppermute | solution.py:839
  748.3 45.7 %collective-permute-start.52 = (bf16[256,384]{1,0:T(8,128)(2,1)}, bf16[256,384]{1,0:T(8,128)(2,1)S(1)}, u32[]{:S(2)}, u32[]{:S(2)}) collective-permute-start(bf16[256,384]{1,0:T(8,128)(2,1)} %get-tuple-element.199), channel_id=1, source_target_pairs={{0,2},{1,3},{2,4},{3,5},{4,6},{5,7},{6,0},{7,1},{8,10},{9,11},{10,... | collective-permute-start | bytes 589832 | tf_op jit(solution)/shard_map/ppermute | solution.py:858
  750.0 50.8 %collective-permute-start.54 = (bf16[256,384]{1,0:T(8,128)(2,1)}, bf16[256,384]{1,0:T(8,128)(2,1)}, u32[]{:S(2)}, u32[]{:S(2)}) collective-permute-start(bf16[256,384]{1,0:T(8,128)(2,1)} %get-tuple-element.200), channel_id=1, source_target_pairs={{0,6},{1,7},{2,0},{3,1},{4,2},{5,3},{6,4},{7,5},{8,14},{9,15},{10,... | collective-permute-start | bytes 589832 | tf_op jit(solution)/shard_map/ppermute | solution.py:858
  750.4 50.4 %collective-permute-start.53 = (bf16[256,384]{1,0:T(8,128)(2,1)}, bf16[256,384]{1,0:T(8,128)(2,1)}, u32[]{:S(2)}, u32[]{:S(2)}) collective-permute-start(bf16[256,384]{1,0:T(8,128)(2,1)} %get-tuple-element.201), channel_id=1, source_target_pairs={{0,4},{1,5},{2,6},{3,7},{4,0},{5,1},{6,2},{7,3},{8,12},{9,13},{10,... | collective-permute-start | bytes 589832 | tf_op jit(solution)/shard_map/ppermute | solution.py:858
  792.0 22.6 %collective-permute-start.47 = (bf16[192,1024]{1,0:T(8,128)(2,1)}, bf16[192,1024]{1,0:T(8,128)(2,1)}, u32[]{:S(2)}, u32[]{:S(2)}) collective-permute-start(bf16[192,1024]{1,0:T(8,128)(2,1)} %get-tuple-element.196), channel_id=1, source_target_pairs={{0,2},{1,3},{2,4},{3,5},{4,6},{5,7},{6,0},{7,1},{8,10},{9,11},{10,... | collective-permute-start | bytes 1179656 | tf_op jit(solution)/shard_map/ppermute | solution.py:858
  794.1 23.7 %collective-permute-start.48 = (bf16[192,1024]{1,0:T(8,128)(2,1)S(1)}, bf16[192,1024]{1,0:T(8,128)(2,1)}, u32[]{:S(2)}, u32[]{:S(2)}) collective-permute-start(bf16[192,1024]{1,0:T(8,128)(2,1)S(1)} %get-tuple-element.198), channel_id=1, source_target_pairs={{0,4},{1,5},{2,6},{3,7},{4,0},{5,1},{6,2},{7,3},{8,12},{9,13},{10,... | collective-permute-start | bytes 1179656 | tf_op jit(solution)/shard_map/ppermute | solution.py:858
  (112 other events, 1712.9 us)
Sparse Core Ops, SparseCore 0:
  9.6 38.9 all-gather.16
  56.5 72.0 all-gather.24
  132.0 85.5 all-gather.18
  220.4 109.4 all-gather.20
  356.7 188.9 reduce-scatter.3
  552.5 47.9 all-gather.22
  616.4 67.5 reduce-scatter.7
  707.5 26.8 reduce-scatter.5
  753.0 50.3 all-gather.26

commit v10 on v9

--- a/solution.py
+++ b/solution.py
@@ -298,6 +298,44 @@
         )
         out_ref[0, at, :] = (dv * pull_ref[0, at, :].astype(F32)).astype(BF16)
         out_ref[1, at, :] = (dv * pull_ref[1, at, :].astype(F32)).astype(BF16)
+
+
+def quarter_kernel(places, quarter_ref, a_ref, b_ref, *refs):
+    del quarter_ref
+    *adds, out_ref = refs
+    total = dot_rows(a_ref[...], b_ref[0])
+    half = out_ref.shape[0] // 2
+    for first in (0, half):
+        part = total[first : first + half]
+        for place, add in zip(places, adds):
+            if place <= first < place + add.shape[0]:
+                part = part + add[pl.ds(first - place, half), :].astype(F32)
+        out_ref[pl.ds(first, half), :] = part.astype(BF16)
+
+
+def quarter_dot(a, first, last, b, quarter, adds):
+    tokens, size = a.shape[0], last - first
+    width = b.shape[2] // 2
+    tile = max(t for t in (128, 256, 384, 768) if width % t == 0)
+    steps = width // tile
+    specs = [
+        pl.BlockSpec((tokens, size), lambda n, q: (0, first // size)),
+        pl.BlockSpec((1, tokens, tile), lambda n, q: (q[0] // 2, 0, (q[0] % 2) * steps + n)),
+    ]
+    for _, add, start, count in adds:
+        specs.append(pl.BlockSpec((count, tile), lambda n, q, block=start // count: (block, n)))
+    return pl.pallas_call(
+        functools.partial(quarter_kernel, tuple(add[0] for add in adds)),
+        grid_spec=pltpu.PrefetchScalarGridSpec(
+            num_scalar_prefetch=1,
+            grid=(steps,),
+            in_specs=specs,
+            out_specs=pl.BlockSpec((size, tile), lambda n, q: (0, n)),
+        ),
+        out_shape=jax.ShapeDtypeStruct((size, width), BF16),
+        compiler_params=PARAMS,
+        name="quarter_dot",
+    )(quarter.reshape(1), a, b, *(add[1] for add in adds))
 
 
 def head_block(lead, rows):
@@ -772,7 +810,7 @@
 
 
 class Reduction:
-    def __init__(self, a_own, a_far, columns, width, fused=False):
+    def __init__(self, a_own, a_far, columns, width, paired=None):
         self.simple = lax.axis_size("grp") != 4
         count = lax.axis_size("seq")
         place = lax.axis_index("seq")
@@ -797,44 +835,48 @@
             self.arrived = self.product
             self.sent = (self.product,)
             return
-        group = lax.axis_index("grp")
+        self.group = lax.axis_index("grp")
         self.x, self.y = xor_pairs("grp", 1), xor_pairs("grp", 2)
-        self.b = [columns(group ^ k) for k in range(4)]
+        self.paired = paired
+        self.columns = columns
+        other = xor_pairs("seq", 1)
+        half = self.half
         self.far = [None] * 4
-        self.product = None
-        other = xor_pairs("seq", 1)
-        if fused:
-            b_all = jnp.concatenate(self.b, axis=1)
+        self.joint = None
+        if paired is None:
+            b_all = jnp.concatenate([columns(self.group ^ k) for k in range(4)], axis=1)
             far = lax.ppermute(dot_rows(a_far, b_all).astype(BF16), "seq", other)
-            self.product = (dot_rows(a_own, b_all) + far.astype(F32)).astype(BF16)
-        for k in () if fused else (3, 1, 2, 0):
-            product = dot_rows(a_far, self.b[k]).astype(BF16)
-            self.far[k] = lax.ppermute(product, "seq", other)
-        half = self.half
-        self.sent = (
-            self.own(3, 0, half).astype(BF16),
-            self.own(3, half, full).astype(BF16),
-        )
+            self.joint = (dot_rows(a_own, b_all) + far.astype(F32)).astype(BF16)
+        else:
+            for k in (3, 1, 2, 0):
+                product = quarter_dot(a_far, 0, full, paired, self.group ^ k, [])
+                self.far[k] = lax.ppermute(product, "seq", other)
+        self.sent = (self.own(3, 0, half), self.own(3, half, full))
         self.diag_a = lax.ppermute(self.sent[0], "grp", self.x)
         self.diag_b = lax.ppermute(self.sent[1], "grp", self.y)
 
-    def own(self, k, first, last):
-        if self.product is not None:
-            left = k * self.width
-            return self.product[first:last, left : left + self.width].astype(F32)
-        product = dot_rows(self.a_own[:, first:last], self.b[k])
-        return product + self.far[k][first:last].astype(F32)
+    def own(self, k, first, last, *adds):
+        if self.joint is None:
+            adds = [(place, add, 0, add.shape[0]) for place, add in adds]
+            adds.append((0, self.far[k], first, last - first))
+            return quarter_dot(self.a_own, first, last, self.paired, self.group ^ k, adds)
+        left = k * self.width
+        total = self.joint[first:last, left : left + self.width].astype(F32)
+        for place, add in adds:
+            after = last - first - place - add.shape[0]
+            total = total + jnp.pad(add.astype(F32), ((place, after), (0, 0)))
+        return total.astype(BF16)
 
     def second(self, *after):
         if self.simple:
             return ()
-        full, none = 2 * self.half, ((0, self.half), (0, 0))
+        full = 2 * self.half
         diag_a, diag_b = self.diag_a, self.diag_b
         if after:
             diag_a, diag_b = tie((diag_a, diag_b), *after)
         sent = (
-            (self.own(1, 0, full) + jnp.pad(diag_b.astype(F32), (none[0][::-1], (0, 0)))).astype(BF16),
-            (self.own(2, 0, full) + jnp.pad(diag_a.astype(F32), none)).astype(BF16),
+            self.own(1, 0, full, (self.half, diag_b)),
+            self.own(2, 0, full, (0, diag_a)),
         )
         self.from_x = lax.ppermute(sent[0], "grp", self.x)
         self.from_y = lax.ppermute(sent[1], "grp", self.y)
@@ -844,8 +886,7 @@
         from_x, from_y = self.from_x, self.from_y
         if after:
             from_x, from_y = tie((from_x, from_y), *after)
-        mine = self.own(0, 0, 2 * self.half) + from_x.astype(F32) + from_y.astype(F32)
-        return mine.astype(BF16)
+        return self.own(0, 0, 2 * self.half, (0, from_x), (0, from_y))
 
     def along_z(self, mine):
         mine = mine.reshape(self.chips, self.rows, -1)
@@ -889,6 +930,19 @@
         return parts.transpose(1, 0, 2).reshape(self.rows, 4 * self.width).astype(F32)
 
 
+def gather_parts(lines, one):
+    if one.simple:
+        return lax.psum(lines.astype(F32), "grp"), one.finish()
+    total = one.total().astype(BF16)
+    blocks = one.width // HS
+    pieces = [lines] + [total[:, n * HS : (n + 1) * HS] for n in range(blocks)]
+    parts = lax.all_gather(jnp.concatenate(pieces, axis=0), "grp")
+    count = lines.shape[0]
+    part = parts[:, count:].reshape(4, blocks, one.rows, HS).transpose(2, 0, 1, 3)
+    found = part.reshape(one.rows, 4 * one.width).astype(F32)
+    return jnp.sum(parts[:, :count].astype(F32), axis=0), found
+
+
 def shard_carry(ends, prods, reverse):
     count = lax.axis_size("seq")
     place = lax.axis_index("seq")
@@ -952,7 +1006,7 @@
         small_all[:, 2 * n_gain + n_lru :].reshape(-1, CONV, n_lru).transpose(1, 0, 2)
     ).reshape(CONV, LRU).astype(F32)
     in_gather = Gather(in_proj)
-    near = in_gather.first()
+    near = in_gather.first(small_all)
     in_gather.second()
     in_gather.third()
     gates_all = lax.all_gather(gate_heads, "seq", axis=0, tiled=True)
@@ -992,7 +1046,7 @@
     carry_in = shard_carry(end_state, end_prod, False)
     carries = chunk_carries(chunks, carry_in, False)
     state, branch, branch_split = mixer_branch(
-        tie(state_part, *up_gather.second(carries)), prod_part, carries, gate_pre, last + 1, place % 2
+        tie(state_part, *up_gather.second(carries, gate_pre)), prod_part, carries, gate_pre, last + 1, place % 2
     )
     branch_split = branch_split.reshape(2, row_count, LRU // 2)
     resid = inputs + jnp.dot(
@@ -1017,7 +1071,7 @@
         )
         return part[0]
 
-    up_sum = Reduction(second_own, second_far, up_columns, quarter)
+    up_sum = Reduction(second_own, second_far, up_columns, quarter, grad_expanded)
     grad_expanded = tie(grad_expanded, *up_sum.sent)
     grad_second_normed = dot_far(grad_expanded[0], proj_gate) + dot_far(
         grad_expanded[1], proj_up
@@ -1045,14 +1099,12 @@
         branch_split[1],
         lambda n: lax.dynamic_slice_in_dim(grad_mixer, n * (D // 4), D // 4, 1),
         D // 4,
-        True,
     )
     in_gate_sum = Reduction(
         first_own,
         first_far,
         lambda n: lax.dynamic_slice_in_dim(grad_gate, n * width, width, 1),
         width,
-        True,
     )
     sent = (*out_sum.sent, *in_gate_sum.sent)
     sent = up_sum.third(down_sum, *sent, offload=True)
@@ -1077,7 +1129,6 @@
         first_far,
         lambda n: lax.dynamic_slice_in_dim(grad_inner, n * width, width, 1),
         width,
-        True,
     )
     grad_inner = tie(grad_inner, *in_value_sum.sent)
 
@@ -1093,25 +1144,25 @@
     )
     lines = flat.shape[1]
     flat = jnp.pad(flat, ((0, 0), (0, -lines % 16), (0, 0))).astype(BF16).reshape(-1, HS)
+    flat = tie(flat, up_sum.arrived)
     flat = lax.psum_scatter(flat, "seq", scatter_dimension=0, tiled=True)
     first_grad = first_grad + dot_far(grad_inner, in_value)
     sent = in_value_sum.second(first_grad)
     out_sum.third(*sent)
-    flat = lax.all_gather(tie(flat, *sent), "grp").astype(F32)
-    flat = jnp.sum(flat, axis=0)[:lines].reshape(-1)
+    up_total = up_sum.finish(edge)
+    flat, out_total = gather_parts(tie(flat, up_total), out_sum)
+    flat = flat[:lines].reshape(-1)
     n_gates = flat.shape[0] - (CONV + 1) * n_lru
     gates_total = flat[:n_gates].reshape(gate_heads.shape)
     taps_total = flat[n_gates : n_gates + CONV * n_lru].reshape(CONV, n_lru)
     decay_total = flat[n_gates + CONV * n_lru :]
 
-    up_total = up_sum.finish(edge)
-    down_total = down_sum.astype(F32)
+    down_total = tie(down_sum, *sent).astype(F32)
     if in_value_sum.simple:
         in_total = jnp.concatenate([in_value_sum.finish(), in_gate_sum.finish()], axis=1)
-        last_sent = ()
     else:
         both = jnp.concatenate([in_value_sum.mine(), in_gate_sum.mine()], axis=1)
-        last_sent = in_value_sum.along_z(both)
+        in_value_sum.along_z(both)
         both = in_value_sum.total().astype(BF16)
         in_total = jnp.concatenate(
             [
@@ -1122,7 +1173,6 @@
             ],
             axis=1,
         ).astype(F32)
-    out_total = out_sum.finish(*last_sent)
     ffn_out = jnp.dot(tie(hidden, *sent), proj_down, preferred_element_type=F32)
     block_out = by_token((resid + ffn_out).astype(BF16).reshape(tokens.shape))
     grad_tokens = grad_resid + norm_back(inputs, first_scale, gain_one, first_grad)

time: 868 us -> 958 us (1.10)
  waiting for transfers between devices: 109 us -> 193 us
  matrix products: 244 us -> 161 us
  Pallas kernels: 212 us -> 276 us
  other arithmetic: 41.3 us -> 53.9 us
    dot_general x16 -> x7, matrix products: 135 us -> 52.5 us  [dot_rows(): lax.dot_general(a, b, (((0,), (0,)), ((), ())), preferred_element_type=F32)]
    pallas_call x0 -> x9, Pallas kernels: none -> 65.2 us  [quarter_dot(): pl.pallas_call(functools.partial(quarter_kernel, tuple((add[0] for add in...]
    ppermute x4, waiting for transfers between devices: 0.6 us -> 59 us  [second(): self.from_x = lax.ppermute(sent[0], 'grp', self.x)]
    ppermute x3, waiting for transfers between devices: 35 us -> 0.01 us  [__init__(): lax.ppermute(own, 'seq', ring_pairs(-2 * j))]
    all_gather x1, blocking collectives: 15.3 us -> 45.1 us  [body(): small_all = lax.all_gather(small, 'seq')]
    all_gather x2 -> x0, blocking collectives: 24.9 us -> none  [the longest x1 14.2 us: body(): flat = lax.all_gather(tie(flat, *sent), 'grp').astype(F32)]
    reduce_scatter x1, waiting for transfers between devices: 0.01 us -> 20.5 us  [body(): flat = lax.psum_scatter(flat, 'seq', scatter_dimension=0, tiled=True)]
    ppermute x4, waiting for transfers between devices: 0.94 us -> 20 us  [__init__(): self.diag_b = lax.ppermute(self.sent[1], 'grp', self.y)]
  transfers between devices with their start and end apart: 64 -> 65, of which waited for: 12 -> 17; matrix products, arithmetic and copies ran while one was open for 40% -> 28% of each run, Pallas kernels for 25% -> 29%
where the time goes in v10:
time: 958 us; the launch traced here: 948 us
  Pallas kernels  276 us (29%)
  waiting for transfers between devices  193 us (20%)
  matrix products  161 us (17%)
  local copies, waits for them, and re-layouts  98.5 us (10%)
  blocking collectives  94.6 us (10%)
  starting transfers between devices  55.9 us (6%)
  other arithmetic  53.9 us (6%)
  between operations  15.9 us (2%)
    dot_general x5, matrix products, dot_far(): lax.dot_general(a, b, (((1,), (1,)), ((), ())), preferred_element_type=F32)  76.9 us
    pallas_call x9, Pallas kernels, quarter_dot(): pl.pallas_call(functools.partial(quarter_kernel, tuple((add[0] for add in...  65.2 us
    pallas_call x3, Pallas kernels, call(): pl.pallas_call(kernel, grid=(steps,), in_specs=[pl.BlockSpec(memory_space...  65.1 us
    ppermute x4, waiting for transfers between devices, second(): self.from_x = lax.ppermute(sent[0], 'grp', self.x)  59 us
    dot_general x7, matrix products, dot_rows(): lax.dot_general(a, b, (((0,), (0,)), ((), ())), preferred_element_type=F32)  52.5 us
    pallas_call x1, Pallas kernels, mixer_backward(): pl.pallas_call(mixer_backward_kernel, grid=(HEADS,), in_specs=[full, full...  46.8 us
    all_gather x1, blocking collectives, body(): small_all = lax.all_gather(small, 'seq')  45.1 us
    unnamed x185, local copies, waits for them, and re-layouts  39.7 us
  transfers between devices with their start and end apart: 65, of which 17 were waited for; matrix products, arithmetic and copies ran while one was open for 28% of the time, Pallas kernels for 29%

profile of v10, /device:TPU:18, one launch (start us, length us, event | category | flops | bytes accessed | tf_op | source)
XLA Modules:
  0.0 947.9 jit_solution(4372228712790558468)
XLA Ops:
  15.8 45.1 %all-gather.8 = bf16[8,1,1664]{2,1,0:T(2,128)(2,1)S(1)} all-gather(bf16[1,1,1664]{2,1,0:T(2,128)(2,1)S(1)} %reshape.2498), channel_id=2, replica_groups=mesh['grp'=4,'seq'=8] {'seq'}, dimensions={0}, use_global_device_ids=true | all-gather | bytes 29952 | tf_op jit(solution)/shard_map/all_gather | solution.py:1000
  73.6 25.9 %collective-permute-done.4.refs_3_ = bf16[576,1024]{1,0:T(8,128)(2,1)} collective-permute-done((bf16[576,1024]{1,0:T(8,128)(2,1)}, bf16[576,1024]{1,0:T(8,128)(2,1)}, u32[]{:S(2)}, u32[]{:S(2)}) %collective-permute-start.4) | collective-permute-done | bytes 1179680 | tf_op jit(solution)/shard_map/ppermute | solution.py:728
  104.6 11.0 %collective-permute-done.5.refs_4_ = bf16[288,1024]{1,0:T(8,128)(2,1)} collective-permute-done((bf16[288,1024]{1,0:T(8,128)(2,1)S(1)}, bf16[288,1024]{1,0:T(8,128)(2,1)}, u32[]{:S(2)}, u32[]{:S(2)}) %collective-permute-start.5) | collective-permute-done | bytes 589856 | tf_op jit(solution)/shard_map/ppermute | solution.py:742
  117.8 5.3 copy.294
  133.9 12.0 %gathered_dot.2 = (bf16[1024,2048]{1,0:T(8,128)(2,1)}, bf16[1536,2048]{1,0:T(8,128)(2,1)}) custom-call(s32[3]{0:T(128)} %pad_add_fusion.1.where_ref, bf16[1024,1536]{1,0:T(8,128)(2,1)} %copy-done.10, bf16[192,4096]{1,0:T(8,128)(2,1)} %refs_0_.4, bf16[576,1024]{1,0:T(8,128)(2,1)} %constant_dynamic-update-slice_fusion.refs_1_, ...), custom_call_target="tpu_custom_call" | custom-call | tf_op jit(solution)/shard_map/gathered_dot/pallas_call | solution.py:753
  158.1 13.1 %gathered_dot.3 = (f32[1024,2048]{1,0:T(8,128)}, bf16[1536,2048]{1,0:T(8,128)(2,1)}) custom-call(s32[3]{0:T(128)} %pad_add_fusion.1.where_ref, bf16[1024,1536]{1,0:T(8,128)(2,1)} %copy-done.10, bf16[192,4096]{1,0:T(8,128)(2,1)} %refs_0_.4, bf16[576,1024]{1,0:T(8,128)(2,1)} %constant_dynamic-update-slice_fusion.refs_1_, ...), custom_call_target="tpu_custom_call" | custom-call | tf_op jit(solution)/shard_map/gathered_dot/pallas_call | solution.py:753
  171.5 28.1 %mixer_forward.1 = (bf16[2,512,2048]{2,1,0:T(8,128)(2,1)S(1)}, f32[2,512,2048]{2,1,0:T(8,128)}, f32[2,512,2048]{2,1,0:T(8,128)}, f32[2,512,2048]{2,1,0:T(8,128)}, f32[2,2,8,2048]{3,2,1,0:T(8,128)S(1)}) custom-call(bf16[2,512,2048]{2,1,0:T(8,128)(2,1)S(1)} %bitcast.739, bf16[2,8,2048]{2,1,0:T(8,128)(2,1)S(1)} %collective-permute-done.13.halo_ref, ...), custom_call_target="tpu_custom_call" | custom-call | tf_op jit(solution)/shard_map/mixer_forward/pallas_call | solution.py:360
  202.2 12.9 %all-gather.2 = f32[16,2,2048]{2,1,0:T(2,128)S(1)} all-gather(f32[2,2,2048]{2,1,0:T(2,128)S(1)} %copy.313), channel_id=4, replica_groups=mesh['grp'=4,'seq'=8] {'seq'}, dimensions={0}, use_global_device_ids=true | all-gather | bytes 294912 | tf_op jit(solution)/shard_map/all_gather | solution.py:949
  215.6 9.5 %collective-permute-done.16.refs_3_ = bf16[576,2304]{1,0:T(8,128)(2,1)} collective-permute-done((bf16[576,2304]{1,0:T(8,128)(2,1)}, bf16[576,2304]{1,0:T(8,128)(2,1)}, u32[]{:S(2)}, u32[]{:S(2)}) %collective-permute-start.16) | collective-permute-done | bytes 2654240 | tf_op jit(solution)/shard_map/ppermute | solution.py:728
  233.8 5.3 copy.328
  239.1 17.8 %mixer_branch.1 = (f32[2,512,2048]{2,1,0:T(8,128)}, bf16[2,512,2048]{2,1,0:T(8,128)(2,1)S(1)}, bf16[2,2,512,1024]{3,2,1,0:T(8,128)(2,1)S(1)}) custom-call(s32[1]{0:T(128)} %bitcast.3.core_ref, f32[2,512,2048]{2,1,0:T(8,128)} %get-tuple-element.94.state_ref, f32[2,512,2048]{2,1,0:T(8,128)} %get-tuple-element.95.prod_ref, ...), custom_call_target="tpu_custom_call" | custom-call | tf_op jit(solution)/shard_map/mixer_branch/pallas_call | solution.py:402
  264.7 5.6 collective-permute-done.17.refs_4_
  270.3 10.5 %convert_add_fusion.x_ref = f32[1024,1536]{1,0:T(8,128)S(1)} fusion(bf16[1024,1536]{1,0:T(8,128)(2,1)} %bitcast.733, bf16[1024,2048]{1,0:T(8,128)(2,1)} %bitcast.746, bf16[2048,1536]{1,0:T(8,128)(2,1)} %all-gather.19.cloned.1.call-done), kind=kOutput, calls=%fused_computation.3 | convolution fusion | flops 6445596672 | bytes 19922944 | tf_op jit(solution)/shard_map/dot_general | solution.py:1052
  287.7 40.0 %gathered_ffn.1 = (bf16[1024,4608]{1,0:T(8,128)(2,1)}, bf16[2,1024,4608]{2,1,0:T(8,128)(2,1)}, bf16[1536,4608]{1,0:T(8,128)(2,1)}, bf16[1536,4608]{1,0:T(8,128)(2,1)}) custom-call(s32[3]{0:T(128)} %pad_add_fusion.1.where_ref, bf16[1024,1536]{1,0:T(8,128)(2,1)} %copy-done.23, bf16[192,9216]{1,0:T(8,128)(2,1)} %refs_0_.5, ...), custom_call_target="tpu_custom_call" | custom-call | tf_op jit(solution)/shard_map/gathered_ffn/pallas_call | solution.py:753
  327.8 21.6 %convolution_convert_fusion = bf16[4608,1536]{1,0:T(8,128)(2,1)} fusion(bf16[1024,4608]{1,0:T(8,128)(2,1)} %get-tuple-element.140, bf16[1024,1536]{1,0:T(8,128)(2,1)S(1)} %bitcast.735), kind=kOutput, calls=%fused_computation | convolution fusion | flops 14502592512 | bytes 26738688 | tf_op jit(solution)/shard_map/dot_general | solution.py:585
  351.4 26.7 %ffn_backward.1.b_ref = bf16[2,1024,4608]{2,1,0:T(8,128)(2,1)} custom-call(bf16[1024,1536]{1,0:T(8,128)(2,1)S(1)} %bitcast.736, bf16[4608,1536]{1,0:T(8,128)(2,1)} %all-gather.21.cloned.1.call-done.down_ref, bf16[2,1024,4608]{2,1,0:T(8,128)(2,1)} %get-tuple-element.102.pull_ref), custom_call_target="tpu_custom_call" | custom-call | tf_op jit(solution)/shard_map/ffn_backward/pallas_call | solution.py:544
  378.1 7.3 quarter_dot.9
  386.5 5.0 fusion.136
  391.9 6.0 quarter_dot.14
  397.9 7.3 quarter_dot.12
  410.9 6.6 quarter_dot.11
  419.3 21.8 %fusion = f32[1024,1536]{1,0:T(8,128)} fusion(bf16[1536,4608]{1,0:T(8,128)(2,1)} %get-tuple-element.107, bf16[2,1024,4608]{2,1,0:T(8,128)(2,1)} %ffn_backward.1.b_ref), kind=kOutput, calls=%fused_computation.4 | convolution fusion | flops 14495514624 | bytes 29884416 | tf_op jit(solution)/shard_map/dot_general | solution.py:595
  441.1 23.0 %fusion.11 = f32[1024,1536]{1,0:T(8,128)} fusion(f32[1024,1536]{1,0:T(8,128)} %fusion, bf16[1536,4608]{1,0:T(8,128)(2,1)} %get-tuple-element.106, bf16[2,1024,4608]{2,1,0:T(8,128)(2,1)} %ffn_backward.1.b_ref), kind=kOutput, calls=%fused_computation.23 | convolution fusion | flops 14497087488 | bytes 36175872 | tf_op jit(solution)/shard_map/dot_general | solution.py:595
  464.1 11.4 %collective-permute-done.26.refs_0_ = bf16[384,2304]{1,0:T(8,128)(2,1)} collective-permute-done((bf16[384,2304]{1,0:T(8,128)(2,1)S(1)}, bf16[384,2304]{1,0:T(8,128)(2,1)}, u32[]{:S(2)}, u32[]{:S(2)}) %collective-permute-start.26) | collective-permute-done | bytes 1769504 | tf_op jit(solution)/shard_map/ppermute | solution.py:855
  476.8 8.6 quarter_dot.13
  485.4 8.7 quarter_dot.15
  498.0 5.6 fusion.129
  503.7 11.0 %fusion.144 = f32[1024,2048]{1,0:T(8,128)} fusion(bf16[1024,1536]{1,0:T(8,128)(2,1)S(1)} %get-tuple-element.118, bf16[2048,1536]{1,0:T(8,128)(2,1)} %all-gather.19.cloned.1.call-done), kind=kOutput, calls=%fused_computation.300 | convolution fusion | flops 6442450944 | bytes 17825792 | tf_op jit(solution)/shard_map/dot_general | solution.py:595
  514.7 22.4 %mixer_reverse.1 = (bf16[2,512,2048]{2,1,0:T(8,128)(2,1)S(1)}, f32[2,512,2048]{2,1,0:T(8,128)S(1)}, f32[2,512,2048]{2,1,0:T(8,128)}, f32[2,2,8,2048]{3,2,1,0:T(8,128)S(1)}) custom-call(f32[2,512,2048]{2,1,0:T(8,128)} %bitcast.754, f32[2,512,2048]{2,1,0:T(8,128)} %bitcast.748, f32[2,512,2048]{2,1,0:T(8,128)} %get-tuple-element.111.keep_ref, ...), custom_call_target="tpu_custom_call" | custom-call | tf_op jit(solution)/shard_map/mixer_reverse/pallas_call | solution.py:424
  540.2 5.5 convolution_convert_fusion.1
  545.8 7.4 quarter_dot.16
  564.3 12.4 %all-gather.3 = f32[16,2,2048]{2,1,0:T(2,128)S(1)} all-gather(f32[2,2,2048]{2,1,0:T(2,128)S(1)} %copy.345), channel_id=5, replica_groups=mesh['grp'=4,'seq'=8] {'seq'}, dimensions={0}, use_global_device_ids=true | all-gather | bytes 294912 | tf_op jit(solution)/shard_map/all_gather | solution.py:949
  576.8 5.9 add_convert_fusion.3
  591.4 56.2 %collective-permute-done.30.refs_0_ = bf16[768,2304]{1,0:T(8,128)(2,1)} collective-permute-done((bf16[768,2304]{1,0:T(8,128)(2,1)}, bf16[768,2304]{1,0:T(8,128)(2,1)}, u32[]{:S(2)}, u32[]{:S(2)}) %collective-permute-start.30) | collective-permute-done | bytes 3538976 | tf_op jit(solution)/shard_map/ppermute | solution.py:881
  650.4 8.3 quarter_dot.17
  664.1 46.8 %mixer_backward.1 = (bf16[2,512,2048]{2,1,0:T(8,128)(2,1)S(1)}, f32[2,32,2048]{2,1,0:T(8,128)S(1)}, f32[2,8,2048]{2,1,0:T(8,128)S(1)}, f32[16,128,256]{2,1,0:T(8...) custom-call(f32[2,512,2048]{2,1,0:T(8,128)} %copy-done.11, f32[2,512,2048]{2,1,0:T(8,128)} %get-tuple-element.124.prod_ref, ...), custom_call_target="tpu_custom_call" | custom-call | tf_op jit(solution)/shard_map/mixer_backward/pallas_call | solution.py:446
  718.9 10.5 %fusion.145 = f32[1024,1536]{1,0:T(8,128)} fusion(bf16[1024,2048]{1,0:T(8,128)(2,1)S(1)} %bitcast.741, bf16[1536,2048]{1,0:T(8,128)(2,1)} %get-tuple-element.134), kind=kOutput, calls=%fused_computation.301 | convolution fusion | flops 6442450944 | bytes 16777216 | tf_op jit(solution)/shard_map/dot_general | solution.py:595
  732.5 5.3 convolution_convert_fusion.2
  748.5 15.0 %collective-permute-done.46 = bf16[768,512]{1,0:T(8,128)(2,1)} collective-permute-done((bf16[768,512]{1,0:T(8,128)(2,1)}, bf16[768,512]{1,0:T(8,128)(2,1)}, u32[]{:S(2)}, u32[]{:S(2)}) %collective-permute-start.46) | collective-permute-done | bytes 786464 | tf_op jit(solution)/shard_map/ppermute | solution.py:882
  768.4 5.8 add_convert_fusion.1
  775.8 10.6 %fusion.10 = (f32[1024]{0:T(1024)S(1)}, f32[1024,1536]{1,0:T(8,128)}) fusion(f32[1536]{0:T(1024)S(1)} %reshape.2482, bf16[2,8,64,1536]{3,1,2,0:T(8,128)(2,1)S(1)} %copy-done.4, f32[1024,1536]{1,0:T(8,128)} %fusion.145, bf16[1024,2048]{1,0:T(8,128)(2,1)S(1)} %bitcast.743, bf16[1536,2048]{1,0:T(8,128)(2,1)S(1)} %bitcast.794), kind=kOutput, calls=%fused_computation.16 | convolution fusion | flops 6450314240 | bytes 26224640 | tf_op jit(solution)/shard_map/dot_general | solution.py:595
  787.0 18.7 %collective-permute-done.42 = bf16[384,512]{1,0:T(8,128)(2,1)S(1)} collective-permute-done((bf16[384,512]{1,0:T(8,128)(2,1)S(1)}, bf16[384,512]{1,0:T(8,128)(2,1)S(1)}, u32[]{:S(2)}, u32[]{:S(2)}) %collective-permute-start.42) | collective-permute-done | bytes 393248 | tf_op jit(solution)/shard_map/ppermute | solution.py:856
  818.4 6.5 fusion.9
  835.1 5.1 collective-permute-start.47
  849.1 20.5 %reduce-scatter.8.cloned.1.call-done = bf16[528,128]{1,0:T(8,128)(2,1)} async-done(((bf16[4224,128]{1,0:T(8,128)(2,1)}), bf16[528,128]{1,0:T(8,128)(2,1)}) %reduce-scatter.8.cloned.1.call-update) | async-done | bytes 135184 | tf_op jit(solution)/shard_map/reduce_scatter | solution.py:1148
  871.3 20.9 %add_convert_fusion = bf16[1024,1536]{1,0:T(8,128)(2,1)S(1)} fusion(f32[1024,1536]{1,0:T(8,128)} %copy-done.2, bf16[1024,4608]{1,0:T(8,128)(2,1)} %get-tuple-element.140, bf16[4608,1536]{1,0:T(8,128)(2,1)} %all-gather.21.cloned.1.call-done.down_ref), kind=kOutput, calls=%fused_computation.17 | convolution fusion | flops 14498660352 | bytes 33030144 | tf_op jit(solution)/shard_map/dot_general | solution.py:1176
  898.5 12.8 %all-gather.4 = bf16[768,512]{1,0:T(8,128)(2,1)S(1)} all-gather(bf16[192,512]{1,0:T(8,128)(2,1)S(1)} %get-tuple-element.254), channel_id=6, replica_groups=mesh['grp'=4,'seq'=8] {'grp'}, dimensions={0}, use_global_device_ids=true | all-gather | bytes 983040 | tf_op jit(solution)/shard_map/all_gather | solution.py:1169
  912.0 11.5 %all-gather.5 = bf16[768,512]{1,0:T(8,128)(2,1)S(1)} all-gather(bf16[192,512]{1,0:T(8,128)(2,1)S(1)} %get-tuple-element.255), channel_id=7, replica_groups=mesh['grp'=4,'seq'=8] {'grp'}, dimensions={0}, use_global_device_ids=true | all-gather | bytes 983040 | tf_op jit(solution)/shard_map/all_gather | solution.py:1169
  (425 shorter events, 211.4 us)
Async XLA Ops:
  7.2 61.1 %all-gather.17.cloned.1.call-start = ((), (), s32[]{:S(2)}) async-start(), calls=%async_computation.3 | async-start | bytes 1179648 | tf_op jit(solution)/shard_map/all_gather | solution.py:1012
  7.9 138.0 %all-gather.25.cloned.1.call-start = ((), (), s32[]{:S(2)}) async-start(), calls=%async_computation.10 | async-start | bytes 4423680 | tf_op jit(solution)/shard_map/all_gather | solution.py:709
  9.8 53.2 %collective-permute-start.2 = (bf16[192,1024]{1,0:T(8,128)(2,1)}, bf16[192,1024]{1,0:T(8,128)(2,1)}, u32[]{:S(2)}, u32[]{:S(2)}) collective-permute-start(bf16[192,1024]{1,0:T(8,128)(2,1)} %constant_dynamic-slice_fusion.15), channel_id=1, source_target_pairs={{0,2},{1,3},{2,4},{3,5},{4,6},{5,7},{6,0},{7,1},{8,10},{9,11},{10,... | collective-permute-start | bytes 1179656 | tf_op jit(solution)/shard_map/ppermute | solution.py:712
  11.3 51.7 %collective-permute-start.1 = (bf16[192,1024]{1,0:T(8,128)(2,1)}, bf16[192,1024]{1,0:T(8,128)(2,1)}, u32[]{:S(2)}, u32[]{:S(2)}) collective-permute-start(bf16[192,1024]{1,0:T(8,128)(2,1)} %constant_dynamic-slice_fusion.15), channel_id=1, source_target_pairs={{0,4},{1,5},{2,6},{3,7},{4,0},{5,1},{6,2},{7,3},{8,12},{9,13},{10,... | collective-permute-start | bytes 1179656 | tf_op jit(solution)/shard_map/ppermute | solution.py:712
  11.7 51.3 %collective-permute-start = (bf16[192,1024]{1,0:T(8,128)(2,1)}, bf16[192,1024]{1,0:T(8,128)(2,1)}, u32[]{:S(2)}, u32[]{:S(2)}) collective-permute-start(bf16[192,1024]{1,0:T(8,128)(2,1)} %constant_dynamic-slice_fusion.15), channel_id=1, source_target_pairs={{0,6},{1,7},{2,0},{3,1},{4,2},{5,3},{6,4},{7,5},{8,14},{9,15},{10,... | collective-permute-start | bytes 1179656 | tf_op jit(solution)/shard_map/ppermute | solution.py:712
  68.3 202.0 %all-gather.19.cloned.1.call-start = ((), (), s32[]{:S(2)}) async-start(), calls=%async_computation.4 | async-start | bytes 6488064 | tf_op jit(solution)/shard_map/all_gather | solution.py:563
  70.0 279.5 %all-gather.21.cloned.1.call-start = ((), (), s32[]{:S(2)}) async-start(), calls=%async_computation.5 | async-start | bytes 14598144 | tf_op jit(solution)/shard_map/all_gather | solution.py:563
  70.9 485.9 %reduce-scatter.4.cloned.1.call-start = ((), (), s32[]{:S(2)}) async-start(), calls=%async_computation.6 | async-start | bytes 14598144 | tf_op jit(solution)/shard_map/reduce_scatter | solution.py:1064
  71.0 28.6 %collective-permute-start.4 = (bf16[576,1024]{1,0:T(8,128)(2,1)}, bf16[576,1024]{1,0:T(8,128)(2,1)}, u32[]{:S(2)}, u32[]{:S(2)}) collective-permute-start(bf16[576,1024]{1,0:T(8,128)(2,1)} %constant_dynamic-update-slice_fusion.refs_1_), channel_id=1, source_target_pairs={{0,16},{8,24},{16,0},{24,8},{1,17},{9,25},{17,1},{25,9},{2,18},{10... | collective-permute-start | bytes 3538952 | tf_op jit(solution)/shard_map/ppermute | solution.py:728
  72.6 28.7 %collective-permute-start.3 = (bf16[576,1024]{1,0:T(8,128)(2,1)}, bf16[576,1024]{1,0:T(8,128)(2,1)}, u32[]{:S(2)}, u32[]{:S(2)}) collective-permute-start(bf16[576,1024]{1,0:T(8,128)(2,1)} %constant_dynamic-update-slice_fusion.refs_1_), channel_id=1, source_target_pairs={{0,8},{8,0},{16,24},{24,16},{1,9},{9,1},{17,25},{25,17},{2,10},{10... | collective-permute-start | bytes 3538952 | tf_op jit(solution)/shard_map/ppermute | solution.py:727
  73.1 30.9 %collective-permute-start.8 = (bf16[576,1024]{1,0:T(8,128)(2,1)}, bf16[576,1024]{1,0:T(8,128)(2,1)S(1)}, u32[]{:S(2)}, u32[]{:S(2)}) collective-permute-start(bf16[576,1024]{1,0:T(8,128)(2,1)} %constant_dynamic-update-slice_fusion.refs_1_), channel_id=1, source_target_pairs={{0,1},{1,0},{2,3},{3,2},{4,5},{5,4},{6,7},{7,6},{8,9},{9,8},{10,11... | collective-permute-start | bytes 3538952 | tf_op jit(solution)/shard_map/ppermute | solution.py:745
  73.1 58.3 %collective-permute-start.7 = (bf16[192,4096]{1,0:T(8,128)(2,1)S(1)}, bf16[192,4096]{1,0:T(8,128)(2,1)}, u32[]{:S(2)}, u32[]{:S(2)}) collective-permute-start(bf16[192,4096]{1,0:T(8,128)(2,1)S(1)} %copy-done.47), channel_id=1, source_target_pairs={{0,1},{1,0},{2,3},{3,2},{4,5},{5,4},{6,7},{7,6},{8,9},{9,8},{10,11... | collective-permute-start | bytes 4718600 | tf_op jit(solution)/shard_map/ppermute | solution.py:745
  104.0 29.9 %collective-permute-start.10 = (bf16[576,1024]{1,0:T(8,128)(2,1)}, bf16[576,1024]{1,0:T(8,128)(2,1)}, u32[]{:S(2)}, u32[]{:S(2)}) collective-permute-start(bf16[576,1024]{1,0:T(8,128)(2,1)} %collective-permute-done.4.refs_3_), channel_id=1, source_target_pairs={{0,1},{1,0},{2,3},{3,2},{4,5},{5,4},{6,7},{7,6},{8,9},{9,8},{10,11... | collective-permute-start | bytes 3538952 | tf_op jit(solution)/shard_map/ppermute | solution.py:745
  104.0 29.9 %collective-permute-start.9 = (bf16[576,1024]{1,0:T(8,128)(2,1)}, bf16[576,1024]{1,0:T(8,128)(2,1)}, u32[]{:S(2)}, u32[]{:S(2)}) collective-permute-start(bf16[576,1024]{1,0:T(8,128)(2,1)} %collective-permute-done.3.refs_2_), channel_id=1, source_target_pairs={{0,1},{1,0},{2,3},{3,2},{4,5},{5,4},{6,7},{7,6},{8,9},{9,8},{10,11... | collective-permute-start | bytes 3538952 | tf_op jit(solution)/shard_map/ppermute | solution.py:745
  131.4 102.2 %collective-permute-start.19 = (bf16[192,9216]{1,0:T(8,128)(2,1)}, bf16[192,9216]{1,0:T(8,128)(2,1)}, u32[]{:S(2)}, u32[]{:S(2)}) collective-permute-start(bf16[192,9216]{1,0:T(8,128)(2,1)} %refs_0_.5), channel_id=1, source_target_pairs={{0,1},{1,0},{2,3},{3,2},{4,5},{5,4},{6,7},{7,6},{8,9},{9,8},{10,11... | collective-permute-start | bytes 10616840 | tf_op jit(solution)/shard_map/ppermute | solution.py:745
  149.5 75.7 %collective-permute-start.16 = (bf16[576,2304]{1,0:T(8,128)(2,1)}, bf16[576,2304]{1,0:T(8,128)(2,1)}, u32[]{:S(2)}, u32[]{:S(2)}) collective-permute-start(bf16[576,2304]{1,0:T(8,128)(2,1)} %pad_maximum_fusion.3.refs_1_), channel_id=1, source_target_pairs={{0,16},{8,24},{16,0},{24,8},{1,17},{9,25},{17,1},{25,9},{2,18},{10... | collective-permute-start | bytes 7962632 | tf_op jit(solution)/shard_map/ppermute | solution.py:728
  151.0 76.3 %collective-permute-start.15 = (bf16[576,2304]{1,0:T(8,128)(2,1)}, bf16[576,2304]{1,0:T(8,128)(2,1)}, u32[]{:S(2)}, u32[]{:S(2)}) collective-permute-start(bf16[576,2304]{1,0:T(8,128)(2,1)} %pad_maximum_fusion.3.refs_1_), channel_id=1, source_target_pairs={{0,8},{8,0},{16,24},{24,16},{1,9},{9,1},{17,25},{25,17},{2,10},{10... | collective-permute-start | bytes 7962632 | tf_op jit(solution)/shard_map/ppermute | solution.py:727
  228.8 35.4 %collective-permute-start.18 = (bf16[288,2304]{1,0:T(8,128)(2,1)S(1)}, bf16[288,2304]{1,0:T(8,128)(2,1)}, u32[]{:S(2)}, u32[]{:S(2)}) collective-permute-start(bf16[288,2304]{1,0:T(8,128)(2,1)S(1)} %slice.419), channel_id=1, source_target_pairs={{0,16},{8,24},{16,0},{24,8},{1,17},{9,25},{17,1},{25,9},{2,18},{10... | collective-permute-start | bytes 3981320 | tf_op jit(solution)/shard_map/ppermute | solution.py:743
  231.5 38.8 %collective-permute-start.17 = (bf16[288,2304]{1,0:T(8,128)(2,1)S(1)}, bf16[288,2304]{1,0:T(8,128)(2,1)}, u32[]{:S(2)}, u32[]{:S(2)}) collective-permute-start(bf16[288,2304]{1,0:T(8,128)(2,1)S(1)} %slice.418), channel_id=1, source_target_pairs={{0,8},{8,0},{16,24},{24,16},{1,9},{9,1},{17,25},{25,17},{2,10},{10... | collective-permute-start | bytes 3981320 | tf_op jit(solution)/shard_map/ppermute | solution.py:742
  233.0 54.7 %collective-permute-start.20 = (bf16[576,2304]{1,0:T(8,128)(2,1)}, bf16[576,2304]{1,0:T(8,128)(2,1)}, u32[]{:S(2)}, u32[]{:S(2)}) collective-permute-start(bf16[576,2304]{1,0:T(8,128)(2,1)} %pad_maximum_fusion.3.refs_1_), channel_id=1, source_target_pairs={{0,1},{1,0},{2,3},{3,2},{4,5},{5,4},{6,7},{7,6},{8,9},{9,8},{10,11... | collective-permute-start | bytes 7962632 | tf_op jit(solution)/shard_map/ppermute | solution.py:745
  233.2 54.5 %collective-permute-start.22 = (bf16[576,2304]{1,0:T(8,128)(2,1)}, bf16[576,2304]{1,0:T(8,128)(2,1)}, u32[]{:S(2)}, u32[]{:S(2)}) collective-permute-start(bf16[576,2304]{1,0:T(8,128)(2,1)} %collective-permute-done.16.refs_3_), channel_id=1, source_target_pairs={{0,1},{1,0},{2,3},{3,2},{4,5},{5,4},{6,7},{7,6},{8,9},{9,8},{10,11... | collective-permute-start | bytes 7962632 | tf_op jit(solution)/shard_map/ppermute | solution.py:745
  233.6 54.2 %collective-permute-start.21 = (bf16[576,2304]{1,0:T(8,128)(2,1)}, bf16[576,2304]{1,0:T(8,128)(2,1)}, u32[]{:S(2)}, u32[]{:S(2)}) collective-permute-start(bf16[576,2304]{1,0:T(8,128)(2,1)} %collective-permute-done.15.refs_2_), channel_id=1, source_target_pairs={{0,1},{1,0},{2,3},{3,2},{4,5},{5,4},{6,7},{7,6},{8,9},{9,8},{10,11... | collective-permute-start | bytes 7962632 | tf_op jit(solution)/shard_map/ppermute | solution.py:745
  349.5 300.9 %all-gather.23.cloned.1.call-start = ((), (), s32[]{:S(2)}) async-start(), calls=%async_computation.7 | async-start | bytes 2211840 | tf_op jit(solution)/shard_map/all_gather | solution.py:1090
  405.2 71.6 %collective-permute-start.28 = (bf16[768,2304]{1,0:T(8,128)(2,1)}, bf16[768,2304]{1,0:T(8,128)(2,1)}, u32[]{:S(2)}, u32[]{:S(2)}) collective-permute-start(bf16[768,2304]{1,0:T(8,128)(2,1)} %quarter_dot.12), channel_id=1, source_target_pairs={{0,1},{1,0},{2,3},{3,2},{4,5},{5,4},{6,7},{7,6},{8,9},{9,8},{10,11... | collective-permute-start | bytes 10616840 | tf_op jit(solution)/shard_map/ppermute | solution.py:853
  405.3 80.1 %collective-permute-start.29 = (bf16[768,2304]{1,0:T(8,128)(2,1)S(1)}, bf16[768,2304]{1,0:T(8,128)(2,1)}, u32[]{:S(2)}, u32[]{:S(2)}) collective-permute-start(bf16[768,2304]{1,0:T(8,128)(2,1)S(1)} %quarter_dot.14), channel_id=1, source_target_pairs={{0,1},{1,0},{2,3},{3,2},{4,5},{5,4},{6,7},{7,6},{8,9},{9,8},{10,11... | collective-permute-start | bytes 10616840 | tf_op jit(solution)/shard_map/ppermute | solution.py:853
  410.7 64.8 %collective-permute-start.26 = (bf16[384,2304]{1,0:T(8,128)(2,1)S(1)}, bf16[384,2304]{1,0:T(8,128)(2,1)}, u32[]{:S(2)}, u32[]{:S(2)}) collective-permute-start(bf16[384,2304]{1,0:T(8,128)(2,1)S(1)} %quarter_dot.10), channel_id=1, source_target_pairs={{0,8},{8,0},{16,24},{24,16},{1,9},{9,1},{17,25},{25,17},{2,10},{10... | collective-permute-start | bytes 5308424 | tf_op jit(solution)/shard_map/ppermute | solution.py:855
  417.4 59.4 %collective-permute-start.27 = (bf16[384,2304]{1,0:T(8,128)(2,1)}, bf16[384,2304]{1,0:T(8,128)(2,1)}, u32[]{:S(2)}, u32[]{:S(2)}) collective-permute-start(bf16[384,2304]{1,0:T(8,128)(2,1)} %quarter_dot.11), channel_id=1, source_target_pairs={{0,16},{8,24},{16,0},{24,8},{1,17},{9,25},{17,1},{25,9},{2,18},{10... | collective-permute-start | bytes 5308424 | tf_op jit(solution)/shard_map/ppermute | solution.py:856
  545.7 31.0 %collective-permute-start.32 = (bf16[1024,1536]{1,0:T(8,128)(2,1)}, bf16[1024,1536]{1,0:T(8,128)(2,1)}, u32[]{:S(2)}, u32[]{:S(2)}) collective-permute-start(bf16[1024,1536]{1,0:T(8,128)(2,1)} %convolution_convert_fusion.1), channel_id=1, source_target_pairs={{0,1},{1,0},{2,3},{3,2},{4,5},{5,4},{6,7},{7,6},{8,9},{9,8},{10,11... | collective-permute-start | bytes 9437192 | tf_op jit(solution)/shard_map/ppermute | solution.py:848
  553.2 97.1 %collective-permute-start.34 = (bf16[768,2304]{1,0:T(8,128)(2,1)}, bf16[768,2304]{1,0:T(8,128)(2,1)}, u32[]{:S(2)}, u32[]{:S(2)}) collective-permute-start(bf16[768,2304]{1,0:T(8,128)(2,1)} %quarter_dot.16), channel_id=1, source_target_pairs={{0,1},{1,0},{2,3},{3,2},{4,5},{5,4},{6,7},{7,6},{8,9},{9,8},{10,11... | collective-permute-start | bytes 10616840 | tf_op jit(solution)/shard_map/ppermute | solution.py:853
  553.6 93.9 %collective-permute-start.30 = (bf16[768,2304]{1,0:T(8,128)(2,1)}, bf16[768,2304]{1,0:T(8,128)(2,1)}, u32[]{:S(2)}, u32[]{:S(2)}) collective-permute-start(bf16[768,2304]{1,0:T(8,128)(2,1)} %quarter_dot.13), channel_id=1, source_target_pairs={{0,8},{8,0},{16,24},{24,16},{1,9},{9,1},{17,25},{25,17},{2,10},{10... | collective-permute-start | bytes 10616840 | tf_op jit(solution)/shard_map/ppermute | solution.py:881
  554.4 94.0 %collective-permute-start.31 = (bf16[768,2304]{1,0:T(8,128)(2,1)}, bf16[768,2304]{1,0:T(8,128)(2,1)}, u32[]{:S(2)}, u32[]{:S(2)}) collective-permute-start(bf16[768,2304]{1,0:T(8,128)(2,1)} %quarter_dot.15), channel_id=1, source_target_pairs={{0,16},{8,24},{16,0},{24,8},{1,17},{9,25},{17,1},{25,9},{2,18},{10... | collective-permute-start | bytes 10616840 | tf_op jit(solution)/shard_map/ppermute | solution.py:882
  556.9 185.7 %reduce-scatter.6.cloned.1.call-start = ((), (), s32[]{:S(2)}) async-start(), calls=%async_computation.8 | async-start | bytes 4423680 | tf_op jit(solution)/shard_map/reduce_scatter | solution.py:910
  584.4 126.6 %collective-permute-start.37 = (bf16[512,384]{1,0:T(8,128)(2,1)S(1)}, bf16[512,384]{1,0:T(8,128)(2,1)}, u32[]{:S(2)}, u32[]{:S(2)}) collective-permute-start(bf16[512,384]{1,0:T(8,128)(2,1)S(1)} %get-tuple-element.242), channel_id=1, source_target_pairs={{0,16},{8,24},{16,0},{24,8},{1,17},{9,25},{17,1},{25,9},{2,18},{10... | collective-permute-start | bytes 1179656 | tf_op jit(solution)/shard_map/ppermute | solution.py:856
  584.9 126.0 %collective-permute-start.36 = (bf16[512,384]{1,0:T(8,128)(2,1)S(1)}, bf16[512,384]{1,0:T(8,128)(2,1)}, u32[]{:S(2)}, u32[]{:S(2)}) collective-permute-start(bf16[512,384]{1,0:T(8,128)(2,1)S(1)} %get-tuple-element.243), channel_id=1, source_target_pairs={{0,8},{8,0},{16,24},{24,16},{1,9},{9,1},{17,25},{25,17},{2,10},{10... | collective-permute-start | bytes 1179656 | tf_op jit(solution)/shard_map/ppermute | solution.py:855
  647.6 65.7 %collective-permute-start.39 = (bf16[384,512]{1,0:T(8,128)(2,1)}, bf16[384,512]{1,0:T(8,128)(2,1)}, u32[]{:S(2)}, u32[]{:S(2)}) collective-permute-start(bf16[384,512]{1,0:T(8,128)(2,1)} %get-tuple-element.240), channel_id=1, source_target_pairs={{0,16},{8,24},{16,0},{24,8},{1,17},{9,25},{17,1},{25,9},{2,18},{10... | collective-permute-start | bytes 1179656 | tf_op jit(solution)/shard_map/ppermute | solution.py:856
  648.4 64.9 %collective-permute-start.38 = (bf16[384,512]{1,0:T(8,128)(2,1)S(1)}, bf16[384,512]{1,0:T(8,128)(2,1)}, u32[]{:S(2)}, u32[]{:S(2)}) collective-permute-start(bf16[384,512]{1,0:T(8,128)(2,1)S(1)} %get-tuple-element.241), channel_id=1, source_target_pairs={{0,8},{8,0},{16,24},{24,16},{1,9},{9,1},{17,25},{25,17},{2,10},{10... | collective-permute-start | bytes 1179656 | tf_op jit(solution)/shard_map/ppermute | solution.py:855
  660.5 182.3 %all-gather.27.cloned.1.call-start = ((), (), s32[]{:S(2)}) async-start(), calls=%async_computation.11 | async-start | bytes 4423680 | tf_op jit(solution)/shard_map/all_gather | solution.py:929
  737.8 30.5 %collective-permute-start.40 = (bf16[768,2048]{1,0:T(8,128)(2,1)}, bf16[768,2048]{1,0:T(8,128)(2,1)}, u32[]{:S(2)}, u32[]{:S(2)}) collective-permute-start(bf16[768,2048]{1,0:T(8,128)(2,1)} %convolution_convert_fusion.2), channel_id=1, source_target_pairs={{0,1},{1,0},{2,3},{3,2},{4,5},{5,4},{6,7},{7,6},{8,9},{9,8},{10,11... | collective-permute-start | bytes 9437192 | tf_op jit(solution)/shard_map/ppermute | solution.py:848
  738.6 27.6 %collective-permute-start.45 = (bf16[768,512]{1,0:T(8,128)(2,1)}, bf16[768,512]{1,0:T(8,128)(2,1)}, u32[]{:S(2)}, u32[]{:S(2)}) collective-permute-start(bf16[768,512]{1,0:T(8,128)(2,1)} %get-tuple-element.237), channel_id=1, source_target_pairs={{0,8},{8,0},{16,24},{24,16},{1,9},{9,1},{17,25},{25,17},{2,10},{10... | collective-permute-start | bytes 2359304 | tf_op jit(solution)/shard_map/ppermute | solution.py:881
  740.5 70.0 %collective-permute-start.51 = (bf16[1024,384]{1,0:T(8,128)(2,1)}, bf16[1024,384]{1,0:T(8,128)(2,1)}, u32[]{:S(2)}, u32[]{:S(2)}) collective-permute-start(bf16[1024,384]{1,0:T(8,128)(2,1)} %get-tuple-element.238), channel_id=1, source_target_pairs={{0,16},{8,24},{16,0},{24,8},{1,17},{9,25},{17,1},{25,9},{2,18},{10... | collective-permute-start | bytes 2359304 | tf_op jit(solution)/shard_map/ppermute | solution.py:882
  741.2 69.3 %collective-permute-start.50 = (bf16[1024,384]{1,0:T(8,128)(2,1)}, bf16[1024,384]{1,0:T(8,128)(2,1)}, u32[]{:S(2)}, u32[]{:S(2)}) collective-permute-start(bf16[1024,384]{1,0:T(8,128)(2,1)} %get-tuple-element.239), channel_id=1, source_target_pairs={{0,8},{8,0},{16,24},{24,16},{1,9},{9,1},{17,25},{25,17},{2,10},{10... | collective-permute-start | bytes 2359304 | tf_op jit(solution)/shard_map/ppermute | solution.py:881
  742.6 127.0 %reduce-scatter.8.cloned.1.call-start = ((), (), s32[]{:S(2)}) async-start(), calls=%async_computation.9 | async-start | bytes 1216512 | tf_op jit(solution)/shard_map/reduce_scatter | solution.py:1148
  774.2 31.4 %collective-permute-start.42 = (bf16[384,512]{1,0:T(8,128)(2,1)S(1)}, bf16[384,512]{1,0:T(8,128)(2,1)S(1)}, u32[]{:S(2)}, u32[]{:S(2)}) collective-permute-start(bf16[384,512]{1,0:T(8,128)(2,1)S(1)} %get-tuple-element.234), channel_id=1, source_target_pairs={{0,16},{8,24},{16,0},{24,8},{1,17},{9,25},{17,1},{25,9},{2,18},{10... | collective-permute-start | bytes 1179656 | tf_op jit(solution)/shard_map/ppermute | solution.py:856
  775.6 32.0 %collective-permute-start.41 = (bf16[384,512]{1,0:T(8,128)(2,1)S(1)}, bf16[384,512]{1,0:T(8,128)(2,1)S(1)}, u32[]{:S(2)}, u32[]{:S(2)}) collective-permute-start(bf16[384,512]{1,0:T(8,128)(2,1)S(1)} %get-tuple-element.235), channel_id=1, source_target_pairs={{0,8},{8,0},{16,24},{24,16},{1,9},{9,1},{17,25},{25,17},{2,10},{10... | collective-permute-start | bytes 1179656 | tf_op jit(solution)/shard_map/ppermute | solution.py:855
  818.4 111.2 %all-gather.29.cloned.1.call-start = ((), (), s32[]{:S(2)}) async-start(), calls=%async_computation.12 | async-start | bytes 1658880 | tf_op jit(solution)/shard_map/all_gather | solution.py:939
  835.1 61.9 %collective-permute-start.47 = (bf16[192,1024]{1,0:T(8,128)(2,1)S(1)}, bf16[192,1024]{1,0:T(8,128)(2,1)S(1)}, u32[]{:S(2)}, u32[]{:S(2)}) collective-permute-start(bf16[192,1024]{1,0:T(8,128)(2,1)S(1)} %get-tuple-element.248), channel_id=1, source_target_pairs={{0,2},{1,3},{2,4},{3,5},{4,6},{5,7},{6,0},{7,1},{8,10},{9,11},{10,... | collective-permute-start | bytes 1179656 | tf_op jit(solution)/shard_map/ppermute | solution.py:899
  840.2 56.9 %collective-permute-start.49 = (bf16[192,1024]{1,0:T(8,128)(2,1)S(1)}, bf16[192,1024]{1,0:T(8,128)(2,1)}, u32[]{:S(2)}, u32[]{:S(2)}) collective-permute-start(bf16[192,1024]{1,0:T(8,128)(2,1)S(1)} %get-tuple-element.249), channel_id=1, source_target_pairs={{0,6},{1,7},{2,0},{3,1},{4,2},{5,3},{6,4},{7,5},{8,14},{9,15},{10,... | collective-permute-start | bytes 1179656 | tf_op jit(solution)/shard_map/ppermute | solution.py:899
  840.3 56.7 %collective-permute-start.48 = (bf16[192,1024]{1,0:T(8,128)(2,1)S(1)}, bf16[192,1024]{1,0:T(8,128)(2,1)}, u32[]{:S(2)}, u32[]{:S(2)}) collective-permute-start(bf16[192,1024]{1,0:T(8,128)(2,1)S(1)} %get-tuple-element.250), channel_id=1, source_target_pairs={{0,4},{1,5},{2,6},{3,7},{4,0},{5,1},{6,2},{7,3},{8,12},{9,13},{10,... | collective-permute-start | bytes 1179656 | tf_op jit(solution)/shard_map/ppermute | solution.py:899
  (104 other events, 1427.7 us)
Sparse Core Ops, SparseCore 0:
  9.6 41.9 all-gather.16
  68.5 70.4 all-gather.24
  142.4 86.1 all-gather.18
  231.3 107.4 all-gather.20
  349.6 185.0 reduce-scatter.3
  557.0 46.7 all-gather.22
  660.7 67.0 reduce-scatter.5
  742.7 70.4 all-gather.26
  818.5 51.0 reduce-scatter.7
  872.0 33.4 all-gather.28

commit v11 on v9

--- a/solution.py
+++ b/solution.py
@@ -49,8 +49,9 @@
     rate = sigmoid(q_rate)
     inp = sigmoid(q_input)
     decay = jnp.exp(-8.0 * rate * soft)
-    root = jnp.sqrt(1.0 - decay * decay + 0.001)
-    return rate, inp, decay, root
+    square = 1.0 - decay * decay + 0.001
+    inverse = lax.rsqrt(square)
+    return rate, inp, decay, square * inverse, inverse
 
 
 def shifted_group(group, step, fill):
@@ -102,7 +103,7 @@
         for b in range(seqs):
             at = pl.ds(pl.multiple_of(j * 8, 8), 8)
             state, prod = carry[b]
-            _, inp, decay, root = drive_values(rate_s[b, at, :], inp_s[b, at, :], soft)
+            _, inp, decay, root, _ = drive_values(rate_s[b, at, :], inp_s[b, at, :], soft)
             keep = jnp.where(dist_ref[b, at, :] >= 1.0, decay, 0.0)
             state = keep * state + root * inp * c_s[b, at, :]
             prod = keep * prod
@@ -196,12 +197,12 @@
             first = pl.multiple_of(n * 32, 32)
             at = pl.ds(first, 32)
             lam = local_ref[b, at, :] + prod_ref[b, at, :] * carry
-            rate, inp, decay, root = drive_values(q_s[at, :HS], q_s[at, HS:], soft)
+            rate, inp, decay, root, inverse = drive_values(q_s[at, :HS], q_s[at, HS:], soft)
             conv = c_ref[b, at, :].astype(F32)
             kept = jnp.where(dist_ref[b, at, :] >= 1.0, h_s[at, :], 0.0)
             lam_root = lam * root
             lam_inp = lam * inp
-            grad_decay = lam * kept - lam_inp * conv * decay / root
+            grad_decay = lam * kept - lam_inp * conv * decay * inverse
             rated = grad_decay * decay * rate
             dq_s[at, :HS] = (-8.0 * soft * rated * (1.0 - rate)).astype(BF16)
             dq_s[at, HS:] = (lam_root * conv * inp * (1.0 - inp)).astype(BF16)
@@ -992,7 +993,7 @@
     carry_in = shard_carry(end_state, end_prod, False)
     carries = chunk_carries(chunks, carry_in, False)
     state, branch, branch_split = mixer_branch(
-        tie(state_part, *up_gather.second(carries)), prod_part, carries, gate_pre, last + 1, place % 2
+        tie(state_part, *up_gather.second(carries, gate_pre)), prod_part, carries, gate_pre, last + 1, place % 2
     )
     branch_split = branch_split.reshape(2, row_count, LRU // 2)
     resid = inputs + jnp.dot(
@@ -1105,7 +1106,7 @@
     decay_total = flat[n_gates + CONV * n_lru :]
 
     up_total = up_sum.finish(edge)
-    down_total = down_sum.astype(F32)
+    down_total = tie(down_sum, *sent).astype(F32)
     if in_value_sum.simple:
         in_total = jnp.concatenate([in_value_sum.finish(), in_gate_sum.finish()], axis=1)
         last_sent = ()

time: 868 us -> 873 us (level)
  transfers between devices with their start and end apart: 64 -> 64, of which waited for: 12 -> 12; matrix products, arithmetic and copies ran while one was open for 40% -> 39% of each run, Pallas kernels for 25% -> 24%
where the time goes in v11:
time: 873 us; the launch traced here: 864 us
  matrix products  244 us (28%)
  Pallas kernels  208 us (24%)
  waiting for transfers between devices  117 us (13%)
  local copies, waits for them, and re-layouts  98.7 us (11%)
  blocking collectives  87.8 us (10%)
  starting transfers between devices  51.6 us (6%)
  other arithmetic  41.1 us (5%)
  between operations  15.5 us (2%)
    dot_general x16, matrix products, dot_rows(): lax.dot_general(a, b, (((0,), (0,)), ((), ())), preferred_element_type=F32)  135 us
    dot_general x5, matrix products, dot_far(): lax.dot_general(a, b, (((1,), (1,)), ((), ())), preferred_element_type=F32)  76.6 us
    pallas_call x3, Pallas kernels, call(): pl.pallas_call(kernel, grid=(steps,), in_specs=[pl.BlockSpec(memory_space...  66.1 us
    pallas_call x1, Pallas kernels, mixer_backward(): pl.pallas_call(mixer_backward_kernel, grid=(HEADS,), in_specs=[full, full...  45.4 us
    unnamed x199, local copies, waits for them, and re-layouts  43.9 us
    ppermute x2, waiting for transfers between devices, first(): self.from_y = lax.ppermute(self.near, 'grp', xor_pairs('grp', 2))  35.4 us
    ppermute x3, waiting for transfers between devices, __init__(): lax.ppermute(own, 'seq', ring_pairs(-2 * j))  35 us
    pallas_call x1, Pallas kernels, mixer_forward(): pl.pallas_call(mixer_forward_kernel, grid=(HEADS,), in_specs=[full, head_...  27.1 us
  transfers between devices with their start and end apart: 64, of which 12 were waited for; matrix products, arithmetic and copies ran while one was open for 39% of the time, Pallas kernels for 24%

profile of v11, /device:TPU:18, one launch (start us, length us, event | category | flops | bytes accessed | tf_op | source)
XLA Modules:
  0.0 863.8 jit_solution(8286219204714789822)
XLA Ops:
  16.1 7.5 collective-permute-done
  25.3 27.5 %collective-permute-done.1 = bf16[192,1024]{1,0:T(8,128)(2,1)} collective-permute-done((bf16[192,1024]{1,0:T(8,128)(2,1)}, bf16[192,1024]{1,0:T(8,128)(2,1)}, u32[]{:S(2)}, u32[]{:S(2)}) %collective-permute-start.1) | collective-permute-done | bytes 393248 | tf_op jit(solution)/shard_map/ppermute | solution.py:675
  61.6 24.6 %collective-permute-done.4.refs_3_ = bf16[576,1024]{1,0:T(8,128)(2,1)} collective-permute-done((bf16[576,1024]{1,0:T(8,128)(2,1)}, bf16[576,1024]{1,0:T(8,128)(2,1)}, u32[]{:S(2)}, u32[]{:S(2)}) %collective-permute-start.4) | collective-permute-done | bytes 1179680 | tf_op jit(solution)/shard_map/ppermute | solution.py:691
  92.0 15.3 %all-gather.9 = bf16[8,1,1664]{2,1,0:T(2,128)(2,1)S(1)} all-gather(bf16[1,1,1664]{2,1,0:T(2,128)(2,1)S(1)} %reshape.2479), channel_id=2, replica_groups=mesh['grp'=4,'seq'=8] {'seq'}, dimensions={0}, use_global_device_ids=true | all-gather | bytes 29952 | tf_op jit(solution)/shard_map/all_gather | solution.py:947
  108.7 5.3 copy.292
  124.8 11.9 %gathered_dot.2 = (bf16[1024,2048]{1,0:T(8,128)(2,1)}, bf16[1536,2048]{1,0:T(8,128)(2,1)}) custom-call(s32[3]{0:T(128)} %pad_add_fusion.1.where_ref, bf16[1024,1536]{1,0:T(8,128)(2,1)} %copy-done.9, bf16[192,4096]{1,0:T(8,128)(2,1)} %refs_0_.4, bf16[576,1024]{1,0:T(8,128)(2,1)} %constant_dynamic-update-slice_fusion.refs_1_, ...), custom_call_target="tpu_custom_call" | custom-call | tf_op jit(solution)/shard_map/gathered_dot/pallas_call | solution.py:716
  147.7 13.1 %gathered_dot.3 = (f32[1024,2048]{1,0:T(8,128)}, bf16[1536,2048]{1,0:T(8,128)(2,1)}) custom-call(s32[3]{0:T(128)} %pad_add_fusion.1.where_ref, bf16[1024,1536]{1,0:T(8,128)(2,1)} %copy-done.9, bf16[192,4096]{1,0:T(8,128)(2,1)} %refs_0_.4, bf16[576,1024]{1,0:T(8,128)(2,1)} %constant_dynamic-update-slice_fusion.refs_1_, ...), custom_call_target="tpu_custom_call" | custom-call | tf_op jit(solution)/shard_map/gathered_dot/pallas_call | solution.py:716
  161.1 27.1 %mixer_forward.1 = (bf16[2,512,2048]{2,1,0:T(8,128)(2,1)S(1)}, f32[2,512,2048]{2,1,0:T(8,128)}, f32[2,512,2048]{2,1,0:T(8,128)}, f32[2,512,2048]{2,1,0:T(8,128)}, f32[2,2,8,2048]{3,2,1,0:T(8,128)S(1)}) custom-call(bf16[2,512,2048]{2,1,0:T(8,128)(2,1)S(1)} %bitcast.780, bf16[2,8,2048]{2,1,0:T(8,128)(2,1)S(1)} %collective-permute-done.13.halo_ref, ...), custom_call_target="tpu_custom_call" | custom-call | tf_op jit(solution)/shard_map/mixer_forward/pallas_call | solution.py:323
  190.7 13.2 %all-gather.2 = f32[16,2,2048]{2,1,0:T(2,128)S(1)} all-gather(f32[2,2,2048]{2,1,0:T(2,128)S(1)} %copy.311), channel_id=4, replica_groups=mesh['grp'=4,'seq'=8] {'seq'}, dimensions={0}, use_global_device_ids=true | all-gather | bytes 294912 | tf_op jit(solution)/shard_map/all_gather | solution.py:896
  204.5 10.8 %collective-permute-done.16.refs_3_ = bf16[576,2304]{1,0:T(8,128)(2,1)} collective-permute-done((bf16[576,2304]{1,0:T(8,128)(2,1)}, bf16[576,2304]{1,0:T(8,128)(2,1)}, u32[]{:S(2)}, u32[]{:S(2)}) %collective-permute-start.16) | collective-permute-done | bytes 2654240 | tf_op jit(solution)/shard_map/ppermute | solution.py:691
  225.2 5.3 copy.326
  230.5 17.7 %mixer_branch.1 = (f32[2,512,2048]{2,1,0:T(8,128)}, bf16[2,512,2048]{2,1,0:T(8,128)(2,1)S(1)}, bf16[2,2,512,1024]{3,2,1,0:T(8,128)(2,1)S(1)}) custom-call(s32[1]{0:T(128)} %bitcast.3.core_ref, f32[2,512,2048]{2,1,0:T(8,128)} %get-tuple-element.88.state_ref, f32[2,512,2048]{2,1,0:T(8,128)} %get-tuple-element.89.prod_ref, ...), custom_call_target="tpu_custom_call" | custom-call | tf_op jit(solution)/shard_map/mixer_branch/pallas_call | solution.py:365
  252.1 6.4 collective-permute-done.18.refs_5_
  258.6 5.4 collective-permute-done.17.refs_4_
  263.9 10.5 %convert_add_fusion.x_ref = f32[1024,1536]{1,0:T(8,128)S(1)} fusion(bf16[1024,1536]{1,0:T(8,128)(2,1)} %bitcast.774, bf16[1024,2048]{1,0:T(8,128)(2,1)} %bitcast.787, bf16[2048,1536]{1,0:T(8,128)(2,1)} %all-gather.19.cloned.1.call-done), kind=kOutput, calls=%fused_computation.3 | convolution fusion | flops 6445596672 | bytes 19922944 | tf_op jit(solution)/shard_map/dot_general | solution.py:999
  281.7 41.0 %gathered_ffn.1 = (bf16[1024,4608]{1,0:T(8,128)(2,1)}, bf16[2,1024,4608]{2,1,0:T(8,128)(2,1)}, bf16[1536,4608]{1,0:T(8,128)(2,1)}, bf16[1536,4608]{1,0:T(8,128)(2,1)}) custom-call(s32[3]{0:T(128)} %pad_add_fusion.1.where_ref, bf16[1024,1536]{1,0:T(8,128)(2,1)} %copy-done.23, bf16[192,9216]{1,0:T(8,128)(2,1)} %refs_0_.5, ...), custom_call_target="tpu_custom_call" | custom-call | tf_op jit(solution)/shard_map/gathered_ffn/pallas_call | solution.py:716
  322.8 31.8 %convolution_convert_fusion = bf16[4608,1536]{1,0:T(8,128)(2,1)} fusion(bf16[1024,4608]{1,0:T(8,128)(2,1)} %get-tuple-element.134, bf16[1024,1536]{1,0:T(8,128)(2,1)S(1)} %bitcast.776), kind=kOutput, calls=%fused_computation | convolution fusion | flops 14502592512 | bytes 26738688 | tf_op jit(solution)/shard_map/dot_general | solution.py:548
  356.6 25.8 %ffn_backward.1 = bf16[2,1024,4608]{2,1,0:T(8,128)(2,1)} custom-call(bf16[1024,1536]{1,0:T(8,128)(2,1)S(1)} %bitcast.777, bf16[4608,1536]{1,0:T(8,128)(2,1)} %all-gather.21.cloned.1.call-done.down_ref, bf16[2,1024,4608]{2,1,0:T(8,128)(2,1)} %get-tuple-element.96.pull_ref), custom_call_target="tpu_custom_call" | custom-call | tf_op jit(solution)/shard_map/ffn_backward/pallas_call | solution.py:507
  382.3 8.0 convolution_convert_fusion.4
  392.0 5.0 fusion.187
  397.4 7.9 convolution_convert_fusion.1
  407.4 5.3 convolution_convert_fusion.2
  412.8 5.6 convolution_convert_fusion.3
  418.9 4.8 fusion.43
  430.6 21.8 %fusion = f32[1024,1536]{1,0:T(8,128)} fusion(bf16[1536,4608]{1,0:T(8,128)(2,1)} %get-tuple-element.101, bf16[2,1024,4608]{2,1,0:T(8,128)(2,1)} %ffn_backward.1), kind=kOutput, calls=%fused_computation.4 | convolution fusion | flops 14495514624 | bytes 29884416 | tf_op jit(solution)/shard_map/dot_general | solution.py:558
  452.4 21.0 %fusion.25 = f32[1024,1536]{1,0:T(8,128)S(1)} fusion(f32[1024,1536]{1,0:T(8,128)} %fusion, bf16[1536,4608]{1,0:T(8,128)(2,1)} %get-tuple-element.100, bf16[2,1024,4608]{2,1,0:T(8,128)(2,1)} %ffn_backward.1), kind=kOutput, calls=%fused_computation.44 | convolution fusion | flops 14497087488 | bytes 36175872 | tf_op jit(solution)/shard_map/dot_general | solution.py:558
  473.4 14.2 %collective-permute-done.27 = bf16[384,2304]{1,0:T(8,128)(2,1)} collective-permute-done((bf16[384,2304]{1,0:T(8,128)(2,1)}, bf16[384,2304]{1,0:T(8,128)(2,1)}, u32[]{:S(2)}, u32[]{:S(2)}) %collective-permute-start.27) | collective-permute-done | bytes 1769504 | tf_op jit(solution)/shard_map/ppermute | solution.py:819
  488.9 9.2 %add_convert_fusion.2 = bf16[768,2304]{1,0:T(8,128)(2,1)} fusion(bf16[768,2304]{1,0:T(8,128)(2,1)} %collective-permute-done.26, bf16[1024,768]{1,0:T(8,128)(2,1)S(1)} %get-tuple-element.97, bf16[2,1024,4608]{2,1,0:T(8,128)(2,1)} %ffn_backward.1, s32[]{:T(128)S(6)} %select_n.797, s32[]{:T(128)S(6)} %select_n.799, bf16[384,2304]{1,0:T(8,128)(2,1)} %collective-permute-done.28), kind=kOutput, calls=%fused_computation.14 | convolution fusion | flops 3632726016 | bytes 15138824 | tf_op jit(solution)/shard_map/dot_general | solution.py:548
  498.6 10.5 %add_convert_fusion.1 = bf16[768,2304]{1,0:T(8,128)(2,1)} fusion(bf16[768,2304]{1,0:T(8,128)(2,1)} %collective-permute-done.29, bf16[1024,768]{1,0:T(8,128)(2,1)S(1)} %get-tuple-element.97, bf16[2,1024,4608]{2,1,0:T(8,128)(2,1)} %ffn_backward.1, s32[]{:T(128)S(6)} %select_n.801, s32[]{:T(128)S(6)} %select_n.803, bf16[384,2304]{1,0:T(8,128)(2,1)} %collective-permute-done.27), kind=kOutput, calls=%fused_computation.13 | convolution fusion | flops 3632726016 | bytes 15138824 | tf_op jit(solution)/shard_map/dot_general | solution.py:548
  514.9 12.0 %fusion.194 = f32[1024,2048]{1,0:T(8,128)} fusion(bf16[1024,1536]{1,0:T(8,128)(2,1)S(1)} %get-tuple-element.112, bf16[2048,1536]{1,0:T(8,128)(2,1)} %all-gather.19.cloned.1.call-done), kind=kOutput, calls=%fused_computation.341 | convolution fusion | flops 6442450944 | bytes 17825792 | tf_op jit(solution)/shard_map/dot_general | solution.py:558
  526.9 22.0 %mixer_reverse.1 = (bf16[2,512,2048]{2,1,0:T(8,128)(2,1)S(1)}, f32[2,512,2048]{2,1,0:T(8,128)S(1)}, f32[2,512,2048]{2,1,0:T(8,128)}, f32[2,2,8,2048]{3,2,1,0:T(8,128)S(1)}) custom-call(f32[2,512,2048]{2,1,0:T(8,128)} %bitcast.795, f32[2,512,2048]{2,1,0:T(8,128)} %bitcast.789, f32[2,512,2048]{2,1,0:T(8,128)} %get-tuple-element.105.keep_ref, ...), custom_call_target="tpu_custom_call" | custom-call | tf_op jit(solution)/shard_map/mixer_reverse/pallas_call | solution.py:387
  558.9 5.7 convolution_convert_fusion.5
  566.1 5.3 convolution_convert_fusion.7
  571.8 12.5 %all-gather.3 = f32[16,2,2048]{2,1,0:T(2,128)S(1)} all-gather(f32[2,2,2048]{2,1,0:T(2,128)S(1)} %copy.343), channel_id=5, replica_groups=mesh['grp'=4,'seq'=8] {'seq'}, dimensions={0}, use_global_device_ids=true | all-gather | bytes 294912 | tf_op jit(solution)/shard_map/all_gather | solution.py:896
  584.9 7.1 add_convert_fusion.6
  597.3 5.8 add_convert_fusion.5
  610.2 11.2 %add_convert_fusion = bf16[768,2304]{1,0:T(8,128)(2,1)} fusion(bf16[768,2304]{1,0:T(8,128)(2,1)} %collective-permute-done.32, bf16[768,2304]{1,0:T(8,128)(2,1)} %collective-permute-done.31, bf16[768,2304]{1,0:T(8,128)(2,1)} %collective-permute-done.30, bf16[1024,768]{1,0:T(8,128)(2,1)S(1)} %get-tuple-element.97, bf16[2,1024,4608]{2,1,0:T(8,128)(2,1)} %ffn_backward.1, ...), kind=kOutput, calls=%fused_computation.12 | convolution fusion | flops 3636264960 | bytes 20447240 | tf_op jit(solution)/shard_map/dot_general | solution.py:548
  624.8 45.4 %mixer_backward.1 = (bf16[2,512,2048]{2,1,0:T(8,128)(2,1)S(1)}, f32[2,32,2048]{2,1,0:T(8,128)S(1)}, f32[2,8,2048]{2,1,0:T(8,128)S(1)}, f32[16,128,256]{2,1,0:T(8...) custom-call(f32[2,512,2048]{2,1,0:T(8,128)} %copy-done.10, f32[2,512,2048]{2,1,0:T(8,128)} %get-tuple-element.118.prod_ref, ...), custom_call_target="tpu_custom_call" | custom-call | tf_op jit(solution)/shard_map/mixer_backward/pallas_call | solution.py:409
  677.8 11.0 %fusion.195 = f32[1024,1536]{1,0:T(8,128)} fusion(bf16[1024,2048]{1,0:T(8,128)(2,1)S(1)} %bitcast.782, bf16[1536,2048]{1,0:T(8,128)(2,1)} %get-tuple-element.128), kind=kOutput, calls=%fused_computation.342 | convolution fusion | flops 6442450944 | bytes 16777216 | tf_op jit(solution)/shard_map/dot_general | solution.py:558
  691.7 5.3 convolution_convert_fusion.6
  707.4 10.8 %collective-permute-done.46 = bf16[768,512]{1,0:T(8,128)(2,1)} collective-permute-done((bf16[768,512]{1,0:T(8,128)(2,1)}, bf16[768,512]{1,0:T(8,128)(2,1)}, u32[]{:S(2)}, u32[]{:S(2)}) %collective-permute-start.46) | collective-permute-done | bytes 786464 | tf_op jit(solution)/shard_map/ppermute | solution.py:841
  720.9 6.8 add_convert_fusion.4
  730.9 10.8 %fusion.10 = (f32[1024]{0:T(1024)S(1)}, f32[1024,1536]{1,0:T(8,128)S(1)}) fusion(f32[1536]{0:T(1024)S(1)} %reshape.2461, bf16[2,8,64,1536]{3,1,2,0:T(8,128)(2,1)S(1)} %copy-done.4, f32[1024,1536]{1,0:T(8,128)} %fusion.195, bf16[1024,2048]{1,0:T(8,128)(2,1)S(1)} %bitcast.784, bf16[1536,2048]{1,0:T(8,128)(2,1)} %get-tuple-element.131), kind=kOutput, calls=%fused_computation.19 | convolution fusion | flops 6450314240 | bytes 26224640 | tf_op jit(solution)/shard_map/dot_general | solution.py:558
  756.3 21.8 %add_convert_fusion.3 = bf16[1024,1536]{1,0:T(8,128)(2,1)} fusion(f32[1024,1536]{1,0:T(8,128)} %copy-done.2, bf16[1024,4608]{1,0:T(8,128)(2,1)} %get-tuple-element.134, bf16[4608,1536]{1,0:T(8,128)(2,1)} %all-gather.21.cloned.1.call-done.down_ref), kind=kOutput, calls=%fused_computation.20 | convolution fusion | flops 14498660352 | bytes 33030144 | tf_op jit(solution)/shard_map/dot_general | solution.py:1127
  778.2 14.0 %all-gather.6 = bf16[2112,128]{1,0:T(8,128)(2,1)S(1)} all-gather(bf16[528,128]{1,0:T(8,128)(2,1)} %reduce-scatter.6.cloned.1.call-done), channel_id=8, replica_groups=mesh['grp'=4,'seq'=8] {'grp'}, dimensions={0}, use_global_device_ids=true | all-gather | bytes 675840 | tf_op jit(solution)/shard_map/all_gather | solution.py:1101
  809.9 10.5 %all-gather.7 = bf16[1024,384]{1,0:T(8,128)(2,1)S(1)} all-gather(bf16[256,384]{1,0:T(8,128)(2,1)S(1)} %fusion.72), channel_id=9, replica_groups=mesh['grp'=4,'seq'=8] {'grp'}, dimensions={0}, use_global_device_ids=true | all-gather | bytes 983040 | tf_op jit(solution)/shard_map/all_gather | solution.py:889
  823.8 11.8 %all-gather.4 = bf16[768,512]{1,0:T(8,128)(2,1)S(1)} all-gather(bf16[192,512]{1,0:T(8,128)(2,1)S(1)} %get-tuple-element.204), channel_id=6, replica_groups=mesh['grp'=4,'seq'=8] {'grp'}, dimensions={0}, use_global_device_ids=true | all-gather | bytes 983040 | tf_op jit(solution)/shard_map/all_gather | solution.py:1119
  836.4 10.5 %all-gather.5 = bf16[768,512]{1,0:T(8,128)(2,1)S(1)} all-gather(bf16[192,512]{1,0:T(8,128)(2,1)S(1)} %get-tuple-element.205), channel_id=7, replica_groups=mesh['grp'=4,'seq'=8] {'grp'}, dimensions={0}, use_global_device_ids=true | all-gather | bytes 983040 | tf_op jit(solution)/shard_map/all_gather | solution.py:1119
  (435 shorter events, 194.4 us)
Async XLA Ops:
  7.2 49.1 %all-gather.17.cloned.1.call-start = ((), (), s32[]{:S(2)}) async-start(), calls=%async_computation.3 | async-start | bytes 1179648 | tf_op jit(solution)/shard_map/all_gather | solution.py:959
  7.9 128.8 %all-gather.25.cloned.1.call-start = ((), (), s32[]{:S(2)}) async-start(), calls=%async_computation.10 | async-start | bytes 4423680 | tf_op jit(solution)/shard_map/all_gather | solution.py:672
  10.4 44.2 %collective-permute-start.2 = (bf16[192,1024]{1,0:T(8,128)(2,1)}, bf16[192,1024]{1,0:T(8,128)(2,1)}, u32[]{:S(2)}, u32[]{:S(2)}) collective-permute-start(bf16[192,1024]{1,0:T(8,128)(2,1)} %constant_dynamic-slice_fusion.15), channel_id=1, source_target_pairs={{0,2},{1,3},{2,4},{3,5},{4,6},{5,7},{6,0},{7,1},{8,10},{9,11},{10,... | collective-permute-start | bytes 1179656 | tf_op jit(solution)/shard_map/ppermute | solution.py:675
  12.0 40.8 %collective-permute-start.1 = (bf16[192,1024]{1,0:T(8,128)(2,1)}, bf16[192,1024]{1,0:T(8,128)(2,1)}, u32[]{:S(2)}, u32[]{:S(2)}) collective-permute-start(bf16[192,1024]{1,0:T(8,128)(2,1)} %constant_dynamic-slice_fusion.15), channel_id=1, source_target_pairs={{0,4},{1,5},{2,6},{3,7},{4,0},{5,1},{6,2},{7,3},{8,12},{9,13},{10,... | collective-permute-start | bytes 1179656 | tf_op jit(solution)/shard_map/ppermute | solution.py:675
  56.4 207.6 %all-gather.19.cloned.1.call-start = ((), (), s32[]{:S(2)}) async-start(), calls=%async_computation.4 | async-start | bytes 6488064 | tf_op jit(solution)/shard_map/all_gather | solution.py:526
  58.1 296.6 %all-gather.21.cloned.1.call-start = ((), (), s32[]{:S(2)}) async-start(), calls=%async_computation.5 | async-start | bytes 14598144 | tf_op jit(solution)/shard_map/all_gather | solution.py:526
  59.0 496.4 %reduce-scatter.4.cloned.1.call-start = ((), (), s32[]{:S(2)}) async-start(), calls=%async_computation.6 | async-start | bytes 14598144 | tf_op jit(solution)/shard_map/reduce_scatter | solution.py:1011
  59.0 27.2 %collective-permute-start.4 = (bf16[576,1024]{1,0:T(8,128)(2,1)}, bf16[576,1024]{1,0:T(8,128)(2,1)}, u32[]{:S(2)}, u32[]{:S(2)}) collective-permute-start(bf16[576,1024]{1,0:T(8,128)(2,1)} %constant_dynamic-update-slice_fusion.refs_1_), channel_id=1, source_target_pairs={{0,16},{8,24},{16,0},{24,8},{1,17},{9,25},{17,1},{25,9},{2,18},{10... | collective-permute-start | bytes 3538952 | tf_op jit(solution)/shard_map/ppermute | solution.py:691
  60.6 27.3 %collective-permute-start.3 = (bf16[576,1024]{1,0:T(8,128)(2,1)}, bf16[576,1024]{1,0:T(8,128)(2,1)}, u32[]{:S(2)}, u32[]{:S(2)}) collective-permute-start(bf16[576,1024]{1,0:T(8,128)(2,1)} %constant_dynamic-update-slice_fusion.refs_1_), channel_id=1, source_target_pairs={{0,8},{8,0},{16,24},{24,16},{1,9},{9,1},{17,25},{25,17},{2,10},{10... | collective-permute-start | bytes 3538952 | tf_op jit(solution)/shard_map/ppermute | solution.py:690
  61.1 30.3 %collective-permute-start.8 = (bf16[576,1024]{1,0:T(8,128)(2,1)}, bf16[576,1024]{1,0:T(8,128)(2,1)S(1)}, u32[]{:S(2)}, u32[]{:S(2)}) collective-permute-start(bf16[576,1024]{1,0:T(8,128)(2,1)} %constant_dynamic-update-slice_fusion.refs_1_), channel_id=1, source_target_pairs={{0,1},{1,0},{2,3},{3,2},{4,5},{5,4},{6,7},{7,6},{8,9},{9,8},{10,11... | collective-permute-start | bytes 3538952 | tf_op jit(solution)/shard_map/ppermute | solution.py:708
  61.1 61.1 %collective-permute-start.7 = (bf16[192,4096]{1,0:T(8,128)(2,1)S(1)}, bf16[192,4096]{1,0:T(8,128)(2,1)}, u32[]{:S(2)}, u32[]{:S(2)}) collective-permute-start(bf16[192,4096]{1,0:T(8,128)(2,1)S(1)} %copy-done.48), channel_id=1, source_target_pairs={{0,1},{1,0},{2,3},{3,2},{4,5},{5,4},{6,7},{7,6},{8,9},{9,8},{10,11... | collective-permute-start | bytes 4718600 | tf_op jit(solution)/shard_map/ppermute | solution.py:708
  91.4 33.4 %collective-permute-start.10 = (bf16[576,1024]{1,0:T(8,128)(2,1)}, bf16[576,1024]{1,0:T(8,128)(2,1)}, u32[]{:S(2)}, u32[]{:S(2)}) collective-permute-start(bf16[576,1024]{1,0:T(8,128)(2,1)} %collective-permute-done.4.refs_3_), channel_id=1, source_target_pairs={{0,1},{1,0},{2,3},{3,2},{4,5},{5,4},{6,7},{7,6},{8,9},{9,8},{10,11... | collective-permute-start | bytes 3538952 | tf_op jit(solution)/shard_map/ppermute | solution.py:708
  91.4 33.4 %collective-permute-start.9 = (bf16[576,1024]{1,0:T(8,128)(2,1)}, bf16[576,1024]{1,0:T(8,128)(2,1)}, u32[]{:S(2)}, u32[]{:S(2)}) collective-permute-start(bf16[576,1024]{1,0:T(8,128)(2,1)} %collective-permute-done.3.refs_2_), channel_id=1, source_target_pairs={{0,1},{1,0},{2,3},{3,2},{4,5},{5,4},{6,7},{7,6},{8,9},{9,8},{10,11... | collective-permute-start | bytes 3538952 | tf_op jit(solution)/shard_map/ppermute | solution.py:708
  122.3 102.5 %collective-permute-start.19 = (bf16[192,9216]{1,0:T(8,128)(2,1)}, bf16[192,9216]{1,0:T(8,128)(2,1)}, u32[]{:S(2)}, u32[]{:S(2)}) collective-permute-start(bf16[192,9216]{1,0:T(8,128)(2,1)} %refs_0_.5), channel_id=1, source_target_pairs={{0,1},{1,0},{2,3},{3,2},{4,5},{5,4},{6,7},{7,6},{8,9},{9,8},{10,11... | collective-permute-start | bytes 10616840 | tf_op jit(solution)/shard_map/ppermute | solution.py:708
  140.3 74.9 %collective-permute-start.16 = (bf16[576,2304]{1,0:T(8,128)(2,1)}, bf16[576,2304]{1,0:T(8,128)(2,1)}, u32[]{:S(2)}, u32[]{:S(2)}) collective-permute-start(bf16[576,2304]{1,0:T(8,128)(2,1)} %pad_maximum_fusion.3.refs_1_), channel_id=1, source_target_pairs={{0,16},{8,24},{16,0},{24,8},{1,17},{9,25},{17,1},{25,9},{2,18},{10... | collective-permute-start | bytes 7962632 | tf_op jit(solution)/shard_map/ppermute | solution.py:691
  141.1 76.7 %collective-permute-start.15 = (bf16[576,2304]{1,0:T(8,128)(2,1)}, bf16[576,2304]{1,0:T(8,128)(2,1)}, u32[]{:S(2)}, u32[]{:S(2)}) collective-permute-start(bf16[576,2304]{1,0:T(8,128)(2,1)} %pad_maximum_fusion.3.refs_1_), channel_id=1, source_target_pairs={{0,8},{8,0},{16,24},{24,16},{1,9},{9,1},{17,25},{25,17},{2,10},{10... | collective-permute-start | bytes 7962632 | tf_op jit(solution)/shard_map/ppermute | solution.py:690
  220.3 38.3 %collective-permute-start.18 = (bf16[288,2304]{1,0:T(8,128)(2,1)}, bf16[288,2304]{1,0:T(8,128)(2,1)}, u32[]{:S(2)}, u32[]{:S(2)}) collective-permute-start(bf16[288,2304]{1,0:T(8,128)(2,1)} %slice.416), channel_id=1, source_target_pairs={{0,16},{8,24},{16,0},{24,8},{1,17},{9,25},{17,1},{25,9},{2,18},{10... | collective-permute-start | bytes 3981320 | tf_op jit(solution)/shard_map/ppermute | solution.py:706
  222.8 41.1 %collective-permute-start.17 = (bf16[288,2304]{1,0:T(8,128)(2,1)S(1)}, bf16[288,2304]{1,0:T(8,128)(2,1)}, u32[]{:S(2)}, u32[]{:S(2)}) collective-permute-start(bf16[288,2304]{1,0:T(8,128)(2,1)S(1)} %slice.415), channel_id=1, source_target_pairs={{0,8},{8,0},{16,24},{24,16},{1,9},{9,1},{17,25},{25,17},{2,10},{10... | collective-permute-start | bytes 3981320 | tf_op jit(solution)/shard_map/ppermute | solution.py:705
  224.2 57.4 %collective-permute-start.20 = (bf16[576,2304]{1,0:T(8,128)(2,1)}, bf16[576,2304]{1,0:T(8,128)(2,1)}, u32[]{:S(2)}, u32[]{:S(2)}) collective-permute-start(bf16[576,2304]{1,0:T(8,128)(2,1)} %pad_maximum_fusion.3.refs_1_), channel_id=1, source_target_pairs={{0,1},{1,0},{2,3},{3,2},{4,5},{5,4},{6,7},{7,6},{8,9},{9,8},{10,11... | collective-permute-start | bytes 7962632 | tf_op jit(solution)/shard_map/ppermute | solution.py:708
  224.6 57.1 %collective-permute-start.22 = (bf16[576,2304]{1,0:T(8,128)(2,1)}, bf16[576,2304]{1,0:T(8,128)(2,1)}, u32[]{:S(2)}, u32[]{:S(2)}) collective-permute-start(bf16[576,2304]{1,0:T(8,128)(2,1)} %collective-permute-done.16.refs_3_), channel_id=1, source_target_pairs={{0,1},{1,0},{2,3},{3,2},{4,5},{5,4},{6,7},{7,6},{8,9},{9,8},{10,11... | collective-permute-start | bytes 7962632 | tf_op jit(solution)/shard_map/ppermute | solution.py:708
  224.8 57.0 %collective-permute-start.21 = (bf16[576,2304]{1,0:T(8,128)(2,1)}, bf16[576,2304]{1,0:T(8,128)(2,1)}, u32[]{:S(2)}, u32[]{:S(2)}) collective-permute-start(bf16[576,2304]{1,0:T(8,128)(2,1)} %collective-permute-done.15.refs_2_), channel_id=1, source_target_pairs={{0,1},{1,0},{2,3},{3,2},{4,5},{5,4},{6,7},{7,6},{8,9},{9,8},{10,11... | collective-permute-start | bytes 7962632 | tf_op jit(solution)/shard_map/ppermute | solution.py:708
  354.6 255.6 %all-gather.23.cloned.1.call-start = ((), (), s32[]{:S(2)}) async-start(), calls=%async_computation.7 | async-start | bytes 2211840 | tf_op jit(solution)/shard_map/all_gather | solution.py:1037
  390.3 28.6 %collective-permute-start.25 = (bf16[768,2304]{1,0:T(8,128)(2,1)}, bf16[768,2304]{1,0:T(8,128)(2,1)}, u32[]{:S(2)}, u32[]{:S(2)}) collective-permute-start(bf16[768,2304]{1,0:T(8,128)(2,1)} %convolution_convert_fusion.4), channel_id=1, source_target_pairs={{0,1},{1,0},{2,3},{3,2},{4,5},{5,4},{6,7},{7,6},{8,9},{9,8},{10,11... | collective-permute-start | bytes 10616840 | tf_op jit(solution)/shard_map/ppermute | solution.py:813
  405.3 205.0 %collective-permute-start.30 = (bf16[768,2304]{1,0:T(8,128)(2,1)}, bf16[768,2304]{1,0:T(8,128)(2,1)}, u32[]{:S(2)}, u32[]{:S(2)}) collective-permute-start(bf16[768,2304]{1,0:T(8,128)(2,1)} %convolution_convert_fusion.1), channel_id=1, source_target_pairs={{0,1},{1,0},{2,3},{3,2},{4,5},{5,4},{6,7},{7,6},{8,9},{9,8},{10,11... | collective-permute-start | bytes 10616840 | tf_op jit(solution)/shard_map/ppermute | solution.py:813
  412.7 85.8 %collective-permute-start.29 = (bf16[768,2304]{1,0:T(8,128)(2,1)}, bf16[768,2304]{1,0:T(8,128)(2,1)}, u32[]{:S(2)}, u32[]{:S(2)}) collective-permute-start(bf16[768,2304]{1,0:T(8,128)(2,1)} %convolution_convert_fusion.2), channel_id=1, source_target_pairs={{0,1},{1,0},{2,3},{3,2},{4,5},{5,4},{6,7},{7,6},{8,9},{9,8},{10,11... | collective-permute-start | bytes 10616840 | tf_op jit(solution)/shard_map/ppermute | solution.py:813
  418.4 70.4 %collective-permute-start.26 = (bf16[768,2304]{1,0:T(8,128)(2,1)}, bf16[768,2304]{1,0:T(8,128)(2,1)}, u32[]{:S(2)}, u32[]{:S(2)}) collective-permute-start(bf16[768,2304]{1,0:T(8,128)(2,1)} %convolution_convert_fusion.3), channel_id=1, source_target_pairs={{0,1},{1,0},{2,3},{3,2},{4,5},{5,4},{6,7},{7,6},{8,9},{9,8},{10,11... | collective-permute-start | bytes 10616840 | tf_op jit(solution)/shard_map/ppermute | solution.py:813
  423.7 63.9 %collective-permute-start.27 = (bf16[384,2304]{1,0:T(8,128)(2,1)}, bf16[384,2304]{1,0:T(8,128)(2,1)}, u32[]{:S(2)}, u32[]{:S(2)}) collective-permute-start(bf16[384,2304]{1,0:T(8,128)(2,1)} %fusion.43), channel_id=1, source_target_pairs={{0,8},{8,0},{16,24},{24,16},{1,9},{9,1},{17,25},{25,17},{2,10},{10... | collective-permute-start | bytes 5308424 | tf_op jit(solution)/shard_map/ppermute | solution.py:819
  430.6 58.3 %collective-permute-start.28 = (bf16[384,2304]{1,0:T(8,128)(2,1)}, bf16[384,2304]{1,0:T(8,128)(2,1)}, u32[]{:S(2)}, u32[]{:S(2)}) collective-permute-start(bf16[384,2304]{1,0:T(8,128)(2,1)} %fusion.40), channel_id=1, source_target_pairs={{0,16},{8,24},{16,0},{24,8},{1,17},{9,25},{17,1},{25,9},{2,18},{10... | collective-permute-start | bytes 5308424 | tf_op jit(solution)/shard_map/ppermute | solution.py:820
  498.0 106.1 %collective-permute-start.31 = (bf16[768,2304]{1,0:T(8,128)(2,1)}, bf16[768,2304]{1,0:T(8,128)(2,1)}, u32[]{:S(2)}, u32[]{:S(2)}) collective-permute-start(bf16[768,2304]{1,0:T(8,128)(2,1)} %add_convert_fusion.2), channel_id=1, source_target_pairs={{0,8},{8,0},{16,24},{24,16},{1,9},{9,1},{17,25},{25,17},{2,10},{10... | collective-permute-start | bytes 10616840 | tf_op jit(solution)/shard_map/ppermute | solution.py:840
  509.1 100.6 %collective-permute-start.32 = (bf16[768,2304]{1,0:T(8,128)(2,1)}, bf16[768,2304]{1,0:T(8,128)(2,1)}, u32[]{:S(2)}, u32[]{:S(2)}) collective-permute-start(bf16[768,2304]{1,0:T(8,128)(2,1)} %add_convert_fusion.1), channel_id=1, source_target_pairs={{0,16},{8,24},{16,0},{24,8},{1,17},{9,25},{17,1},{25,9},{2,18},{10... | collective-permute-start | bytes 10616840 | tf_op jit(solution)/shard_map/ppermute | solution.py:841
  555.3 200.9 %reduce-scatter.8.cloned.1.call-start = ((), (), s32[]{:S(2)}) async-start(), calls=%async_computation.9 | async-start | bytes 4423680 | tf_op jit(solution)/shard_map/reduce_scatter | solution.py:870
  571.4 24.4 %collective-permute-start.34 = (bf16[768,2048]{1,0:T(8,128)(2,1)}, bf16[768,2048]{1,0:T(8,128)(2,1)}, u32[]{:S(2)}, u32[]{:S(2)}) collective-permute-start(bf16[768,2048]{1,0:T(8,128)(2,1)} %convolution_convert_fusion.7), channel_id=1, source_target_pairs={{0,1},{1,0},{2,3},{3,2},{4,5},{5,4},{6,7},{7,6},{8,9},{9,8},{10,11... | collective-permute-start | bytes 9437192 | tf_op jit(solution)/shard_map/ppermute | solution.py:809
  594.6 75.7 %collective-permute-start.37 = (bf16[512,384]{1,0:T(8,128)(2,1)}, bf16[512,384]{1,0:T(8,128)(2,1)}, u32[]{:S(2)}, u32[]{:S(2)}) collective-permute-start(bf16[512,384]{1,0:T(8,128)(2,1)} %get-tuple-element.192), channel_id=1, source_target_pairs={{0,16},{8,24},{16,0},{24,8},{1,17},{9,25},{17,1},{25,9},{2,18},{10... | collective-permute-start | bytes 1179656 | tf_op jit(solution)/shard_map/ppermute | solution.py:820
  595.8 74.5 %collective-permute-start.36 = (bf16[512,384]{1,0:T(8,128)(2,1)}, bf16[512,384]{1,0:T(8,128)(2,1)}, u32[]{:S(2)}, u32[]{:S(2)}) collective-permute-start(bf16[512,384]{1,0:T(8,128)(2,1)} %get-tuple-element.193), channel_id=1, source_target_pairs={{0,8},{8,0},{16,24},{24,16},{1,9},{9,1},{17,25},{25,17},{2,10},{10... | collective-permute-start | bytes 1179656 | tf_op jit(solution)/shard_map/ppermute | solution.py:819
  604.2 68.5 %collective-permute-start.39 = (bf16[384,512]{1,0:T(8,128)(2,1)}, bf16[384,512]{1,0:T(8,128)(2,1)}, u32[]{:S(2)}, u32[]{:S(2)}) collective-permute-start(bf16[384,512]{1,0:T(8,128)(2,1)} %get-tuple-element.190), channel_id=1, source_target_pairs={{0,16},{8,24},{16,0},{24,8},{1,17},{9,25},{17,1},{25,9},{2,18},{10... | collective-permute-start | bytes 1179656 | tf_op jit(solution)/shard_map/ppermute | solution.py:820
  609.8 62.9 %collective-permute-start.38 = (bf16[384,512]{1,0:T(8,128)(2,1)}, bf16[384,512]{1,0:T(8,128)(2,1)}, u32[]{:S(2)}, u32[]{:S(2)}) collective-permute-start(bf16[384,512]{1,0:T(8,128)(2,1)} %get-tuple-element.191), channel_id=1, source_target_pairs={{0,8},{8,0},{16,24},{24,16},{1,9},{9,1},{17,25},{25,17},{2,10},{10... | collective-permute-start | bytes 1179656 | tf_op jit(solution)/shard_map/ppermute | solution.py:819
  621.5 156.7 %reduce-scatter.6.cloned.1.call-start = ((), (), s32[]{:S(2)}) async-start(), calls=%async_computation.8 | async-start | bytes 1216512 | tf_op jit(solution)/shard_map/reduce_scatter | solution.py:1097
  700.0 49.5 %collective-permute-start.51 = (bf16[1024,384]{1,0:T(8,128)(2,1)}, bf16[1024,384]{1,0:T(8,128)(2,1)}, u32[]{:S(2)}, u32[]{:S(2)}) collective-permute-start(bf16[1024,384]{1,0:T(8,128)(2,1)} %get-tuple-element.188), channel_id=1, source_target_pairs={{0,16},{8,24},{16,0},{24,8},{1,17},{9,25},{17,1},{25,9},{2,18},{10... | collective-permute-start | bytes 2359304 | tf_op jit(solution)/shard_map/ppermute | solution.py:841
  701.7 47.8 %collective-permute-start.50 = (bf16[1024,384]{1,0:T(8,128)(2,1)}, bf16[1024,384]{1,0:T(8,128)(2,1)}, u32[]{:S(2)}, u32[]{:S(2)}) collective-permute-start(bf16[1024,384]{1,0:T(8,128)(2,1)} %get-tuple-element.189), channel_id=1, source_target_pairs={{0,8},{8,0},{16,24},{24,16},{1,9},{9,1},{17,25},{25,17},{2,10},{10... | collective-permute-start | bytes 2359304 | tf_op jit(solution)/shard_map/ppermute | solution.py:840
  707.4 142.4 %all-gather.27.cloned.1.call-start = ((), (), s32[]{:S(2)}) async-start(), calls=%async_computation.11 | async-start | bytes 4423680 | tf_op jit(solution)/shard_map/all_gather | solution.py:889
  748.0 44.3 %collective-permute-start.44 = (bf16[768,512]{1,0:T(8,128)(2,1)}, bf16[768,512]{1,0:T(8,128)(2,1)S(1)}, u32[]{:S(2)}, u32[]{:S(2)}) collective-permute-start(bf16[768,512]{1,0:T(8,128)(2,1)} %get-tuple-element.182), channel_id=1, source_target_pairs={{0,16},{8,24},{16,0},{24,8},{1,17},{9,25},{17,1},{25,9},{2,18},{10... | collective-permute-start | bytes 2359304 | tf_op jit(solution)/shard_map/ppermute | solution.py:841
  748.3 44.0 %collective-permute-start.43 = (bf16[768,512]{1,0:T(8,128)(2,1)}, bf16[768,512]{1,0:T(8,128)(2,1)}, u32[]{:S(2)}, u32[]{:S(2)}) collective-permute-start(bf16[768,512]{1,0:T(8,128)(2,1)} %get-tuple-element.183), channel_id=1, source_target_pairs={{0,8},{8,0},{16,24},{24,16},{1,9},{9,1},{17,25},{25,17},{2,10},{10... | collective-permute-start | bytes 2359304 | tf_op jit(solution)/shard_map/ppermute | solution.py:840
  752.2 45.2 %collective-permute-start.52 = (bf16[256,384]{1,0:T(8,128)(2,1)}, bf16[256,384]{1,0:T(8,128)(2,1)S(1)}, u32[]{:S(2)}, u32[]{:S(2)}) collective-permute-start(bf16[256,384]{1,0:T(8,128)(2,1)} %get-tuple-element.201), channel_id=1, source_target_pairs={{0,2},{1,3},{2,4},{3,5},{4,6},{5,7},{6,0},{7,1},{8,10},{9,11},{10,... | collective-permute-start | bytes 589832 | tf_op jit(solution)/shard_map/ppermute | solution.py:859
  753.5 55.3 %collective-permute-start.54 = (bf16[256,384]{1,0:T(8,128)(2,1)}, bf16[256,384]{1,0:T(8,128)(2,1)}, u32[]{:S(2)}, u32[]{:S(2)}) collective-permute-start(bf16[256,384]{1,0:T(8,128)(2,1)} %get-tuple-element.202), channel_id=1, source_target_pairs={{0,6},{1,7},{2,0},{3,1},{4,2},{5,3},{6,4},{7,5},{8,14},{9,15},{10,... | collective-permute-start | bytes 589832 | tf_op jit(solution)/shard_map/ppermute | solution.py:859
  754.2 54.5 %collective-permute-start.53 = (bf16[256,384]{1,0:T(8,128)(2,1)}, bf16[256,384]{1,0:T(8,128)(2,1)}, u32[]{:S(2)}, u32[]{:S(2)}) collective-permute-start(bf16[256,384]{1,0:T(8,128)(2,1)} %get-tuple-element.203), channel_id=1, source_target_pairs={{0,4},{1,5},{2,6},{3,7},{4,0},{5,1},{6,2},{7,3},{8,12},{9,13},{10,... | collective-permute-start | bytes 589832 | tf_op jit(solution)/shard_map/ppermute | solution.py:859
  795.3 26.9 %collective-permute-start.47 = (bf16[192,1024]{1,0:T(8,128)(2,1)}, bf16[192,1024]{1,0:T(8,128)(2,1)}, u32[]{:S(2)}, u32[]{:S(2)}) collective-permute-start(bf16[192,1024]{1,0:T(8,128)(2,1)} %get-tuple-element.198), channel_id=1, source_target_pairs={{0,2},{1,3},{2,4},{3,5},{4,6},{5,7},{6,0},{7,1},{8,10},{9,11},{10,... | collective-permute-start | bytes 1179656 | tf_op jit(solution)/shard_map/ppermute | solution.py:859
  795.3 26.9 %collective-permute-start.49 = (bf16[192,1024]{1,0:T(8,128)(2,1)}, bf16[192,1024]{1,0:T(8,128)(2,1)}, u32[]{:S(2)}, u32[]{:S(2)}) collective-permute-start(bf16[192,1024]{1,0:T(8,128)(2,1)} %get-tuple-element.199), channel_id=1, source_target_pairs={{0,6},{1,7},{2,0},{3,1},{4,2},{5,3},{6,4},{7,5},{8,14},{9,15},{10,... | collective-permute-start | bytes 1179656 | tf_op jit(solution)/shard_map/ppermute | solution.py:859
  797.4 24.9 %collective-permute-start.48 = (bf16[192,1024]{1,0:T(8,128)(2,1)S(1)}, bf16[192,1024]{1,0:T(8,128)(2,1)}, u32[]{:S(2)}, u32[]{:S(2)}) collective-permute-start(bf16[192,1024]{1,0:T(8,128)(2,1)S(1)} %get-tuple-element.200), channel_id=1, source_target_pairs={{0,4},{1,5},{2,6},{3,7},{4,0},{5,1},{6,2},{7,3},{8,12},{9,13},{10,... | collective-permute-start | bytes 1179656 | tf_op jit(solution)/shard_map/ppermute | solution.py:859
  (112 other events, 1698.0 us)
Sparse Core Ops, SparseCore 0:
  9.6 38.9 all-gather.16
  56.5 72.0 all-gather.24
  132.0 85.5 all-gather.18
  220.4 109.4 all-gather.20
  354.7 199.1 reduce-scatter.3
  555.6 47.5 all-gather.22
  621.6 67.0 reduce-scatter.7
  707.5 26.1 reduce-scatter.5
  756.4 49.5 all-gather.26

commit v12 on v11

--- a/solution.py
+++ b/solution.py
@@ -120,8 +120,9 @@
         chunk_ref[b, 1] = ends[b][1]
 
 
-def branch_kernel(core_ref, state_ref, prod_ref, carry_ref, gate_ref, out_ref, branch_ref, split_ref):
-    del core_ref
+def branch_kernel(
+    per, core_ref, state_ref, prod_ref, carry_ref, gate_ref, out_ref, branch_ref, own_ref, far_ref
+):
     seqs, rows, _ = state_ref.shape
     for b in range(seqs):
         carry = jnp.concatenate([carry_ref[b]] * 4, axis=0)
@@ -132,10 +133,18 @@
             out_ref[b, at, :] = state
             low = (state * gelu_tanh(gate_ref[b, at, :])).astype(BF16)
             branch_ref[b, at, :] = low
-            split_ref[0, b, at, :] = low
             return 0
 
         lax.fori_loop(0, rows // 32, point, 0, unroll=4)
+    own = (pl.program_id(0) // per) % 2 == core_ref[0]
+
+    @pl.when(own)
+    def _():
+        own_ref[...] = branch_ref[...]
+
+    @pl.when(jnp.logical_not(own))
+    def _():
+        far_ref[...] = branch_ref[...]
 
 
 def reverse_kernel(
@@ -313,7 +322,8 @@
     return pl.BlockSpec((seqs, 2, CHUNKS, HS), lambda h: (0, 0, 0, h))
 
 
-PARAMS = pltpu.CompilerParams(vmem_limit_bytes=40 * 1024 * 1024)
+VMEM_BYTES = 60 * 1024 * 1024
+PARAMS = pltpu.CompilerParams(vmem_limit_bytes=VMEM_BYTES)
 
 
 def mixer_forward(u, halo, dist, gates, taps, soft):
@@ -357,23 +367,31 @@
     def at(h, core_ref):
         return (0, 0, h)
 
-    def split_at(h, core_ref):
+    def split_at(parity, h):
         shard = h // per
-        return ((shard % 2 + core_ref[0]) % 2, 0, 0, (shard // 2) * per + h % per)
+        count = jnp.where(parity == 0, shard // 2 * per + per, shard // 2 * per)
+        count = jnp.where(shard % 2 == parity, shard // 2 * per + h % per + 1, count)
+        return (0, 0, jnp.maximum(count - 1, 0))
 
     full = pl.BlockSpec((seqs, rows, HS), at)
     return pl.pallas_call(
-        branch_kernel,
+        functools.partial(branch_kernel, per),
         grid_spec=pltpu.PrefetchScalarGridSpec(
             num_scalar_prefetch=1,
             grid=(HEADS,),
             in_specs=[full, full, pl.BlockSpec((seqs, CHUNKS, HS), at), full],
-            out_specs=[full, full, pl.BlockSpec((1, seqs, rows, HS), split_at)],
+            out_specs=[
+                full,
+                full,
+                pl.BlockSpec((seqs, rows, HS), lambda h, core_ref: split_at(core_ref[0], h)),
+                pl.BlockSpec((seqs, rows, HS), lambda h, core_ref: split_at(1 - core_ref[0], h)),
+            ],
         ),
         out_shape=[
             jax.ShapeDtypeStruct((seqs, rows, LRU), F32),
             jax.ShapeDtypeStruct((seqs, rows, LRU), BF16),
-            jax.ShapeDtypeStruct((2, seqs, rows, LRU // 2), BF16),
+            jax.ShapeDtypeStruct((seqs, rows, LRU // 2), BF16),
+            jax.ShapeDtypeStruct((seqs, rows, LRU // 2), BF16),
         ],
         compiler_params=PARAMS,
         name="mixer_branch",
@@ -727,7 +745,7 @@
                 pltpu.VMEM((2, weights, depth, tile), BF16),
                 pltpu.SemaphoreType.DMA((2, weights)),
             ],
-            compiler_params=pltpu.CompilerParams(vmem_limit_bytes=56 * 1024 * 1024),
+            compiler_params=PARAMS,
             name=name,
         )(where, normed, *own, *far)
 
@@ -992,10 +1010,9 @@
     gate_pre = gate_pre.reshape(wide)
     carry_in = shard_carry(end_state, end_prod, False)
     carries = chunk_carries(chunks, carry_in, False)
-    state, branch, branch_split = mixer_branch(
+    state, branch, branch_own, branch_far = mixer_branch(
         tie(state_part, *up_gather.second(carries, gate_pre)), prod_part, carries, gate_pre, last + 1, place % 2
     )
-    branch_split = branch_split.reshape(2, row_count, LRU // 2)
     resid = inputs + jnp.dot(
         branch.reshape(row_count, LRU), proj_out, preferred_element_type=F32
     )
@@ -1042,8 +1059,8 @@
     rev_carries = chunk_carries(rev_chunks, rev_carry, True)
     grad_mixer, grad_gate = tie((grad_mixer, grad_gate), rev_carry)
     out_sum = Reduction(
-        branch_split[0],
-        branch_split[1],
+        branch_own.reshape(row_count, LRU // 2),
+        branch_far.reshape(row_count, LRU // 2),
         lambda n: lax.dynamic_slice_in_dim(grad_mixer, n * (D // 4), D // 4, 1),
         D // 4,
         True,

time: 873 us -> 875 us (level)
  local copies, waits for them, and re-layouts: 98.7 us -> 72.3 us
  Pallas kernels: 208 us -> 225 us
  waiting for transfers between devices: 117 us -> 126 us
    unnamed x199 -> x145, local copies, waits for them, and re-layouts: 43.9 us -> 16.3 us
  transfers between devices with their start and end apart: 64 -> 64, of which waited for: 12 -> 13; matrix products, arithmetic and copies ran while one was open for 39% -> 40% of each run, Pallas kernels for 24% -> 26%
where the time goes in v12:
time: 875 us; the launch traced here: 865 us
  matrix products  246 us (28%)
  Pallas kernels  225 us (26%)
  waiting for transfers between devices  126 us (14%)
  blocking collectives  89.5 us (10%)
  local copies, waits for them, and re-layouts  72.3 us (8%)
  starting transfers between devices  49.9 us (6%)
  other arithmetic  41.4 us (5%)
  between operations  15.3 us (2%)
    dot_general x16, matrix products, dot_rows(): lax.dot_general(a, b, (((0,), (0,)), ((), ())), preferred_element_type=F32)  133 us
    dot_general x5, matrix products, dot_far(): lax.dot_general(a, b, (((1,), (1,)), ((), ())), preferred_element_type=F32)  77.9 us
    pallas_call x3, Pallas kernels, call(): pl.pallas_call(kernel, grid=(steps,), in_specs=[pl.BlockSpec(memory_space...  65.4 us
    pallas_call x1, Pallas kernels, mixer_backward(): pl.pallas_call(mixer_backward_kernel, grid=(HEADS,), in_specs=[full, full...  45.8 us
    ppermute x2, waiting for transfers between devices, first(): self.from_y = lax.ppermute(self.near, 'grp', xor_pairs('grp', 2))  35.7 us
    ppermute x3, waiting for transfers between devices, __init__(): lax.ppermute(own, 'seq', ring_pairs(-2 * j))  35 us
    pallas_call x1, Pallas kernels, ffn_backward(): pl.pallas_call(ffn_backward_kernel, grid=(FF // FF_TILE,), in_specs=[pl.B...  28.7 us
    all_gather x2, blocking collectives, shard_carry(): both = lax.all_gather(jnp.stack([ends, prods]), 'seq')  27.4 us
  transfers between devices with their start and end apart: 64, of which 13 were waited for; matrix products, arithmetic and copies ran while one was open for 40% of the time, Pallas kernels for 26%

profile of v12, /device:TPU:18, one launch (start us, length us, event | category | flops | bytes accessed | tf_op | source)
XLA Modules:
  0.0 865.2 jit_solution(14779842556058317013)
XLA Ops:
  16.1 7.5 collective-permute-done
  25.3 27.5 %collective-permute-done.1 = bf16[192,1024]{1,0:T(8,128)(2,1)} collective-permute-done((bf16[192,1024]{1,0:T(8,128)(2,1)}, bf16[192,1024]{1,0:T(8,128)(2,1)}, u32[]{:S(2)}, u32[]{:S(2)}) %collective-permute-start.1) | collective-permute-done | bytes 393248 | tf_op jit(solution)/shard_map/ppermute | solution.py:693
  61.6 24.5 %collective-permute-done.4.refs_3_ = bf16[576,1024]{1,0:T(8,128)(2,1)S(1)} collective-permute-done((bf16[576,1024]{1,0:T(8,128)(2,1)}, bf16[576,1024]{1,0:T(8,128)(2,1)S(1)}, u32[]{:S(2)}, u32[]{:S(2)}) %collective-permute-start.4) | collective-permute-done | bytes 1179680 | tf_op jit(solution)/shard_map/ppermute | solution.py:709
  91.6 15.3 %all-gather.9 = bf16[8,1,1664]{2,1,0:T(2,128)(2,1)S(1)} all-gather(bf16[1,1,1664]{2,1,0:T(2,128)(2,1)S(1)} %reshape.2482), channel_id=2, replica_groups=mesh['grp'=4,'seq'=8] {'seq'}, dimensions={0}, use_global_device_ids=true | all-gather | bytes 29952 | tf_op jit(solution)/shard_map/all_gather | solution.py:965
  114.3 5.9 rms_norm.2
  123.9 11.9 %gathered_dot.2 = (bf16[1024,2048]{1,0:T(8,128)(2,1)}, bf16[1536,2048]{1,0:T(8,128)(2,1)}) custom-call(s32[3]{0:T(128)} %pad_add_fusion.1.where_ref, bf16[1024,1536]{1,0:T(8,128)(2,1)} %get-tuple-element.79.n_ref, bf16[192,4096]{1,0:T(8,128)(2,1)} %refs_0_.4, bf16[576,1024]{1,0:T(8,128)(2,1)} %constant_dynamic-update-slice_fusion.refs_1_, ...), custom_call_target="tpu_custom_call" | custom-call | tf_op jit(solution)/shard_map/gathered_dot/pallas_call | solution.py:734
  147.3 12.6 %gathered_dot.3 = (f32[1024,2048]{1,0:T(8,128)}, bf16[1536,2048]{1,0:T(8,128)(2,1)}) custom-call(s32[3]{0:T(128)} %pad_add_fusion.1.where_ref, bf16[1024,1536]{1,0:T(8,128)(2,1)} %get-tuple-element.79.n_ref, bf16[192,4096]{1,0:T(8,128)(2,1)} %refs_0_.4, bf16[576,1024]{1,0:T(8,128)(2,1)} %constant_dynamic-update-slice_fusion.refs_1_, ...), custom_call_target="tpu_custom_call" | custom-call | tf_op jit(solution)/shard_map/gathered_dot/pallas_call | solution.py:734
  160.9 26.3 %mixer_forward.1 = (bf16[2,512,2048]{2,1,0:T(8,128)(2,1)}, f32[2,512,2048]{2,1,0:T(8,128)}, f32[2,512,2048]{2,1,0:T(8,128)}, f32[2,512,2048]{2,1,0:T(8,128)}, f32[2,2,8,2048]{3,2,1,0:T(8,128)}) custom-call(bf16[2,512,2048]{2,1,0:T(8,128)(2,1)} %bitcast.785, bf16[2,8,2048]{2,1,0:T(8,128)(2,1)} %copy-done.44, f32[2,512,128]{2,1,0:T(8,128)} %broadcast_in_dim.21.dist_ref, ...), custom_call_target="tpu_custom_call" | custom-call | tf_op jit(solution)/shard_map/mixer_forward/pallas_call | solution.py:333
  188.8 13.7 %all-gather.2 = f32[16,2,2048]{2,1,0:T(2,128)S(1)} all-gather(f32[2,2,2048]{2,1,0:T(2,128)S(1)} %copy.311), channel_id=4, replica_groups=mesh['grp'=4,'seq'=8] {'seq'}, dimensions={0}, use_global_device_ids=true | all-gather | bytes 294912 | tf_op jit(solution)/shard_map/all_gather | solution.py:914
  203.6 11.2 %collective-permute-done.16.refs_3_ = bf16[576,2304]{1,0:T(8,128)(2,1)} collective-permute-done((bf16[576,2304]{1,0:T(8,128)(2,1)}, bf16[576,2304]{1,0:T(8,128)(2,1)}, u32[]{:S(2)}, u32[]{:S(2)}) %collective-permute-start.16) | collective-permute-done | bytes 2654240 | tf_op jit(solution)/shard_map/ppermute | solution.py:709
  225.7 5.4 copy.326
  231.1 20.9 %mixer_branch.1 = (f32[2,512,2048]{2,1,0:T(8,128)}, bf16[2,512,2048]{2,1,0:T(8,128)(2,1)}, bf16[2,512,1024]{2,1,0:T(8,128)(2,1)}, bf16[2,512,1024]{2,1,0:T(8,128)(2,1)}) custom-call(s32[1]{0:T(128)} %bitcast.3.core_ref, f32[2,512,2048]{2,1,0:T(8,128)} %get-tuple-element.89.state_ref, f32[2,512,2048]{2,1,0:T(8,128)} %get-tuple-element.90.prod_ref, ...), custom_call_target="tpu_custom_call" | custom-call | tf_op jit(solution)/shard_map/mixer_branch/pallas_call | solution.py:377
  252.0 5.7 collective-permute-done.18.refs_5_
  257.7 7.1 collective-permute-done.17.refs_4_
  264.8 12.6 %convert_add_fusion.x_ref = f32[1024,1536]{1,0:T(8,128)} fusion(bf16[1024,1536]{1,0:T(8,128)(2,1)} %bitcast.779, bf16[1024,2048]{1,0:T(8,128)(2,1)} %bitcast.831, bf16[2048,1536]{1,0:T(8,128)(2,1)} %all-gather.19.cloned.1.call-done), kind=kOutput, calls=%fused_computation.3 | convolution fusion | flops 6445596672 | bytes 19922944 | tf_op jit(solution)/shard_map/dot_general | solution.py:1016
  277.4 6.6 rms_norm.3
  284.1 40.8 %gathered_ffn.1 = (bf16[1024,4608]{1,0:T(8,128)(2,1)}, bf16[2,1024,4608]{2,1,0:T(8,128)(2,1)}, bf16[1536,4608]{1,0:T(8,128)(2,1)}, bf16[1536,4608]{1,0:T(8,128)(2,1)}) custom-call(s32[3]{0:T(128)} %pad_add_fusion.1.where_ref, bf16[1024,1536]{1,0:T(8,128)(2,1)} %get-tuple-element.92.n_ref, bf16[192,9216]{1,0:T(8,128)(2,1)} %refs_0_.5, ...), custom_call_target="tpu_custom_call" | custom-call | tf_op jit(solution)/shard_map/gathered_ffn/pallas_call | solution.py:734
  324.9 30.3 %convolution_convert_fusion = bf16[4608,1536]{1,0:T(8,128)(2,1)} fusion(bf16[1024,4608]{1,0:T(8,128)(2,1)} %get-tuple-element.136, bf16[1024,1536]{1,0:T(8,128)(2,1)} %bitcast.780), kind=kOutput, calls=%fused_computation | convolution fusion | flops 14502592512 | bytes 26738688 | tf_op jit(solution)/shard_map/dot_general | solution.py:566
  355.4 28.7 %ffn_backward.1 = bf16[2,1024,4608]{2,1,0:T(8,128)(2,1)} custom-call(bf16[1024,1536]{1,0:T(8,128)(2,1)} %bitcast.781, bf16[4608,1536]{1,0:T(8,128)(2,1)} %all-gather.21.cloned.1.call-done.down_ref, bf16[2,1024,4608]{2,1,0:T(8,128)(2,1)} %get-tuple-element.97.pull_ref), custom_call_target="tpu_custom_call" | custom-call | tf_op jit(solution)/shard_map/ffn_backward/pallas_call | solution.py:525
  384.1 8.0 convolution_convert_fusion.4
  392.6 8.1 convolution_convert_fusion.1
  402.6 5.3 convolution_convert_fusion.2
  408.2 5.6 convolution_convert_fusion.3
  424.9 23.0 %fusion = f32[1024,1536]{1,0:T(8,128)} fusion(bf16[1536,4608]{1,0:T(8,128)(2,1)} %get-tuple-element.102, bf16[2,1024,4608]{2,1,0:T(8,128)(2,1)} %ffn_backward.1), kind=kOutput, calls=%fused_computation.4 | convolution fusion | flops 14495514624 | bytes 29884416 | tf_op jit(solution)/shard_map/dot_general | solution.py:576
  447.8 21.0 %fusion.25 = f32[1024,1536]{1,0:T(8,128)S(1)} fusion(f32[1024,1536]{1,0:T(8,128)} %fusion, bf16[1536,4608]{1,0:T(8,128)(2,1)} %get-tuple-element.101, bf16[2,1024,4608]{2,1,0:T(8,128)(2,1)} %ffn_backward.1), kind=kOutput, calls=%fused_computation.44 | convolution fusion | flops 14497087488 | bytes 36175872 | tf_op jit(solution)/shard_map/dot_general | solution.py:576
  468.9 10.2 %collective-permute-done.27 = bf16[384,2304]{1,0:T(8,128)(2,1)} collective-permute-done((bf16[384,2304]{1,0:T(8,128)(2,1)}, bf16[384,2304]{1,0:T(8,128)(2,1)}, u32[]{:S(2)}, u32[]{:S(2)}) %collective-permute-start.27) | collective-permute-done | bytes 1769504 | tf_op jit(solution)/shard_map/ppermute | solution.py:837
  479.0 10.0 %collective-permute-done.28 = bf16[384,2304]{1,0:T(8,128)(2,1)} collective-permute-done((bf16[384,2304]{1,0:T(8,128)(2,1)}, bf16[384,2304]{1,0:T(8,128)(2,1)}, u32[]{:S(2)}, u32[]{:S(2)}) %collective-permute-start.28) | collective-permute-done | bytes 1769504 | tf_op jit(solution)/shard_map/ppermute | solution.py:838
  489.0 9.1 %add_convert_fusion.2 = bf16[768,2304]{1,0:T(8,128)(2,1)} fusion(bf16[768,2304]{1,0:T(8,128)(2,1)} %collective-permute-done.26, bf16[1024,768]{1,0:T(8,128)(2,1)S(1)} %copy-done.22, bf16[2,1024,4608]{2,1,0:T(8,128)(2,1)} %ffn_backward.1, s32[]{:T(128)S(6)} %select_n.797, s32[]{:T(128)S(6)} %select_n.799, bf16[384,2304]{1,0:T(8,128)(2,1)} %collective-permute-done.28), kind=kOutput, calls=%fused_computation.14 | convolution fusion | flops 3632726016 | bytes 15138824 | tf_op jit(solution)/shard_map/dot_general | solution.py:566
  499.8 9.8 %add_convert_fusion.1 = bf16[768,2304]{1,0:T(8,128)(2,1)} fusion(bf16[768,2304]{1,0:T(8,128)(2,1)} %collective-permute-done.29, bf16[1024,768]{1,0:T(8,128)(2,1)S(1)} %copy-done.22, bf16[2,1024,4608]{2,1,0:T(8,128)(2,1)} %ffn_backward.1, s32[]{:T(128)S(6)} %select_n.801, s32[]{:T(128)S(6)} %select_n.803, bf16[384,2304]{1,0:T(8,128)(2,1)} %collective-permute-done.27), kind=kOutput, calls=%fused_computation.13 | convolution fusion | flops 3632726016 | bytes 15138824 | tf_op jit(solution)/shard_map/dot_general | solution.py:566
  515.9 12.0 %fusion.193 = f32[1024,2048]{1,0:T(8,128)} fusion(bf16[1024,1536]{1,0:T(8,128)(2,1)S(1)} %get-tuple-element.113, bf16[2048,1536]{1,0:T(8,128)(2,1)} %all-gather.19.cloned.1.call-done), kind=kOutput, calls=%fused_computation.340 | convolution fusion | flops 6442450944 | bytes 17825792 | tf_op jit(solution)/shard_map/dot_general | solution.py:576
  527.9 25.3 %mixer_reverse.1 = (bf16[2,512,2048]{2,1,0:T(8,128)(2,1)}, f32[2,512,2048]{2,1,0:T(8,128)}, f32[2,512,2048]{2,1,0:T(8,128)}, f32[2,2,8,2048]{3,2,1,0:T(8,128)}) custom-call(f32[2,512,2048]{2,1,0:T(8,128)} %bitcast.788, f32[2,512,2048]{2,1,0:T(8,128)} %bitcast.775, f32[2,512,2048]{2,1,0:T(8,128)} %get-tuple-element.106.keep_ref, ...), custom_call_target="tpu_custom_call" | custom-call | tf_op jit(solution)/shard_map/mixer_reverse/pallas_call | solution.py:405
  561.3 5.7 convolution_convert_fusion.5
  568.5 5.3 convolution_convert_fusion.7
  574.3 13.7 %all-gather.3 = f32[16,2,2048]{2,1,0:T(2,128)S(1)} all-gather(f32[2,2,2048]{2,1,0:T(2,128)S(1)} %copy.343), channel_id=5, replica_groups=mesh['grp'=4,'seq'=8] {'seq'}, dimensions={0}, use_global_device_ids=true | all-gather | bytes 294912 | tf_op jit(solution)/shard_map/all_gather | solution.py:914
  589.2 7.1 add_convert_fusion.6
  600.8 5.8 add_convert_fusion.5
  612.6 11.2 %add_convert_fusion = bf16[768,2304]{1,0:T(8,128)(2,1)} fusion(bf16[768,2304]{1,0:T(8,128)(2,1)} %collective-permute-done.32, bf16[768,2304]{1,0:T(8,128)(2,1)} %collective-permute-done.31, bf16[768,2304]{1,0:T(8,128)(2,1)} %collective-permute-done.30, bf16[1024,768]{1,0:T(8,128)(2,1)S(1)} %copy-done.22, bf16[2,1024,4608]{2,1,0:T(8,128)(2,1)} %ffn_backward.1, ...), kind=kOutput, calls=%fused_computation.12 | convolution fusion | flops 3636264960 | bytes 20447240 | tf_op jit(solution)/shard_map/dot_general | solution.py:566
  623.8 45.8 %mixer_backward.1 = (bf16[2,512,2048]{2,1,0:T(8,128)(2,1)}, f32[2,32,2048]{2,1,0:T(8,128)}, f32[2,8,2048]{2,1,0:T(8,128)}, f32[16,128,256]{2,1,0:T(8,128)}, f32[8,2048]{1,0:T(8,128)}, /*index=5*/f32[8,2048]{1,0:T(8,128)}) custom-call(f32[2,512,2048]{2,1,0:T(8,128)} %get-tuple-element.119.local_ref, f32[2,512,2048]{2,1,0:T(8,128)} %get-tuple-element.120.prod_ref, ...), custom_call_target="tpu_custom_call" | custom-call | tf_op jit(solution)/shard_map/mixer_backward/pallas_call | solution.py:427
  678.8 11.2 %fusion.194 = f32[1024,1536]{1,0:T(8,128)} fusion(bf16[1024,2048]{1,0:T(8,128)(2,1)S(1)} %bitcast.794, bf16[1536,2048]{1,0:T(8,128)(2,1)} %get-tuple-element.130), kind=kOutput, calls=%fused_computation.341 | convolution fusion | flops 6442450944 | bytes 16777216 | tf_op jit(solution)/shard_map/dot_general | solution.py:576
  693.0 5.3 convolution_convert_fusion.6
  708.5 11.1 %collective-permute-done.46 = bf16[768,512]{1,0:T(8,128)(2,1)} collective-permute-done((bf16[768,512]{1,0:T(8,128)(2,1)}, bf16[768,512]{1,0:T(8,128)(2,1)}, u32[]{:S(2)}, u32[]{:S(2)}) %collective-permute-start.46) | collective-permute-done | bytes 786464 | tf_op jit(solution)/shard_map/ppermute | solution.py:859
  722.2 7.0 add_convert_fusion.4
  732.4 10.8 %fusion.10 = (f32[1024]{0:T(1024)S(1)}, f32[1024,1536]{1,0:T(8,128)S(1)}) fusion(f32[1536]{0:T(1024)S(1)} %reshape.2464, bf16[2,8,64,1536]{3,1,2,0:T(8,128)(2,1)S(1)} %copy-done.4, f32[1024,1536]{1,0:T(8,128)} %fusion.194, bf16[1024,2048]{1,0:T(8,128)(2,1)S(1)} %bitcast.796, bf16[1536,2048]{1,0:T(8,128)(2,1)} %get-tuple-element.133), kind=kOutput, calls=%fused_computation.19 | convolution fusion | flops 6450314240 | bytes 26224640 | tf_op jit(solution)/shard_map/dot_general | solution.py:576
  757.8 21.8 %add_convert_fusion.3 = bf16[1024,1536]{1,0:T(8,128)(2,1)} fusion(f32[1024,1536]{1,0:T(8,128)} %convert_add_fusion.x_ref, bf16[1024,4608]{1,0:T(8,128)(2,1)} %get-tuple-element.136, bf16[4608,1536]{1,0:T(8,128)(2,1)} %all-gather.21.cloned.1.call-done.down_ref), kind=kOutput, calls=%fused_computation.20 | convolution fusion | flops 14498660352 | bytes 33030144 | tf_op jit(solution)/shard_map/dot_general | solution.py:1144
  779.7 14.0 %all-gather.6 = bf16[2112,128]{1,0:T(8,128)(2,1)S(1)} all-gather(bf16[528,128]{1,0:T(8,128)(2,1)} %reduce-scatter.6.cloned.1.call-done), channel_id=8, replica_groups=mesh['grp'=4,'seq'=8] {'grp'}, dimensions={0}, use_global_device_ids=true | all-gather | bytes 675840 | tf_op jit(solution)/shard_map/all_gather | solution.py:1118
  811.3 10.6 %all-gather.7 = bf16[1024,384]{1,0:T(8,128)(2,1)S(1)} all-gather(bf16[256,384]{1,0:T(8,128)(2,1)S(1)} %fusion.72), channel_id=9, replica_groups=mesh['grp'=4,'seq'=8] {'grp'}, dimensions={0}, use_global_device_ids=true | all-gather | bytes 983040 | tf_op jit(solution)/shard_map/all_gather | solution.py:907
  825.4 11.7 %all-gather.4 = bf16[768,512]{1,0:T(8,128)(2,1)S(1)} all-gather(bf16[192,512]{1,0:T(8,128)(2,1)S(1)} %get-tuple-element.204), channel_id=6, replica_groups=mesh['grp'=4,'seq'=8] {'grp'}, dimensions={0}, use_global_device_ids=true | all-gather | bytes 983040 | tf_op jit(solution)/shard_map/all_gather | solution.py:1136
  837.8 10.5 %all-gather.5 = bf16[768,512]{1,0:T(8,128)(2,1)S(1)} all-gather(bf16[192,512]{1,0:T(8,128)(2,1)S(1)} %get-tuple-element.205), channel_id=7, replica_groups=mesh['grp'=4,'seq'=8] {'grp'}, dimensions={0}, use_global_device_ids=true | all-gather | bytes 983040 | tf_op jit(solution)/shard_map/all_gather | solution.py:1136
  (380 shorter events, 179.4 us)
Async XLA Ops:
  7.2 49.1 %all-gather.17.cloned.1.call-start = ((), (), s32[]{:S(2)}) async-start(), calls=%async_computation.3 | async-start | bytes 1179648 | tf_op jit(solution)/shard_map/all_gather | solution.py:977
  7.9 127.9 %all-gather.25.cloned.1.call-start = ((), (), s32[]{:S(2)}) async-start(), calls=%async_computation.10 | async-start | bytes 4423680 | tf_op jit(solution)/shard_map/all_gather | solution.py:690
  10.4 44.2 %collective-permute-start.2 = (bf16[192,1024]{1,0:T(8,128)(2,1)}, bf16[192,1024]{1,0:T(8,128)(2,1)}, u32[]{:S(2)}, u32[]{:S(2)}) collective-permute-start(bf16[192,1024]{1,0:T(8,128)(2,1)} %constant_dynamic-slice_fusion.15), channel_id=1, source_target_pairs={{0,2},{1,3},{2,4},{3,5},{4,6},{5,7},{6,0},{7,1},{8,10},{9,11},{10,... | collective-permute-start | bytes 1179656 | tf_op jit(solution)/shard_map/ppermute | solution.py:693
  12.0 40.8 %collective-permute-start.1 = (bf16[192,1024]{1,0:T(8,128)(2,1)}, bf16[192,1024]{1,0:T(8,128)(2,1)}, u32[]{:S(2)}, u32[]{:S(2)}) collective-permute-start(bf16[192,1024]{1,0:T(8,128)(2,1)} %constant_dynamic-slice_fusion.15), channel_id=1, source_target_pairs={{0,4},{1,5},{2,6},{3,7},{4,0},{5,1},{6,2},{7,3},{8,12},{9,13},{10,... | collective-permute-start | bytes 1179656 | tf_op jit(solution)/shard_map/ppermute | solution.py:693
  56.4 208.4 %all-gather.19.cloned.1.call-start = ((), (), s32[]{:S(2)}) async-start(), calls=%async_computation.4 | async-start | bytes 6488064 | tf_op jit(solution)/shard_map/all_gather | solution.py:544
  58.1 297.3 %all-gather.21.cloned.1.call-start = ((), (), s32[]{:S(2)}) async-start(), calls=%async_computation.5 | async-start | bytes 14598144 | tf_op jit(solution)/shard_map/all_gather | solution.py:544
  58.9 499.7 %reduce-scatter.4.cloned.1.call-start = ((), (), s32[]{:S(2)}) async-start(), calls=%async_computation.6 | async-start | bytes 14598144 | tf_op jit(solution)/shard_map/reduce_scatter | solution.py:1028
  59.0 27.1 %collective-permute-start.4 = (bf16[576,1024]{1,0:T(8,128)(2,1)}, bf16[576,1024]{1,0:T(8,128)(2,1)S(1)}, u32[]{:S(2)}, u32[]{:S(2)}) collective-permute-start(bf16[576,1024]{1,0:T(8,128)(2,1)} %constant_dynamic-update-slice_fusion.refs_1_), channel_id=1, source_target_pairs={{0,16},{8,24},{16,0},{24,8},{1,17},{9,25},{17,1},{25,9},{2,18},{10... | collective-permute-start | bytes 3538952 | tf_op jit(solution)/shard_map/ppermute | solution.py:709
  60.6 27.0 %collective-permute-start.3 = (bf16[576,1024]{1,0:T(8,128)(2,1)}, bf16[576,1024]{1,0:T(8,128)(2,1)}, u32[]{:S(2)}, u32[]{:S(2)}) collective-permute-start(bf16[576,1024]{1,0:T(8,128)(2,1)} %constant_dynamic-update-slice_fusion.refs_1_), channel_id=1, source_target_pairs={{0,8},{8,0},{16,24},{24,16},{1,9},{9,1},{17,25},{25,17},{2,10},{10... | collective-permute-start | bytes 3538952 | tf_op jit(solution)/shard_map/ppermute | solution.py:708
  61.1 29.9 %collective-permute-start.8 = (bf16[576,1024]{1,0:T(8,128)(2,1)}, bf16[576,1024]{1,0:T(8,128)(2,1)}, u32[]{:S(2)}, u32[]{:S(2)}) collective-permute-start(bf16[576,1024]{1,0:T(8,128)(2,1)} %constant_dynamic-update-slice_fusion.refs_1_), channel_id=1, source_target_pairs={{0,1},{1,0},{2,3},{3,2},{4,5},{5,4},{6,7},{7,6},{8,9},{9,8},{10,11... | collective-permute-start | bytes 3538952 | tf_op jit(solution)/shard_map/ppermute | solution.py:726
  61.1 60.3 %collective-permute-start.7 = (bf16[192,4096]{1,0:T(8,128)(2,1)S(1)}, bf16[192,4096]{1,0:T(8,128)(2,1)}, u32[]{:S(2)}, u32[]{:S(2)}) collective-permute-start(bf16[192,4096]{1,0:T(8,128)(2,1)S(1)} %copy-done.7), channel_id=1, source_target_pairs={{0,1},{1,0},{2,3},{3,2},{4,5},{5,4},{6,7},{7,6},{8,9},{9,8},{10,11... | collective-permute-start | bytes 4718600 | tf_op jit(solution)/shard_map/ppermute | solution.py:726
  91.0 32.8 %collective-permute-start.10 = (bf16[576,1024]{1,0:T(8,128)(2,1)S(1)}, bf16[576,1024]{1,0:T(8,128)(2,1)}, u32[]{:S(2)}, u32[]{:S(2)}) collective-permute-start(bf16[576,1024]{1,0:T(8,128)(2,1)S(1)} %collective-permute-done.4.refs_3_), channel_id=1, source_target_pairs={{0,1},{1,0},{2,3},{3,2},{4,5},{5,4},{6,7},{7,6},{8,9},{9,8},{10,11... | collective-permute-start | bytes 3538952 | tf_op jit(solution)/shard_map/ppermute | solution.py:726
  91.0 32.8 %collective-permute-start.9 = (bf16[576,1024]{1,0:T(8,128)(2,1)}, bf16[576,1024]{1,0:T(8,128)(2,1)}, u32[]{:S(2)}, u32[]{:S(2)}) collective-permute-start(bf16[576,1024]{1,0:T(8,128)(2,1)} %collective-permute-done.3.refs_2_), channel_id=1, source_target_pairs={{0,1},{1,0},{2,3},{3,2},{4,5},{5,4},{6,7},{7,6},{8,9},{9,8},{10,11... | collective-permute-start | bytes 3538952 | tf_op jit(solution)/shard_map/ppermute | solution.py:726
  121.4 103.1 %collective-permute-start.19 = (bf16[192,9216]{1,0:T(8,128)(2,1)}, bf16[192,9216]{1,0:T(8,128)(2,1)}, u32[]{:S(2)}, u32[]{:S(2)}) collective-permute-start(bf16[192,9216]{1,0:T(8,128)(2,1)} %refs_0_.5), channel_id=1, source_target_pairs={{0,1},{1,0},{2,3},{3,2},{4,5},{5,4},{6,7},{7,6},{8,9},{9,8},{10,11... | collective-permute-start | bytes 10616840 | tf_op jit(solution)/shard_map/ppermute | solution.py:726
  139.4 75.5 %collective-permute-start.16 = (bf16[576,2304]{1,0:T(8,128)(2,1)}, bf16[576,2304]{1,0:T(8,128)(2,1)}, u32[]{:S(2)}, u32[]{:S(2)}) collective-permute-start(bf16[576,2304]{1,0:T(8,128)(2,1)} %pad_maximum_fusion.3.refs_1_), channel_id=1, source_target_pairs={{0,16},{8,24},{16,0},{24,8},{1,17},{9,25},{17,1},{25,9},{2,18},{10... | collective-permute-start | bytes 7962632 | tf_op jit(solution)/shard_map/ppermute | solution.py:709
  140.3 77.2 %collective-permute-start.15 = (bf16[576,2304]{1,0:T(8,128)(2,1)}, bf16[576,2304]{1,0:T(8,128)(2,1)}, u32[]{:S(2)}, u32[]{:S(2)}) collective-permute-start(bf16[576,2304]{1,0:T(8,128)(2,1)} %pad_maximum_fusion.3.refs_1_), channel_id=1, source_target_pairs={{0,8},{8,0},{16,24},{24,16},{1,9},{9,1},{17,25},{25,17},{2,10},{10... | collective-permute-start | bytes 7962632 | tf_op jit(solution)/shard_map/ppermute | solution.py:708
  220.0 37.7 %collective-permute-start.18 = (bf16[288,2304]{1,0:T(8,128)(2,1)}, bf16[288,2304]{1,0:T(8,128)(2,1)S(1)}, u32[]{:S(2)}, u32[]{:S(2)}) collective-permute-start(bf16[288,2304]{1,0:T(8,128)(2,1)} %slice.408), channel_id=1, source_target_pairs={{0,16},{8,24},{16,0},{24,8},{1,17},{9,25},{17,1},{25,9},{2,18},{10... | collective-permute-start | bytes 3981320 | tf_op jit(solution)/shard_map/ppermute | solution.py:724
  222.9 41.9 %collective-permute-start.17 = (bf16[288,2304]{1,0:T(8,128)(2,1)}, bf16[288,2304]{1,0:T(8,128)(2,1)S(1)}, u32[]{:S(2)}, u32[]{:S(2)}) collective-permute-start(bf16[288,2304]{1,0:T(8,128)(2,1)} %slice.407), channel_id=1, source_target_pairs={{0,8},{8,0},{16,24},{24,16},{1,9},{9,1},{17,25},{25,17},{2,10},{10... | collective-permute-start | bytes 3981320 | tf_op jit(solution)/shard_map/ppermute | solution.py:723
  223.7 60.3 %collective-permute-start.20 = (bf16[576,2304]{1,0:T(8,128)(2,1)}, bf16[576,2304]{1,0:T(8,128)(2,1)}, u32[]{:S(2)}, u32[]{:S(2)}) collective-permute-start(bf16[576,2304]{1,0:T(8,128)(2,1)} %pad_maximum_fusion.3.refs_1_), channel_id=1, source_target_pairs={{0,1},{1,0},{2,3},{3,2},{4,5},{5,4},{6,7},{7,6},{8,9},{9,8},{10,11... | collective-permute-start | bytes 7962632 | tf_op jit(solution)/shard_map/ppermute | solution.py:726
  224.5 59.6 %collective-permute-start.22 = (bf16[576,2304]{1,0:T(8,128)(2,1)}, bf16[576,2304]{1,0:T(8,128)(2,1)}, u32[]{:S(2)}, u32[]{:S(2)}) collective-permute-start(bf16[576,2304]{1,0:T(8,128)(2,1)} %collective-permute-done.16.refs_3_), channel_id=1, source_target_pairs={{0,1},{1,0},{2,3},{3,2},{4,5},{5,4},{6,7},{7,6},{8,9},{9,8},{10,11... | collective-permute-start | bytes 7962632 | tf_op jit(solution)/shard_map/ppermute | solution.py:726
  224.6 59.6 %collective-permute-start.21 = (bf16[576,2304]{1,0:T(8,128)(2,1)}, bf16[576,2304]{1,0:T(8,128)(2,1)}, u32[]{:S(2)}, u32[]{:S(2)}) collective-permute-start(bf16[576,2304]{1,0:T(8,128)(2,1)} %collective-permute-done.15.refs_2_), channel_id=1, source_target_pairs={{0,1},{1,0},{2,3},{3,2},{4,5},{5,4},{6,7},{7,6},{8,9},{9,8},{10,11... | collective-permute-start | bytes 7962632 | tf_op jit(solution)/shard_map/ppermute | solution.py:726
  257.7 26.4 %collective-permute-start.24 = (bf16[288,2304]{1,0:T(8,128)(2,1)S(1)}, bf16[288,2304]{1,0:T(8,128)(2,1)}, u32[]{:S(2)}, u32[]{:S(2)}) collective-permute-start(bf16[288,2304]{1,0:T(8,128)(2,1)S(1)} %collective-permute-done.18.refs_5_), channel_id=1, source_target_pairs={{0,1},{1,0},{2,3},{3,2},{4,5},{5,4},{6,7},{7,6},{8,9},{9,8},{10,11... | collective-permute-start | bytes 3981320 | tf_op jit(solution)/shard_map/ppermute | solution.py:726
  355.3 257.3 %all-gather.23.cloned.1.call-start = ((), (), s32[]{:S(2)}) async-start(), calls=%async_computation.7 | async-start | bytes 2211840 | tf_op jit(solution)/shard_map/all_gather | solution.py:1054
  400.8 211.8 %collective-permute-start.30 = (bf16[768,2304]{1,0:T(8,128)(2,1)}, bf16[768,2304]{1,0:T(8,128)(2,1)}, u32[]{:S(2)}, u32[]{:S(2)}) collective-permute-start(bf16[768,2304]{1,0:T(8,128)(2,1)} %convolution_convert_fusion.1), channel_id=1, source_target_pairs={{0,1},{1,0},{2,3},{3,2},{4,5},{5,4},{6,7},{7,6},{8,9},{9,8},{10,11... | collective-permute-start | bytes 10616840 | tf_op jit(solution)/shard_map/ppermute | solution.py:831
  407.9 91.9 %collective-permute-start.29 = (bf16[768,2304]{1,0:T(8,128)(2,1)}, bf16[768,2304]{1,0:T(8,128)(2,1)}, u32[]{:S(2)}, u32[]{:S(2)}) collective-permute-start(bf16[768,2304]{1,0:T(8,128)(2,1)} %convolution_convert_fusion.2), channel_id=1, source_target_pairs={{0,1},{1,0},{2,3},{3,2},{4,5},{5,4},{6,7},{7,6},{8,9},{9,8},{10,11... | collective-permute-start | bytes 10616840 | tf_op jit(solution)/shard_map/ppermute | solution.py:831
  413.8 75.2 %collective-permute-start.26 = (bf16[768,2304]{1,0:T(8,128)(2,1)}, bf16[768,2304]{1,0:T(8,128)(2,1)}, u32[]{:S(2)}, u32[]{:S(2)}) collective-permute-start(bf16[768,2304]{1,0:T(8,128)(2,1)} %convolution_convert_fusion.3), channel_id=1, source_target_pairs={{0,1},{1,0},{2,3},{3,2},{4,5},{5,4},{6,7},{7,6},{8,9},{9,8},{10,11... | collective-permute-start | bytes 10616840 | tf_op jit(solution)/shard_map/ppermute | solution.py:831
  418.9 60.1 %collective-permute-start.27 = (bf16[384,2304]{1,0:T(8,128)(2,1)}, bf16[384,2304]{1,0:T(8,128)(2,1)}, u32[]{:S(2)}, u32[]{:S(2)}) collective-permute-start(bf16[384,2304]{1,0:T(8,128)(2,1)} %fusion.43), channel_id=1, source_target_pairs={{0,8},{8,0},{16,24},{24,16},{1,9},{9,1},{17,25},{25,17},{2,10},{10... | collective-permute-start | bytes 5308424 | tf_op jit(solution)/shard_map/ppermute | solution.py:837
  424.0 65.0 %collective-permute-start.28 = (bf16[384,2304]{1,0:T(8,128)(2,1)}, bf16[384,2304]{1,0:T(8,128)(2,1)}, u32[]{:S(2)}, u32[]{:S(2)}) collective-permute-start(bf16[384,2304]{1,0:T(8,128)(2,1)} %fusion.40), channel_id=1, source_target_pairs={{0,16},{8,24},{16,0},{24,8},{1,17},{9,25},{17,1},{25,9},{2,18},{10... | collective-permute-start | bytes 5308424 | tf_op jit(solution)/shard_map/ppermute | solution.py:838
  498.1 110.3 %collective-permute-start.31 = (bf16[768,2304]{1,0:T(8,128)(2,1)}, bf16[768,2304]{1,0:T(8,128)(2,1)}, u32[]{:S(2)}, u32[]{:S(2)}) collective-permute-start(bf16[768,2304]{1,0:T(8,128)(2,1)} %add_convert_fusion.2), channel_id=1, source_target_pairs={{0,8},{8,0},{16,24},{24,16},{1,9},{9,1},{17,25},{25,17},{2,10},{10... | collective-permute-start | bytes 10616840 | tf_op jit(solution)/shard_map/ppermute | solution.py:858
  509.6 102.5 %collective-permute-start.32 = (bf16[768,2304]{1,0:T(8,128)(2,1)}, bf16[768,2304]{1,0:T(8,128)(2,1)}, u32[]{:S(2)}, u32[]{:S(2)}) collective-permute-start(bf16[768,2304]{1,0:T(8,128)(2,1)} %add_convert_fusion.1), channel_id=1, source_target_pairs={{0,16},{8,24},{16,0},{24,8},{1,17},{9,25},{17,1},{25,9},{2,18},{10... | collective-permute-start | bytes 10616840 | tf_op jit(solution)/shard_map/ppermute | solution.py:859
  558.7 199.1 %reduce-scatter.8.cloned.1.call-start = ((), (), s32[]{:S(2)}) async-start(), calls=%async_computation.9 | async-start | bytes 4423680 | tf_op jit(solution)/shard_map/reduce_scatter | solution.py:888
  573.9 25.5 %collective-permute-start.34 = (bf16[768,2048]{1,0:T(8,128)(2,1)}, bf16[768,2048]{1,0:T(8,128)(2,1)}, u32[]{:S(2)}, u32[]{:S(2)}) collective-permute-start(bf16[768,2048]{1,0:T(8,128)(2,1)} %convolution_convert_fusion.7), channel_id=1, source_target_pairs={{0,1},{1,0},{2,3},{3,2},{4,5},{5,4},{6,7},{7,6},{8,9},{9,8},{10,11... | collective-permute-start | bytes 9437192 | tf_op jit(solution)/shard_map/ppermute | solution.py:827
  598.8 72.0 %collective-permute-start.37 = (bf16[512,384]{1,0:T(8,128)(2,1)}, bf16[512,384]{1,0:T(8,128)(2,1)}, u32[]{:S(2)}, u32[]{:S(2)}) collective-permute-start(bf16[512,384]{1,0:T(8,128)(2,1)} %get-tuple-element.192), channel_id=1, source_target_pairs={{0,16},{8,24},{16,0},{24,8},{1,17},{9,25},{17,1},{25,9},{2,18},{10... | collective-permute-start | bytes 1179656 | tf_op jit(solution)/shard_map/ppermute | solution.py:838
  599.3 71.4 %collective-permute-start.36 = (bf16[512,384]{1,0:T(8,128)(2,1)S(1)}, bf16[512,384]{1,0:T(8,128)(2,1)}, u32[]{:S(2)}, u32[]{:S(2)}) collective-permute-start(bf16[512,384]{1,0:T(8,128)(2,1)S(1)} %get-tuple-element.193), channel_id=1, source_target_pairs={{0,8},{8,0},{16,24},{24,16},{1,9},{9,1},{17,25},{25,17},{2,10},{10... | collective-permute-start | bytes 1179656 | tf_op jit(solution)/shard_map/ppermute | solution.py:837
  608.4 64.4 %collective-permute-start.39 = (bf16[384,512]{1,0:T(8,128)(2,1)S(1)}, bf16[384,512]{1,0:T(8,128)(2,1)S(1)}, u32[]{:S(2)}, u32[]{:S(2)}) collective-permute-start(bf16[384,512]{1,0:T(8,128)(2,1)S(1)} %get-tuple-element.190), channel_id=1, source_target_pairs={{0,16},{8,24},{16,0},{24,8},{1,17},{9,25},{17,1},{25,9},{2,18},{10... | collective-permute-start | bytes 1179656 | tf_op jit(solution)/shard_map/ppermute | solution.py:838
  612.1 60.8 %collective-permute-start.38 = (bf16[384,512]{1,0:T(8,128)(2,1)S(1)}, bf16[384,512]{1,0:T(8,128)(2,1)}, u32[]{:S(2)}, u32[]{:S(2)}) collective-permute-start(bf16[384,512]{1,0:T(8,128)(2,1)S(1)} %get-tuple-element.191), channel_id=1, source_target_pairs={{0,8},{8,0},{16,24},{24,16},{1,9},{9,1},{17,25},{25,17},{2,10},{10... | collective-permute-start | bytes 1179656 | tf_op jit(solution)/shard_map/ppermute | solution.py:837
  623.8 155.9 %reduce-scatter.6.cloned.1.call-start = ((), (), s32[]{:S(2)}) async-start(), calls=%async_computation.8 | async-start | bytes 1216512 | tf_op jit(solution)/shard_map/reduce_scatter | solution.py:1114
  701.4 49.6 %collective-permute-start.51 = (bf16[1024,384]{1,0:T(8,128)(2,1)}, bf16[1024,384]{1,0:T(8,128)(2,1)}, u32[]{:S(2)}, u32[]{:S(2)}) collective-permute-start(bf16[1024,384]{1,0:T(8,128)(2,1)} %get-tuple-element.188), channel_id=1, source_target_pairs={{0,16},{8,24},{16,0},{24,8},{1,17},{9,25},{17,1},{25,9},{2,18},{10... | collective-permute-start | bytes 2359304 | tf_op jit(solution)/shard_map/ppermute | solution.py:859
  703.0 47.9 %collective-permute-start.50 = (bf16[1024,384]{1,0:T(8,128)(2,1)}, bf16[1024,384]{1,0:T(8,128)(2,1)}, u32[]{:S(2)}, u32[]{:S(2)}) collective-permute-start(bf16[1024,384]{1,0:T(8,128)(2,1)} %get-tuple-element.189), channel_id=1, source_target_pairs={{0,8},{8,0},{16,24},{24,16},{1,9},{9,1},{17,25},{25,17},{2,10},{10... | collective-permute-start | bytes 2359304 | tf_op jit(solution)/shard_map/ppermute | solution.py:858
  708.5 142.7 %all-gather.27.cloned.1.call-start = ((), (), s32[]{:S(2)}) async-start(), calls=%async_computation.11 | async-start | bytes 4423680 | tf_op jit(solution)/shard_map/all_gather | solution.py:907
  749.5 44.3 %collective-permute-start.44 = (bf16[768,512]{1,0:T(8,128)(2,1)}, bf16[768,512]{1,0:T(8,128)(2,1)S(1)}, u32[]{:S(2)}, u32[]{:S(2)}) collective-permute-start(bf16[768,512]{1,0:T(8,128)(2,1)} %get-tuple-element.182), channel_id=1, source_target_pairs={{0,16},{8,24},{16,0},{24,8},{1,17},{9,25},{17,1},{25,9},{2,18},{10... | collective-permute-start | bytes 2359304 | tf_op jit(solution)/shard_map/ppermute | solution.py:859
  749.9 43.9 %collective-permute-start.43 = (bf16[768,512]{1,0:T(8,128)(2,1)}, bf16[768,512]{1,0:T(8,128)(2,1)}, u32[]{:S(2)}, u32[]{:S(2)}) collective-permute-start(bf16[768,512]{1,0:T(8,128)(2,1)} %get-tuple-element.183), channel_id=1, source_target_pairs={{0,8},{8,0},{16,24},{24,16},{1,9},{9,1},{17,25},{25,17},{2,10},{10... | collective-permute-start | bytes 2359304 | tf_op jit(solution)/shard_map/ppermute | solution.py:858
  753.7 45.2 %collective-permute-start.52 = (bf16[256,384]{1,0:T(8,128)(2,1)}, bf16[256,384]{1,0:T(8,128)(2,1)S(1)}, u32[]{:S(2)}, u32[]{:S(2)}) collective-permute-start(bf16[256,384]{1,0:T(8,128)(2,1)} %get-tuple-element.201), channel_id=1, source_target_pairs={{0,2},{1,3},{2,4},{3,5},{4,6},{5,7},{6,0},{7,1},{8,10},{9,11},{10,... | collective-permute-start | bytes 589832 | tf_op jit(solution)/shard_map/ppermute | solution.py:877
  755.4 54.7 %collective-permute-start.54 = (bf16[256,384]{1,0:T(8,128)(2,1)}, bf16[256,384]{1,0:T(8,128)(2,1)}, u32[]{:S(2)}, u32[]{:S(2)}) collective-permute-start(bf16[256,384]{1,0:T(8,128)(2,1)} %get-tuple-element.202), channel_id=1, source_target_pairs={{0,6},{1,7},{2,0},{3,1},{4,2},{5,3},{6,4},{7,5},{8,14},{9,15},{10,... | collective-permute-start | bytes 589832 | tf_op jit(solution)/shard_map/ppermute | solution.py:877
  755.7 54.5 %collective-permute-start.53 = (bf16[256,384]{1,0:T(8,128)(2,1)}, bf16[256,384]{1,0:T(8,128)(2,1)}, u32[]{:S(2)}, u32[]{:S(2)}) collective-permute-start(bf16[256,384]{1,0:T(8,128)(2,1)} %get-tuple-element.203), channel_id=1, source_target_pairs={{0,4},{1,5},{2,6},{3,7},{4,0},{5,1},{6,2},{7,3},{8,12},{9,13},{10,... | collective-permute-start | bytes 589832 | tf_op jit(solution)/shard_map/ppermute | solution.py:877
  796.9 26.9 %collective-permute-start.47 = (bf16[192,1024]{1,0:T(8,128)(2,1)}, bf16[192,1024]{1,0:T(8,128)(2,1)}, u32[]{:S(2)}, u32[]{:S(2)}) collective-permute-start(bf16[192,1024]{1,0:T(8,128)(2,1)} %get-tuple-element.198), channel_id=1, source_target_pairs={{0,2},{1,3},{2,4},{3,5},{4,6},{5,7},{6,0},{7,1},{8,10},{9,11},{10,... | collective-permute-start | bytes 1179656 | tf_op jit(solution)/shard_map/ppermute | solution.py:877
  796.9 26.9 %collective-permute-start.49 = (bf16[192,1024]{1,0:T(8,128)(2,1)}, bf16[192,1024]{1,0:T(8,128)(2,1)}, u32[]{:S(2)}, u32[]{:S(2)}) collective-permute-start(bf16[192,1024]{1,0:T(8,128)(2,1)} %get-tuple-element.199), channel_id=1, source_target_pairs={{0,6},{1,7},{2,0},{3,1},{4,2},{5,3},{6,4},{7,5},{8,14},{9,15},{10,... | collective-permute-start | bytes 1179656 | tf_op jit(solution)/shard_map/ppermute | solution.py:877
  798.9 24.9 %collective-permute-start.48 = (bf16[192,1024]{1,0:T(8,128)(2,1)S(1)}, bf16[192,1024]{1,0:T(8,128)(2,1)}, u32[]{:S(2)}, u32[]{:S(2)}) collective-permute-start(bf16[192,1024]{1,0:T(8,128)(2,1)S(1)} %get-tuple-element.200), channel_id=1, source_target_pairs={{0,4},{1,5},{2,6},{3,7},{4,0},{5,1},{6,2},{7,3},{8,12},{9,13},{10,... | collective-permute-start | bytes 1179656 | tf_op jit(solution)/shard_map/ppermute | solution.py:877
  (85 other events, 1318.8 us)
Sparse Core Ops, SparseCore 0:
  9.6 38.9 all-gather.16
  56.5 72.0 all-gather.24
  131.5 85.6 all-gather.18
  220.0 110.4 all-gather.20
  355.4 203.2 reduce-scatter.3
  560.3 46.8 all-gather.22
  623.9 67.3 reduce-scatter.7
  708.6 26.7 reduce-scatter.5
  758.0 49.5 all-gather.26

commit v13 on v11

--- a/solution.py
+++ b/solution.py
@@ -176,7 +176,7 @@
     local_ref, prod_ref, carry_ref, state_ref, before_ref, c_ref, u_ref, halo_ref, dist_ref,
     gates_ref, taps_ref, soft_ref,
     du_ref, tail_ref, edge_ref, ggate_ref, gtaps_ref, gdecay_ref,
-    q_s, dq_s, dc_s, h_s, ext_s, dist_s,
+    q_s, dq_s, dc_s, h_s, ext_s, dist_s, last_s,
 ):
     seqs, rows, _ = local_ref.shape
     soft = soft_ref[...]
@@ -209,7 +209,7 @@
             dc_s[at, :] = lam_root * inp
             return total + fold(rated)
 
-        decay_sum = lax.fori_loop(0, rows // 32, point, decay_sum, unroll=2)
+        decay_sum = lax.fori_loop(0, rows // 32, point, decay_sum, unroll=4)
         dc_s[pl.ds(0, rows), :] += lax.dot_general(
             dq_s[...], gates_ref[0], (((1,), (1,)), ((), ())), preferred_element_type=F32
         )
@@ -236,14 +236,11 @@
                 value = taps_ref[k : k + 1, :] * dc_s[ahead, :]
                 out = out + jnp.where(dist_s[ahead, :] >= float(k), value, 0.0)
             du_ref[b, pl.ds(at, 64), :] = out.astype(BF16)
-
-            @pl.when(n == rows // 64 - 1)
-            def _():
-                tail_ref[b] = out[64 - TAIL :, :]
-
+            last_s[...] = out[64 - TAIL :, :]
             return tuple(totals)
 
-        taps_sum = list(lax.fori_loop(0, rows // 64, conv_chunk, tuple(taps_sum)))
+        taps_sum = list(lax.fori_loop(0, rows // 64, conv_chunk, tuple(taps_sum), unroll=2))
+        tail_ref[b] = last_s[...]
         edges = [jnp.zeros((HALO - CONV + 1, HS), F32)]
         for m in range(CONV - 1, 0, -1):
             edge = jnp.zeros((1, HS), F32)
@@ -292,8 +289,8 @@
 
 
 def ffn_backward_kernel(grad_ref, down_ref, pull_ref, out_ref):
-    for m in range(0, grad_ref.shape[0], 256):
-        at = pl.ds(m, 256)
+    for m in range(0, grad_ref.shape[0], 512):
+        at = pl.ds(m, 512)
         dv = lax.dot_general(
             grad_ref[at, :], down_ref[...], (((1,), (1,)), ((), ())), preferred_element_type=F32
         )
@@ -439,6 +436,7 @@
             pltpu.VMEM((rows + 8, HS), F32),
             pltpu.VMEM((rows + BACK, HS), F32),
             pltpu.VMEM((rows + BACK, HS), F32),
+            pltpu.VMEM((TAIL, HS), F32),
         ],
         compiler_params=PARAMS,
         name="mixer_backward",
@@ -473,7 +471,7 @@
     )(core.reshape(1), x, gain.reshape(1, D))
 
 
-FF_TILE = 512
+FF_TILE = 768
 GATHER_TILE = 768
 DOT_TILE = 512
 

time: 873 us -> 869 us (level)
  transfers between devices with their start and end apart: 64 -> 64, of which waited for: 12 -> 12; matrix products, arithmetic and copies ran while one was open for 39% -> 40% of each run, Pallas kernels for 24% -> 24%
where the time goes in v13:
time: 869 us; the launch traced here: 860 us
  matrix products  244 us (28%)
  Pallas kernels  205 us (24%)
  waiting for transfers between devices  117 us (13%)
  local copies, waits for them, and re-layouts  99.2 us (11%)
  blocking collectives  88.1 us (10%)
  starting transfers between devices  49.7 us (6%)
  other arithmetic  41.1 us (5%)
  between operations  15.6 us (2%)
    dot_general x16, matrix products, dot_rows(): lax.dot_general(a, b, (((0,), (0,)), ((), ())), preferred_element_type=F32)  136 us
    dot_general x5, matrix products, dot_far(): lax.dot_general(a, b, (((1,), (1,)), ((), ())), preferred_element_type=F32)  76.5 us
    pallas_call x3, Pallas kernels, call(): pl.pallas_call(kernel, grid=(steps,), in_specs=[pl.BlockSpec(memory_space...  66.1 us
    unnamed x199, local copies, waits for them, and re-layouts  44.3 us
    pallas_call x1, Pallas kernels, mixer_backward(): pl.pallas_call(mixer_backward_kernel, grid=(HEADS,), in_specs=[full, full...  42.7 us
    ppermute x2, waiting for transfers between devices, first(): self.from_y = lax.ppermute(self.near, 'grp', xor_pairs('grp', 2))  35.4 us
    ppermute x3, waiting for transfers between devices, __init__(): lax.ppermute(own, 'seq', ring_pairs(-2 * j))  35 us
    pallas_call x1, Pallas kernels, mixer_forward(): pl.pallas_call(mixer_forward_kernel, grid=(HEADS,), in_specs=[full, head_...  27.1 us
  transfers between devices with their start and end apart: 64, of which 12 were waited for; matrix products, arithmetic and copies ran while one was open for 40% of the time, Pallas kernels for 24%

profile of v13, /device:TPU:18, one launch (start us, length us, event | category | flops | bytes accessed | tf_op | source)
XLA Modules:
  0.0 860.4 jit_solution(18179991485979957186)
XLA Ops:
  16.1 7.5 collective-permute-done
  25.3 27.5 %collective-permute-done.1 = bf16[192,1024]{1,0:T(8,128)(2,1)} collective-permute-done((bf16[192,1024]{1,0:T(8,128)(2,1)}, bf16[192,1024]{1,0:T(8,128)(2,1)}, u32[]{:S(2)}, u32[]{:S(2)}) %collective-permute-start.1) | collective-permute-done | bytes 393248 | tf_op jit(solution)/shard_map/ppermute | solution.py:673
  61.6 24.6 %collective-permute-done.4.refs_3_ = bf16[576,1024]{1,0:T(8,128)(2,1)} collective-permute-done((bf16[576,1024]{1,0:T(8,128)(2,1)}, bf16[576,1024]{1,0:T(8,128)(2,1)}, u32[]{:S(2)}, u32[]{:S(2)}) %collective-permute-start.4) | collective-permute-done | bytes 1179680 | tf_op jit(solution)/shard_map/ppermute | solution.py:689
  92.0 15.3 %all-gather.9 = bf16[8,1,1664]{2,1,0:T(2,128)(2,1)S(1)} all-gather(bf16[1,1,1664]{2,1,0:T(2,128)(2,1)S(1)} %reshape.2479), channel_id=2, replica_groups=mesh['grp'=4,'seq'=8] {'seq'}, dimensions={0}, use_global_device_ids=true | all-gather | bytes 29952 | tf_op jit(solution)/shard_map/all_gather | solution.py:945
  108.7 5.3 copy.292
  124.8 11.9 %gathered_dot.2 = (bf16[1024,2048]{1,0:T(8,128)(2,1)}, bf16[1536,2048]{1,0:T(8,128)(2,1)}) custom-call(s32[3]{0:T(128)} %pad_add_fusion.1.where_ref, bf16[1024,1536]{1,0:T(8,128)(2,1)} %copy-done.9, bf16[192,4096]{1,0:T(8,128)(2,1)} %refs_0_.4, bf16[576,1024]{1,0:T(8,128)(2,1)} %constant_dynamic-update-slice_fusion.refs_1_, ...), custom_call_target="tpu_custom_call" | custom-call | tf_op jit(solution)/shard_map/gathered_dot/pallas_call | solution.py:714
  147.7 13.1 %gathered_dot.3 = (f32[1024,2048]{1,0:T(8,128)}, bf16[1536,2048]{1,0:T(8,128)(2,1)}) custom-call(s32[3]{0:T(128)} %pad_add_fusion.1.where_ref, bf16[1024,1536]{1,0:T(8,128)(2,1)} %copy-done.9, bf16[192,4096]{1,0:T(8,128)(2,1)} %refs_0_.4, bf16[576,1024]{1,0:T(8,128)(2,1)} %constant_dynamic-update-slice_fusion.refs_1_, ...), custom_call_target="tpu_custom_call" | custom-call | tf_op jit(solution)/shard_map/gathered_dot/pallas_call | solution.py:714
  161.1 27.1 %mixer_forward.1 = (bf16[2,512,2048]{2,1,0:T(8,128)(2,1)S(1)}, f32[2,512,2048]{2,1,0:T(8,128)}, f32[2,512,2048]{2,1,0:T(8,128)}, f32[2,512,2048]{2,1,0:T(8,128)}, f32[2,2,8,2048]{3,2,1,0:T(8,128)S(1)}) custom-call(bf16[2,512,2048]{2,1,0:T(8,128)(2,1)S(1)} %bitcast.780, bf16[2,8,2048]{2,1,0:T(8,128)(2,1)S(1)} %collective-permute-done.13.halo_ref, ...), custom_call_target="tpu_custom_call" | custom-call | tf_op jit(solution)/shard_map/mixer_forward/pallas_call | solution.py:320
  190.7 13.2 %all-gather.2 = f32[16,2,2048]{2,1,0:T(2,128)S(1)} all-gather(f32[2,2,2048]{2,1,0:T(2,128)S(1)} %copy.311), channel_id=4, replica_groups=mesh['grp'=4,'seq'=8] {'seq'}, dimensions={0}, use_global_device_ids=true | all-gather | bytes 294912 | tf_op jit(solution)/shard_map/all_gather | solution.py:894
  204.5 10.8 %collective-permute-done.16.refs_3_ = bf16[576,2304]{1,0:T(8,128)(2,1)} collective-permute-done((bf16[576,2304]{1,0:T(8,128)(2,1)}, bf16[576,2304]{1,0:T(8,128)(2,1)}, u32[]{:S(2)}, u32[]{:S(2)}) %collective-permute-start.16) | collective-permute-done | bytes 2654240 | tf_op jit(solution)/shard_map/ppermute | solution.py:689
  225.2 5.3 copy.326
  230.5 17.7 %mixer_branch.1 = (f32[2,512,2048]{2,1,0:T(8,128)}, bf16[2,512,2048]{2,1,0:T(8,128)(2,1)S(1)}, bf16[2,2,512,1024]{3,2,1,0:T(8,128)(2,1)S(1)}) custom-call(s32[1]{0:T(128)} %bitcast.3.core_ref, f32[2,512,2048]{2,1,0:T(8,128)} %get-tuple-element.88.state_ref, f32[2,512,2048]{2,1,0:T(8,128)} %get-tuple-element.89.prod_ref, ...), custom_call_target="tpu_custom_call" | custom-call | tf_op jit(solution)/shard_map/mixer_branch/pallas_call | solution.py:362
  252.1 6.4 collective-permute-done.18.refs_5_
  258.6 5.4 collective-permute-done.17.refs_4_
  263.9 10.5 %convert_add_fusion.x_ref = f32[1024,1536]{1,0:T(8,128)S(1)} fusion(bf16[1024,1536]{1,0:T(8,128)(2,1)} %bitcast.774, bf16[1024,2048]{1,0:T(8,128)(2,1)} %bitcast.787, bf16[2048,1536]{1,0:T(8,128)(2,1)} %all-gather.19.cloned.1.call-done), kind=kOutput, calls=%fused_computation.3 | convolution fusion | flops 6445596672 | bytes 19922944 | tf_op jit(solution)/shard_map/dot_general | solution.py:997
  281.7 41.0 %gathered_ffn.1 = (bf16[1024,4608]{1,0:T(8,128)(2,1)}, bf16[2,1024,4608]{2,1,0:T(8,128)(2,1)}, bf16[1536,4608]{1,0:T(8,128)(2,1)}, bf16[1536,4608]{1,0:T(8,128)(2,1)}) custom-call(s32[3]{0:T(128)} %pad_add_fusion.1.where_ref, bf16[1024,1536]{1,0:T(8,128)(2,1)} %copy-done.23, bf16[192,9216]{1,0:T(8,128)(2,1)} %refs_0_.5, ...), custom_call_target="tpu_custom_call" | custom-call | tf_op jit(solution)/shard_map/gathered_ffn/pallas_call | solution.py:714
  322.8 32.1 %convolution_convert_fusion = bf16[4608,1536]{1,0:T(8,128)(2,1)} fusion(bf16[1024,4608]{1,0:T(8,128)(2,1)} %get-tuple-element.134, bf16[1024,1536]{1,0:T(8,128)(2,1)S(1)} %bitcast.776), kind=kOutput, calls=%fused_computation | convolution fusion | flops 14502592512 | bytes 26738688 | tf_op jit(solution)/shard_map/dot_general | solution.py:546
  356.9 25.4 %ffn_backward.1 = bf16[2,1024,4608]{2,1,0:T(8,128)(2,1)} custom-call(bf16[1024,1536]{1,0:T(8,128)(2,1)S(1)} %bitcast.777, bf16[4608,1536]{1,0:T(8,128)(2,1)} %all-gather.21.cloned.1.call-done.down_ref, bf16[2,1024,4608]{2,1,0:T(8,128)(2,1)} %get-tuple-element.96.pull_ref), custom_call_target="tpu_custom_call" | custom-call | tf_op jit(solution)/shard_map/ffn_backward/pallas_call | solution.py:505
  382.3 8.0 convolution_convert_fusion.4
  391.2 5.0 fusion.187
  396.6 8.0 convolution_convert_fusion.1
  406.9 5.3 convolution_convert_fusion.2
  412.2 5.6 convolution_convert_fusion.3
  418.4 4.8 fusion.43
  429.4 21.9 %fusion = f32[1024,1536]{1,0:T(8,128)} fusion(bf16[1536,4608]{1,0:T(8,128)(2,1)} %get-tuple-element.101, bf16[2,1024,4608]{2,1,0:T(8,128)(2,1)} %ffn_backward.1), kind=kOutput, calls=%fused_computation.4 | convolution fusion | flops 14495514624 | bytes 29884416 | tf_op jit(solution)/shard_map/dot_general | solution.py:556
  451.3 21.0 %fusion.25 = f32[1024,1536]{1,0:T(8,128)S(1)} fusion(f32[1024,1536]{1,0:T(8,128)} %fusion, bf16[1536,4608]{1,0:T(8,128)(2,1)} %get-tuple-element.100, bf16[2,1024,4608]{2,1,0:T(8,128)(2,1)} %ffn_backward.1), kind=kOutput, calls=%fused_computation.44 | convolution fusion | flops 14497087488 | bytes 36175872 | tf_op jit(solution)/shard_map/dot_general | solution.py:556
  472.3 14.5 %collective-permute-done.27 = bf16[384,2304]{1,0:T(8,128)(2,1)} collective-permute-done((bf16[384,2304]{1,0:T(8,128)(2,1)}, bf16[384,2304]{1,0:T(8,128)(2,1)}, u32[]{:S(2)}, u32[]{:S(2)}) %collective-permute-start.27) | collective-permute-done | bytes 1769504 | tf_op jit(solution)/shard_map/ppermute | solution.py:817
  488.1 9.2 %add_convert_fusion.2 = bf16[768,2304]{1,0:T(8,128)(2,1)} fusion(bf16[768,2304]{1,0:T(8,128)(2,1)} %collective-permute-done.26, bf16[1024,768]{1,0:T(8,128)(2,1)S(1)} %get-tuple-element.97, bf16[2,1024,4608]{2,1,0:T(8,128)(2,1)} %ffn_backward.1, s32[]{:T(128)S(6)} %select_n.797, s32[]{:T(128)S(6)} %select_n.799, bf16[384,2304]{1,0:T(8,128)(2,1)} %collective-permute-done.28), kind=kOutput, calls=%fused_computation.14 | convolution fusion | flops 3632726016 | bytes 15138824 | tf_op jit(solution)/shard_map/dot_general | solution.py:546
  497.9 10.5 %add_convert_fusion.1 = bf16[768,2304]{1,0:T(8,128)(2,1)} fusion(bf16[768,2304]{1,0:T(8,128)(2,1)} %collective-permute-done.29, bf16[1024,768]{1,0:T(8,128)(2,1)S(1)} %get-tuple-element.97, bf16[2,1024,4608]{2,1,0:T(8,128)(2,1)} %ffn_backward.1, s32[]{:T(128)S(6)} %select_n.801, s32[]{:T(128)S(6)} %select_n.803, bf16[384,2304]{1,0:T(8,128)(2,1)} %collective-permute-done.27), kind=kOutput, calls=%fused_computation.13 | convolution fusion | flops 3632726016 | bytes 15138824 | tf_op jit(solution)/shard_map/dot_general | solution.py:546
  514.2 12.0 %fusion.194 = f32[1024,2048]{1,0:T(8,128)} fusion(bf16[1024,1536]{1,0:T(8,128)(2,1)S(1)} %get-tuple-element.112, bf16[2048,1536]{1,0:T(8,128)(2,1)} %all-gather.19.cloned.1.call-done), kind=kOutput, calls=%fused_computation.341 | convolution fusion | flops 6442450944 | bytes 17825792 | tf_op jit(solution)/shard_map/dot_general | solution.py:556
  526.2 22.0 %mixer_reverse.1 = (bf16[2,512,2048]{2,1,0:T(8,128)(2,1)S(1)}, f32[2,512,2048]{2,1,0:T(8,128)S(1)}, f32[2,512,2048]{2,1,0:T(8,128)}, f32[2,2,8,2048]{3,2,1,0:T(8,128)S(1)}) custom-call(f32[2,512,2048]{2,1,0:T(8,128)} %bitcast.795, f32[2,512,2048]{2,1,0:T(8,128)} %bitcast.789, f32[2,512,2048]{2,1,0:T(8,128)} %get-tuple-element.105.keep_ref, ...), custom_call_target="tpu_custom_call" | custom-call | tf_op jit(solution)/shard_map/mixer_reverse/pallas_call | solution.py:384
  558.2 5.7 convolution_convert_fusion.5
  565.3 5.3 convolution_convert_fusion.7
  571.1 12.5 %all-gather.3 = f32[16,2,2048]{2,1,0:T(2,128)S(1)} all-gather(f32[2,2,2048]{2,1,0:T(2,128)S(1)} %copy.343), channel_id=5, replica_groups=mesh['grp'=4,'seq'=8] {'seq'}, dimensions={0}, use_global_device_ids=true | all-gather | bytes 294912 | tf_op jit(solution)/shard_map/all_gather | solution.py:894
  584.2 7.1 add_convert_fusion.6
  596.5 5.8 add_convert_fusion.5
  609.5 11.2 %add_convert_fusion = bf16[768,2304]{1,0:T(8,128)(2,1)} fusion(bf16[768,2304]{1,0:T(8,128)(2,1)} %collective-permute-done.32, bf16[768,2304]{1,0:T(8,128)(2,1)} %collective-permute-done.31, bf16[768,2304]{1,0:T(8,128)(2,1)} %collective-permute-done.30, bf16[1024,768]{1,0:T(8,128)(2,1)S(1)} %get-tuple-element.97, bf16[2,1024,4608]{2,1,0:T(8,128)(2,1)} %ffn_backward.1, ...), kind=kOutput, calls=%fused_computation.12 | convolution fusion | flops 3636264960 | bytes 20447240 | tf_op jit(solution)/shard_map/dot_general | solution.py:546
  624.1 42.7 %mixer_backward.1 = (bf16[2,512,2048]{2,1,0:T(8,128)(2,1)S(1)}, f32[2,32,2048]{2,1,0:T(8,128)S(1)}, f32[2,8,2048]{2,1,0:T(8,128)S(1)}, f32[16,128,256]{2,1,0:T(8...) custom-call(f32[2,512,2048]{2,1,0:T(8,128)} %copy-done.10, f32[2,512,2048]{2,1,0:T(8,128)} %get-tuple-element.118.prod_ref, ...), custom_call_target="tpu_custom_call" | custom-call | tf_op jit(solution)/shard_map/mixer_backward/pallas_call | solution.py:406
  674.3 10.9 %fusion.195 = f32[1024,1536]{1,0:T(8,128)} fusion(bf16[1024,2048]{1,0:T(8,128)(2,1)S(1)} %bitcast.782, bf16[1536,2048]{1,0:T(8,128)(2,1)} %get-tuple-element.128), kind=kOutput, calls=%fused_computation.342 | convolution fusion | flops 6442450944 | bytes 16777216 | tf_op jit(solution)/shard_map/dot_general | solution.py:556
  688.2 5.3 convolution_convert_fusion.6
  703.9 10.8 %collective-permute-done.46 = bf16[768,512]{1,0:T(8,128)(2,1)} collective-permute-done((bf16[768,512]{1,0:T(8,128)(2,1)}, bf16[768,512]{1,0:T(8,128)(2,1)}, u32[]{:S(2)}, u32[]{:S(2)}) %collective-permute-start.46) | collective-permute-done | bytes 786464 | tf_op jit(solution)/shard_map/ppermute | solution.py:839
  717.4 6.8 add_convert_fusion.4
  727.4 10.8 %fusion.10 = (f32[1024]{0:T(1024)S(1)}, f32[1024,1536]{1,0:T(8,128)S(1)}) fusion(f32[1536]{0:T(1024)S(1)} %reshape.2461, bf16[2,8,64,1536]{3,1,2,0:T(8,128)(2,1)S(1)} %copy-done.4, f32[1024,1536]{1,0:T(8,128)} %fusion.195, bf16[1024,2048]{1,0:T(8,128)(2,1)S(1)} %bitcast.784, bf16[1536,2048]{1,0:T(8,128)(2,1)} %get-tuple-element.131), kind=kOutput, calls=%fused_computation.19 | convolution fusion | flops 6450314240 | bytes 26224640 | tf_op jit(solution)/shard_map/dot_general | solution.py:556
  752.9 21.8 %add_convert_fusion.3 = bf16[1024,1536]{1,0:T(8,128)(2,1)} fusion(f32[1024,1536]{1,0:T(8,128)} %copy-done.2, bf16[1024,4608]{1,0:T(8,128)(2,1)} %get-tuple-element.134, bf16[4608,1536]{1,0:T(8,128)(2,1)} %all-gather.21.cloned.1.call-done.down_ref), kind=kOutput, calls=%fused_computation.20 | convolution fusion | flops 14498660352 | bytes 33030144 | tf_op jit(solution)/shard_map/dot_general | solution.py:1125
  774.7 14.2 %all-gather.6 = bf16[2112,128]{1,0:T(8,128)(2,1)S(1)} all-gather(bf16[528,128]{1,0:T(8,128)(2,1)} %reduce-scatter.6.cloned.1.call-done), channel_id=8, replica_groups=mesh['grp'=4,'seq'=8] {'grp'}, dimensions={0}, use_global_device_ids=true | all-gather | bytes 675840 | tf_op jit(solution)/shard_map/all_gather | solution.py:1099
  806.3 10.6 %all-gather.7 = bf16[1024,384]{1,0:T(8,128)(2,1)S(1)} all-gather(bf16[256,384]{1,0:T(8,128)(2,1)S(1)} %fusion.72), channel_id=9, replica_groups=mesh['grp'=4,'seq'=8] {'grp'}, dimensions={0}, use_global_device_ids=true | all-gather | bytes 983040 | tf_op jit(solution)/shard_map/all_gather | solution.py:887
  820.4 11.7 %all-gather.4 = bf16[768,512]{1,0:T(8,128)(2,1)S(1)} all-gather(bf16[192,512]{1,0:T(8,128)(2,1)S(1)} %get-tuple-element.204), channel_id=6, replica_groups=mesh['grp'=4,'seq'=8] {'grp'}, dimensions={0}, use_global_device_ids=true | all-gather | bytes 983040 | tf_op jit(solution)/shard_map/all_gather | solution.py:1117
  832.9 10.5 %all-gather.5 = bf16[768,512]{1,0:T(8,128)(2,1)S(1)} all-gather(bf16[192,512]{1,0:T(8,128)(2,1)S(1)} %get-tuple-element.205), channel_id=7, replica_groups=mesh['grp'=4,'seq'=8] {'grp'}, dimensions={0}, use_global_device_ids=true | all-gather | bytes 983040 | tf_op jit(solution)/shard_map/all_gather | solution.py:1117
  (435 shorter events, 193.0 us)
Async XLA Ops:
  7.2 49.1 %all-gather.17.cloned.1.call-start = ((), (), s32[]{:S(2)}) async-start(), calls=%async_computation.3 | async-start | bytes 1179648 | tf_op jit(solution)/shard_map/all_gather | solution.py:957
  7.9 128.8 %all-gather.25.cloned.1.call-start = ((), (), s32[]{:S(2)}) async-start(), calls=%async_computation.10 | async-start | bytes 4423680 | tf_op jit(solution)/shard_map/all_gather | solution.py:670
  10.4 44.2 %collective-permute-start.2 = (bf16[192,1024]{1,0:T(8,128)(2,1)}, bf16[192,1024]{1,0:T(8,128)(2,1)}, u32[]{:S(2)}, u32[]{:S(2)}) collective-permute-start(bf16[192,1024]{1,0:T(8,128)(2,1)} %constant_dynamic-slice_fusion.15), channel_id=1, source_target_pairs={{0,2},{1,3},{2,4},{3,5},{4,6},{5,7},{6,0},{7,1},{8,10},{9,11},{10,... | collective-permute-start | bytes 1179656 | tf_op jit(solution)/shard_map/ppermute | solution.py:673
  12.0 40.8 %collective-permute-start.1 = (bf16[192,1024]{1,0:T(8,128)(2,1)}, bf16[192,1024]{1,0:T(8,128)(2,1)}, u32[]{:S(2)}, u32[]{:S(2)}) collective-permute-start(bf16[192,1024]{1,0:T(8,128)(2,1)} %constant_dynamic-slice_fusion.15), channel_id=1, source_target_pairs={{0,4},{1,5},{2,6},{3,7},{4,0},{5,1},{6,2},{7,3},{8,12},{9,13},{10,... | collective-permute-start | bytes 1179656 | tf_op jit(solution)/shard_map/ppermute | solution.py:673
  56.4 207.6 %all-gather.19.cloned.1.call-start = ((), (), s32[]{:S(2)}) async-start(), calls=%async_computation.4 | async-start | bytes 6488064 | tf_op jit(solution)/shard_map/all_gather | solution.py:524
  58.1 296.9 %all-gather.21.cloned.1.call-start = ((), (), s32[]{:S(2)}) async-start(), calls=%async_computation.5 | async-start | bytes 14598144 | tf_op jit(solution)/shard_map/all_gather | solution.py:524
  59.0 495.6 %reduce-scatter.4.cloned.1.call-start = ((), (), s32[]{:S(2)}) async-start(), calls=%async_computation.6 | async-start | bytes 14598144 | tf_op jit(solution)/shard_map/reduce_scatter | solution.py:1009
  59.0 27.2 %collective-permute-start.4 = (bf16[576,1024]{1,0:T(8,128)(2,1)}, bf16[576,1024]{1,0:T(8,128)(2,1)}, u32[]{:S(2)}, u32[]{:S(2)}) collective-permute-start(bf16[576,1024]{1,0:T(8,128)(2,1)} %constant_dynamic-update-slice_fusion.refs_1_), channel_id=1, source_target_pairs={{0,16},{8,24},{16,0},{24,8},{1,17},{9,25},{17,1},{25,9},{2,18},{10... | collective-permute-start | bytes 3538952 | tf_op jit(solution)/shard_map/ppermute | solution.py:689
  60.6 27.3 %collective-permute-start.3 = (bf16[576,1024]{1,0:T(8,128)(2,1)}, bf16[576,1024]{1,0:T(8,128)(2,1)}, u32[]{:S(2)}, u32[]{:S(2)}) collective-permute-start(bf16[576,1024]{1,0:T(8,128)(2,1)} %constant_dynamic-update-slice_fusion.refs_1_), channel_id=1, source_target_pairs={{0,8},{8,0},{16,24},{24,16},{1,9},{9,1},{17,25},{25,17},{2,10},{10... | collective-permute-start | bytes 3538952 | tf_op jit(solution)/shard_map/ppermute | solution.py:688
  61.1 30.3 %collective-permute-start.8 = (bf16[576,1024]{1,0:T(8,128)(2,1)}, bf16[576,1024]{1,0:T(8,128)(2,1)S(1)}, u32[]{:S(2)}, u32[]{:S(2)}) collective-permute-start(bf16[576,1024]{1,0:T(8,128)(2,1)} %constant_dynamic-update-slice_fusion.refs_1_), channel_id=1, source_target_pairs={{0,1},{1,0},{2,3},{3,2},{4,5},{5,4},{6,7},{7,6},{8,9},{9,8},{10,11... | collective-permute-start | bytes 3538952 | tf_op jit(solution)/shard_map/ppermute | solution.py:706
  61.1 61.1 %collective-permute-start.7 = (bf16[192,4096]{1,0:T(8,128)(2,1)S(1)}, bf16[192,4096]{1,0:T(8,128)(2,1)}, u32[]{:S(2)}, u32[]{:S(2)}) collective-permute-start(bf16[192,4096]{1,0:T(8,128)(2,1)S(1)} %copy-done.48), channel_id=1, source_target_pairs={{0,1},{1,0},{2,3},{3,2},{4,5},{5,4},{6,7},{7,6},{8,9},{9,8},{10,11... | collective-permute-start | bytes 4718600 | tf_op jit(solution)/shard_map/ppermute | solution.py:706
  91.4 33.4 %collective-permute-start.10 = (bf16[576,1024]{1,0:T(8,128)(2,1)}, bf16[576,1024]{1,0:T(8,128)(2,1)}, u32[]{:S(2)}, u32[]{:S(2)}) collective-permute-start(bf16[576,1024]{1,0:T(8,128)(2,1)} %collective-permute-done.4.refs_3_), channel_id=1, source_target_pairs={{0,1},{1,0},{2,3},{3,2},{4,5},{5,4},{6,7},{7,6},{8,9},{9,8},{10,11... | collective-permute-start | bytes 3538952 | tf_op jit(solution)/shard_map/ppermute | solution.py:706
  91.4 33.4 %collective-permute-start.9 = (bf16[576,1024]{1,0:T(8,128)(2,1)}, bf16[576,1024]{1,0:T(8,128)(2,1)}, u32[]{:S(2)}, u32[]{:S(2)}) collective-permute-start(bf16[576,1024]{1,0:T(8,128)(2,1)} %collective-permute-done.3.refs_2_), channel_id=1, source_target_pairs={{0,1},{1,0},{2,3},{3,2},{4,5},{5,4},{6,7},{7,6},{8,9},{9,8},{10,11... | collective-permute-start | bytes 3538952 | tf_op jit(solution)/shard_map/ppermute | solution.py:706
  122.3 102.5 %collective-permute-start.19 = (bf16[192,9216]{1,0:T(8,128)(2,1)}, bf16[192,9216]{1,0:T(8,128)(2,1)}, u32[]{:S(2)}, u32[]{:S(2)}) collective-permute-start(bf16[192,9216]{1,0:T(8,128)(2,1)} %refs_0_.5), channel_id=1, source_target_pairs={{0,1},{1,0},{2,3},{3,2},{4,5},{5,4},{6,7},{7,6},{8,9},{9,8},{10,11... | collective-permute-start | bytes 10616840 | tf_op jit(solution)/shard_map/ppermute | solution.py:706
  140.3 74.9 %collective-permute-start.16 = (bf16[576,2304]{1,0:T(8,128)(2,1)}, bf16[576,2304]{1,0:T(8,128)(2,1)}, u32[]{:S(2)}, u32[]{:S(2)}) collective-permute-start(bf16[576,2304]{1,0:T(8,128)(2,1)} %pad_maximum_fusion.3.refs_1_), channel_id=1, source_target_pairs={{0,16},{8,24},{16,0},{24,8},{1,17},{9,25},{17,1},{25,9},{2,18},{10... | collective-permute-start | bytes 7962632 | tf_op jit(solution)/shard_map/ppermute | solution.py:689
  141.1 76.7 %collective-permute-start.15 = (bf16[576,2304]{1,0:T(8,128)(2,1)}, bf16[576,2304]{1,0:T(8,128)(2,1)}, u32[]{:S(2)}, u32[]{:S(2)}) collective-permute-start(bf16[576,2304]{1,0:T(8,128)(2,1)} %pad_maximum_fusion.3.refs_1_), channel_id=1, source_target_pairs={{0,8},{8,0},{16,24},{24,16},{1,9},{9,1},{17,25},{25,17},{2,10},{10... | collective-permute-start | bytes 7962632 | tf_op jit(solution)/shard_map/ppermute | solution.py:688
  220.3 38.3 %collective-permute-start.18 = (bf16[288,2304]{1,0:T(8,128)(2,1)}, bf16[288,2304]{1,0:T(8,128)(2,1)}, u32[]{:S(2)}, u32[]{:S(2)}) collective-permute-start(bf16[288,2304]{1,0:T(8,128)(2,1)} %slice.416), channel_id=1, source_target_pairs={{0,16},{8,24},{16,0},{24,8},{1,17},{9,25},{17,1},{25,9},{2,18},{10... | collective-permute-start | bytes 3981320 | tf_op jit(solution)/shard_map/ppermute | solution.py:704
  222.8 41.1 %collective-permute-start.17 = (bf16[288,2304]{1,0:T(8,128)(2,1)S(1)}, bf16[288,2304]{1,0:T(8,128)(2,1)}, u32[]{:S(2)}, u32[]{:S(2)}) collective-permute-start(bf16[288,2304]{1,0:T(8,128)(2,1)S(1)} %slice.415), channel_id=1, source_target_pairs={{0,8},{8,0},{16,24},{24,16},{1,9},{9,1},{17,25},{25,17},{2,10},{10... | collective-permute-start | bytes 3981320 | tf_op jit(solution)/shard_map/ppermute | solution.py:703
  224.2 57.4 %collective-permute-start.20 = (bf16[576,2304]{1,0:T(8,128)(2,1)}, bf16[576,2304]{1,0:T(8,128)(2,1)}, u32[]{:S(2)}, u32[]{:S(2)}) collective-permute-start(bf16[576,2304]{1,0:T(8,128)(2,1)} %pad_maximum_fusion.3.refs_1_), channel_id=1, source_target_pairs={{0,1},{1,0},{2,3},{3,2},{4,5},{5,4},{6,7},{7,6},{8,9},{9,8},{10,11... | collective-permute-start | bytes 7962632 | tf_op jit(solution)/shard_map/ppermute | solution.py:706
  224.6 57.1 %collective-permute-start.22 = (bf16[576,2304]{1,0:T(8,128)(2,1)}, bf16[576,2304]{1,0:T(8,128)(2,1)}, u32[]{:S(2)}, u32[]{:S(2)}) collective-permute-start(bf16[576,2304]{1,0:T(8,128)(2,1)} %collective-permute-done.16.refs_3_), channel_id=1, source_target_pairs={{0,1},{1,0},{2,3},{3,2},{4,5},{5,4},{6,7},{7,6},{8,9},{9,8},{10,11... | collective-permute-start | bytes 7962632 | tf_op jit(solution)/shard_map/ppermute | solution.py:706
  224.8 57.0 %collective-permute-start.21 = (bf16[576,2304]{1,0:T(8,128)(2,1)}, bf16[576,2304]{1,0:T(8,128)(2,1)}, u32[]{:S(2)}, u32[]{:S(2)}) collective-permute-start(bf16[576,2304]{1,0:T(8,128)(2,1)} %collective-permute-done.15.refs_2_), channel_id=1, source_target_pairs={{0,1},{1,0},{2,3},{3,2},{4,5},{5,4},{6,7},{7,6},{8,9},{9,8},{10,11... | collective-permute-start | bytes 7962632 | tf_op jit(solution)/shard_map/ppermute | solution.py:706
  354.9 254.6 %all-gather.23.cloned.1.call-start = ((), (), s32[]{:S(2)}) async-start(), calls=%async_computation.7 | async-start | bytes 2211840 | tf_op jit(solution)/shard_map/all_gather | solution.py:1035
  390.3 28.1 %collective-permute-start.25 = (bf16[768,2304]{1,0:T(8,128)(2,1)}, bf16[768,2304]{1,0:T(8,128)(2,1)}, u32[]{:S(2)}, u32[]{:S(2)}) collective-permute-start(bf16[768,2304]{1,0:T(8,128)(2,1)} %convolution_convert_fusion.4), channel_id=1, source_target_pairs={{0,1},{1,0},{2,3},{3,2},{4,5},{5,4},{6,7},{7,6},{8,9},{9,8},{10,11... | collective-permute-start | bytes 10616840 | tf_op jit(solution)/shard_map/ppermute | solution.py:811
  404.6 204.9 %collective-permute-start.30 = (bf16[768,2304]{1,0:T(8,128)(2,1)}, bf16[768,2304]{1,0:T(8,128)(2,1)}, u32[]{:S(2)}, u32[]{:S(2)}) collective-permute-start(bf16[768,2304]{1,0:T(8,128)(2,1)} %convolution_convert_fusion.1), channel_id=1, source_target_pairs={{0,1},{1,0},{2,3},{3,2},{4,5},{5,4},{6,7},{7,6},{8,9},{9,8},{10,11... | collective-permute-start | bytes 10616840 | tf_op jit(solution)/shard_map/ppermute | solution.py:811
  412.2 85.7 %collective-permute-start.29 = (bf16[768,2304]{1,0:T(8,128)(2,1)}, bf16[768,2304]{1,0:T(8,128)(2,1)}, u32[]{:S(2)}, u32[]{:S(2)}) collective-permute-start(bf16[768,2304]{1,0:T(8,128)(2,1)} %convolution_convert_fusion.2), channel_id=1, source_target_pairs={{0,1},{1,0},{2,3},{3,2},{4,5},{5,4},{6,7},{7,6},{8,9},{9,8},{10,11... | collective-permute-start | bytes 10616840 | tf_op jit(solution)/shard_map/ppermute | solution.py:811
  417.8 70.3 %collective-permute-start.26 = (bf16[768,2304]{1,0:T(8,128)(2,1)}, bf16[768,2304]{1,0:T(8,128)(2,1)}, u32[]{:S(2)}, u32[]{:S(2)}) collective-permute-start(bf16[768,2304]{1,0:T(8,128)(2,1)} %convolution_convert_fusion.3), channel_id=1, source_target_pairs={{0,1},{1,0},{2,3},{3,2},{4,5},{5,4},{6,7},{7,6},{8,9},{9,8},{10,11... | collective-permute-start | bytes 10616840 | tf_op jit(solution)/shard_map/ppermute | solution.py:811
  423.2 63.7 %collective-permute-start.27 = (bf16[384,2304]{1,0:T(8,128)(2,1)}, bf16[384,2304]{1,0:T(8,128)(2,1)}, u32[]{:S(2)}, u32[]{:S(2)}) collective-permute-start(bf16[384,2304]{1,0:T(8,128)(2,1)} %fusion.43), channel_id=1, source_target_pairs={{0,8},{8,0},{16,24},{24,16},{1,9},{9,1},{17,25},{25,17},{2,10},{10... | collective-permute-start | bytes 5308424 | tf_op jit(solution)/shard_map/ppermute | solution.py:817
  429.4 58.7 %collective-permute-start.28 = (bf16[384,2304]{1,0:T(8,128)(2,1)}, bf16[384,2304]{1,0:T(8,128)(2,1)}, u32[]{:S(2)}, u32[]{:S(2)}) collective-permute-start(bf16[384,2304]{1,0:T(8,128)(2,1)} %fusion.40), channel_id=1, source_target_pairs={{0,16},{8,24},{16,0},{24,8},{1,17},{9,25},{17,1},{25,9},{2,18},{10... | collective-permute-start | bytes 5308424 | tf_op jit(solution)/shard_map/ppermute | solution.py:818
  497.3 106.1 %collective-permute-start.31 = (bf16[768,2304]{1,0:T(8,128)(2,1)}, bf16[768,2304]{1,0:T(8,128)(2,1)}, u32[]{:S(2)}, u32[]{:S(2)}) collective-permute-start(bf16[768,2304]{1,0:T(8,128)(2,1)} %add_convert_fusion.2), channel_id=1, source_target_pairs={{0,8},{8,0},{16,24},{24,16},{1,9},{9,1},{17,25},{25,17},{2,10},{10... | collective-permute-start | bytes 10616840 | tf_op jit(solution)/shard_map/ppermute | solution.py:838
  508.4 100.6 %collective-permute-start.32 = (bf16[768,2304]{1,0:T(8,128)(2,1)}, bf16[768,2304]{1,0:T(8,128)(2,1)}, u32[]{:S(2)}, u32[]{:S(2)}) collective-permute-start(bf16[768,2304]{1,0:T(8,128)(2,1)} %add_convert_fusion.1), channel_id=1, source_target_pairs={{0,16},{8,24},{16,0},{24,8},{1,17},{9,25},{17,1},{25,9},{2,18},{10... | collective-permute-start | bytes 10616840 | tf_op jit(solution)/shard_map/ppermute | solution.py:839
  554.6 198.2 %reduce-scatter.8.cloned.1.call-start = ((), (), s32[]{:S(2)}) async-start(), calls=%async_computation.9 | async-start | bytes 4423680 | tf_op jit(solution)/shard_map/reduce_scatter | solution.py:868
  570.6 24.5 %collective-permute-start.34 = (bf16[768,2048]{1,0:T(8,128)(2,1)}, bf16[768,2048]{1,0:T(8,128)(2,1)}, u32[]{:S(2)}, u32[]{:S(2)}) collective-permute-start(bf16[768,2048]{1,0:T(8,128)(2,1)} %convolution_convert_fusion.7), channel_id=1, source_target_pairs={{0,1},{1,0},{2,3},{3,2},{4,5},{5,4},{6,7},{7,6},{8,9},{9,8},{10,11... | collective-permute-start | bytes 9437192 | tf_op jit(solution)/shard_map/ppermute | solution.py:807
  593.9 72.9 %collective-permute-start.37 = (bf16[512,384]{1,0:T(8,128)(2,1)}, bf16[512,384]{1,0:T(8,128)(2,1)}, u32[]{:S(2)}, u32[]{:S(2)}) collective-permute-start(bf16[512,384]{1,0:T(8,128)(2,1)} %get-tuple-element.192), channel_id=1, source_target_pairs={{0,16},{8,24},{16,0},{24,8},{1,17},{9,25},{17,1},{25,9},{2,18},{10... | collective-permute-start | bytes 1179656 | tf_op jit(solution)/shard_map/ppermute | solution.py:818
  595.1 71.8 %collective-permute-start.36 = (bf16[512,384]{1,0:T(8,128)(2,1)}, bf16[512,384]{1,0:T(8,128)(2,1)}, u32[]{:S(2)}, u32[]{:S(2)}) collective-permute-start(bf16[512,384]{1,0:T(8,128)(2,1)} %get-tuple-element.193), channel_id=1, source_target_pairs={{0,8},{8,0},{16,24},{24,16},{1,9},{9,1},{17,25},{25,17},{2,10},{10... | collective-permute-start | bytes 1179656 | tf_op jit(solution)/shard_map/ppermute | solution.py:817
  603.4 65.8 %collective-permute-start.39 = (bf16[384,512]{1,0:T(8,128)(2,1)}, bf16[384,512]{1,0:T(8,128)(2,1)}, u32[]{:S(2)}, u32[]{:S(2)}) collective-permute-start(bf16[384,512]{1,0:T(8,128)(2,1)} %get-tuple-element.190), channel_id=1, source_target_pairs={{0,16},{8,24},{16,0},{24,8},{1,17},{9,25},{17,1},{25,9},{2,18},{10... | collective-permute-start | bytes 1179656 | tf_op jit(solution)/shard_map/ppermute | solution.py:818
  609.1 60.1 %collective-permute-start.38 = (bf16[384,512]{1,0:T(8,128)(2,1)}, bf16[384,512]{1,0:T(8,128)(2,1)}, u32[]{:S(2)}, u32[]{:S(2)}) collective-permute-start(bf16[384,512]{1,0:T(8,128)(2,1)} %get-tuple-element.191), channel_id=1, source_target_pairs={{0,8},{8,0},{16,24},{24,16},{1,9},{9,1},{17,25},{25,17},{2,10},{10... | collective-permute-start | bytes 1179656 | tf_op jit(solution)/shard_map/ppermute | solution.py:817
  620.7 154.0 %reduce-scatter.6.cloned.1.call-start = ((), (), s32[]{:S(2)}) async-start(), calls=%async_computation.8 | async-start | bytes 1216512 | tf_op jit(solution)/shard_map/reduce_scatter | solution.py:1095
  696.4 49.5 %collective-permute-start.51 = (bf16[1024,384]{1,0:T(8,128)(2,1)}, bf16[1024,384]{1,0:T(8,128)(2,1)}, u32[]{:S(2)}, u32[]{:S(2)}) collective-permute-start(bf16[1024,384]{1,0:T(8,128)(2,1)} %get-tuple-element.188), channel_id=1, source_target_pairs={{0,16},{8,24},{16,0},{24,8},{1,17},{9,25},{17,1},{25,9},{2,18},{10... | collective-permute-start | bytes 2359304 | tf_op jit(solution)/shard_map/ppermute | solution.py:839
  698.2 47.7 %collective-permute-start.50 = (bf16[1024,384]{1,0:T(8,128)(2,1)}, bf16[1024,384]{1,0:T(8,128)(2,1)}, u32[]{:S(2)}, u32[]{:S(2)}) collective-permute-start(bf16[1024,384]{1,0:T(8,128)(2,1)} %get-tuple-element.189), channel_id=1, source_target_pairs={{0,8},{8,0},{16,24},{24,16},{1,9},{9,1},{17,25},{25,17},{2,10},{10... | collective-permute-start | bytes 2359304 | tf_op jit(solution)/shard_map/ppermute | solution.py:838
  703.9 142.5 %all-gather.27.cloned.1.call-start = ((), (), s32[]{:S(2)}) async-start(), calls=%async_computation.11 | async-start | bytes 4423680 | tf_op jit(solution)/shard_map/all_gather | solution.py:887
  744.5 44.5 %collective-permute-start.44 = (bf16[768,512]{1,0:T(8,128)(2,1)}, bf16[768,512]{1,0:T(8,128)(2,1)S(1)}, u32[]{:S(2)}, u32[]{:S(2)}) collective-permute-start(bf16[768,512]{1,0:T(8,128)(2,1)} %get-tuple-element.182), channel_id=1, source_target_pairs={{0,16},{8,24},{16,0},{24,8},{1,17},{9,25},{17,1},{25,9},{2,18},{10... | collective-permute-start | bytes 2359304 | tf_op jit(solution)/shard_map/ppermute | solution.py:839
  744.8 44.2 %collective-permute-start.43 = (bf16[768,512]{1,0:T(8,128)(2,1)}, bf16[768,512]{1,0:T(8,128)(2,1)}, u32[]{:S(2)}, u32[]{:S(2)}) collective-permute-start(bf16[768,512]{1,0:T(8,128)(2,1)} %get-tuple-element.183), channel_id=1, source_target_pairs={{0,8},{8,0},{16,24},{24,16},{1,9},{9,1},{17,25},{25,17},{2,10},{10... | collective-permute-start | bytes 2359304 | tf_op jit(solution)/shard_map/ppermute | solution.py:838
  748.7 45.4 %collective-permute-start.52 = (bf16[256,384]{1,0:T(8,128)(2,1)}, bf16[256,384]{1,0:T(8,128)(2,1)S(1)}, u32[]{:S(2)}, u32[]{:S(2)}) collective-permute-start(bf16[256,384]{1,0:T(8,128)(2,1)} %get-tuple-element.201), channel_id=1, source_target_pairs={{0,2},{1,3},{2,4},{3,5},{4,6},{5,7},{6,0},{7,1},{8,10},{9,11},{10,... | collective-permute-start | bytes 589832 | tf_op jit(solution)/shard_map/ppermute | solution.py:857
  750.1 55.1 %collective-permute-start.54 = (bf16[256,384]{1,0:T(8,128)(2,1)}, bf16[256,384]{1,0:T(8,128)(2,1)}, u32[]{:S(2)}, u32[]{:S(2)}) collective-permute-start(bf16[256,384]{1,0:T(8,128)(2,1)} %get-tuple-element.202), channel_id=1, source_target_pairs={{0,6},{1,7},{2,0},{3,1},{4,2},{5,3},{6,4},{7,5},{8,14},{9,15},{10,... | collective-permute-start | bytes 589832 | tf_op jit(solution)/shard_map/ppermute | solution.py:857
  750.7 54.5 %collective-permute-start.53 = (bf16[256,384]{1,0:T(8,128)(2,1)}, bf16[256,384]{1,0:T(8,128)(2,1)}, u32[]{:S(2)}, u32[]{:S(2)}) collective-permute-start(bf16[256,384]{1,0:T(8,128)(2,1)} %get-tuple-element.203), channel_id=1, source_target_pairs={{0,4},{1,5},{2,6},{3,7},{4,0},{5,1},{6,2},{7,3},{8,12},{9,13},{10,... | collective-permute-start | bytes 589832 | tf_op jit(solution)/shard_map/ppermute | solution.py:857
  792.1 26.7 %collective-permute-start.47 = (bf16[192,1024]{1,0:T(8,128)(2,1)}, bf16[192,1024]{1,0:T(8,128)(2,1)}, u32[]{:S(2)}, u32[]{:S(2)}) collective-permute-start(bf16[192,1024]{1,0:T(8,128)(2,1)} %get-tuple-element.198), channel_id=1, source_target_pairs={{0,2},{1,3},{2,4},{3,5},{4,6},{5,7},{6,0},{7,1},{8,10},{9,11},{10,... | collective-permute-start | bytes 1179656 | tf_op jit(solution)/shard_map/ppermute | solution.py:857
  792.1 26.7 %collective-permute-start.49 = (bf16[192,1024]{1,0:T(8,128)(2,1)}, bf16[192,1024]{1,0:T(8,128)(2,1)}, u32[]{:S(2)}, u32[]{:S(2)}) collective-permute-start(bf16[192,1024]{1,0:T(8,128)(2,1)} %get-tuple-element.199), channel_id=1, source_target_pairs={{0,6},{1,7},{2,0},{3,1},{4,2},{5,3},{6,4},{7,5},{8,14},{9,15},{10,... | collective-permute-start | bytes 1179656 | tf_op jit(solution)/shard_map/ppermute | solution.py:857
  794.1 24.7 %collective-permute-start.48 = (bf16[192,1024]{1,0:T(8,128)(2,1)S(1)}, bf16[192,1024]{1,0:T(8,128)(2,1)}, u32[]{:S(2)}, u32[]{:S(2)}) collective-permute-start(bf16[192,1024]{1,0:T(8,128)(2,1)S(1)} %get-tuple-element.200), channel_id=1, source_target_pairs={{0,4},{1,5},{2,6},{3,7},{4,0},{5,1},{6,2},{7,3},{8,12},{9,13},{10,... | collective-permute-start | bytes 1179656 | tf_op jit(solution)/shard_map/ppermute | solution.py:857
  (112 other events, 1691.1 us)
Sparse Core Ops, SparseCore 0:
  9.6 38.9 all-gather.16
  56.5 72.0 all-gather.24
  132.0 85.5 all-gather.18
  220.4 109.4 all-gather.20
  355.0 198.1 reduce-scatter.3
  554.9 47.5 all-gather.22
  620.8 67.0 reduce-scatter.7
  704.0 26.4 reduce-scatter.5
  753.0 49.5 all-gather.26
